TPU v7x, 128 devices: a whole 4x4x4 slice. The times are simulated.
128 devices in a mesh: wide: 16 (over z, y), narrow: 8 (over x, core).
Axes of the slice: x: 4, y: 4, z: 4, core: 2. Of those that a mesh axis runs over, the one named last changes fastest.
Arguments:
- grid_feat: bfloat16 [1048576, 227], P(('wide', 'narrow')), may hold values from -6 to 6
- grid_send: int32 [128, 128], P(('wide', 'narrow')), may hold values from 0 to 127, each once within a row
- w_embed: bfloat16 [227, 512], replicated, may hold values from -0.375 to 0.375
- g2m_src: int32 [2048, 8], P(('wide', 'narrow')), may hold values from 0 to 127
- g2m_coef: bfloat16 [2048, 8, 64, 64], P(('wide', 'narrow')), may hold values from -0.25 to 0.25
- mesh_src: int32 [2048, 6], P(('wide', 'narrow')), may hold values from 0 to 31
- mesh_coef: bfloat16 [2048, 6, 64, 64], P(('wide', 'narrow')), may hold values from -0.3125 to 0.3125
- halo_send: int32 [128, 4], P(('wide', 'narrow')), may hold values from 0 to 15
- message_weight: bfloat16 [2, 512, 512], replicated, may hold values from -0.25 to 0.25
- update_weight: bfloat16 [2, 512, 512], replicated, may hold values from -0.25 to 0.25
- cotangent: bfloat16 [131072, 512], P(('wide', 'narrow')), may hold values from -6 to 6
Outputs:
- mesh_out: bfloat16 [131072, 512], P(('wide', 'narrow'))
- d_embed: float32 [227, 512], replicated
- message_weight_gradient: float32 [2, 512, 512], replicated
- update_weight_gradient: float32 [2, 512, 512], replicated
Inputs may be any that keep to these rules, and one draw needn't show every extreme that they name: `grid_send`: each row names every local grid block once. `g2m_src`: an index into the device's received grid blocks. `mesh_src`: an index into the device's own blocks followed by its four halo groups. `halo_send`: a local mesh block of the device.
All inputs are finite; a program needn't handle non-finite values.
Results may differ from a plain program's by a relative error of at most 0.017.
Values may be sent and summed in bfloat16 or wider, within the bound.
No kernel may reach another device: no remote copies, remote signals or barrier semaphores. Data moves between devices by JAX's collectives and lax.ppermute only.
A program may use at most 192 MiB of HBM per device.

v0:
```python
import jax
import jax.numpy as jnp
from jax import lax
from jax.sharding import PartitionSpec as P

CHAN = 227
LATENT_WIDTH = 512
BLOCK = 64
GB_DEV = 128
MB_DEV = 16
HB = 4
PROCESSOR_LAYERS = 2


def from_behind(value, axis, steps):
    count = lax.axis_size(axis)
    pairs = [(source, (source + steps) % count) for source in range(count)]
    return lax.ppermute(value, axis, pairs)


def with_halo(x, sides, width):
    for axis, dim in sides:
        devices, length = (lax.axis_size(axis), x.shape[dim])
        up = [(i, (i + 1) % devices) for i in range(devices)]
        down = [(j, i) for i, j in up]
        last = lax.slice_in_dim(x, length - width, length, axis=dim)
        leading = lax.slice_in_dim(x, 0, width, axis=dim)
        before = lax.ppermute(last, axis, up)
        after = lax.ppermute(leading, axis, down)
        x = jnp.concatenate([before, x, after], axis=dim)
    return x


def silu_grad(values):
    sigmoid_v = jax.nn.sigmoid(values)
    return sigmoid_v * (1.0 + values * (1.0 - sigmoid_v))


def transposed(left, right):
    return lax.dot_general(
        left, right, (((0,), (0,)), ((), ())), preferred_element_type=jnp.float32
    )


def mix_blocks(coeffs, source, indices):
    accum_sum = jnp.zeros((coeffs.shape[0], source.shape[1], source.shape[2]), jnp.float32)
    for slot in range(coeffs.shape[1]):
        picked = source[indices[:, slot]]
        accum_sum = accum_sum + jnp.einsum(
            "bij,bjl->bil", coeffs[:, slot], picked, preferred_element_type=jnp.float32
        )
    return accum_sum


def mix_back(coeffs, gradient, indices, block_count):
    lowered = gradient.astype(jnp.bfloat16)
    portions = jnp.einsum("bkji,bjl->bkil", coeffs, lowered, preferred_element_type=jnp.float32)
    flat_parts = portions.reshape(-1, gradient.shape[1], gradient.shape[2])
    return jax.ops.segment_sum(flat_parts, indices.reshape(-1), num_segments=block_count)


def return_wide(portion, step):
    return from_behind(portion.astype(jnp.bfloat16), "wide", step).astype(portion.dtype)


def return_narrow(portion, step):
    return from_behind(portion.astype(jnp.bfloat16), "narrow", step).astype(portion.dtype)


def on_device(
    grid_feat,
    grid_send,
    w_embed,
    g2m_src,
    g2m_coef,
    mesh_src,
    mesh_coef,
    halo_send,
    message_weight,
    update_weight,
    cotangent,
):
    n_devices = lax.axis_size(("wide", "narrow"))
    per_peer = GB_DEV // n_devices
    all_blocks = MB_DEV + 4 * HB
    features = grid_feat.reshape(GB_DEV, BLOCK, CHAN)
    ordered = features[grid_send.reshape(-1)]
    in_rows = ordered.reshape(-1, CHAN)
    pre_enc = jnp.dot(in_rows, w_embed, preferred_element_type=jnp.float32)
    embedded = (
        jax.nn.silu(pre_enc).astype(jnp.bfloat16).reshape(n_devices, per_peer, BLOCK, LATENT_WIDTH)
    )
    received = lax.all_to_all(
        embedded, ("wide", "narrow"), split_axis=0, concat_axis=0, tiled=True
    ).reshape(GB_DEV, BLOCK, LATENT_WIDTH)
    mesh_state = mix_blocks(g2m_coef, received, g2m_src).astype(jnp.bfloat16)
    shown = halo_send.reshape(-1)
    saved = []
    for layer_number in range(PROCESSOR_LAYERS):
        pre_act = jnp.dot(
            mesh_state.reshape(-1, LATENT_WIDTH),
            message_weight[layer_number],
            preferred_element_type=jnp.float32,
        )
        sent = jax.nn.silu(pre_act).astype(jnp.bfloat16).reshape(MB_DEV, BLOCK, LATENT_WIDTH)
        beside_all = with_halo(sent[shown][None, None], (("wide", 0), ("narrow", 1)), 1)
        extended = jnp.concatenate(
            [sent, beside_all[0, 1], beside_all[2, 1], beside_all[1, 0], beside_all[1, 2]], 0
        )
        aggregate = (
            mix_blocks(mesh_coef, extended, mesh_src).astype(jnp.bfloat16).reshape(-1, LATENT_WIDTH)
        )
        update = jnp.dot(aggregate, update_weight[layer_number], preferred_element_type=jnp.float32)
        saved.append((mesh_state, pre_act, aggregate))
        fresh = mesh_state.reshape(-1, LATENT_WIDTH).astype(jnp.float32) + update
        mesh_state = fresh.astype(jnp.bfloat16).reshape(MB_DEV, BLOCK, LATENT_WIDTH)
    gradient = cotangent.reshape(MB_DEV, BLOCK, LATENT_WIDTH).astype(jnp.float32)
    message_weight_gradient = [None] * PROCESSOR_LAYERS
    update_weight_gradient = [None] * PROCESSOR_LAYERS
    one_hot = (shown[:, None] == jnp.arange(MB_DEV, dtype=jnp.int32)[None, :]).astype(jnp.float32)
    for layer_number in reversed(range(PROCESSOR_LAYERS)):
        state_in, pre_act, aggregate = saved[layer_number]
        grad_low = gradient.reshape(-1, LATENT_WIDTH).astype(jnp.bfloat16)
        update_weight_gradient[layer_number] = transposed(aggregate, grad_low)
        grad_agg = jnp.dot(
            grad_low, update_weight[layer_number].T, preferred_element_type=jnp.float32
        )
        grad_ext = mix_back(
            mesh_coef, grad_agg.reshape(MB_DEV, BLOCK, LATENT_WIDTH), mesh_src, all_blocks
        )
        grad_halo = grad_ext[MB_DEV:].reshape(4, HB, BLOCK, LATENT_WIDTH)
        returned = (
            return_wide(grad_halo[0], -1)
            + return_wide(grad_halo[1], 1)
            + (return_narrow(grad_halo[2], -1) + return_narrow(grad_halo[3], 1))
        )
        grad_msg = grad_ext[:MB_DEV] + jnp.einsum(
            "hm,hil->mil", one_hot, returned, precision=lax.Precision.HIGHEST
        )
        own_rows = state_in.reshape(-1, LATENT_WIDTH)
        grad_pre = (grad_msg.reshape(-1, LATENT_WIDTH) * silu_grad(pre_act)).astype(jnp.bfloat16)
        message_weight_gradient[layer_number] = transposed(own_rows, grad_pre)
        carried = jnp.dot(
            grad_pre, message_weight[layer_number].T, preferred_element_type=jnp.float32
        )
        gradient = gradient + carried.reshape(MB_DEV, BLOCK, LATENT_WIDTH)
    grad_table = lax.optimization_barrier(
        mix_back(g2m_coef, gradient, g2m_src, GB_DEV).astype(jnp.bfloat16)
    )
    grad_home = lax.all_to_all(
        grad_table.reshape(n_devices, per_peer, BLOCK, LATENT_WIDTH),
        ("wide", "narrow"),
        split_axis=0,
        concat_axis=0,
        tiled=True,
    ).reshape(-1, LATENT_WIDTH)
    grad_grid = (grad_home.astype(jnp.float32) * silu_grad(pre_enc)).astype(jnp.bfloat16)
    d_embed = transposed(in_rows, grad_grid)
    totals = lax.psum(
        (d_embed, jnp.stack(message_weight_gradient), jnp.stack(update_weight_gradient)),
        ("wide", "narrow"),
    )
    return (mesh_state.reshape(-1, LATENT_WIDTH), totals[0], totals[1], totals[2])


def solution(mesh):
    return jax.shard_map(
        on_device,
        mesh=mesh,
        in_specs=(
            P(("wide", "narrow"), None),
            P(("wide", "narrow"), None),
            P(),
            P(("wide", "narrow"), None),
            P(("wide", "narrow"), None, None, None),
            P(("wide", "narrow"), None),
            P(("wide", "narrow"), None, None, None),
            P(("wide", "narrow"), None),
            P(),
            P(),
            P(("wide", "narrow"), None),
        ),
        out_specs=(P(("wide", "narrow"), None), P(), P(), P()),
        check_vma=False,
    )
```

profile of v0, /device:TPU:1, one launch (start us, length us, event | category | flops | bytes accessed | tf_op | source)
XLA Modules:
  0.0 712.7 jit_solution(1592547176977917908)
XLA Ops:
  8.5 6.3 copy.64
  14.8 5.1 gather_fusion
  19.9 12.9 %multiply_convert_fusion = (bf16[8192,512]{1,0:T(8,128)(2,1)}, f32[8192,512]{1,0:T(8,128)}) fusion(bf16[8192,227]{1,0:T(8,128)(2,1)} %bitcast.290, bf16[227,512]{1,0:T(8,128)(2,1)S(1)} %copy-done), kind=kOutput, calls=%fused_computation.28 | convolution fusion | flops 1925185536 | bytes 29117440 | tf_op jit(solution)/shard_map/dot_general | solution.py:89
  32.8 11.9 %all-to-all-start = ((bf16[128,1,64,512]{3,2,1,0:T(8,128)(2,1)}), bf16[128,1,64,512]{3,2,1,0:T(8,128)(2,1)}, u32[]{:S(2)}, u32[]{:S(2)}) async-start(bf16[128,1,64,512]{3,2,1,0:T(8,128)(2,1)} %bitcast.295), calls=%async_computation | async-start | bytes 16777216 | tf_op jit(solution)/shard_map/all_to_all | solution.py:93
  45.9 8.9 %fusion.3 = f32[16,512,384]{1,2,0} fusion(bf16[16,64,384]{1,2,0:T(8,128)(2,1)S(1)} %bitcast.293, bf16[16,64,512]{2,1,0:T(8,128)(2,1)} %bitcast.298, bf16[2,512,512]{2,1,0:T(8,128)(2,1)} %param.20), kind=kOutput, calls=%fused_computation.55 | convolution fusion | flops 940048384 | bytes 14942208
  54.8 2.5 broadcast.86.clone
  57.2 28.6 %scatter_fusion = f32[32,64,512]{2,1,0:T(8,128)} fusion(f32[32,64,512]{2,1,0:T(8,128)} %broadcast.86.clone, s32[96]{0:T(128)S(1)} %reshape.358, f32[96,64,512]{2,1,0:T(8,128)} %bitcast.288), kind=kCustom, calls=%fused_computation.23 | custom fusion | flops 3145728 | bytes 37749120 | tf_op jit(solution)/shard_map/scatter-add | solution.py:59
  85.8 2.7 convert.13
  89.5 5.6 collective-permute-start.8
  95.1 1.7 collective-permute-start.11
  97.6 46.2 %all-to-all-done = bf16[128,1,64,512]{3,2,1,0:T(8,128)(2,1)} async-done(((bf16[128,1,64,512]{3,2,1,0:T(8,128)(2,1)}), bf16[128,1,64,512]{3,2,1,0:T(8,128)(2,1)}, u32[]{:S(2)}, u32[]{:S(2)}) %all-to-all-start) | async-done | bytes 8388640 | tf_op jit(solution)/shard_map/all_to_all | solution.py:93
  143.9 4.0 gather_fusion.8
  147.9 5.0 gather_fusion.7
  152.8 5.0 gather_fusion.6
  157.8 5.0 gather_fusion.5
  162.8 5.0 gather_fusion.4
  167.8 5.0 gather_fusion.3
  172.8 5.0 gather_fusion.2
  177.7 5.0 gather_fusion.1
  182.7 1.9 fusion.75
  192.7 2.2 multiply_convert_fusion.2
  199.0 3.8 collective-permute-done.1
  202.8 3.2 collective-permute-done
  207.1 9.0 %collective-permute-start.2 = (bf16[3,1,4,64,512]{4,3,2,1,0:T(8,128)(2,1)S(1)}, bf16[3,1,4,64,512]{4,3,2,1,0:T(8,128)(2,1)S(1)}, u32[]{:S(2)}, u32[]{:S(2)}) collective-permute-start(bf16[3,1,4,64,512]{4,3,2,1,0:T(8,128)(2,1)S(1)} %pad_maximum_fusion.2), channel_id=1, source_target_pairs={{0,1},{1,2},{2,3},{3,4},{4,5},{5,6},{6,7},{7,0},{8,9},{9,10},{10,1... | collective-permute-start | bytes 2359304 | tf_op jit(solution)/shard_map/ppermute | solution.py:28
  216.1 2.4 copy_add_fusion.1
  218.6 2.5 copy.85
  221.3 3.8 collective-permute-done.2
  225.1 7.5 %collective-permute-done.3 = bf16[3,1,4,64,512]{4,3,2,1,0:T(8,128)(2,1)S(1)} collective-permute-done((bf16[3,1,4,64,512]{4,3,2,1,0:T(8,128)(2,1)S(1)}, bf16[3,1,4,64,512]{4,3,2,1,0:T(8,128)(2,1)S(1)}, u32[]{:S(2)}, u32[]{:S(2)}) %collective-permute-start.3) | collective-permute-done | bytes 786464 | tf_op jit(solution)/shard_map/ppermute | solution.py:29
  234.8 3.0 fusion.42
  239.4 3.1 fusion.46
  242.5 1.6 gather_fusion.12
  244.1 3.1 fusion.50
  248.8 1.7 gather_fusion.10
  250.5 1.9 fusion.58
  252.4 1.9 fusion.54
  254.5 1.8 add_convert_fusion.2
  258.6 2.4 fusion.2
  263.2 7.7 %fusion.4 = f32[16,512,384]{1,2,0} fusion(bf16[16,64,384]{1,2,0:T(8,128)(2,1)} %bitcast.294, f32[16,64,512]{2,1,0:T(8,128)S(1)} %convert_add_fusion, bf16[2,512,512]{2,1,0:T(8,128)(2,1)S(1)} %copy-done.30), kind=kOutput, calls=%fused_computation.56 | convolution fusion | flops 940572672 | bytes 15990784
  270.9 2.5 broadcast.86
  273.4 28.5 %scatter_fusion.1 = f32[32,64,512]{2,1,0:T(8,128)} fusion(f32[32,64,512]{2,1,0:T(8,128)} %broadcast.86, s32[96]{0:T(128)S(1)} %reshape.358, f32[96,64,512]{2,1,0:T(8,128)} %bitcast.287), kind=kCustom, calls=%fused_computation.24 | custom fusion | flops 3145728 | bytes 37749120 | tf_op jit(solution)/shard_map/scatter-add | solution.py:59
  301.9 2.5 convert.14
  307.5 4.3 copy.90
  311.9 1.8 slice.281
  313.7 3.9 collective-permute-done.13
  317.8 2.4 copy_add_fusion
  322.5 10.4 %fusion.5 = f32[16,512,512]{1,2,0} fusion(bf16[16,64,512]{1,2,0:T(8,128)(2,1)} %bitcast.296, f32[16,64,512]{2,1,0:T(8,128)S(1)} %convert_add_fusion, bf16[16,64,512]{2,1,0:T(8,128)(2,1)S(1)} %bitcast.297, bf16[2,512,512]{2,1,0:T(8,128)(2,1)} %param.19), kind=kOutput, calls=%fused_computation.57 | convolution fusion | flops 1074790400 | bytes 22544384
  333.0 7.9 %broadcast_in_dim.8 = f32[128,64,512]{2,1,0:T(8,128)} broadcast(f32[]{:T(128)} %constant.11.clone.1), dimensions={} | broadcast | bytes 16777220 | tf_op jit(solution)/shard_map/broadcast_in_dim | solution.py:59
  340.9 38.7 %scatter_fusion.2 = f32[128,64,512]{2,1,0:T(8,128)} fusion(f32[128,64,512]{2,1,0:T(8,128)} %broadcast_in_dim.8, s32[128]{0:T(128)S(1)} %reshape.374, f32[128,64,512]{2,1,0:T(8,128)} %bitcast.286), kind=kCustom, calls=%fused_computation.25 | custom fusion | flops 4194304 | bytes 50332160 | tf_op jit(solution)/shard_map/scatter-add | solution.py:59
  379.5 9.1 %convert_element_type.125 = bf16[128,64,512]{2,1,0:T(8,128)(2,1)} convert(f32[128,64,512]{2,1,0:T(8,128)} %scatter_fusion.2) | non-fusion elementwise | flops 4194304 | bytes 25165824 | tf_op jit(solution)/shard_map/convert_element_type | solution.py:148
  388.6 5.8 all-to-all-start.1
  394.4 2.5 gather_fusion.16
  396.9 5.7 collective-permute-start.5
  402.8 2.9 convolution_bitcast_fusion.1
  408.0 83.3 %collective-permute-done.5 = bf16[1,1,4,64,512]{4,3,2,1,0:T(8,128)(2,1)S(1)} collective-permute-done((bf16[1,1,4,64,512]{4,3,2,1,0:T(8,128)(2,1)}, bf16[1,1,4,64,512]{4,3,2,1,0:T(8,128)(2,1)S(1)}, u32[]{:S(2)}, u32[]{:S(2)}) %collective-permute-start.5) | collective-permute-done | bytes 262176 | tf_op jit(solution)/shard_map/ppermute | solution.py:29
  491.3 4.9 collective-permute-done.4
  497.3 5.3 collective-permute-start.6
  504.9 6.7 collective-permute-done.6
  520.8 1.9 fusion.60
  530.9 11.3 %fusion = bf16[8192,512]{1,0:T(8,128)(2,1)S(1)} fusion(f32[8192,512]{1,0:T(8,128)} %get-tuple-element.32, bf16[128,1,64,512]{3,2,1,0:T(8,128)(2,1)} %all-to-all-done.1), kind=kLoop, calls=%fused_computation.27 | loop fusion | flops 41943040 | bytes 33554432 | tf_op jit(solution)/shard_map/convert_element_type | solution.py:157
  542.3 2.9 fusion.120
  546.7 1.7 add_convert_fusion.4
  548.4 150.9 %all-reduce.3.cloned.1.call-done = (f32[227,512]{1,0:T(8,128)}, f32[2,512,512]{2,1,0:T(8,128)}, f32[2,512,512]{2,1,0:T(8,128)}) async-done(((f32[227,512]{1,0:T(8,128)}, f32[2,512,512]{2,1,0:T(8,128)}, f32[2,512,512]{2,1,0:T(8,128)}), (f32[227,512]{1,0:T(8,128)}, f32[2,512,512]{2,1,0:T(8,128)}, f32[2,512,512]{2,1,0:T(8,128)})) %all-reduce.3.cloned.1.call-update) | async-done | bytes 4659216 | tf_op jit(solution)/shard_map/psum | solution.py:159
  699.3 1.8 copy.127
  701.1 3.2 copy.128
  (181 shorter events, 59.5 us)
Async XLA Ops:
  7.2 12.7 %copy-start = (bf16[227,512]{1,0:T(8,128)(2,1)S(1)}, bf16[227,512]{1,0:T(8,128)(2,1)}, u32[]{:S(2)}) copy-start(bf16[227,512]{1,0:T(8,128)(2,1)} %param.13) | copy-start | bytes 697348
  32.8 12.0 %copy-start.41 = (s32[16,6]{0,1:T(8,128)S(1)}, s32[16,6]{0,1:T(8,128)}, u32[]{:S(2)}) copy-start(s32[16,6]{0,1:T(8,128)} %param.16) | copy-start | bytes 1156
  32.8 12.1 %copy-start.5 = (bf16[16,6,64,64]{3,2,1,0:T(8,128)(2,1)S(1)}, bf16[16,6,64,64]{3,2,1,0:T(8,128)(2,1)}, u32[]{:S(2)}) copy-start(bf16[16,6,64,64]{3,2,1,0:T(8,128)(2,1)} %param.17) | copy-start | bytes 2359300
  32.8 111.1 %all-to-all-start = ((bf16[128,1,64,512]{3,2,1,0:T(8,128)(2,1)}), bf16[128,1,64,512]{3,2,1,0:T(8,128)(2,1)}, u32[]{:S(2)}, u32[]{:S(2)}) async-start(bf16[128,1,64,512]{3,2,1,0:T(8,128)(2,1)} %bitcast.295), calls=%async_computation | async-start | bytes 16777216 | tf_op jit(solution)/shard_map/all_to_all | solution.py:93
  45.8 8.9 %copy-start.4 = (bf16[16,6,64,64]{2,3,1,0:T(8,128)(2,1)}, bf16[16,6,64,64]{2,3,1,0:T(8,128)(2,1)S(1)}, u32[]{:S(2)}) copy-start(bf16[16,6,64,64]{2,3,1,0:T(8,128)(2,1)S(1)} %copy.82) | copy-start | bytes 2359300
  85.8 11.2 %copy-start.2 = (f32[32,64,512]{2,1,0:T(8,128)S(1)}, f32[32,64,512]{2,1,0:T(8,128)}, u32[]{:S(2)}) copy-start(f32[32,64,512]{2,1,0:T(8,128)} %scatter_fusion) | copy-start | bytes 12582916
  89.5 106.7 %collective-permute-start.8 = (bf16[4,64,512]{2,1,0:T(8,128)(2,1)}, bf16[4,64,512]{2,1,0:T(8,128)(2,1)}, u32[]{:S(2)}, u32[]{:S(2)}) collective-permute-start(bf16[4,64,512]{2,1,0:T(8,128)(2,1)} %get-tuple-element.13), channel_id=1, source_target_pairs={{0,120},{8,0},{16,8},{24,16},{32,24},{40,32},{48,40},{56,48},{64,5... | collective-permute-start | bytes 786440 | tf_op jit(solution)/shard_map/ppermute | solution.py:18
  95.1 102.6 %collective-permute-start.11 = (bf16[4,64,512]{2,1,0:T(8,128)(2,1)}, bf16[4,64,512]{2,1,0:T(8,128)(2,1)}, u32[]{:S(2)}, u32[]{:S(2)}) collective-permute-start(bf16[4,64,512]{2,1,0:T(8,128)(2,1)} %get-tuple-element.14), channel_id=1, source_target_pairs={{0,1},{1,2},{2,3},{3,4},{4,5},{5,6},{6,7},{7,0},{8,9},{9,10},{10,1... | collective-permute-start | bytes 786440 | tf_op jit(solution)/shard_map/ppermute | solution.py:18
  96.8 100.9 %collective-permute-start.10 = (bf16[4,64,512]{2,1,0:T(8,128)(2,1)}, bf16[4,64,512]{2,1,0:T(8,128)(2,1)}, u32[]{:S(2)}, u32[]{:S(2)}) collective-permute-start(bf16[4,64,512]{2,1,0:T(8,128)(2,1)} %get-tuple-element.15), channel_id=1, source_target_pairs={{0,7},{1,0},{2,1},{3,2},{4,3},{5,4},{6,5},{7,6},{8,15},{9,8},{10,9... | collective-permute-start | bytes 786440 | tf_op jit(solution)/shard_map/ppermute | solution.py:18
  96.8 100.9 %collective-permute-start.9 = (bf16[4,64,512]{2,1,0:T(8,128)(2,1)}, bf16[4,64,512]{2,1,0:T(8,128)(2,1)}, u32[]{:S(2)}, u32[]{:S(2)}) collective-permute-start(bf16[4,64,512]{2,1,0:T(8,128)(2,1)} %get-tuple-element.16), channel_id=1, source_target_pairs={{0,8},{8,16},{16,24},{24,32},{32,40},{40,48},{48,56},{56,64},{64,7... | collective-permute-start | bytes 786440 | tf_op jit(solution)/shard_map/ppermute | solution.py:18
  182.7 2.0 copy-start.10
  182.7 2.2 copy-start.19
  184.9 1.2 copy-start.17
  186.2 1.2 copy-start.15
  187.4 1.2 copy-start.13
  188.6 1.2 copy-start.12
  189.8 1.2 copy-start.11
  191.5 1.2 copy-start.27
  192.4 2.5 copy-start.32
  194.9 21.2 %copy-start.42 = (s32[1,4]{1,0:T(1,128)S(1)}, s32[1,4]{1,0:T(1,128)}, u32[]{:S(2)}) copy-start(s32[1,4]{1,0:T(1,128)} %param.18) | copy-start | bytes 52
  196.2 6.6 collective-permute-start.1
  196.2 9.8 %collective-permute-start = (bf16[1,1,4,64,512]{4,3,2,1,0:T(8,128)(2,1)}, bf16[1,1,4,64,512]{4,3,2,1,0:T(8,128)(2,1)S(1)}, u32[]{:S(2)}, u32[]{:S(2)}) collective-permute-start(bf16[1,1,4,64,512]{4,3,2,1,0:T(8,128)(2,1)} %bitcast.311), channel_id=1, source_target_pairs={{0,8},{8,16},{16,24},{24,32},{32,40},{40,48},{48,56},{56,64},{64,7... | collective-permute-start | bytes 786440 | tf_op jit(solution)/shard_map/ppermute | solution.py:28
  207.1 18.0 %collective-permute-start.2 = (bf16[3,1,4,64,512]{4,3,2,1,0:T(8,128)(2,1)S(1)}, bf16[3,1,4,64,512]{4,3,2,1,0:T(8,128)(2,1)S(1)}, u32[]{:S(2)}, u32[]{:S(2)}) collective-permute-start(bf16[3,1,4,64,512]{4,3,2,1,0:T(8,128)(2,1)S(1)} %pad_maximum_fusion.2), channel_id=1, source_target_pairs={{0,1},{1,2},{2,3},{3,4},{4,5},{5,6},{6,7},{7,0},{8,9},{9,10},{10,1... | collective-permute-start | bytes 2359304 | tf_op jit(solution)/shard_map/ppermute | solution.py:28
  221.1 11.4 %collective-permute-start.3 = (bf16[3,1,4,64,512]{4,3,2,1,0:T(8,128)(2,1)S(1)}, bf16[3,1,4,64,512]{4,3,2,1,0:T(8,128)(2,1)S(1)}, u32[]{:S(2)}, u32[]{:S(2)}) collective-permute-start(bf16[3,1,4,64,512]{4,3,2,1,0:T(8,128)(2,1)S(1)} %pad_maximum_fusion.2), channel_id=1, source_target_pairs={{1,0},{2,1},{3,2},{4,3},{5,4},{6,5},{7,6},{0,7},{9,8},{10,9},{11,1... | collective-permute-start | bytes 2359304 | tf_op jit(solution)/shard_map/ppermute | solution.py:29
  250.5 3.7 copy-start.8
  250.5 3.8 copy-start.9
  252.4 2.2 copy-start.7
  254.5 1.9 copy-start.29
  254.5 1.9 copy-start.33
  256.4 4.6 copy-start.35
  256.4 2.0 copy-start.24
  256.4 2.2 copy-start.28
  258.6 2.4 copy-start.43
  258.6 3.4 copy-start.21
  261.0 1.0 copy-start.37
  262.0 1.2 copy-start.30
  305.4 8.3 %collective-permute-start.12 = (bf16[4,64,512]{2,1,0:T(8,128)(2,1)}, bf16[4,64,512]{2,1,0:T(8,128)(2,1)S(1)}, u32[]{:S(2)}, u32[]{:S(2)}) collective-permute-start(bf16[4,64,512]{2,1,0:T(8,128)(2,1)} %get-tuple-element.7), channel_id=1, source_target_pairs={{0,120},{8,0},{16,8},{24,16},{32,24},{40,32},{48,40},{56,48},{64,5... | collective-permute-start | bytes 786440 | tf_op jit(solution)/shard_map/ppermute | solution.py:18
  305.7 8.0 %collective-permute-start.15 = (bf16[4,64,512]{2,1,0:T(8,128)(2,1)}, bf16[4,64,512]{2,1,0:T(8,128)(2,1)S(1)}, u32[]{:S(2)}, u32[]{:S(2)}) collective-permute-start(bf16[4,64,512]{2,1,0:T(8,128)(2,1)} %get-tuple-element.8), channel_id=1, source_target_pairs={{0,1},{1,2},{2,3},{3,4},{4,5},{5,6},{6,7},{7,0},{8,9},{9,10},{10,1... | collective-permute-start | bytes 786440 | tf_op jit(solution)/shard_map/ppermute | solution.py:18
  305.7 8.0 %collective-permute-start.14 = (bf16[4,64,512]{2,1,0:T(8,128)(2,1)}, bf16[4,64,512]{2,1,0:T(8,128)(2,1)S(1)}, u32[]{:S(2)}, u32[]{:S(2)}) collective-permute-start(bf16[4,64,512]{2,1,0:T(8,128)(2,1)} %get-tuple-element.9), channel_id=1, source_target_pairs={{0,7},{1,0},{2,1},{3,2},{4,3},{5,4},{6,5},{7,6},{8,15},{9,8},{10,9... | collective-permute-start | bytes 786440 | tf_op jit(solution)/shard_map/ppermute | solution.py:18
  306.2 11.5 %collective-permute-start.13 = (bf16[4,64,512]{2,1,0:T(8,128)(2,1)}, bf16[4,64,512]{2,1,0:T(8,128)(2,1)S(1)}, u32[]{:S(2)}, u32[]{:S(2)}) collective-permute-start(bf16[4,64,512]{2,1,0:T(8,128)(2,1)} %get-tuple-element.10), channel_id=1, source_target_pairs={{0,8},{8,16},{16,24},{24,32},{32,40},{40,48},{48,56},{56,64},{64,7... | collective-permute-start | bytes 786440 | tf_op jit(solution)/shard_map/ppermute | solution.py:18
  320.2 1.6 copy-start.23
  388.6 142.3 %all-to-all-start.1 = ((bf16[128,1,64,512]{3,2,1,0:T(8,128)(2,1)}), bf16[128,1,64,512]{3,2,1,0:T(8,128)(2,1)}, u32[]{:S(2)}, u32[]{:S(2)}) async-start(bf16[128,1,64,512]{3,2,1,0:T(8,128)(2,1)} %bitcast.289), calls=%async_computation.1 | async-start | bytes 16777216 | tf_op jit(solution)/shard_map/all_to_all | solution.py:150
  394.4 304.9 %all-reduce.3.cloned.1.call-start = ((), (), s32[]{:S(2)}) async-start(), calls=%async_computation.2 | async-start | bytes 9338880 | tf_op jit(solution)/shard_map/psum | solution.py:159
  396.9 8.8 %copy-start.26 = (bf16[1024,512]{1,0:T(8,128)(2,1)S(1)}, bf16[1024,512]{1,0:T(8,128)(2,1)}, u32[]{:S(2)}) copy-start(bf16[1024,512]{1,0:T(8,128)(2,1)} %get-tuple-element.12) | copy-start | bytes 3145732
  396.9 94.3 %collective-permute-start.5 = (bf16[1,1,4,64,512]{4,3,2,1,0:T(8,128)(2,1)}, bf16[1,1,4,64,512]{4,3,2,1,0:T(8,128)(2,1)S(1)}, u32[]{:S(2)}, u32[]{:S(2)}) collective-permute-start(bf16[1,1,4,64,512]{4,3,2,1,0:T(8,128)(2,1)} %bitcast.313), channel_id=1, source_target_pairs={{8,0},{16,8},{24,16},{32,24},{40,32},{48,40},{56,48},{64,56},{72,6... | collective-permute-start | bytes 786440 | tf_op jit(solution)/shard_map/ppermute | solution.py:29
  402.6 93.5 %collective-permute-start.4 = (bf16[1,1,4,64,512]{4,3,2,1,0:T(8,128)(2,1)}, bf16[1,1,4,64,512]{4,3,2,1,0:T(8,128)(2,1)S(1)}, u32[]{:S(2)}, u32[]{:S(2)}) collective-permute-start(bf16[1,1,4,64,512]{4,3,2,1,0:T(8,128)(2,1)} %bitcast.314), channel_id=1, source_target_pairs={{0,8},{8,16},{16,24},{24,32},{32,40},{40,48},{48,56},{56,64},{64,7... | collective-permute-start | bytes 786440 | tf_op jit(solution)/shard_map/ppermute | solution.py:28
  405.7 1.2 copy-start.38
  405.7 1.5 copy-start.44
  407.3 88.9 %copy-start.36 = (bf16[4,64,512]{2,1,0:T(8,128)(2,1)S(1)}, bf16[4,64,512]{2,1,0:T(8,128)(2,1)}, u32[]{:S(2)}) copy-start(bf16[4,64,512]{2,1,0:T(8,128)(2,1)} %gather_fusion.16) | copy-start | bytes 786436
  407.3 95.3 %copy-start.34 = (bf16[16,512,64]{1,2,0:T(8,128)(2,1)S(1)}, bf16[16,512,64]{1,2,0:T(8,128)(2,1)}, u32[]{:S(2)}) copy-start(bf16[16,512,64]{1,2,0:T(8,128)(2,1)} %copy-done.32) | copy-start | bytes 3145732
  496.3 16.0 %collective-permute-start.7 = (bf16[3,1,4,64,512]{4,3,2,1,0:T(8,128)(2,1)S(1)}, bf16[3,1,4,64,512]{4,3,2,1,0:T(8,128)(2,1)S(1)}, u32[]{:S(2)}, u32[]{:S(2)}) collective-permute-start(bf16[3,1,4,64,512]{4,3,2,1,0:T(8,128)(2,1)S(1)} %pad_maximum_fusion.3), channel_id=1, source_target_pairs={{1,0},{2,1},{3,2},{4,3},{5,4},{6,5},{7,6},{0,7},{9,8},{10,9},{11,1... | collective-permute-start | bytes 2359304 | tf_op jit(solution)/shard_map/ppermute | solution.py:29
  497.3 14.2 %collective-permute-start.6 = (bf16[3,1,4,64,512]{4,3,2,1,0:T(8,128)(2,1)S(1)}, bf16[3,1,4,64,512]{4,3,2,1,0:T(8,128)(2,1)S(1)}, u32[]{:S(2)}, u32[]{:S(2)}) collective-permute-start(bf16[3,1,4,64,512]{4,3,2,1,0:T(8,128)(2,1)S(1)} %pad_maximum_fusion.3), channel_id=1, source_target_pairs={{0,1},{1,2},{2,3},{3,4},{4,5},{5,6},{6,7},{7,0},{8,9},{9,10},{10,1... | collective-permute-start | bytes 2359304 | tf_op jit(solution)/shard_map/ppermute | solution.py:28
  520.8 1.9 copy-start.6
  520.8 2.1 copy-start.20
  522.9 1.2 copy-start.18
  524.1 1.2 copy-start.16
  525.4 1.2 copy-start.14
  527.0 1.2 copy-start.22
  528.2 1.2 copy-start.39
  530.9 11.3 %copy-start.3 = (bf16[128,64,227]{2,1,0:T(8,128)(2,1)S(1)}, bf16[128,64,227]{2,1,0:T(8,128)(2,1)}, u32[]{:S(2)}) copy-start(bf16[128,64,227]{2,1,0:T(8,128)(2,1)} %gather_fusion) | copy-start | bytes 11157508
  545.2 1.2 copy-start.31
  545.2 1.5 copy-start.45
  701.1 3.2 copy-start.25
  701.1 4.6 copy-start.1
  (1 other events, 0.7 us)
Sparse Core Ops, SparseCore 0:
  545.3 153.9 all-reduce.2
where the time goes:
time: 721 us; the launch traced here: 713 us
  waiting for transfers between devices  315 us (44%)
  other arithmetic  129 us (18%)
  local copies, waits for them, and re-layouts  119 us (17%)
  matrix products  84.7 us (12%)
  starting transfers between devices  49.9 us (7%)
  between operations  14.8 us (2%)
    psum x1, waiting for transfers between devices, on_device(): lax.psum((d_embed, jnp.stack(message_weight_gradient), jnp.stack(update_w...  151 us
    scatter-add x3, other arithmetic, mix_back(): jax.ops.segment_sum(flat_parts, indices.reshape(-1), num_segments=block_c...  95.8 us
    ppermute x4, waiting for transfers between devices, with_halo(): after = lax.ppermute(leading, axis, down)  95.2 us
    gather x20, local copies, waits for them, and re-layouts, mix_blocks(): picked = source[indices[:, slot]]  56.1 us
    all_to_all x1, waiting for transfers between devices, on_device(): lax.all_to_all(embedded, ('wide', 'narrow'), split_axis=0, concat_axis=0,...  46.2 us
    unnamed x108, local copies, waits for them, and re-layouts  33.6 us
    unnamed x3, matrix products  27 us
    dot_general x20, matrix products, mix_blocks(): jnp.einsum('bij,bjl->bil', coeffs[:, slot], picked, preferred_element_typ...  24.2 us
  transfers between devices with their start and end apart: 19, of which 11 were waited for; matrix products, arithmetic and copies ran while one was open for 18% of the time, Pallas kernels for 0%

commit v1 on v0

v1 whole, which is shorter than its diff:
```python
import functools

import jax
import jax.numpy as jnp
from jax import lax
from jax.experimental import pallas as pl
from jax.experimental.pallas import tpu as pltpu
from jax.sharding import PartitionSpec as P

CHAN = 227
WIDTH = 512
BLOCK = 64
GRID_BLOCKS = 128
MESH_BLOCKS = 16
SHOWN = 4
G_SLOTS = 8
M_SLOTS = 6
EXTENDED = MESH_BLOCKS + 4 * SHOWN
MESH_ROWS = MESH_BLOCKS * BLOCK
GRID_ROWS = GRID_BLOCKS * BLOCK
SPLIT = 112
PACKED = CHAN - SPLIT
TAIL = 256
AXES = ("wide", "narrow")
BF16 = jnp.bfloat16
F32 = jnp.float32
MIB = 1 << 20

VM = pl.BlockSpec(memory_space=pltpu.VMEM)
SM = pl.BlockSpec(memory_space=pltpu.SMEM)
HBM = pl.BlockSpec(memory_space=pl.ANY)


def kernel_call(body, outs, ins, scratch=(), flops=0, moved=0, limit=56):
    return pl.pallas_call(
        body,
        out_shape=[jax.ShapeDtypeStruct(shape, dtype) for shape, dtype in outs],
        in_specs=ins,
        out_specs=[VM] * len(outs),
        scratch_shapes=list(scratch),
        compiler_params=pltpu.CompilerParams(vmem_limit_bytes=limit * MIB),
        cost_estimate=pl.CostEstimate(flops=flops, bytes_accessed=moved, transcendentals=0),
    )


def times(left, right, left_dim=1, right_dim=0):
    return lax.dot_general(
        left, right, (((left_dim,), (right_dim,)), ((), ())), preferred_element_type=F32
    )


def sigmoid(values):
    return 0.5 * jnp.tanh(0.5 * values) + 0.5


def silu_grad(values):
    s = sigmoid(values)
    return s * (1.0 + values * (1.0 - s))


def swap_halves(tile):
    return jnp.concatenate([tile[:, BLOCK:], tile[:, :BLOCK]], axis=1)


def low_lanes(rows):
    return lax.broadcasted_iota(jnp.int32, (rows, 2 * BLOCK), 1) < BLOCK


def rows_of(block):
    return pl.ds(pl.multiple_of(block * BLOCK, BLOCK), BLOCK)


def chunk(step, size):
    return pl.ds(pl.multiple_of(step * size, size), size)


def pack_body(send, features, out, target):
    def invert(j, carry):
        target[send[0, j]] = j
        return carry

    lax.fori_loop(0, GRID_BLOCKS, invert, 0)
    low = low_lanes(PACKED)

    def pair(i, carry):
        lanes = chunk(i, 2 * BLOCK)
        first = features[0:PACKED, lanes]
        second = features[SPLIT:CHAN, lanes]
        out[target[2 * i]] = jnp.where(low, first, swap_halves(second))
        out[target[2 * i + 1]] = jnp.where(low, swap_halves(first), second)
        return carry

    lax.fori_loop(0, GRID_BLOCKS // 2, pair, 0, unroll=2)


def scatter_back(coeffs_t, gradient, source, table, slots, zero_blocks):
    def clear(i, carry):
        table[i] = jnp.zeros((BLOCK, WIDTH), F32)
        return carry

    lax.fori_loop(0, zero_blocks, clear, 0)

    def one(b, carry):
        parts = times(coeffs_t[b], gradient[rows_of(b), :])
        for k in range(slots):
            at = source[b, k]
            table[at] = table[at] + parts[k * BLOCK : (k + 1) * BLOCK]
        return carry

    lax.fori_loop(0, MESH_BLOCKS, one, 0)


def gather_mix(coeffs, pick, slots, b):
    picked = jnp.concatenate([pick(b, k) for k in range(slots)], axis=0)
    return times(coeffs[b], picked)


def add_returned(own, returned, shown, take):
    for h in range(SHOWN):
        at = shown[0, h]
        extra = (returned[0][h].astype(F32) + returned[1][h].astype(F32)) + (
            returned[2][h].astype(F32) + returned[3][h].astype(F32)
        )
        take[rows_of(at), :] = take[rows_of(at), :] + extra


def write_halo(table, own, halos):
    for i in range(MESH_BLOCKS):
        own[i * BLOCK : (i + 1) * BLOCK, :] = table[i]
    for e in range(4):
        for h in range(SHOWN):
            halos[e][h] = table[MESH_BLOCKS + e * SHOWN + h].astype(BF16)


def early_back_body(source, cot, up, coeffs_t, own, h0, h1, h2, h3, table, lowered):
    def step(c, carry):
        rows = chunk(c, 256)
        lowered[rows, :] = times(cot[rows, :], up[...], 1, 1).astype(BF16)
        return carry

    lax.fori_loop(0, MESH_ROWS // 256, step, 0)
    scatter_back(coeffs_t, lowered, source, table, M_SLOTS, EXTENDED)
    write_halo(table, own, (h0, h1, h2, h3))


def encode_body(source, shown, packed, weight, coeffs, message, points, mesh, sent, mine, embedded):
    low = low_lanes(PACKED)

    def embed(c, carry):
        for p in range(4):
            a = packed[c * 8 + 2 * p]
            b = packed[c * 8 + 2 * p + 1]
            lanes = pl.ds(pl.multiple_of(c * 512 + p * 128, 128), 128)
            points[0:SPLIT, lanes] = jnp.where(low, a, swap_halves(b))[0:SPLIT]
            points[SPLIT:CHAN, lanes] = jnp.where(low, swap_halves(a), b)
        rows = chunk(c, 512)
        pre = times(points[:, rows], weight[...], 0, 0)
        embedded[rows, :] = (pre * sigmoid(pre)).astype(BF16)
        return carry

    lax.fori_loop(0, GRID_ROWS // 512, embed, 0)

    def mix(b, carry):
        pick = lambda b, k: embedded[rows_of(source[b, k]), :]
        mesh[rows_of(b), :] = gather_mix(coeffs, pick, G_SLOTS, b).astype(BF16)
        return carry

    lax.fori_loop(0, MESH_BLOCKS, mix, 0)

    def talk(c, carry):
        rows = chunk(c, 256)
        pre = times(mesh[rows, :], message[...])
        sent[rows, :] = (pre * sigmoid(pre)).astype(BF16)
        return carry

    lax.fori_loop(0, MESH_ROWS // 256, talk, 0)
    for h in range(SHOWN):
        mine[h] = sent[rows_of(shown[0, h]), :]


def slopes_body(points, weight, mesh, message, slope, slope_m):
    pre = times(points[...], weight[...], 0, 0)
    slope[...] = silu_grad(pre).astype(BF16)

    @pl.when(pl.program_id(0) < 4)
    def _():
        slope_m[...] = silu_grad(times(mesh[...], message[...]))


def extend(extended, sent, halos):
    extended[0:MESH_ROWS, :] = sent[...]
    for e in range(4):
        for h in range(SHOWN):
            at = MESH_ROWS + (e * SHOWN + h) * BLOCK
            extended[at : at + BLOCK, :] = halos[e][h]


def middle_body(
    source, shown, sent, n0, n1, n2, n3, coeffs, coeffs_t, mesh, up, message, own, r0, r1, r2, r3,
    cot, aggregate, mesh_1, sent_1, mine, grad_pre, grad_1, own_0, h0, h1, h2, h3,
    extended, table, lowered, grad_msg,
):
    extend(extended, sent, (n0, n1, n2, n3))
    grad_msg[...] = own[...]
    add_returned(own, (r0, r1, r2, r3), shown, grad_msg)

    def mix(b, carry):
        pick = lambda b, k: extended[rows_of(source[b, k]), :]
        aggregate[rows_of(b), :] = gather_mix(coeffs, pick, M_SLOTS, b).astype(BF16)
        return carry

    lax.fori_loop(0, MESH_BLOCKS, mix, 0)

    def step(c, carry):
        rows = chunk(c, 256)
        state = (mesh[rows, :].astype(F32) + times(aggregate[rows, :], up[...])).astype(BF16)
        mesh_1[rows, :] = state
        pre = times(state, message[...])
        s = sigmoid(pre)
        sent_1[rows, :] = (pre * s).astype(BF16)
        gp = (grad_msg[rows, :] * (s * (1.0 + pre * (1.0 - s)))).astype(BF16)
        grad_pre[rows, :] = gp
        g = cot[rows, :].astype(F32) + times(gp, message[...], 1, 1)
        grad_1[rows, :] = g
        lowered[rows, :] = times(g.astype(BF16), up[...], 1, 1).astype(BF16)
        return carry

    lax.fori_loop(0, MESH_ROWS // 256, step, 0)
    for h in range(SHOWN):
        mine[h] = sent_1[rows_of(shown[0, h]), :]
    scatter_back(coeffs_t, lowered, source, table, M_SLOTS, EXTENDED)
    write_halo(table, own_0, (h0, h1, h2, h3))


def two_grads_body(aggregate, grad_1, mesh_1, grad_pre, up_grad, ms_grad):
    up_grad[...] = times(aggregate[...], grad_1[...].astype(BF16), 0, 0).astype(BF16)
    ms_grad[...] = times(mesh_1[...], grad_pre[...], 0, 0).astype(BF16)


def last_body(
    source, sent, n0, n1, n2, n3, coeffs, mesh, up, cot, mesh_out, up_grad, extended, aggregate
):
    extend(extended, sent, (n0, n1, n2, n3))

    def mix(b, carry):
        pick = lambda b, k: extended[rows_of(source[b, k]), :]
        aggregate[rows_of(b), :] = gather_mix(coeffs, pick, M_SLOTS, b).astype(BF16)
        return carry

    lax.fori_loop(0, MESH_BLOCKS, mix, 0)

    def step(c, carry):
        rows = chunk(c, 256)
        update = times(aggregate[rows, :], up[...])
        mesh_out[rows, :] = (mesh[rows, :].astype(F32) + update).astype(BF16)
        return carry

    lax.fori_loop(0, MESH_ROWS // 256, step, 0)
    up_grad[...] = times(aggregate[...], cot[...], 0, 0).astype(BF16)


def final_body(
    source, shown, own, r0, r1, r2, r3, slope_m, grad_1, message, mesh, coeffs_t, slope_hbm,
    points_hbm, grads, slope, points, table, grad_pre, lowered, grad_msg, total, sems,
):
    load_slope = pltpu.make_async_copy(slope_hbm, slope, sems.at[0])
    load_points = pltpu.make_async_copy(points_hbm, points, sems.at[1])
    load_slope.start()
    load_points.start()
    grad_msg[...] = own[...]
    add_returned(own, (r0, r1, r2, r3), shown, grad_msg)

    def step(c, carry):
        rows = chunk(c, 256)
        gp = (grad_msg[rows, :] * slope_m[rows, :]).astype(BF16)
        grad_pre[rows, :] = gp
        lowered[rows, :] = (grad_1[rows, :] + times(gp, message[...], 1, 1)).astype(BF16)
        return carry

    lax.fori_loop(0, MESH_ROWS // 256, step, 0)
    scatter_back(coeffs_t, lowered, source, table, G_SLOTS, GRID_BLOCKS)
    grads[0:WIDTH, :] = times(mesh[...], grad_pre[...], 0, 0).astype(BF16)
    load_slope.wait()
    load_points.wait()
    total[...] = jnp.zeros_like(total)

    def grid_step(c, carry):
        rows = chunk(c, 512)
        grad = table[pl.ds(pl.multiple_of(c * 8, 8), 8)].reshape(512, WIDTH).astype(BF16)
        grad = (grad.astype(F32) * slope[rows, :].astype(F32)).astype(BF16)
        total[0:CHAN, :] = total[0:CHAN, :] + times(points[:, rows], grad)
        return carry

    lax.fori_loop(0, GRID_ROWS // 512, grid_step, 0)
    grads[WIDTH : WIDTH + TAIL, :] = total[...].astype(BF16)


def shift(value, axis, steps):
    count = lax.axis_size(axis)
    return lax.ppermute(value, axis, [(i, (i + steps) % count) for i in range(count)])


def show(mine):
    return (shift(mine, "wide", 1), shift(mine, "wide", -1), shift(mine, "narrow", 1), shift(mine, "narrow", -1))


def give_back(h0, h1, h2, h3):
    return (shift(h0, "wide", -1), shift(h1, "wide", 1), shift(h2, "narrow", -1), shift(h3, "narrow", 1))


def exchange(parts, axis):
    return lax.all_to_all(parts, axis, split_axis=0, concat_axis=0, tiled=True)


def add_up(parts):
    return jnp.sum(parts.astype(F32), axis=0).astype(BF16)


def scatter_sum(rows, axis):
    count = lax.axis_size(axis)
    return add_up(exchange(rows.reshape(count, rows.shape[0] // count, rows.shape[1]), axis))


def gather_all(rows, axis):
    count = lax.axis_size(axis)
    return exchange(jnp.broadcast_to(rows[None], (count,) + rows.shape), axis)


def sum_narrow_first(rows):
    part = scatter_sum(scatter_sum(rows, "narrow"), "wide")
    part = gather_all(part, "wide").reshape(-1, rows.shape[1])
    return gather_all(part, "narrow").reshape(rows.shape)


def sum_wide_first(rows):
    part = add_up(gather_all(scatter_sum(rows, "wide"), "narrow"))
    return gather_all(part, "wide").reshape(rows.shape)


def on_device(
    grid_feat, grid_send, w_embed, g2m_src, g2m_coef, mesh_src, mesh_coef, halo_send,
    message_weight, update_weight, cotangent,
):
    rows_bf16 = ((MESH_ROWS, WIDTH), BF16)
    rows_f32 = ((MESH_ROWS, WIDTH), F32)
    halo = ((SHOWN, BLOCK, WIDTH), BF16)
    square = ((WIDTH, WIDTH), BF16)
    points_shape = ((CHAN, GRID_ROWS), BF16)
    mesh_scratch = pltpu.VMEM((MESH_ROWS, WIDTH), BF16)
    mesh_scratch32 = pltpu.VMEM((MESH_ROWS, WIDTH), F32)
    extended_scratch = pltpu.VMEM((EXTENDED * BLOCK, WIDTH), BF16)
    table_scratch = pltpu.VMEM((EXTENDED, BLOCK, WIDTH), F32)
    w_m = (message_weight[0], message_weight[1])
    w_u = (update_weight[0], update_weight[1])

    packed = kernel_call(
        pack_body, [((GRID_BLOCKS, PACKED, 2 * BLOCK), BF16)], [SM, VM],
        [pltpu.SMEM((GRID_BLOCKS,), jnp.int32)], moved=8 * MIB,
    )(grid_send, grid_feat.T)[0]
    received = lax.all_to_all(packed, AXES, split_axis=0, concat_axis=0, tiled=True)

    g_mix = g2m_coef.transpose(0, 2, 1, 3).reshape(MESH_BLOCKS, BLOCK, G_SLOTS * BLOCK)
    g_back = g2m_coef.transpose(0, 1, 3, 2).reshape(MESH_BLOCKS, G_SLOTS * BLOCK, BLOCK)
    m_mix = mesh_coef.transpose(0, 2, 1, 3).reshape(MESH_BLOCKS, BLOCK, M_SLOTS * BLOCK)
    m_back = mesh_coef.transpose(0, 1, 3, 2).reshape(MESH_BLOCKS, M_SLOTS * BLOCK, BLOCK)

    own_1, *halos = kernel_call(
        early_back_body, [rows_f32] + [halo] * 4, [SM] + [VM] * 3, [table_scratch, mesh_scratch],
        flops=2 * 10**9, moved=8 * MIB,
    )(mesh_src, cotangent, w_u[1], m_back)
    returned_1 = give_back(*halos)

    received, g_mix, g_back, m_mix, m_back = lax.optimization_barrier(
        (received, g_mix, g_back, m_mix, m_back)
    )
    points, mesh_0, sent_0, mine_0 = kernel_call(
        encode_body, [points_shape, rows_bf16, rows_bf16, halo], [SM, SM] + [VM] * 4,
        [pltpu.VMEM((GRID_ROWS, WIDTH), BF16)], flops=4 * 10**9, moved=16 * MIB,
    )(g2m_src, halo_send, received, w_embed, g_mix, w_m[0])
    shown_0 = show(mine_0)

    slope, slope_m = pl.pallas_call(
        slopes_body,
        grid=(16,),
        out_shape=[
            jax.ShapeDtypeStruct((GRID_ROWS, WIDTH), BF16),
            jax.ShapeDtypeStruct((MESH_ROWS, WIDTH), F32),
        ],
        in_specs=[
            pl.BlockSpec((CHAN, 512), lambda i: (0, i)),
            pl.BlockSpec((CHAN, WIDTH), lambda i: (0, 0)),
            pl.BlockSpec((256, WIDTH), lambda i: (jnp.minimum(i, 3), 0)),
            pl.BlockSpec((WIDTH, WIDTH), lambda i: (0, 0)),
        ],
        out_specs=[
            pl.BlockSpec((512, WIDTH), lambda i: (i, 0)),
            pl.BlockSpec((256, WIDTH), lambda i: (jnp.minimum(i, 3), 0)),
        ],
        compiler_params=pltpu.CompilerParams(vmem_limit_bytes=56 * MIB),
        cost_estimate=pl.CostEstimate(flops=3 * 10**9, bytes_accessed=16 * MIB, transcendentals=0),
    )(points, w_embed, mesh_0, w_m[0])
    sent_0, slope, slope_m = lax.optimization_barrier((sent_0, slope, slope_m))

    aggregate_0, mesh_1, sent_1, mine_1, grad_pre_1, grad_1, own_0, *halos = kernel_call(
        middle_body,
        [rows_bf16, rows_bf16, rows_bf16, halo, rows_bf16, rows_f32, rows_f32] + [halo] * 4,
        [SM, SM] + [VM] * 16,
        [extended_scratch, table_scratch, mesh_scratch, mesh_scratch32],
        flops=5 * 10**9, moved=20 * MIB,
    )(
        mesh_src, halo_send, sent_0, *shown_0, m_mix, m_back, mesh_0, w_u[0], w_m[1], own_1,
        *returned_1, cotangent,
    )
    returned_0 = give_back(*halos)
    shown_1 = show(mine_1)

    up_0, ms_1 = kernel_call(
        two_grads_body, [square, square], [VM] * 4, flops=10**9, moved=5 * MIB
    )(aggregate_0, grad_1, mesh_1, grad_pre_1)

    mesh_out, up_1 = kernel_call(
        last_body, [rows_bf16, square], [SM] + [VM] * 9, [extended_scratch, mesh_scratch],
        flops=2 * 10**9, moved=8 * MIB,
    )(mesh_src, sent_1, *shown_1, m_mix, mesh_1, w_u[1], cotangent)
    own_0, up_0, ms_1, up_1 = lax.optimization_barrier((own_0, up_0, ms_1, up_1))
    early = jnp.concatenate([up_0, ms_1, up_1], axis=0)
    late = kernel_call(
        final_body, [((WIDTH + TAIL, WIDTH), BF16)], [SM, SM] + [VM] * 10 + [HBM, HBM],
        [
            pltpu.VMEM((GRID_ROWS, WIDTH), BF16),
            pltpu.VMEM((CHAN, GRID_ROWS), BF16),
            pltpu.VMEM((GRID_BLOCKS, BLOCK, WIDTH), F32),
            mesh_scratch, mesh_scratch, mesh_scratch32,
            pltpu.VMEM((TAIL, WIDTH), F32),
            pltpu.SemaphoreType.DMA((2,)),
        ],
        flops=4 * 10**9, moved=24 * MIB,
    )(
        g2m_src, halo_send, own_0, *returned_0, slope_m, grad_1, w_m[0], mesh_0, g_back, slope,
        points,
    )[0]
    early = sum_narrow_first(early).astype(F32)
    late = sum_wide_first(late).astype(F32)
    up_0, ms_1, up_1 = early[:WIDTH], early[WIDTH : 2 * WIDTH], early[2 * WIDTH :]
    ms_0, d_embed = late[:WIDTH], late[WIDTH : WIDTH + CHAN]
    return mesh_out, d_embed, jnp.stack([ms_0, ms_1]), jnp.stack([up_0, up_1])


def solution(mesh):
    split = P(AXES, None)
    return jax.shard_map(
        on_device,
        mesh=mesh,
        in_specs=(
            split, split, P(), split, P(AXES, None, None, None), split, P(AXES, None, None, None),
            split, P(), P(), split,
        ),
        out_specs=(split, P(), P(), P()),
        check_vma=False,
    )
```

time: 721 us -> 316 us (0.44); the launches traced: 713 us -> 315 us
  waiting for transfers between devices: 315 us -> 105 us
  other arithmetic: 129 us -> 6.53 us
  Pallas kernels: 0 us -> 105 us
  local copies, waits for them, and re-layouts: 119 us -> 30 us
  matrix products: 84.7 us -> 0 us
  starting transfers between devices: 49.9 us -> 67.8 us
  between operations: 14.8 us -> 0.92 us
    psum x1 -> x0, waiting for transfers between devices: 151 us -> none  [on_device(): lax.psum((d_embed, jnp.stack(message_weight_gradient), jnp.stack(update_w...]
    pallas_call x0 -> x8, Pallas kernels: none -> 105 us  [the longest x1 19.5 us: on_device(): kernel_call(middle_body, [rows_bf16, rows_bf16, rows_bf16, halo, rows_bf1...]
    scatter-add x3 -> x0, other arithmetic: 95.8 us -> none  [mix_back(): jax.ops.segment_sum(flat_parts, indices.reshape(-1), num_segments=block_c...]
    ppermute x16, waiting for transfers between devices: 118 us -> 25.4 us  [shift(): lax.ppermute(value, axis, [(i, (i + steps) % count) for i in range(count)])]
    gather x23 -> x0, local copies, waits for them, and re-layouts: 64.9 us -> none  [the longest x20 56.1 us: mix_blocks(): picked = source[indices[:, slot]]]
    dot_general x33 -> x0, matrix products: 57.7 us -> none  [the longest x20 24.2 us: mix_blocks(): jnp.einsum('bij,bjl->bil', coeffs[:, slot], picked, preferred_element_typ...]
    all_to_all x2 -> x8, waiting for transfers between devices: 46.2 us -> 79.8 us  [the longest x7 67.6 us: exchange(): return lax.all_to_all(parts, axis, split_axis=0, concat_axis=0, tiled=True)]
    unnamed x108 -> x52, local copies, waits for them, and re-layouts: 33.6 us -> 4.41 us
  transfers between devices with their start and end apart: 19 -> 24, of which waited for: 11 -> 12; matrix products, arithmetic and copies ran while one was open for 18% -> 8% of each run, Pallas kernels for 0% -> 22%
where the time goes in v1:
time: 316 us; the launch traced here: 315 us
  Pallas kernels  105 us (33%)
  waiting for transfers between devices  105 us (33%)
  starting transfers between devices  67.8 us (21%)
  local copies, waits for them, and re-layouts  30 us (9%)
  other arithmetic  6.53 us (2%)
    all_to_all x7, waiting for transfers between devices, exchange(): return lax.all_to_all(parts, axis, split_axis=0, concat_axis=0, tiled=True)  67.6 us
    all_to_all x7, starting transfers between devices, exchange(): return lax.all_to_all(parts, axis, split_axis=0, concat_axis=0, tiled=True)  32.4 us
    ppermute x16, waiting for transfers between devices, shift(): lax.ppermute(value, axis, [(i, (i + steps) % count) for i in range(count)])  25.4 us
    ppermute x16, starting transfers between devices, shift(): lax.ppermute(value, axis, [(i, (i + steps) % count) for i in range(count)])  23.5 us
    pallas_call x1, Pallas kernels, on_device(): kernel_call(middle_body, [rows_bf16, rows_bf16, rows_bf16, halo, rows_bf1...  19.5 us
    pallas_call x1, Pallas kernels, on_device(): kernel_call(final_body, [((WIDTH + TAIL, WIDTH), BF16)], [SM, SM] + [VM]...  18.8 us
    pallas_call x1, Pallas kernels, on_device(): kernel_call(encode_body, [points_shape, rows_bf16, rows_bf16, halo], [SM,...  18.5 us
    pallas_call x1, Pallas kernels, on_device(): pl.pallas_call(slopes_body, grid=(16,), out_shape=[jax.ShapeDtypeStruct((...  16.9 us
  transfers between devices with their start and end apart: 24, of which 12 were waited for; matrix products, arithmetic and copies ran while one was open for 8% of the time, Pallas kernels for 22%

profile of v1, /device:TPU:1, one launch (start us, length us, event | category | flops | bytes accessed | tf_op | source)
XLA Modules:
  0.0 315.0 jit_solution(17087320722004124233)
XLA Ops:
  0.6 8.6 %shard_map.138 = bf16[128,115,128]{2,1,0:T(8,128)(2,1)} custom-call(s32[1,128]{1,0:T(1,128)} %send.1, bf16[227,8192]{1,0:T(8,128)(2,1)} %bitcast.38), custom_call_target="tpu_custom_call" | custom-call | bytes 8388608 | tf_op jit(solution)/shard_map/pallas_call | solution.py:356
  9.2 11.9 %all-to-all-start = ((bf16[128,115,128]{2,1,0:T(8,128)(2,1)}), bf16[128,115,128]{2,1,0:T(8,128)(2,1)}, u32[]{:S(2)}, u32[]{:S(2)}) async-start(bf16[128,115,128]{2,1,0:T(8,128)(2,1)} %shard_map.138), calls=%async_computation | async-start | bytes 7864320 | tf_op jit(solution)/shard_map/all_to_all | solution.py:360
  21.2 0.7 copy.40.source
  21.8 1.6 copy.36
  23.4 1.1 slice_bitcast_fusion.4
  24.5 9.2 %shard_map.141 = (f32[1024,512]{1,0:T(8,128)}, bf16[4,64,512]{2,1,0:T(8,128)(2,1)}, bf16[4,64,512]{2,1,0:T(8,128)(2,1)}, bf16[4,64,512]{2,1,0:T(8,128)(2,1)}, bf16[4,64,512]{2,1,0:T(8,128)(2,1)}) custom-call(s32[16,6]{1,0:T(8,128)} %copy.40.source, bf16[1024,512]{1,0:T(8,128)(2,1)} %cot.5, bf16[512,512]{1,0:T(8,128)(2,1)} %get-tuple-element.83.up, ...), custom_call_target="tpu_custom_call" | custom-call | flops 2000000000 | bytes 8388608 | tf_op jit(solution)/shard_map/pallas_call | solution.py:367
  33.6 5.6 %collective-permute-start.4 = (bf16[4,64,512]{2,1,0:T(8,128)(2,1)}, bf16[4,64,512]{2,1,0:T(8,128)(2,1)S(1)}, u32[]{:S(2)}, u32[]{:S(2)}) collective-permute-start(bf16[4,64,512]{2,1,0:T(8,128)(2,1)} %get-tuple-element.54), channel_id=1, source_target_pairs={{0,120},{8,0},{16,8},{24,16},{32,24},{40,32},{48,40},{56,48},{64,5... | collective-permute-start | bytes 786440 | tf_op jit(solution)/shard_map/ppermute | solution.py:300
  39.2 0.6 collective-permute-start.6
  39.8 1.1 collective-permute-start.7
  41.0 0.7 copy.37.source
  41.6 2.7 copy.35
  44.3 2.0 reshape.41.coeffs
  46.3 4.7 %copy.33 = bf16[16,64,8,64]{3,2,1,0:T(8,128)(2,1)} copy(bf16[16,64,8,64]{3,1,2,0:T(8,128)(2,1)} %bitcast.34) | data formatting | bytes 2097152 | tf_op jit(solution)/shard_map/transpose | solution.py:362
  51.0 4.2 %reshape.39.coeffs = bf16[16,64,512]{2,1,0:T(8,128)(2,1)} reshape(bf16[16,64,8,64]{3,2,1,0:T(8,128)(2,1)} %copy.33) | data formatting | bytes 2097152 | tf_op jit(solution)/shard_map/reshape | solution.py:362
  55.2 2.7 copy.34
  57.9 1.0 slice_bitcast_fusion.5
  58.9 12.2 %all-to-all-done.packed = bf16[128,115,128]{2,1,0:T(8,128)(2,1)} async-done(((bf16[128,115,128]{2,1,0:T(8,128)(2,1)}), bf16[128,115,128]{2,1,0:T(8,128)(2,1)}, u32[]{:S(2)}, u32[]{:S(2)}) %all-to-all-start) | async-done | bytes 3768352 | tf_op jit(solution)/shard_map/all_to_all | solution.py:360
  71.1 18.5 %shard_map.139 = (bf16[227,8192]{1,0:T(8,128)(2,1)}, bf16[1024,512]{1,0:T(8,128)(2,1)}, bf16[1024,512]{1,0:T(8,128)(2,1)}, bf16[4,64,512]{2,1,0:T(8,128)(2,1)}) custom-call(s32[16,8]{1,0:T(8,128)} %copy.37.source, s32[1,4]{1,0:T(1,128)} %shown.5, bf16[128,115,128]{2,1,0:T(8,128)(2,1)} %all-to-all-done.packed, bf16[227,512]{1,0:T(8,128)(2,1)} %weight.3, ...), custom_call_target="tpu_custom_call" | custom-call | flops 4000000000 | bytes 16777216 | tf_op jit(solution)/shard_map/pallas_call | solution.py:376
  89.6 1.4 collective-permute-start.3
  91.0 0.4 collective-permute-start.2
  91.3 4.3 %collective-permute-start.1 = (bf16[4,64,512]{2,1,0:T(8,128)(2,1)}, bf16[4,64,512]{2,1,0:T(8,128)(2,1)S(1)}, u32[]{:S(2)}, u32[]{:S(2)}) collective-permute-start(bf16[4,64,512]{2,1,0:T(8,128)(2,1)} %get-tuple-element.50), channel_id=1, source_target_pairs={{0,120},{8,0},{16,8},{24,16},{32,24},{40,32},{48,40},{56,48},{64,5... | collective-permute-start | bytes 786440 | tf_op jit(solution)/shard_map/ppermute | solution.py:300
  95.6 16.9 %shard_map.140 = (bf16[8192,512]{1,0:T(8,128)(2,1)}, f32[1024,512]{1,0:T(8,128)}) custom-call(bf16[227,8192]{1,0:T(8,128)(2,1)} %get-tuple-element.45.points.points_hbm, bf16[227,512]{1,0:T(8,128)(2,1)} %weight.3, bf16[1024,512]{1,0:T(8,128)(2,1)} %get-tuple-element.46.mesh, bf16[512,512]{1,0:T(8,128)(2,1)} %get-tuple-element.86.message), custom_call_target="tpu_custom_call" | custom-call | flops 3000000000 | bytes 16777216 | tf_op jit(solution)/shard_map/pallas_call | solution.py:382
  112.6 0.6 copy-done.17
  113.5 19.5 %shard_map.142 = (bf16[1024,512]{1,0:T(8,128)(2,1)}, bf16[1024,512]{1,0:T(8,128)(2,1)}, bf16[1024,512]{1,0:T(8,128)(2,1)}, bf16[4,64,512]{2,1,0:T(8,128)(2,1)}, ...) custom-call(s32[16,6]{1,0:T(8,128)} %copy.40.source, ...), custom_call_target="tpu_custom_call" | custom-call | flops 5000000000 | bytes 20971520 | tf_op jit(solution)/shard_map/pallas_call | solution.py:404
  133.0 1.7 collective-permute-start.10
  134.7 4.8 %collective-permute-start.9 = (bf16[4,64,512]{2,1,0:T(8,128)(2,1)}, bf16[4,64,512]{2,1,0:T(8,128)(2,1)S(1)}, u32[]{:S(2)}, u32[]{:S(2)}) collective-permute-start(bf16[4,64,512]{2,1,0:T(8,128)(2,1)} %get-tuple-element.59), channel_id=1, source_target_pairs={{0,120},{8,0},{16,8},{24,16},{32,24},{40,32},{48,40},{56,48},{64,5... | collective-permute-start | bytes 786440 | tf_op jit(solution)/shard_map/ppermute | solution.py:300
  139.5 4.6 %shard_map.144 = (bf16[512,512]{1,0:T(8,128)(2,1)}, bf16[512,512]{1,0:T(8,128)(2,1)}) custom-call(bf16[1024,512]{1,0:T(8,128)(2,1)} %get-tuple-element.63.aggregate, f32[1024,512]{1,0:T(8,128)} %get-tuple-element.64.grad_1, bf16[1024,512]{1,0:T(8,128)(2,1)} %get-tuple-element.60.mesh.mesh_1, bf16[1024,512]{1,0:T(8,128)(2,1)} %get-tuple-element.65.grad_pre), custom_call_target="tpu_custom_call" | custom-call | flops 1000000000 | bytes 5242880 | tf_op jit(solution)/shard_map/pallas_call | solution.py:417
  144.1 1.1 collective-permute-done.9.n1
  145.2 5.4 %collective-permute-done.8.n0 = bf16[4,64,512]{2,1,0:T(8,128)(2,1)S(1)} collective-permute-done((bf16[4,64,512]{2,1,0:T(8,128)(2,1)}, bf16[4,64,512]{2,1,0:T(8,128)(2,1)S(1)}, u32[]{:S(2)}, u32[]{:S(2)}) %collective-permute-start.8) | collective-permute-done | bytes 262176 | tf_op jit(solution)/shard_map/ppermute | solution.py:300
  150.6 0.7 copy-done.24
  151.3 8.6 %shard_map.143 = (bf16[1024,512]{1,0:T(8,128)(2,1)}, bf16[512,512]{1,0:T(8,128)(2,1)}) custom-call(s32[16,6]{1,0:T(8,128)} %copy.40.source, bf16[1024,512]{1,0:T(8,128)(2,1)} %get-tuple-element.58.sent, bf16[4,64,512]{2,1,0:T(8,128)(2,1)} %copy-done.24, bf16[4,64,512]{2,1,0:T(8,128)(2,1)} %copy-done.23, bf16[4,64,512]{2,1,0:T(8,128)(2,1)} %copy-done.22, ...), custom_call_target="tpu_custom_call" | custom-call | flops 2000000000 | bytes 8388608 | tf_op jit(solution)/shard_map/pallas_call | solution.py:421
  159.9 2.3 pad_maximum_fusion.2
  162.2 4.5 %all-to-all-start.4 = ((bf16[8,192,512]{2,1,0:T(8,128)(2,1)}), bf16[8,192,512]{2,1,0:T(8,128)(2,1)S(1)}, u32[]{:S(2)}, u32[]{:S(2)}) async-start(bf16[8,192,512]{2,1,0:T(8,128)(2,1)} %bitcast.15), calls=%async_computation.4 | async-start | bytes 3145728 | tf_op jit(solution)/shard_map/all_to_all | solution.py:312
  166.7 1.5 collective-permute-start.13
  168.2 0.6 collective-permute-start.14
  168.8 1.6 collective-permute-start.15
  170.4 4.2 %collective-permute-done.12.r0 = bf16[4,64,512]{2,1,0:T(8,128)(2,1)S(1)} collective-permute-done((bf16[4,64,512]{2,1,0:T(8,128)(2,1)S(1)}, bf16[4,64,512]{2,1,0:T(8,128)(2,1)S(1)}, u32[]{:S(2)}, u32[]{:S(2)}) %collective-permute-start.12) | collective-permute-done | bytes 262176 | tf_op jit(solution)/shard_map/ppermute | solution.py:300
  174.6 3.4 %collective-permute-done.13.r1 = bf16[4,64,512]{2,1,0:T(8,128)(2,1)S(1)} collective-permute-done((bf16[4,64,512]{2,1,0:T(8,128)(2,1)S(1)}, bf16[4,64,512]{2,1,0:T(8,128)(2,1)S(1)}, u32[]{:S(2)}, u32[]{:S(2)}) %collective-permute-start.13) | collective-permute-done | bytes 262176 | tf_op jit(solution)/shard_map/ppermute | solution.py:300
  178.0 11.3 %collective-permute-done.14.r2 = bf16[4,64,512]{2,1,0:T(8,128)(2,1)S(1)} collective-permute-done((bf16[4,64,512]{2,1,0:T(8,128)(2,1)S(1)}, bf16[4,64,512]{2,1,0:T(8,128)(2,1)S(1)}, u32[]{:S(2)}, u32[]{:S(2)}) %collective-permute-start.14) | collective-permute-done | bytes 262176 | tf_op jit(solution)/shard_map/ppermute | solution.py:300
  189.3 0.7 copy-done.8
  189.9 0.7 copy-done.9
  190.7 18.8 %shard_map.145 = bf16[768,512]{1,0:T(8,128)(2,1)} custom-call(s32[16,8]{1,0:T(8,128)} %copy.37.source, s32[1,4]{1,0:T(1,128)} %shown.5, f32[1024,512]{1,0:T(8,128)} %get-tuple-element.69.own, bf16[4,64,512]{2,1,0:T(8,128)(2,1)} %copy-done.6, bf16[4,64,512]{2,1,0:T(8,128)(2,1)} %copy-done.7, bf16[4,64,512]{2,1,0:T(8,128)(2,1)} %copy-done.8, ...), custom_call_target="tpu_custom_call" | custom-call | flops 4000000000 | bytes 25165824 | tf_op jit(solution)/shard_map/pallas_call | solution.py:427
  209.5 3.6 %all-to-all-start.1 = ((bf16[16,48,512]{2,1,0:T(8,128)(2,1)}), bf16[16,48,512]{2,1,0:T(8,128)(2,1)S(1)}, u32[]{:S(2)}, u32[]{:S(2)}) async-start(bf16[16,48,512]{2,1,0:T(8,128)(2,1)} %bitcast.39), calls=%async_computation.1 | async-start | bytes 1572864 | tf_op jit(solution)/shard_map/all_to_all | solution.py:312
  213.4 0.7 reshape.45
  214.1 12.2 %all-to-all-done.1 = bf16[16,48,512]{2,1,0:T(8,128)(2,1)S(1)} async-done(((bf16[16,48,512]{2,1,0:T(8,128)(2,1)}), bf16[16,48,512]{2,1,0:T(8,128)(2,1)S(1)}, u32[]{:S(2)}, u32[]{:S(2)}) %all-to-all-start.1) | async-done | bytes 786464 | tf_op jit(solution)/shard_map/all_to_all | solution.py:312
  226.3 3.6 %all-to-all-start.5 = ((bf16[16,12,512]{2,1,0:T(8,128)(2,1)}), bf16[16,12,512]{2,1,0:T(8,128)(2,1)S(1)}, u32[]{:S(2)}, u32[]{:S(2)}) async-start(bf16[16,12,512]{2,1,0:T(8,128)(2,1)} %reshape.45), calls=%async_computation.5 | async-start | bytes 524288 | tf_op jit(solution)/shard_map/all_to_all | solution.py:312
  230.1 7.4 %all-to-all-done.5 = bf16[16,12,512]{2,1,0:T(8,128)(2,1)S(1)} async-done(((bf16[16,12,512]{2,1,0:T(8,128)(2,1)}), bf16[16,12,512]{2,1,0:T(8,128)(2,1)S(1)}, u32[]{:S(2)}, u32[]{:S(2)}) %all-to-all-start.5) | async-done | bytes 196640 | tf_op jit(solution)/shard_map/all_to_all | solution.py:312
  237.5 0.8 broadcast_in_dim.10
  238.3 7.3 %all-to-all-start.2 = ((bf16[8,48,512]{2,1,0:T(8,128)(2,1)}), bf16[8,48,512]{2,1,0:T(8,128)(2,1)S(1)}, u32[]{:S(2)}, u32[]{:S(2)}) async-start(bf16[8,48,512]{2,1,0:T(8,128)(2,1)} %broadcast_in_dim.10), calls=%async_computation.2 | async-start | bytes 786432 | tf_op jit(solution)/shard_map/all_to_all | solution.py:312
  245.7 8.0 %all-to-all-done.2 = bf16[8,48,512]{2,1,0:T(8,128)(2,1)S(1)} async-done(((bf16[8,48,512]{2,1,0:T(8,128)(2,1)}), bf16[8,48,512]{2,1,0:T(8,128)(2,1)S(1)}, u32[]{:S(2)}, u32[]{:S(2)}) %all-to-all-start.2) | async-done | bytes 393248 | tf_op jit(solution)/shard_map/all_to_all | solution.py:312
  253.7 0.7 broadcast_in_dim.12
  254.5 3.5 %all-to-all-start.6 = ((bf16[16,12,512]{2,1,0:T(8,128)(2,1)}), bf16[16,12,512]{2,1,0:T(8,128)(2,1)S(1)}, u32[]{:S(2)}, u32[]{:S(2)}) async-start(bf16[16,12,512]{2,1,0:T(8,128)(2,1)} %broadcast_in_dim.12), calls=%async_computation.6 | async-start | bytes 524288 | tf_op jit(solution)/shard_map/all_to_all | solution.py:312
  258.1 7.8 %all-to-all-done.6 = bf16[16,12,512]{2,1,0:T(8,128)(2,1)S(1)} async-done(((bf16[16,12,512]{2,1,0:T(8,128)(2,1)}), bf16[16,12,512]{2,1,0:T(8,128)(2,1)S(1)}, u32[]{:S(2)}, u32[]{:S(2)}) %all-to-all-start.6) | async-done | bytes 196640 | tf_op jit(solution)/shard_map/all_to_all | solution.py:312
  265.8 1.0 broadcast_in_dim.11
  266.8 3.6 %all-to-all-start.3 = ((bf16[16,48,512]{2,1,0:T(8,128)(2,1)}), bf16[16,48,512]{2,1,0:T(8,128)(2,1)S(1)}, u32[]{:S(2)}, u32[]{:S(2)}) async-start(bf16[16,48,512]{2,1,0:T(8,128)(2,1)} %broadcast_in_dim.11), calls=%async_computation.3 | async-start | bytes 1572864 | tf_op jit(solution)/shard_map/all_to_all | solution.py:312
  270.5 12.6 %all-to-all-done.3 = bf16[16,48,512]{2,1,0:T(8,128)(2,1)S(1)} async-done(((bf16[16,48,512]{2,1,0:T(8,128)(2,1)}), bf16[16,48,512]{2,1,0:T(8,128)(2,1)S(1)}, u32[]{:S(2)}, u32[]{:S(2)}) %all-to-all-start.3) | async-done | bytes 786464 | tf_op jit(solution)/shard_map/all_to_all | solution.py:312
  283.0 1.3 broadcast_in_dim.14
  284.3 6.2 %all-to-all-start.7 = ((bf16[8,192,512]{2,1,0:T(8,128)(2,1)}), bf16[8,192,512]{2,1,0:T(8,128)(2,1)S(1)}, u32[]{:S(2)}, u32[]{:S(2)}) async-start(bf16[8,192,512]{2,1,0:T(8,128)(2,1)} %broadcast_in_dim.14), calls=%async_computation.7 | async-start | bytes 3145728 | tf_op jit(solution)/shard_map/all_to_all | solution.py:312
  290.7 0.8 slice.36
  291.6 19.6 %all-to-all-done.7 = bf16[8,192,512]{2,1,0:T(8,128)(2,1)S(1)} async-done(((bf16[8,192,512]{2,1,0:T(8,128)(2,1)}), bf16[8,192,512]{2,1,0:T(8,128)(2,1)S(1)}, u32[]{:S(2)}, u32[]{:S(2)}) %all-to-all-start.7) | async-done | bytes 1572896 | tf_op jit(solution)/shard_map/all_to_all | solution.py:312
  311.2 0.5 bitcast_convert_fusion
  311.7 0.3 slice_bitcast_fusion.1
  312.1 1.5 pad_maximum_fusion.1
  313.5 1.5 pad_maximum_fusion
  (70 shorter events, 1.2 us)
Async XLA Ops:
  9.2 11.9 %copy-start.10 = (s32[16,6]{0,1:T(8,128)S(1)}, s32[16,6]{0,1:T(8,128)}, u32[]{:S(2)}) copy-start(s32[16,6]{0,1:T(8,128)} %param.16) | copy-start | bytes 1156
  9.2 12.6 %copy-start.1 = (bf16[16,6,64,64]{3,2,1,0:T(8,128)(2,1)S(1)}, bf16[16,6,64,64]{3,2,1,0:T(8,128)(2,1)}, u32[]{:S(2)}) copy-start(bf16[16,6,64,64]{3,2,1,0:T(8,128)(2,1)} %param.17) | copy-start | bytes 2359300
  9.2 61.9 %all-to-all-start = ((bf16[128,115,128]{2,1,0:T(8,128)(2,1)}), bf16[128,115,128]{2,1,0:T(8,128)(2,1)}, u32[]{:S(2)}, u32[]{:S(2)}) async-start(bf16[128,115,128]{2,1,0:T(8,128)(2,1)} %shard_map.138), calls=%async_computation | async-start | bytes 7864320 | tf_op jit(solution)/shard_map/all_to_all | solution.py:360
  21.1 2.3 copy-start.2
  24.5 16.5 %copy-start.11 = (s32[16,8]{0,1:T(8,128)S(1)}, s32[16,8]{0,1:T(8,128)}, u32[]{:S(2)}) copy-start(s32[16,8]{0,1:T(8,128)} %param.14) | copy-start | bytes 1540
  33.6 57.3 %collective-permute-start.4 = (bf16[4,64,512]{2,1,0:T(8,128)(2,1)}, bf16[4,64,512]{2,1,0:T(8,128)(2,1)S(1)}, u32[]{:S(2)}, u32[]{:S(2)}) collective-permute-start(bf16[4,64,512]{2,1,0:T(8,128)(2,1)} %get-tuple-element.54), channel_id=1, source_target_pairs={{0,120},{8,0},{16,8},{24,16},{32,24},{40,32},{48,40},{56,48},{64,5... | collective-permute-start | bytes 786440 | tf_op jit(solution)/shard_map/ppermute | solution.py:300
  39.2 52.1 %collective-permute-start.5 = (bf16[4,64,512]{2,1,0:T(8,128)(2,1)}, bf16[4,64,512]{2,1,0:T(8,128)(2,1)}, u32[]{:S(2)}, u32[]{:S(2)}) collective-permute-start(bf16[4,64,512]{2,1,0:T(8,128)(2,1)} %get-tuple-element.55), channel_id=1, source_target_pairs={{0,8},{8,16},{16,24},{24,32},{32,40},{40,48},{48,56},{56,64},{64,7... | collective-permute-start | bytes 786440 | tf_op jit(solution)/shard_map/ppermute | solution.py:300
  39.2 56.4 %collective-permute-start.6 = (bf16[4,64,512]{2,1,0:T(8,128)(2,1)}, bf16[4,64,512]{2,1,0:T(8,128)(2,1)}, u32[]{:S(2)}, u32[]{:S(2)}) collective-permute-start(bf16[4,64,512]{2,1,0:T(8,128)(2,1)} %get-tuple-element.56), channel_id=1, source_target_pairs={{0,7},{1,0},{2,1},{3,2},{4,3},{5,4},{6,5},{7,6},{8,15},{9,8},{10,9... | collective-permute-start | bytes 786440 | tf_op jit(solution)/shard_map/ppermute | solution.py:300
  39.8 72.6 %collective-permute-start.7 = (bf16[4,64,512]{2,1,0:T(8,128)(2,1)}, bf16[4,64,512]{2,1,0:T(8,128)(2,1)}, u32[]{:S(2)}, u32[]{:S(2)}) collective-permute-start(bf16[4,64,512]{2,1,0:T(8,128)(2,1)} %get-tuple-element.57), channel_id=1, source_target_pairs={{0,1},{1,2},{2,3},{3,4},{4,5},{5,6},{6,7},{7,0},{8,9},{9,10},{10,1... | collective-permute-start | bytes 786440 | tf_op jit(solution)/shard_map/ppermute | solution.py:300
  51.0 4.2 %copy-start = (bf16[16,8,64,64]{3,2,1,0:T(8,128)(2,1)S(1)}, bf16[16,8,64,64]{3,2,1,0:T(8,128)(2,1)}, u32[]{:S(2)}) copy-start(bf16[16,8,64,64]{3,2,1,0:T(8,128)(2,1)} %param.15) | copy-start | bytes 3145732
  55.2 2.7 copy-start.3
  89.6 22.9 %collective-permute-start.3 = (bf16[4,64,512]{2,1,0:T(8,128)(2,1)}, bf16[4,64,512]{2,1,0:T(8,128)(2,1)S(1)}, u32[]{:S(2)}, u32[]{:S(2)}) collective-permute-start(bf16[4,64,512]{2,1,0:T(8,128)(2,1)} %get-tuple-element.50), channel_id=1, source_target_pairs={{0,7},{1,0},{2,1},{3,2},{4,3},{5,4},{6,5},{7,6},{8,15},{9,8},{10,9... | collective-permute-start | bytes 786440 | tf_op jit(solution)/shard_map/ppermute | solution.py:300
  90.9 21.5 %copy-start.12 = (bf16[4,64,512]{2,1,0:T(8,128)(2,1)}, bf16[4,64,512]{2,1,0:T(8,128)(2,1)S(1)}, u32[]{:S(2)}) copy-start(bf16[4,64,512]{2,1,0:T(8,128)(2,1)S(1)} %collective-permute-done.4.r0) | copy-start | bytes 786436
  91.0 21.6 %collective-permute-start.2 = (bf16[4,64,512]{2,1,0:T(8,128)(2,1)}, bf16[4,64,512]{2,1,0:T(8,128)(2,1)S(1)}, u32[]{:S(2)}, u32[]{:S(2)}) collective-permute-start(bf16[4,64,512]{2,1,0:T(8,128)(2,1)} %get-tuple-element.50), channel_id=1, source_target_pairs={{0,1},{1,2},{2,3},{3,4},{4,5},{5,6},{6,7},{7,0},{8,9},{9,10},{10,1... | collective-permute-start | bytes 786440 | tf_op jit(solution)/shard_map/ppermute | solution.py:300
  91.3 21.2 %collective-permute-start.1 = (bf16[4,64,512]{2,1,0:T(8,128)(2,1)}, bf16[4,64,512]{2,1,0:T(8,128)(2,1)S(1)}, u32[]{:S(2)}, u32[]{:S(2)}) collective-permute-start(bf16[4,64,512]{2,1,0:T(8,128)(2,1)} %get-tuple-element.50), channel_id=1, source_target_pairs={{0,120},{8,0},{16,8},{24,16},{32,24},{40,32},{48,40},{56,48},{64,5... | collective-permute-start | bytes 786440 | tf_op jit(solution)/shard_map/ppermute | solution.py:300
  95.6 17.0 %collective-permute-start = (bf16[4,64,512]{2,1,0:T(8,128)(2,1)}, bf16[4,64,512]{2,1,0:T(8,128)(2,1)S(1)}, u32[]{:S(2)}, u32[]{:S(2)}) collective-permute-start(bf16[4,64,512]{2,1,0:T(8,128)(2,1)} %get-tuple-element.50), channel_id=1, source_target_pairs={{0,8},{8,16},{16,24},{24,32},{32,40},{40,48},{48,56},{56,64},{64,7... | collective-permute-start | bytes 786440 | tf_op jit(solution)/shard_map/ppermute | solution.py:300
  112.5 0.7 copy-start.17
  112.5 0.8 copy-start.18
  112.5 0.8 copy-start.19
  112.6 0.9 copy-start.20
  133.0 11.1 %collective-permute-start.11 = (bf16[4,64,512]{2,1,0:T(8,128)(2,1)}, bf16[4,64,512]{2,1,0:T(8,128)(2,1)S(1)}, u32[]{:S(2)}, u32[]{:S(2)}) collective-permute-start(bf16[4,64,512]{2,1,0:T(8,128)(2,1)} %get-tuple-element.59), channel_id=1, source_target_pairs={{0,7},{1,0},{2,1},{3,2},{4,3},{5,4},{6,5},{7,6},{8,15},{9,8},{10,9... | collective-permute-start | bytes 786440 | tf_op jit(solution)/shard_map/ppermute | solution.py:300
  133.0 11.1 %collective-permute-start.10 = (bf16[4,64,512]{2,1,0:T(8,128)(2,1)}, bf16[4,64,512]{2,1,0:T(8,128)(2,1)S(1)}, u32[]{:S(2)}, u32[]{:S(2)}) collective-permute-start(bf16[4,64,512]{2,1,0:T(8,128)(2,1)} %get-tuple-element.59), channel_id=1, source_target_pairs={{0,1},{1,2},{2,3},{3,4},{4,5},{5,6},{6,7},{7,0},{8,9},{9,10},{10,1... | collective-permute-start | bytes 786440 | tf_op jit(solution)/shard_map/ppermute | solution.py:300
  134.7 10.5 %collective-permute-start.9 = (bf16[4,64,512]{2,1,0:T(8,128)(2,1)}, bf16[4,64,512]{2,1,0:T(8,128)(2,1)S(1)}, u32[]{:S(2)}, u32[]{:S(2)}) collective-permute-start(bf16[4,64,512]{2,1,0:T(8,128)(2,1)} %get-tuple-element.59), channel_id=1, source_target_pairs={{0,120},{8,0},{16,8},{24,16},{32,24},{40,32},{48,40},{56,48},{64,5... | collective-permute-start | bytes 786440 | tf_op jit(solution)/shard_map/ppermute | solution.py:300
  139.5 11.1 %collective-permute-start.8 = (bf16[4,64,512]{2,1,0:T(8,128)(2,1)}, bf16[4,64,512]{2,1,0:T(8,128)(2,1)S(1)}, u32[]{:S(2)}, u32[]{:S(2)}) collective-permute-start(bf16[4,64,512]{2,1,0:T(8,128)(2,1)} %get-tuple-element.59), channel_id=1, source_target_pairs={{0,8},{8,16},{16,24},{24,32},{32,40},{40,48},{48,56},{56,64},{64,7... | collective-permute-start | bytes 786440 | tf_op jit(solution)/shard_map/ppermute | solution.py:300
  144.1 6.5 %copy-start.21 = (bf16[4,64,512]{2,1,0:T(8,128)(2,1)}, bf16[4,64,512]{2,1,0:T(8,128)(2,1)S(1)}, u32[]{:S(2)}) copy-start(bf16[4,64,512]{2,1,0:T(8,128)(2,1)S(1)} %collective-permute-done.11.n3) | copy-start | bytes 786436
  144.1 6.5 %copy-start.22 = (bf16[4,64,512]{2,1,0:T(8,128)(2,1)}, bf16[4,64,512]{2,1,0:T(8,128)(2,1)S(1)}, u32[]{:S(2)}) copy-start(bf16[4,64,512]{2,1,0:T(8,128)(2,1)S(1)} %collective-permute-done.10.n2) | copy-start | bytes 786436
  145.2 5.4 %copy-start.23 = (bf16[4,64,512]{2,1,0:T(8,128)(2,1)}, bf16[4,64,512]{2,1,0:T(8,128)(2,1)S(1)}, u32[]{:S(2)}) copy-start(bf16[4,64,512]{2,1,0:T(8,128)(2,1)S(1)} %collective-permute-done.9.n1) | copy-start | bytes 786436
  150.6 0.7 copy-start.24
  151.3 8.6 %copy-start.4 = (bf16[512,512]{1,0:T(8,128)(2,1)S(1)}, bf16[512,512]{1,0:T(8,128)(2,1)}, u32[]{:S(2)}) copy-start(bf16[512,512]{1,0:T(8,128)(2,1)} %get-tuple-element.77) | copy-start | bytes 1572868
  151.3 8.6 %copy-start.5 = (bf16[512,512]{1,0:T(8,128)(2,1)S(1)}, bf16[512,512]{1,0:T(8,128)(2,1)}, u32[]{:S(2)}) copy-start(bf16[512,512]{1,0:T(8,128)(2,1)} %get-tuple-element.78) | copy-start | bytes 1572868
  162.2 4.5 %copy-start.16 = (bf16[4,64,512]{2,1,0:T(8,128)(2,1)S(1)}, bf16[4,64,512]{2,1,0:T(8,128)(2,1)}, u32[]{:S(2)}) copy-start(bf16[4,64,512]{2,1,0:T(8,128)(2,1)} %get-tuple-element.70) | copy-start | bytes 786436
  162.2 4.5 %copy-start.15 = (bf16[4,64,512]{2,1,0:T(8,128)(2,1)S(1)}, bf16[4,64,512]{2,1,0:T(8,128)(2,1)}, u32[]{:S(2)}) copy-start(bf16[4,64,512]{2,1,0:T(8,128)(2,1)} %get-tuple-element.71) | copy-start | bytes 786436
  162.2 6.0 %copy-start.14 = (bf16[4,64,512]{2,1,0:T(8,128)(2,1)S(1)}, bf16[4,64,512]{2,1,0:T(8,128)(2,1)}, u32[]{:S(2)}) copy-start(bf16[4,64,512]{2,1,0:T(8,128)(2,1)} %get-tuple-element.72) | copy-start | bytes 786436
  162.2 6.6 %copy-start.13 = (bf16[4,64,512]{2,1,0:T(8,128)(2,1)S(1)}, bf16[4,64,512]{2,1,0:T(8,128)(2,1)}, u32[]{:S(2)}) copy-start(bf16[4,64,512]{2,1,0:T(8,128)(2,1)} %get-tuple-element.73) | copy-start | bytes 786436
  162.2 47.3 %all-to-all-start.4 = ((bf16[8,192,512]{2,1,0:T(8,128)(2,1)}), bf16[8,192,512]{2,1,0:T(8,128)(2,1)S(1)}, u32[]{:S(2)}, u32[]{:S(2)}) async-start(bf16[8,192,512]{2,1,0:T(8,128)(2,1)} %bitcast.15), calls=%async_computation.4 | async-start | bytes 3145728 | tf_op jit(solution)/shard_map/all_to_all | solution.py:312
  166.7 7.9 %collective-permute-start.12 = (bf16[4,64,512]{2,1,0:T(8,128)(2,1)S(1)}, bf16[4,64,512]{2,1,0:T(8,128)(2,1)S(1)}, u32[]{:S(2)}, u32[]{:S(2)}) collective-permute-start(bf16[4,64,512]{2,1,0:T(8,128)(2,1)S(1)} %copy-done.16), channel_id=1, source_target_pairs={{0,120},{8,0},{16,8},{24,16},{32,24},{40,32},{48,40},{56,48},{64,5... | collective-permute-start | bytes 786440 | tf_op jit(solution)/shard_map/ppermute | solution.py:300
  166.7 11.3 %collective-permute-start.13 = (bf16[4,64,512]{2,1,0:T(8,128)(2,1)S(1)}, bf16[4,64,512]{2,1,0:T(8,128)(2,1)S(1)}, u32[]{:S(2)}, u32[]{:S(2)}) collective-permute-start(bf16[4,64,512]{2,1,0:T(8,128)(2,1)S(1)} %copy-done.15), channel_id=1, source_target_pairs={{0,8},{8,16},{16,24},{24,32},{32,40},{40,48},{48,56},{56,64},{64,7... | collective-permute-start | bytes 786440 | tf_op jit(solution)/shard_map/ppermute | solution.py:300
  168.2 21.1 %collective-permute-start.14 = (bf16[4,64,512]{2,1,0:T(8,128)(2,1)S(1)}, bf16[4,64,512]{2,1,0:T(8,128)(2,1)S(1)}, u32[]{:S(2)}, u32[]{:S(2)}) collective-permute-start(bf16[4,64,512]{2,1,0:T(8,128)(2,1)S(1)} %copy-done.14), channel_id=1, source_target_pairs={{0,7},{1,0},{2,1},{3,2},{4,3},{5,4},{6,5},{7,6},{8,15},{9,8},{10,9... | collective-permute-start | bytes 786440 | tf_op jit(solution)/shard_map/ppermute | solution.py:300
  168.8 20.4 %collective-permute-start.15 = (bf16[4,64,512]{2,1,0:T(8,128)(2,1)S(1)}, bf16[4,64,512]{2,1,0:T(8,128)(2,1)S(1)}, u32[]{:S(2)}, u32[]{:S(2)}) collective-permute-start(bf16[4,64,512]{2,1,0:T(8,128)(2,1)S(1)} %copy-done.13), channel_id=1, source_target_pairs={{0,1},{1,2},{2,3},{3,4},{4,5},{5,6},{6,7},{7,0},{8,9},{9,10},{10,1... | collective-permute-start | bytes 786440 | tf_op jit(solution)/shard_map/ppermute | solution.py:300
  174.6 14.7 %copy-start.6 = (bf16[4,64,512]{2,1,0:T(8,128)(2,1)}, bf16[4,64,512]{2,1,0:T(8,128)(2,1)S(1)}, u32[]{:S(2)}) copy-start(bf16[4,64,512]{2,1,0:T(8,128)(2,1)S(1)} %collective-permute-done.12.r0) | copy-start | bytes 786436
  178.0 11.3 %copy-start.7 = (bf16[4,64,512]{2,1,0:T(8,128)(2,1)}, bf16[4,64,512]{2,1,0:T(8,128)(2,1)S(1)}, u32[]{:S(2)}) copy-start(bf16[4,64,512]{2,1,0:T(8,128)(2,1)S(1)} %collective-permute-done.13.r1) | copy-start | bytes 786436
  189.2 0.7 copy-start.8
  189.9 0.7 copy-start.9
  209.5 16.9 %all-to-all-start.1 = ((bf16[16,48,512]{2,1,0:T(8,128)(2,1)}), bf16[16,48,512]{2,1,0:T(8,128)(2,1)S(1)}, u32[]{:S(2)}, u32[]{:S(2)}) async-start(bf16[16,48,512]{2,1,0:T(8,128)(2,1)} %bitcast.39), calls=%async_computation.1 | async-start | bytes 1572864 | tf_op jit(solution)/shard_map/all_to_all | solution.py:312
  226.3 11.2 %all-to-all-start.5 = ((bf16[16,12,512]{2,1,0:T(8,128)(2,1)}), bf16[16,12,512]{2,1,0:T(8,128)(2,1)S(1)}, u32[]{:S(2)}, u32[]{:S(2)}) async-start(bf16[16,12,512]{2,1,0:T(8,128)(2,1)} %reshape.45), calls=%async_computation.5 | async-start | bytes 524288 | tf_op jit(solution)/shard_map/all_to_all | solution.py:312
  238.3 15.4 %all-to-all-start.2 = ((bf16[8,48,512]{2,1,0:T(8,128)(2,1)}), bf16[8,48,512]{2,1,0:T(8,128)(2,1)S(1)}, u32[]{:S(2)}, u32[]{:S(2)}) async-start(bf16[8,48,512]{2,1,0:T(8,128)(2,1)} %broadcast_in_dim.10), calls=%async_computation.2 | async-start | bytes 786432 | tf_op jit(solution)/shard_map/all_to_all | solution.py:312
  254.5 11.4 %all-to-all-start.6 = ((bf16[16,12,512]{2,1,0:T(8,128)(2,1)}), bf16[16,12,512]{2,1,0:T(8,128)(2,1)S(1)}, u32[]{:S(2)}, u32[]{:S(2)}) async-start(bf16[16,12,512]{2,1,0:T(8,128)(2,1)} %broadcast_in_dim.12), calls=%async_computation.6 | async-start | bytes 524288 | tf_op jit(solution)/shard_map/all_to_all | solution.py:312
  266.8 16.2 %all-to-all-start.3 = ((bf16[16,48,512]{2,1,0:T(8,128)(2,1)}), bf16[16,48,512]{2,1,0:T(8,128)(2,1)S(1)}, u32[]{:S(2)}, u32[]{:S(2)}) async-start(bf16[16,48,512]{2,1,0:T(8,128)(2,1)} %broadcast_in_dim.11), calls=%async_computation.3 | async-start | bytes 1572864 | tf_op jit(solution)/shard_map/all_to_all | solution.py:312
  284.3 26.9 %all-to-all-start.7 = ((bf16[8,192,512]{2,1,0:T(8,128)(2,1)}), bf16[8,192,512]{2,1,0:T(8,128)(2,1)S(1)}, u32[]{:S(2)}, u32[]{:S(2)}) async-start(bf16[8,192,512]{2,1,0:T(8,128)(2,1)} %broadcast_in_dim.14), calls=%async_computation.7 | async-start | bytes 3145728 | tf_op jit(solution)/shard_map/all_to_all | solution.py:312

commit v2 on v1

v2 whole, which is shorter than its diff:
```python
import jax
import jax.numpy as jnp
from jax import lax
from jax.experimental import pallas as pl
from jax.experimental.pallas import tpu as pltpu
from jax.sharding import PartitionSpec as P

CHAN = 227
WIDTH = 512
BLOCK = 64
GRID_BLOCKS = 128
MESH_BLOCKS = 16
SHOWN = 4
G_SLOTS = 8
M_SLOTS = 6
EXTENDED = MESH_BLOCKS + 4 * SHOWN
MESH_ROWS = MESH_BLOCKS * BLOCK
GRID_ROWS = GRID_BLOCKS * BLOCK
SPLIT = 112
PACKED = CHAN - SPLIT
TAIL = 256
DEVICES = 128
SLAB = 4 * WIDTH
EARLY = 3 * SLAB // DEVICES
LATE = (SLAB + 4 * TAIL) // DEVICES
AXES = ("wide", "narrow")
BF16 = jnp.bfloat16
F32 = jnp.float32
MIB = 1 << 20

VM = pl.BlockSpec(memory_space=pltpu.VMEM)
SM = pl.BlockSpec(memory_space=pltpu.SMEM)


def kernel_call(body, outs, ins, scratch=(), flops=0, moved=0, limit=56):
    return pl.pallas_call(
        body,
        out_shape=[jax.ShapeDtypeStruct(shape, dtype) for shape, dtype in outs],
        in_specs=ins,
        out_specs=[VM] * len(outs),
        scratch_shapes=list(scratch),
        compiler_params=pltpu.CompilerParams(vmem_limit_bytes=limit * MIB),
        cost_estimate=pl.CostEstimate(flops=flops, bytes_accessed=moved, transcendentals=0),
    )


def times(left, right, left_dim=1, right_dim=0):
    return lax.dot_general(
        left, right, (((left_dim,), (right_dim,)), ((), ())), preferred_element_type=F32
    )


def sigmoid(values):
    return 0.5 * jnp.tanh(0.5 * values) + 0.5


def silu_grad(values):
    s = sigmoid(values)
    return s * (1.0 + values * (1.0 - s))


def swap_halves(tile):
    return jnp.concatenate([tile[:, BLOCK:], tile[:, :BLOCK]], axis=1)


def low_lanes(rows):
    return lax.broadcasted_iota(jnp.int32, (rows, 2 * BLOCK), 1) < BLOCK


def rows_of(block):
    return pl.ds(pl.multiple_of(block * BLOCK, BLOCK), BLOCK)


def chunk(step, size):
    return pl.ds(pl.multiple_of(step * size, size), size)


def pack_body(send, features, out):
    low = low_lanes(PACKED)
    step = pl.program_id(0)

    def one(j, carry):
        block = send[0, step * 16 + j]
        lanes = chunk(block // 2, 2 * BLOCK)

        @pl.when(block % 2 == 0)
        def _():
            out[j] = jnp.where(low, features[0:PACKED, lanes], swap_halves(features[SPLIT:CHAN, lanes]))

        @pl.when(block % 2 == 1)
        def _():
            out[j] = jnp.where(low, swap_halves(features[0:PACKED, lanes]), features[SPLIT:CHAN, lanes])

        return carry

    lax.fori_loop(0, 16, one, 0, unroll=4)


def scatter_back(coeffs, gradient, source, table, slots, blocks):
    def clear(i, carry):
        table[i] = jnp.zeros((BLOCK, WIDTH), F32)
        return carry

    lax.fori_loop(0, blocks, clear, 0, unroll=4)

    def one(b, carry):
        parts = times(coeffs[b], gradient[rows_of(b), :], 0, 0)
        for k in range(slots):
            at = source[b, k]
            table[at] = table[at] + parts[k * BLOCK : (k + 1) * BLOCK]
        return carry

    lax.fori_loop(0, MESH_BLOCKS, one, 0)


def gather_mix(coeffs, pick, slots, b):
    picked = jnp.concatenate([pick(b, k) for k in range(slots)], axis=0)
    return times(coeffs[b], picked)


def add_returned(own, returned, shown, take):
    for h in range(SHOWN):
        at = shown[0, h]
        extra = (returned[0][h].astype(F32) + returned[1][h].astype(F32)) + (
            returned[2][h].astype(F32) + returned[3][h].astype(F32)
        )
        take[rows_of(at), :] = take[rows_of(at), :] + extra


def write_halo(table, own, halos):
    for i in range(MESH_BLOCKS):
        own[i * BLOCK : (i + 1) * BLOCK, :] = table[i].astype(own.dtype)
    for e in range(4):
        for h in range(SHOWN):
            halos[e][h] = table[MESH_BLOCKS + e * SHOWN + h].astype(BF16)


def early_back_body(source, cot, up, coeffs, own, h0, h1, h2, h3, table, lowered):
    def step(c, carry):
        rows = chunk(c, 256)
        lowered[rows, :] = times(cot[rows, :], up[...], 1, 1).astype(BF16)
        return carry

    lax.fori_loop(0, MESH_ROWS // 256, step, 0)
    scatter_back(coeffs, lowered, source, table, M_SLOTS, EXTENDED)
    write_halo(table, own, (h0, h1, h2, h3))


def encode_body(
    source, shown, packed, weight, coeffs, message, points, slope, mesh, sent, slope_m, mine, embedded
):
    step = pl.program_id(0)
    low = low_lanes(PACKED)
    for p in range(4):
        a = packed[2 * p]
        b = packed[2 * p + 1]
        lanes = slice(p * 128, p * 128 + 128)
        points[0:SPLIT, lanes] = jnp.where(low, a, swap_halves(b))[0:SPLIT]
        points[SPLIT:CHAN, lanes] = jnp.where(low, swap_halves(a), b)
    pre = times(points[...], weight[...], 0, 0)
    s = sigmoid(pre)
    e = pre * s
    embedded[chunk(step, 512), :] = e.astype(BF16)
    slope[...] = (s + e * (1.0 - s)).astype(BF16)

    @pl.when(step == GRID_ROWS // 512 - 1)
    def _():
        def mix(b, carry):
            pick = lambda b, k: embedded[rows_of(source[b, k]), :]
            mesh[rows_of(b), :] = gather_mix(coeffs, pick, G_SLOTS, b).astype(BF16)
            return carry

        lax.fori_loop(0, MESH_BLOCKS, mix, 0, unroll=2)

        def talk(c, carry):
            rows = chunk(c, 256)
            pre = times(mesh[rows, :], message[...])
            s = sigmoid(pre)
            e = pre * s
            sent[rows, :] = e.astype(BF16)
            slope_m[rows, :] = (s + e * (1.0 - s)).astype(BF16)
            return carry

        lax.fori_loop(0, MESH_ROWS // 256, talk, 0)
        for h in range(SHOWN):
            mine[h] = sent[rows_of(shown[0, h]), :]


def extend(extended, sent, halos):
    extended[0:MESH_ROWS, :] = sent[...]
    for e in range(4):
        for h in range(SHOWN):
            at = MESH_ROWS + (e * SHOWN + h) * BLOCK
            extended[at : at + BLOCK, :] = halos[e][h]


def mix_mesh(coeffs, extended, source, aggregate):
    def mix(b, carry):
        pick = lambda b, k: extended[rows_of(source[b, k]), :]
        aggregate[rows_of(b), :] = gather_mix(coeffs, pick, M_SLOTS, b).astype(BF16)
        return carry

    lax.fori_loop(0, MESH_BLOCKS, mix, 0, unroll=2)


def forward_body(
    source, shown, sent, n0, n1, n2, n3, coeffs, mesh, up, message,
    aggregate, mesh_1, sent_1, slope_m, mine, extended,
):
    extend(extended, sent, (n0, n1, n2, n3))
    mix_mesh(coeffs, extended, source, aggregate)

    def step(c, carry):
        rows = chunk(c, 256)
        state = (mesh[rows, :].astype(F32) + times(aggregate[rows, :], up[...])).astype(BF16)
        mesh_1[rows, :] = state
        pre = times(state, message[...])
        s = sigmoid(pre)
        e = pre * s
        sent_1[rows, :] = e.astype(BF16)
        slope_m[rows, :] = (s + e * (1.0 - s)).astype(BF16)
        return carry

    lax.fori_loop(0, MESH_ROWS // 256, step, 0)
    for h in range(SHOWN):
        mine[h] = sent_1[rows_of(shown[0, h]), :]


def backward_body(
    source, shown, own, r0, r1, r2, r3, slope_m, cot, message, up, coeffs,
    grad_pre, grad_1, own_0, h0, h1, h2, h3, table, lowered, grad_msg,
):
    grad_msg[...] = own[...].astype(F32)
    add_returned(own, (r0, r1, r2, r3), shown, grad_msg)

    def step(c, carry):
        rows = chunk(c, 256)
        gp = (grad_msg[rows, :] * slope_m[rows, :].astype(F32)).astype(BF16)
        grad_pre[rows, :] = gp
        g = cot[rows, :].astype(F32) + times(gp, message[...], 1, 1)
        grad_1[rows, :] = g
        lowered[rows, :] = times(g.astype(BF16), up[...], 1, 1).astype(BF16)
        return carry

    lax.fori_loop(0, MESH_ROWS // 256, step, 0)
    scatter_back(coeffs, lowered, source, table, M_SLOTS, EXTENDED)
    write_halo(table, own_0, (h0, h1, h2, h3))


def write_slabs(out, first, values):
    rows = values.shape[0]
    for c in range(4):
        out[first + c * rows : first + (c + 1) * rows, :] = values[:, c * 128 : (c + 1) * 128].astype(BF16)


def grads_body(
    source, sent, n0, n1, n2, n3, coeffs, mesh, up, cot, aggregate_0, grad_1, grad_pre,
    mesh_out, grads, extended, aggregate,
):
    write_slabs(grads, 0, times(aggregate_0[...], grad_1[...].astype(BF16), 0, 0))
    write_slabs(grads, SLAB, times(mesh[...], grad_pre[...], 0, 0))
    extend(extended, sent, (n0, n1, n2, n3))
    mix_mesh(coeffs, extended, source, aggregate)

    def step(c, carry):
        rows = chunk(c, 256)
        update = times(aggregate[rows, :], up[...])
        mesh_out[rows, :] = (mesh[rows, :].astype(F32) + update).astype(BF16)
        return carry

    lax.fori_loop(0, MESH_ROWS // 256, step, 0)
    write_slabs(grads, 2 * SLAB, times(aggregate[...], cot[...], 0, 0))


def final_body(
    source, shown, own, r0, r1, r2, r3, slope_m, grad_1, message, mesh, coeffs, slope, points,
    grads, table, grad_pre, lowered, grad_msg, total,
):
    c = pl.program_id(0)

    @pl.when(c == 0)
    def _():
        grad_msg[...] = own[...].astype(F32)
        add_returned(own, (r0, r1, r2, r3), shown, grad_msg)

        def step(c, carry):
            rows = chunk(c, 256)
            gp = (grad_msg[rows, :] * slope_m[rows, :].astype(F32)).astype(BF16)
            grad_pre[rows, :] = gp
            lowered[rows, :] = (grad_1[rows, :] + times(gp, message[...], 1, 1)).astype(BF16)
            return carry

        lax.fori_loop(0, MESH_ROWS // 256, step, 0)
        scatter_back(coeffs, lowered, source, table, G_SLOTS, GRID_BLOCKS)
        write_slabs(grads, 0, times(mesh[...], grad_pre[...], 0, 0))
        total[...] = jnp.zeros_like(total)

    grad = table[pl.ds(pl.multiple_of(c * 8, 8), 8)].reshape(512, WIDTH).astype(BF16)
    grad = (grad.astype(F32) * slope[...].astype(F32)).astype(BF16)
    total[0:CHAN, :] = total[0:CHAN, :] + times(points[...], grad)

    @pl.when(c == GRID_ROWS // 512 - 1)
    def _():
        write_slabs(grads, SLAB, total[...])


def sum_body(early, late, out, total):
    total[0:EARLY, :] = jnp.sum(early[...].astype(F32), axis=0)
    total[EARLY : EARLY + LATE, :] = jnp.sum(late[...].astype(F32), axis=0)
    rounded = total[...].astype(BF16)

    def one(i, carry):
        out[i] = rounded
        return carry

    lax.fori_loop(0, DEVICES, one, 0, unroll=8)


def unpack_body(parts, d_embed, ms_grad, up_grad, early, late):
    def one(i, carry):
        part = parts[i].astype(F32)
        early[pl.ds(pl.multiple_of(i * EARLY, 8), EARLY), :] = part[0:EARLY]
        late[pl.ds(pl.multiple_of(i * LATE, 8), LATE), :] = part[EARLY : EARLY + LATE]
        return carry

    lax.fori_loop(0, DEVICES, one, 0, unroll=4)
    for c in range(4):
        columns = slice(c * 128, (c + 1) * 128)
        at = lambda first: slice(first + c * WIDTH, first + (c + 1) * WIDTH)
        up_grad[0, :, columns] = early[at(0), :]
        ms_grad[1, :, columns] = early[at(SLAB), :]
        up_grad[1, :, columns] = early[at(2 * SLAB), :]
        ms_grad[0, :, columns] = late[at(0), :]
        d_embed[:, columns] = late[SLAB + c * TAIL : SLAB + c * TAIL + CHAN, :]


def shift(value, axis, steps):
    count = lax.axis_size(axis)
    return lax.ppermute(value, axis, [(i, (i + steps) % count) for i in range(count)])


def show(mine):
    return (shift(mine, "wide", 1), shift(mine, "wide", -1), shift(mine, "narrow", 1), shift(mine, "narrow", -1))


def give_back(h0, h1, h2, h3):
    return (shift(h0, "wide", -1), shift(h1, "wide", 1), shift(h2, "narrow", -1), shift(h3, "narrow", 1))


def exchange(parts):
    return lax.all_to_all(parts, AXES, split_axis=0, concat_axis=0, tiled=True)


def on_device(
    grid_feat, grid_send, w_embed, g2m_src, g2m_coef, mesh_src, mesh_coef, halo_send,
    message_weight, update_weight, cotangent,
):
    rows_bf16 = ((MESH_ROWS, WIDTH), BF16)
    rows_f32 = ((MESH_ROWS, WIDTH), F32)
    halo = ((SHOWN, BLOCK, WIDTH), BF16)
    mesh_scratch = pltpu.VMEM((MESH_ROWS, WIDTH), BF16)
    mesh_scratch32 = pltpu.VMEM((MESH_ROWS, WIDTH), F32)
    extended_scratch = pltpu.VMEM((EXTENDED * BLOCK, WIDTH), BF16)
    table_scratch = pltpu.VMEM((EXTENDED, BLOCK, WIDTH), F32)
    w_m = (message_weight[0], message_weight[1])
    w_u = (update_weight[0], update_weight[1])

    packed = pl.pallas_call(
        pack_body,
        grid=(GRID_BLOCKS // 16,),
        out_shape=jax.ShapeDtypeStruct((GRID_BLOCKS, PACKED, 2 * BLOCK), BF16),
        in_specs=[SM, pl.BlockSpec((CHAN, GRID_ROWS), lambda i: (0, 0))],
        out_specs=pl.BlockSpec((16, PACKED, 2 * BLOCK), lambda i: (i, 0, 0)),
        compiler_params=pltpu.CompilerParams(vmem_limit_bytes=56 * MIB),
        cost_estimate=pl.CostEstimate(flops=0, bytes_accessed=8 * MIB, transcendentals=0),
    )(grid_send, grid_feat.T)
    received = exchange(packed)

    g_mix = g2m_coef.transpose(0, 2, 1, 3).reshape(MESH_BLOCKS, BLOCK, G_SLOTS * BLOCK)
    m_mix = mesh_coef.transpose(0, 2, 1, 3).reshape(MESH_BLOCKS, BLOCK, M_SLOTS * BLOCK)

    own_1, *halos = kernel_call(
        early_back_body, [rows_f32] + [halo] * 4, [SM] + [VM] * 3, [table_scratch, mesh_scratch],
        flops=2 * 10**9, moved=8 * MIB,
    )(mesh_src, cotangent, w_u[1], m_mix)
    returned_1 = give_back(*halos)

    received, g_mix, m_mix = lax.optimization_barrier((received, g_mix, m_mix))
    whole = lambda *shape: pl.BlockSpec(shape, lambda i: (0,) * len(shape))
    points, slope, mesh_0, sent_0, slope_0, mine_0 = pl.pallas_call(
        encode_body,
        grid=(GRID_ROWS // 512,),
        out_shape=[
            jax.ShapeDtypeStruct((CHAN, GRID_ROWS), BF16),
            jax.ShapeDtypeStruct((GRID_ROWS, WIDTH), BF16),
            jax.ShapeDtypeStruct((MESH_ROWS, WIDTH), BF16),
            jax.ShapeDtypeStruct((MESH_ROWS, WIDTH), BF16),
            jax.ShapeDtypeStruct((MESH_ROWS, WIDTH), BF16),
            jax.ShapeDtypeStruct((SHOWN, BLOCK, WIDTH), BF16),
        ],
        in_specs=[
            SM, SM,
            pl.BlockSpec((8, PACKED, 2 * BLOCK), lambda i: (i, 0, 0)),
            whole(CHAN, WIDTH), whole(MESH_BLOCKS, BLOCK, G_SLOTS * BLOCK), whole(WIDTH, WIDTH),
        ],
        out_specs=[
            pl.BlockSpec((CHAN, 512), lambda i: (0, i)),
            pl.BlockSpec((512, WIDTH), lambda i: (i, 0)),
            whole(MESH_ROWS, WIDTH), whole(MESH_ROWS, WIDTH), whole(MESH_ROWS, WIDTH),
            whole(SHOWN, BLOCK, WIDTH),
        ],
        scratch_shapes=[pltpu.VMEM((GRID_ROWS, WIDTH), BF16)],
        compiler_params=pltpu.CompilerParams(vmem_limit_bytes=56 * MIB),
        cost_estimate=pl.CostEstimate(flops=4 * 10**9, bytes_accessed=20 * MIB, transcendentals=0),
    )(g2m_src, halo_send, received, w_embed, g_mix, w_m[0])
    shown_0 = show(mine_0)

    aggregate_0, mesh_1, sent_1, slope_1, mine_1 = kernel_call(
        forward_body, [rows_bf16] * 4 + [halo], [SM, SM] + [VM] * 9, [extended_scratch],
        flops=2 * 10**9, moved=10 * MIB,
    )(mesh_src, halo_send, sent_0, *shown_0, m_mix, mesh_0, w_u[0], w_m[1])
    shown_1 = show(mine_1)

    grad_pre_1, grad_1, own_0, *halos = kernel_call(
        backward_body, [rows_bf16, rows_f32, rows_f32] + [halo] * 4, [SM, SM] + [VM] * 10,
        [table_scratch, mesh_scratch, mesh_scratch32], flops=2 * 10**9, moved=16 * MIB,
    )(mesh_src, halo_send, own_1, *returned_1, slope_1, cotangent, w_m[1], w_u[0], m_mix)
    returned_0 = give_back(*halos)

    mesh_out, early = kernel_call(
        grads_body, [rows_bf16, ((3 * SLAB, 128), BF16)], [SM] + [VM] * 12,
        [extended_scratch, mesh_scratch], flops=4 * 10**9, moved=14 * MIB,
    )(
        mesh_src, sent_1, *shown_1, m_mix, mesh_1, w_u[1], cotangent, aggregate_0, grad_1,
        grad_pre_1,
    )
    own_0, early = lax.optimization_barrier((own_0, early))
    early = exchange(early.reshape(DEVICES, EARLY, 128))

    late = pl.pallas_call(
        final_body,
        grid=(GRID_ROWS // 512,),
        out_shape=jax.ShapeDtypeStruct((SLAB + 4 * TAIL, 128), BF16),
        in_specs=[
            SM, SM, whole(MESH_ROWS, WIDTH), *[whole(SHOWN, BLOCK, WIDTH)] * 4,
            whole(MESH_ROWS, WIDTH), whole(MESH_ROWS, WIDTH), whole(WIDTH, WIDTH),
            whole(MESH_ROWS, WIDTH), whole(MESH_BLOCKS, BLOCK, G_SLOTS * BLOCK),
            pl.BlockSpec((512, WIDTH), lambda i: (i, 0)),
            pl.BlockSpec((CHAN, 512), lambda i: (0, i)),
        ],
        out_specs=whole(SLAB + 4 * TAIL, 128),
        scratch_shapes=[
            pltpu.VMEM((GRID_BLOCKS, BLOCK, WIDTH), F32),
            mesh_scratch, mesh_scratch, mesh_scratch32,
            pltpu.VMEM((TAIL, WIDTH), F32),
        ],
        compiler_params=pltpu.CompilerParams(vmem_limit_bytes=56 * MIB),
        cost_estimate=pl.CostEstimate(flops=4 * 10**9, bytes_accessed=24 * MIB, transcendentals=0),
    )(
        g2m_src, halo_send, own_0, *returned_0, slope_0, grad_1, w_m[0], mesh_0, g_mix, slope,
        points,
    )
    late = exchange(late.reshape(DEVICES, LATE, 128))

    totals = kernel_call(
        sum_body, [((DEVICES, EARLY + LATE, 128), BF16)], [VM, VM],
        [pltpu.VMEM((EARLY + LATE, 128), F32)], moved=5 * MIB,
    )(early, late)[0]
    d_embed, ms_grad, up_grad = kernel_call(
        unpack_body,
        [((CHAN, WIDTH), F32), ((2, WIDTH, WIDTH), F32), ((2, WIDTH, WIDTH), F32)],
        [VM],
        [pltpu.VMEM((3 * SLAB, 128), F32), pltpu.VMEM((SLAB + 4 * TAIL, 128), F32)],
        moved=7 * MIB,
    )(exchange(totals))
    return mesh_out, d_embed, ms_grad, up_grad


def solution(mesh):
    split = P(AXES, None)
    return jax.shard_map(
        on_device,
        mesh=mesh,
        in_specs=(
            split, split, P(), split, P(AXES, None, None, None), split, P(AXES, None, None, None),
            split, P(), P(), split,
        ),
        out_specs=(split, P(), P(), P()),
        check_vma=False,
    )
```

time: 316 us -> 293 us (0.927)
  blocking collectives: 0 us -> 91.3 us
  waiting for transfers between devices: 105 us -> 38.1 us
  starting transfers between devices: 67.8 us -> 34.1 us
  local copies, waits for them, and re-layouts: 30 us -> 16.7 us
  other arithmetic: 6.53 us -> 0 us
  Pallas kernels: 105 us -> 111 us
    all_to_all x0 -> x3, blocking collectives: none -> 91.3 us  [exchange(): return lax.all_to_all(parts, AXES, split_axis=0, concat_axis=0, tiled=True)]
    all_to_all x8 -> x1, waiting for transfers between devices: 79.8 us -> 38 us  [exchange(): return lax.all_to_all(parts, AXES, split_axis=0, concat_axis=0, tiled=True)]
    all_to_all x8 -> x1, starting transfers between devices: 44.3 us -> 11.9 us  [exchange(): return lax.all_to_all(parts, AXES, split_axis=0, concat_axis=0, tiled=True)]
    ppermute x16, waiting for transfers between devices: 25.4 us -> 0.04 us  [shift(): lax.ppermute(value, axis, [(i, (i + steps) % count) for i in range(count)])]
    pallas_call x7 -> x8, Pallas kernels: 95.4 us -> 102 us  [the longest x1 24.9 us: on_device(): pl.pallas_call(final_body, grid=(GRID_ROWS // 512,), out_shape=jax.ShapeD...]
    transpose x2 -> x0, local copies, waits for them, and re-layouts: 4.26 us -> none  [the longest x1 2.68 us: on_device(): g2m_coef.transpose(0, 1, 3, 2).reshape(MESH_BLOCKS, G_SLOTS * BLOCK, BLOCK)]
    broadcast_in_dim x5 -> x0, local copies, waits for them, and re-layouts: 3.79 us -> none  [gather_all(): return exchange(jnp.broadcast_to(rows[None], (count,) + rows.shape), axis)]
  transfers between devices with their start and end apart: 24 -> 17, of which waited for: 12 -> 1; matrix products, arithmetic and copies ran while one was open for 8% -> 5% of each run, Pallas kernels for 22% -> 14%
where the time goes in v2:
time: 293 us; the launch traced here: 292 us
  Pallas kernels  111 us (38%)
  blocking collectives  91.3 us (31%)
  waiting for transfers between devices  38.1 us (13%)
  starting transfers between devices  34.1 us (12%)
  local copies, waits for them, and re-layouts  16.7 us (6%)
    all_to_all x3, blocking collectives, exchange(): return lax.all_to_all(parts, AXES, split_axis=0, concat_axis=0, tiled=True)  91.3 us
    all_to_all x1, waiting for transfers between devices, exchange(): return lax.all_to_all(parts, AXES, split_axis=0, concat_axis=0, tiled=True)  38 us
    pallas_call x1, Pallas kernels, on_device(): pl.pallas_call(final_body, grid=(GRID_ROWS // 512,), out_shape=jax.ShapeD...  24.9 us
    pallas_call x1, Pallas kernels, on_device(): pl.pallas_call(encode_body, grid=(GRID_ROWS // 512,), out_shape=[jax.Shap...  22.4 us
    ppermute x16, starting transfers between devices, shift(): lax.ppermute(value, axis, [(i, (i + steps) % count) for i in range(count)])  22.2 us
    pallas_call x1, Pallas kernels, on_device(): pl.pallas_call(pack_body, grid=(GRID_BLOCKS // 16,), out_shape=jax.ShapeD...  14.4 us
    pallas_call x1, Pallas kernels, on_device(): kernel_call(backward_body, [rows_bf16, rows_f32, rows_f32] + [halo] * 4,...  12.8 us
    all_to_all x1, starting transfers between devices, exchange(): return lax.all_to_all(parts, AXES, split_axis=0, concat_axis=0, tiled=True)  11.9 us
  transfers between devices with their start and end apart: 17, of which 1 were waited for; matrix products, arithmetic and copies ran while one was open for 5% of the time, Pallas kernels for 14%

profile of v2, /device:TPU:1, one launch (start us, length us, event | category | flops | bytes accessed | tf_op | source)
XLA Modules:
  0.0 292.1 jit_solution(2881125459587837174)
XLA Ops:
  0.6 14.4 %shard_map.138 = bf16[128,115,128]{2,1,0:T(8,128)(2,1)} custom-call(s32[1,128]{1,0:T(1,128)} %send.1, bf16[227,8192]{1,0:T(8,128)(2,1)} %bitcast.15), custom_call_target="tpu_custom_call" | custom-call | bytes 8388608 | tf_op jit(solution)/shard_map/pallas_call | solution.py:368
  15.0 11.9 %all-to-all-start = ((bf16[128,115,128]{2,1,0:T(8,128)(2,1)}), bf16[128,115,128]{2,1,0:T(8,128)(2,1)}, u32[]{:S(2)}, u32[]{:S(2)}) async-start(bf16[128,115,128]{2,1,0:T(8,128)(2,1)} %shard_map.138), calls=%async_computation | async-start | bytes 7864320 | tf_op jit(solution)/shard_map/all_to_all | solution.py:351
  26.9 2.7 copy.24
  29.6 2.0 reshape.21.coeffs
  31.6 3.4 %copy.23 = bf16[16,64,8,64]{3,2,1,0:T(8,128)(2,1)S(1)} copy(bf16[16,64,8,64]{3,1,2,0:T(8,128)(2,1)} %bitcast.17) | data formatting | bytes 2097152 | tf_op jit(solution)/shard_map/transpose | solution.py:379
  35.0 0.0 copy-start.7
  35.0 0.0 copy-start.1
  35.0 2.1 reshape.20.coeffs
  37.0 0.7 copy.25.source
  37.7 1.1 slice_bitcast_fusion.1
  38.8 38.0 %all-to-all-done.packed = bf16[128,115,128]{2,1,0:T(8,128)(2,1)} async-done(((bf16[128,115,128]{2,1,0:T(8,128)(2,1)}), bf16[128,115,128]{2,1,0:T(8,128)(2,1)}, u32[]{:S(2)}, u32[]{:S(2)}) %all-to-all-start) | async-done | bytes 3768352 | tf_op jit(solution)/shard_map/all_to_all | solution.py:351
  76.8 22.4 %shard_map.139 = (bf16[227,8192]{1,0:T(8,128)(2,1)}, bf16[8192,512]{1,0:T(8,128)(2,1)}, bf16[1024,512]{1,0:T(8,128)(2,1)}, bf16[1024,512]{1,0:T(8,128)(2,1)}, bf...) custom-call(s32[16,8]{1,0:T(8,128)} %copy.25.source, s32[1,4]{1,0:T(1,128)} %shown.7, ...), custom_call_target="tpu_custom_call" | custom-call | flops 4000000000 | bytes 20971520 | tf_op jit(solution)/shard_map/pallas_call | solution.py:390
  99.2 0.0 copy-start.8
  99.3 0.1 collective-permute-start
  99.3 4.8 %collective-permute-start.1 = (bf16[4,64,512]{2,1,0:T(8,128)(2,1)}, bf16[4,64,512]{2,1,0:T(8,128)(2,1)S(1)}, u32[]{:S(2)}, u32[]{:S(2)}) collective-permute-start(bf16[4,64,512]{2,1,0:T(8,128)(2,1)} %get-tuple-element.40), channel_id=1, source_target_pairs={{0,120},{8,0},{16,8},{24,16},{32,24},{40,32},{48,40},{56,48},{64,5... | collective-permute-start | bytes 786440 | tf_op jit(solution)/shard_map/ppermute | solution.py:339
  104.1 1.6 collective-permute-start.2
  105.8 0.0 collective-permute-start.3
  105.8 1.1 slice_bitcast_fusion
  106.8 0.7 copy.29.source
  107.5 9.5 %shard_map.141 = (f32[1024,512]{1,0:T(8,128)}, bf16[4,64,512]{2,1,0:T(8,128)(2,1)}, bf16[4,64,512]{2,1,0:T(8,128)(2,1)}, bf16[4,64,512]{2,1,0:T(8,128)(2,1)}, bf16[4,64,512]{2,1,0:T(8,128)(2,1)}) custom-call(s32[16,6]{1,0:T(8,128)} %copy.29.source, bf16[1024,512]{1,0:T(8,128)(2,1)} %cot.5, bf16[512,512]{1,0:T(8,128)(2,1)} %get-tuple-element.70.up, ...), custom_call_target="tpu_custom_call" | custom-call | flops 2000000000 | bytes 8388608 | tf_op jit(solution)/shard_map/pallas_call | solution.py:382
  117.0 2.8 collective-permute-start.10
  119.8 0.0 collective-permute-done.n0
  119.8 0.0 collective-permute-start.11
  119.8 0.0 collective-permute-done.1.n1
  119.8 0.1 collective-permute-start.8
  119.9 0.0 collective-permute-done.2.n2
  119.9 1.4 collective-permute-start.9
  121.3 0.0 collective-permute-done.3.n3
  121.4 0.7 copy-done.20
  122.1 8.6 %shard_map.140 = (bf16[1024,512]{1,0:T(8,128)(2,1)}, bf16[1024,512]{1,0:T(8,128)(2,1)}, bf16[1024,512]{1,0:T(8,128)(2,1)}, bf16[1024,512]{1,0:T(8,128)(2,1)}, bf16[4,64,512]{2,1,0:T(8,128)(2,1)}) custom-call(s32[16,6]{1,0:T(8,128)} %copy.29.source, s32[1,4]{1,0:T(1,128)} %shown.7, bf16[1024,512]{1,0:T(8,128)(2,1)} %get-tuple-element.39.sent, ...), custom_call_target="tpu_custom_call" | custom-call | flops 2000000000 | bytes 10485760 | tf_op jit(solution)/shard_map/pallas_call | solution.py:418
  130.7 0.1 collective-permute-start.4
  130.8 0.0 collective-permute-done.10.r2
  130.8 4.7 %collective-permute-start.5 = (bf16[4,64,512]{2,1,0:T(8,128)(2,1)}, bf16[4,64,512]{2,1,0:T(8,128)(2,1)S(1)}, u32[]{:S(2)}, u32[]{:S(2)}) collective-permute-start(bf16[4,64,512]{2,1,0:T(8,128)(2,1)} %get-tuple-element.44), channel_id=1, source_target_pairs={{0,120},{8,0},{16,8},{24,16},{32,24},{40,32},{48,40},{56,48},{64,5... | collective-permute-start | bytes 786440 | tf_op jit(solution)/shard_map/ppermute | solution.py:339
  135.5 0.0 collective-permute-done.11.r3
  135.5 0.5 collective-permute-start.6
  136.0 0.0 collective-permute-done.8.r0
  136.0 1.1 collective-permute-start.7
  137.0 0.0 collective-permute-done.9.r1
  137.1 0.7 copy-done.15
  137.8 12.8 %shard_map.142 = (bf16[1024,512]{1,0:T(8,128)(2,1)}, f32[1024,512]{1,0:T(8,128)}, f32[1024,512]{1,0:T(8,128)}, bf16[4,64,512]{2,1,0:T(8,128)(2,1)}, bf16[4,64,51...) custom-call(s32[16,6]{1,0:T(8,128)} %copy.29.source, s32[1,4]{1,0:T(1,128)} %shown.7, ...), custom_call_target="tpu_custom_call" | custom-call | flops 2000000000 | bytes 16777216 | tf_op jit(solution)/shard_map/pallas_call | solution.py:424
  150.6 0.1 collective-permute-start.12
  150.7 0.0 collective-permute-done.4.n0
  150.7 0.0 copy-start.9
  150.7 1.4 collective-permute-start.13
  152.2 0.0 collective-permute-done.5.n1
  152.2 3.5 %collective-permute-start.14 = (bf16[4,64,512]{2,1,0:T(8,128)(2,1)}, bf16[4,64,512]{2,1,0:T(8,128)(2,1)S(1)}, u32[]{:S(2)}, u32[]{:S(2)}) collective-permute-start(bf16[4,64,512]{2,1,0:T(8,128)(2,1)} %get-tuple-element.62), channel_id=1, source_target_pairs={{0,7},{1,0},{2,1},{3,2},{4,3},{5,4},{6,5},{7,6},{8,15},{9,8},{10,9... | collective-permute-start | bytes 786440 | tf_op jit(solution)/shard_map/ppermute | solution.py:339
  155.7 0.0 collective-permute-done.6.n2
  155.7 0.0 collective-permute-start.15
  155.7 0.7 copy-done.14
  156.4 0.1 copy-done.16
  156.5 10.3 %shard_map.143 = (bf16[1024,512]{1,0:T(8,128)(2,1)}, bf16[6144,128]{1,0:T(8,128)(2,1)}) custom-call(s32[16,6]{1,0:T(8,128)} %copy.29.source, bf16[1024,512]{1,0:T(8,128)(2,1)} %get-tuple-element.43.sent, bf16[4,64,512]{2,1,0:T(8,128)(2,1)} %copy-done.9, bf16[4,64,512]{2,1,0:T(8,128)(2,1)} %copy-done.11, bf16[4,64,512]{2,1,0:T(8,128)(2,1)} %copy-done.14, ...), custom_call_target="tpu_custom_call" | custom-call | flops 4000000000 | bytes 14680064 | tf_op jit(solution)/shard_map/pallas_call | solution.py:430
  166.8 0.0 collective-permute-done.12.r0
  166.8 0.0 collective-permute-done.13.r1
  166.8 0.0 collective-permute-done.15.r3
  166.9 0.6 copy-done.3
  167.5 0.1 copy-done.4
  167.6 0.1 copy-done.5
  167.7 0.1 copy-done.6
  167.8 24.9 %shard_map.144 = bf16[3072,128]{1,0:T(8,128)(2,1)} custom-call(s32[16,8]{1,0:T(8,128)} %copy.25.source, s32[1,4]{1,0:T(1,128)} %shown.7, f32[1024,512]{1,0:T(8,128)} %get-tuple-element.59.own, bf16[4,64,512]{2,1,0:T(8,128)(2,1)} %copy-done.3, bf16[4,64,512]{2,1,0:T(8,128)(2,1)} %copy-done.4, bf16[4,64,512]{2,1,0:T(8,128)(2,1)} %copy-done.5, ...), custom_call_target="tpu_custom_call" | custom-call | flops 4000000000 | bytes 25165824 | tf_op jit(solution)/shard_map/pallas_call | solution.py:440
  192.6 23.3 %all_to_all.20.late = bf16[128,24,128]{2,1,0:T(8,128)(2,1)} all-to-all(bf16[128,24,128]{2,1,0:T(8,128)(2,1)} %bitcast.16), channel_id=1, replica_groups=mesh['wide'=16,'narrow'=8] {'wide','narrow'}, dimensions={0} | all-to-all | bytes 1572864 | tf_op jit(solution)/shard_map/all_to_all | solution.py:351
  215.9 29.4 %all_to_all.21.early = bf16[128,48,128]{2,1,0:T(8,128)(2,1)} all-to-all(bf16[128,48,128]{2,1,0:T(8,128)(2,1)S(1)} %bitcast.19), channel_id=1, replica_groups=mesh['wide'=16,'narrow'=8] {'wide','narrow'}, dimensions={0} | all-to-all | bytes 3145728 | tf_op jit(solution)/shard_map/all_to_all | solution.py:351
  245.3 3.6 %shard_map.145 = bf16[128,72,128]{2,1,0:T(8,128)(2,1)} custom-call(bf16[128,48,128]{2,1,0:T(8,128)(2,1)} %all_to_all.21.early, bf16[128,24,128]{2,1,0:T(8,128)(2,1)} %all_to_all.20.late), custom_call_target="tpu_custom_call" | custom-call | bytes 5242880 | tf_op jit(solution)/shard_map/pallas_call | solution.py:465
  248.9 38.7 %all_to_all.22.parts = bf16[128,72,128]{2,1,0:T(8,128)(2,1)} all-to-all(bf16[128,72,128]{2,1,0:T(8,128)(2,1)} %shard_map.145), channel_id=1, replica_groups=mesh['wide'=16,'narrow'=8] {'wide','narrow'}, dimensions={0} | all-to-all | bytes 4718592 | tf_op jit(solution)/shard_map/all_to_all | solution.py:351
  287.6 4.5 %shard_map.146 = (f32[227,512]{1,0:T(8,128)}, f32[2,512,512]{2,1,0:T(8,128)}, f32[2,512,512]{2,1,0:T(8,128)}) custom-call(bf16[128,72,128]{2,1,0:T(8,128)(2,1)} %all_to_all.22.parts), custom_call_target="tpu_custom_call" | custom-call | bytes 7340032 | tf_op jit(solution)/shard_map/pallas_call | solution.py:469
  (32 shorter events, 0.1 us)
Async XLA Ops:
  15.0 61.9 %all-to-all-start = ((bf16[128,115,128]{2,1,0:T(8,128)(2,1)}), bf16[128,115,128]{2,1,0:T(8,128)(2,1)}, u32[]{:S(2)}, u32[]{:S(2)}) async-start(bf16[128,115,128]{2,1,0:T(8,128)(2,1)} %shard_map.138), calls=%async_computation | async-start | bytes 7864320 | tf_op jit(solution)/shard_map/all_to_all | solution.py:351
  35.0 2.1 copy-start.7
  35.0 2.7 copy-start.1
  76.8 28.9 %copy-start.2 = (bf16[2,512,512]{2,1,0:T(8,128)(2,1)S(1)}, bf16[2,512,512]{2,1,0:T(8,128)(2,1)}, u32[]{:S(2)}) copy-start(bf16[2,512,512]{2,1,0:T(8,128)(2,1)} %param.20) | copy-start | bytes 3145732
  99.2 7.6 %copy-start.8 = (s32[16,6]{0,1:T(8,128)S(1)}, s32[16,6]{0,1:T(8,128)}, u32[]{:S(2)}) copy-start(s32[16,6]{0,1:T(8,128)} %param.16) | copy-start | bytes 1156
  99.3 20.5 %collective-permute-start = (bf16[4,64,512]{2,1,0:T(8,128)(2,1)}, bf16[4,64,512]{2,1,0:T(8,128)(2,1)S(1)}, u32[]{:S(2)}, u32[]{:S(2)}) collective-permute-start(bf16[4,64,512]{2,1,0:T(8,128)(2,1)} %get-tuple-element.40), channel_id=1, source_target_pairs={{0,8},{8,16},{16,24},{24,32},{32,40},{40,48},{48,56},{56,64},{64,7... | collective-permute-start | bytes 786440 | tf_op jit(solution)/shard_map/ppermute | solution.py:339
  99.3 20.4 %collective-permute-start.1 = (bf16[4,64,512]{2,1,0:T(8,128)(2,1)}, bf16[4,64,512]{2,1,0:T(8,128)(2,1)S(1)}, u32[]{:S(2)}, u32[]{:S(2)}) collective-permute-start(bf16[4,64,512]{2,1,0:T(8,128)(2,1)} %get-tuple-element.40), channel_id=1, source_target_pairs={{0,120},{8,0},{16,8},{24,16},{32,24},{40,32},{48,40},{56,48},{64,5... | collective-permute-start | bytes 786440 | tf_op jit(solution)/shard_map/ppermute | solution.py:339
  104.1 15.8 %collective-permute-start.2 = (bf16[4,64,512]{2,1,0:T(8,128)(2,1)}, bf16[4,64,512]{2,1,0:T(8,128)(2,1)S(1)}, u32[]{:S(2)}, u32[]{:S(2)}) collective-permute-start(bf16[4,64,512]{2,1,0:T(8,128)(2,1)} %get-tuple-element.40), channel_id=1, source_target_pairs={{0,1},{1,2},{2,3},{3,4},{4,5},{5,6},{6,7},{7,0},{8,9},{9,10},{10,1... | collective-permute-start | bytes 786440 | tf_op jit(solution)/shard_map/ppermute | solution.py:339
  105.8 15.6 %collective-permute-start.3 = (bf16[4,64,512]{2,1,0:T(8,128)(2,1)}, bf16[4,64,512]{2,1,0:T(8,128)(2,1)S(1)}, u32[]{:S(2)}, u32[]{:S(2)}) collective-permute-start(bf16[4,64,512]{2,1,0:T(8,128)(2,1)} %get-tuple-element.40), channel_id=1, source_target_pairs={{0,7},{1,0},{2,1},{3,2},{4,3},{5,4},{6,5},{7,6},{8,15},{9,8},{10,9... | collective-permute-start | bytes 786440 | tf_op jit(solution)/shard_map/ppermute | solution.py:339
  117.0 13.7 %collective-permute-start.10 = (bf16[4,64,512]{2,1,0:T(8,128)(2,1)}, bf16[4,64,512]{2,1,0:T(8,128)(2,1)S(1)}, u32[]{:S(2)}, u32[]{:S(2)}) collective-permute-start(bf16[4,64,512]{2,1,0:T(8,128)(2,1)} %get-tuple-element.50), channel_id=1, source_target_pairs={{0,7},{1,0},{2,1},{3,2},{4,3},{5,4},{6,5},{7,6},{8,15},{9,8},{10,9... | collective-permute-start | bytes 786440 | tf_op jit(solution)/shard_map/ppermute | solution.py:339
  119.8 1.6 copy-start.17
  119.8 15.7 %collective-permute-start.11 = (bf16[4,64,512]{2,1,0:T(8,128)(2,1)}, bf16[4,64,512]{2,1,0:T(8,128)(2,1)S(1)}, u32[]{:S(2)}, u32[]{:S(2)}) collective-permute-start(bf16[4,64,512]{2,1,0:T(8,128)(2,1)} %get-tuple-element.51), channel_id=1, source_target_pairs={{0,1},{1,2},{2,3},{3,4},{4,5},{5,6},{6,7},{7,0},{8,9},{9,10},{10,1... | collective-permute-start | bytes 786440 | tf_op jit(solution)/shard_map/ppermute | solution.py:339
  119.8 1.6 copy-start.18
  119.8 16.2 %collective-permute-start.8 = (bf16[4,64,512]{2,1,0:T(8,128)(2,1)}, bf16[4,64,512]{2,1,0:T(8,128)(2,1)S(1)}, u32[]{:S(2)}, u32[]{:S(2)}) collective-permute-start(bf16[4,64,512]{2,1,0:T(8,128)(2,1)} %get-tuple-element.48), channel_id=1, source_target_pairs={{0,120},{8,0},{16,8},{24,16},{32,24},{40,32},{48,40},{56,48},{64,5... | collective-permute-start | bytes 786440 | tf_op jit(solution)/shard_map/ppermute | solution.py:339
  119.9 1.5 copy-start.19
  119.9 17.1 %collective-permute-start.9 = (bf16[4,64,512]{2,1,0:T(8,128)(2,1)}, bf16[4,64,512]{2,1,0:T(8,128)(2,1)S(1)}, u32[]{:S(2)}, u32[]{:S(2)}) collective-permute-start(bf16[4,64,512]{2,1,0:T(8,128)(2,1)} %get-tuple-element.49), channel_id=1, source_target_pairs={{0,8},{8,16},{16,24},{24,32},{32,40},{40,48},{48,56},{56,64},{64,7... | collective-permute-start | bytes 786440 | tf_op jit(solution)/shard_map/ppermute | solution.py:339
  121.3 0.7 copy-start.20
  130.7 20.0 %collective-permute-start.4 = (bf16[4,64,512]{2,1,0:T(8,128)(2,1)}, bf16[4,64,512]{2,1,0:T(8,128)(2,1)S(1)}, u32[]{:S(2)}, u32[]{:S(2)}) collective-permute-start(bf16[4,64,512]{2,1,0:T(8,128)(2,1)} %get-tuple-element.44), channel_id=1, source_target_pairs={{0,8},{8,16},{16,24},{24,32},{32,40},{40,48},{48,56},{56,64},{64,7... | collective-permute-start | bytes 786440 | tf_op jit(solution)/shard_map/ppermute | solution.py:339
  130.8 6.3 %copy-start.10 = (bf16[4,64,512]{2,1,0:T(8,128)(2,1)}, bf16[4,64,512]{2,1,0:T(8,128)(2,1)S(1)}, u32[]{:S(2)}) copy-start(bf16[4,64,512]{2,1,0:T(8,128)(2,1)S(1)} %collective-permute-done.10.r2) | copy-start | bytes 786436
  130.8 21.4 %collective-permute-start.5 = (bf16[4,64,512]{2,1,0:T(8,128)(2,1)}, bf16[4,64,512]{2,1,0:T(8,128)(2,1)S(1)}, u32[]{:S(2)}, u32[]{:S(2)}) collective-permute-start(bf16[4,64,512]{2,1,0:T(8,128)(2,1)} %get-tuple-element.44), channel_id=1, source_target_pairs={{0,120},{8,0},{16,8},{24,16},{32,24},{40,32},{48,40},{56,48},{64,5... | collective-permute-start | bytes 786440 | tf_op jit(solution)/shard_map/ppermute | solution.py:339
  135.5 1.6 copy-start.12
  135.5 20.2 %collective-permute-start.6 = (bf16[4,64,512]{2,1,0:T(8,128)(2,1)}, bf16[4,64,512]{2,1,0:T(8,128)(2,1)S(1)}, u32[]{:S(2)}, u32[]{:S(2)}) collective-permute-start(bf16[4,64,512]{2,1,0:T(8,128)(2,1)} %get-tuple-element.44), channel_id=1, source_target_pairs={{0,1},{1,2},{2,3},{3,4},{4,5},{5,6},{6,7},{7,0},{8,9},{9,10},{10,1... | collective-permute-start | bytes 786440 | tf_op jit(solution)/shard_map/ppermute | solution.py:339
  136.0 1.1 copy-start.13
  136.0 19.7 %collective-permute-start.7 = (bf16[4,64,512]{2,1,0:T(8,128)(2,1)}, bf16[4,64,512]{2,1,0:T(8,128)(2,1)S(1)}, u32[]{:S(2)}, u32[]{:S(2)}) collective-permute-start(bf16[4,64,512]{2,1,0:T(8,128)(2,1)} %get-tuple-element.44), channel_id=1, source_target_pairs={{0,7},{1,0},{2,1},{3,2},{4,3},{5,4},{6,5},{7,6},{8,15},{9,8},{10,9... | collective-permute-start | bytes 786440 | tf_op jit(solution)/shard_map/ppermute | solution.py:339
  137.1 0.7 copy-start.15
  150.6 16.2 %collective-permute-start.12 = (bf16[4,64,512]{2,1,0:T(8,128)(2,1)}, bf16[4,64,512]{2,1,0:T(8,128)(2,1)S(1)}, u32[]{:S(2)}, u32[]{:S(2)}) collective-permute-start(bf16[4,64,512]{2,1,0:T(8,128)(2,1)} %get-tuple-element.60), channel_id=1, source_target_pairs={{0,120},{8,0},{16,8},{24,16},{32,24},{40,32},{48,40},{56,48},{64,5... | collective-permute-start | bytes 786440 | tf_op jit(solution)/shard_map/ppermute | solution.py:339
  150.7 5.0 %copy-start.9 = (bf16[4,64,512]{2,1,0:T(8,128)(2,1)}, bf16[4,64,512]{2,1,0:T(8,128)(2,1)S(1)}, u32[]{:S(2)}) copy-start(bf16[4,64,512]{2,1,0:T(8,128)(2,1)S(1)} %collective-permute-done.4.n0) | copy-start | bytes 786436
  150.7 16.1 %collective-permute-start.13 = (bf16[4,64,512]{2,1,0:T(8,128)(2,1)}, bf16[4,64,512]{2,1,0:T(8,128)(2,1)S(1)}, u32[]{:S(2)}, u32[]{:S(2)}) collective-permute-start(bf16[4,64,512]{2,1,0:T(8,128)(2,1)} %get-tuple-element.61), channel_id=1, source_target_pairs={{0,8},{8,16},{16,24},{24,32},{32,40},{40,48},{48,56},{56,64},{64,7... | collective-permute-start | bytes 786440 | tf_op jit(solution)/shard_map/ppermute | solution.py:339
  152.2 3.5 %copy-start.11 = (bf16[4,64,512]{2,1,0:T(8,128)(2,1)}, bf16[4,64,512]{2,1,0:T(8,128)(2,1)S(1)}, u32[]{:S(2)}) copy-start(bf16[4,64,512]{2,1,0:T(8,128)(2,1)S(1)} %collective-permute-done.5.n1) | copy-start | bytes 786436
  152.2 14.6 %collective-permute-start.14 = (bf16[4,64,512]{2,1,0:T(8,128)(2,1)}, bf16[4,64,512]{2,1,0:T(8,128)(2,1)S(1)}, u32[]{:S(2)}, u32[]{:S(2)}) collective-permute-start(bf16[4,64,512]{2,1,0:T(8,128)(2,1)} %get-tuple-element.62), channel_id=1, source_target_pairs={{0,7},{1,0},{2,1},{3,2},{4,3},{5,4},{6,5},{7,6},{8,15},{9,8},{10,9... | collective-permute-start | bytes 786440 | tf_op jit(solution)/shard_map/ppermute | solution.py:339
  155.7 0.7 copy-start.14
  155.7 11.2 %collective-permute-start.15 = (bf16[4,64,512]{2,1,0:T(8,128)(2,1)}, bf16[4,64,512]{2,1,0:T(8,128)(2,1)S(1)}, u32[]{:S(2)}, u32[]{:S(2)}) collective-permute-start(bf16[4,64,512]{2,1,0:T(8,128)(2,1)} %get-tuple-element.63), channel_id=1, source_target_pairs={{0,1},{1,2},{2,3},{3,4},{4,5},{5,6},{6,7},{7,0},{8,9},{9,10},{10,1... | collective-permute-start | bytes 786440 | tf_op jit(solution)/shard_map/ppermute | solution.py:339
  155.7 0.8 copy-start.16
  166.8 0.7 copy-start.3
  166.8 0.8 copy-start.4
  166.8 0.9 copy-start.5
  166.8 0.9 copy-start.6
  192.6 23.3 %copy-start = (bf16[6144,128]{1,0:T(8,128)(2,1)S(1)}, bf16[6144,128]{1,0:T(8,128)(2,1)}, u32[]{:S(2)}) copy-start(bf16[6144,128]{1,0:T(8,128)(2,1)} %get-tuple-element.58) | copy-start | bytes 4718596

commit v3 on v2

--- a/solution.py
+++ b/solution.py
@@ -21,8 +21,10 @@
 TAIL = 256
 DEVICES = 128
 SLAB = 4 * WIDTH
-EARLY = 3 * SLAB // DEVICES
-LATE = (SLAB + 4 * TAIL) // DEVICES
+EARLY = 3 * SLAB // 16
+LATE = (SLAB + 4 * TAIL) // 16
+PART = (EARLY + LATE) // 8
+HALF = 40
 AXES = ("wide", "narrow")
 BF16 = jnp.bfloat16
 F32 = jnp.float32
@@ -60,7 +62,7 @@
 
 
 def swap_halves(tile):
-    return jnp.concatenate([tile[:, BLOCK:], tile[:, :BLOCK]], axis=1)
+    return pltpu.roll(tile, BLOCK, 1)
 
 
 def low_lanes(rows):
@@ -75,25 +77,29 @@
     return pl.ds(pl.multiple_of(step * size, size), size)
 
 
-def pack_body(send, features, out):
+def pack_body(send, features, out, target):
+    step = pl.program_id(0)
+
+    @pl.when(step == 0)
+    def _():
+        def invert(j, carry):
+            target[send[0, j]] = j
+            return carry
+
+        lax.fori_loop(0, GRID_BLOCKS, invert, 0, unroll=8)
+
     low = low_lanes(PACKED)
-    step = pl.program_id(0)
-
-    def one(j, carry):
-        block = send[0, step * 16 + j]
-        lanes = chunk(block // 2, 2 * BLOCK)
-
-        @pl.when(block % 2 == 0)
-        def _():
-            out[j] = jnp.where(low, features[0:PACKED, lanes], swap_halves(features[SPLIT:CHAN, lanes]))
-
-        @pl.when(block % 2 == 1)
-        def _():
-            out[j] = jnp.where(low, swap_halves(features[0:PACKED, lanes]), features[SPLIT:CHAN, lanes])
-
-        return carry
-
-    lax.fori_loop(0, 16, one, 0, unroll=4)
+
+    def pair(i, carry):
+        lanes = chunk(i, 2 * BLOCK)
+        first = features[0:PACKED, lanes]
+        second = features[SPLIT:CHAN, lanes]
+        at = step * 32 + 2 * i
+        out[target[at]] = jnp.where(low, first, swap_halves(second))
+        out[target[at + 1]] = jnp.where(low, swap_halves(first), second)
+        return carry
+
+    lax.fori_loop(0, 16, pair, 0, unroll=4)
 
 
 def scatter_back(coeffs, gradient, source, table, slots, blocks):
@@ -147,43 +153,58 @@
 
 
 def encode_body(
-    source, shown, packed, weight, coeffs, message, points, slope, mesh, sent, slope_m, mine, embedded
+    source, shown, packed, weight, coeffs, message, points, slope, table, mine, embedded, mesh
 ):
     step = pl.program_id(0)
     low = low_lanes(PACKED)
-    for p in range(4):
-        a = packed[2 * p]
-        b = packed[2 * p + 1]
-        lanes = slice(p * 128, p * 128 + 128)
-        points[0:SPLIT, lanes] = jnp.where(low, a, swap_halves(b))[0:SPLIT]
-        points[SPLIT:CHAN, lanes] = jnp.where(low, swap_halves(a), b)
-    pre = times(points[...], weight[...], 0, 0)
-    s = sigmoid(pre)
-    e = pre * s
-    embedded[chunk(step, 512), :] = e.astype(BF16)
-    slope[...] = (s + e * (1.0 - s)).astype(BF16)
-
-    @pl.when(step == GRID_ROWS // 512 - 1)
+
+    def embed(c, carry):
+        for p in range(4):
+            a = packed[c * 8 + 2 * p]
+            b = packed[c * 8 + 2 * p + 1]
+            lanes = pl.ds(pl.multiple_of(c * 512 + p * 128, 128), 128)
+            points[0:SPLIT, lanes] = jnp.where(low, a, swap_halves(b))[0:SPLIT]
+            points[SPLIT:CHAN, lanes] = jnp.where(low, swap_halves(a), b)
+        rows = chunk(c, 512)
+        pre = times(points[:, rows], weight[...], 0, 0)
+        s = sigmoid(pre)
+        e = pre * s
+        low_e = e.astype(BF16)
+        table[rows, :] = low_e
+        embedded[chunk(step * 4 + c, 512), :] = low_e
+        slope[rows, :] = (s + e * (1.0 - s)).astype(BF16)
+        return carry
+
+    lax.fori_loop(0, 4, embed, 0)
+
+    @pl.when(step == 3)
     def _():
-        def mix(b, carry):
-            pick = lambda b, k: embedded[rows_of(source[b, k]), :]
-            mesh[rows_of(b), :] = gather_mix(coeffs, pick, G_SLOTS, b).astype(BF16)
-            return carry
-
-        lax.fori_loop(0, MESH_BLOCKS, mix, 0, unroll=2)
-
-        def talk(c, carry):
-            rows = chunk(c, 256)
-            pre = times(mesh[rows, :], message[...])
-            s = sigmoid(pre)
-            e = pre * s
-            sent[rows, :] = e.astype(BF16)
-            slope_m[rows, :] = (s + e * (1.0 - s)).astype(BF16)
-            return carry
-
-        lax.fori_loop(0, MESH_ROWS // 256, talk, 0)
+        pick = lambda b, k: embedded[rows_of(source[b, k]), :]
         for h in range(SHOWN):
-            mine[h] = sent[rows_of(shown[0, h]), :]
+            row = gather_mix(coeffs, pick, G_SLOTS, shown[0, h])
+            mesh[h * BLOCK : (h + 1) * BLOCK, :] = row.astype(BF16)
+        pre = times(mesh[...], message[...])
+        mine[...] = (pre * sigmoid(pre)).astype(BF16).reshape(SHOWN, BLOCK, WIDTH)
+
+
+def mesh_body(source, embedded, coeffs, message, mesh, sent, slope_m):
+    def mix(b, carry):
+        pick = lambda b, k: embedded[rows_of(source[b, k]), :]
+        mesh[rows_of(b), :] = gather_mix(coeffs, pick, G_SLOTS, b).astype(BF16)
+        return carry
+
+    lax.fori_loop(0, MESH_BLOCKS, mix, 0, unroll=2)
+
+    def talk(c, carry):
+        rows = chunk(c, 256)
+        pre = times(mesh[rows, :], message[...])
+        s = sigmoid(pre)
+        e = pre * s
+        sent[rows, :] = e.astype(BF16)
+        slope_m[rows, :] = (s + e * (1.0 - s)).astype(BF16)
+        return carry
+
+    lax.fori_loop(0, MESH_ROWS // 256, talk, 0)
 
 
 def extend(extended, sent, halos):
@@ -295,43 +316,72 @@
         write_slabs(grads, 0, times(mesh[...], grad_pre[...], 0, 0))
         total[...] = jnp.zeros_like(total)
 
-    grad = table[pl.ds(pl.multiple_of(c * 8, 8), 8)].reshape(512, WIDTH).astype(BF16)
-    grad = (grad.astype(F32) * slope[...].astype(F32)).astype(BF16)
-    total[0:CHAN, :] = total[0:CHAN, :] + times(points[...], grad)
-
-    @pl.when(c == GRID_ROWS // 512 - 1)
+    def grid_step(i, carry):
+        rows = chunk(i, 512)
+        grad = table[pl.ds(c * 32 + i * 8, 8)].reshape(512, WIDTH).astype(BF16)
+        grad = (grad.astype(F32) * slope[rows, :].astype(F32)).astype(BF16)
+        total[0:CHAN, :] = total[0:CHAN, :] + times(points[:, rows], grad)
+        return carry
+
+    lax.fori_loop(0, 4, grid_step, 0)
+
+    @pl.when(c == 3)
     def _():
         write_slabs(grads, SLAB, total[...])
 
 
-def sum_body(early, late, out, total):
-    total[0:EARLY, :] = jnp.sum(early[...].astype(F32), axis=0)
-    total[EARLY : EARLY + LATE, :] = jnp.sum(late[...].astype(F32), axis=0)
-    rounded = total[...].astype(BF16)
+def sum_wide_body(early, late, out):
+    out[0:EARLY, :] = jnp.sum(early[...].astype(F32), axis=0).astype(BF16)
+    out[EARLY : EARLY + LATE, :] = jnp.sum(late[...].astype(F32), axis=0).astype(BF16)
+
+
+def sum_narrow_body(parts, out):
+    total = jnp.sum(parts[...].astype(F32), axis=0)
+    halves = (total[0:HALF].astype(BF16), total[PART - HALF : PART].astype(BF16))
 
     def one(i, carry):
-        out[i] = rounded
-        return carry
-
-    lax.fori_loop(0, DEVICES, one, 0, unroll=8)
-
-
-def unpack_body(parts, d_embed, ms_grad, up_grad, early, late):
+        out[2 * i] = halves[0]
+        out[2 * i + 1] = halves[1]
+        return carry
+
+    lax.fori_loop(0, DEVICES // 2, one, 0, unroll=8)
+
+
+def unpack_body(odd, own, other, d_embed, ms_grad, up_grad, sums):
     def one(i, carry):
-        part = parts[i].astype(F32)
-        early[pl.ds(pl.multiple_of(i * EARLY, 8), EARLY), :] = part[0:EARLY]
-        late[pl.ds(pl.multiple_of(i * LATE, 8), LATE), :] = part[EARLY : EARLY + LATE]
-        return carry
-
-    lax.fori_loop(0, DEVICES, one, 0, unroll=4)
+        at = pl.multiple_of(i * PART, 8)
+
+        @pl.when(odd[0] == 0)
+        def _():
+            sums[pl.ds(at + PART - HALF, HALF), :] = other[i].astype(F32)
+            sums[pl.ds(at, HALF), :] = own[i].astype(F32)
+
+        @pl.when(odd[0] == 1)
+        def _():
+            sums[pl.ds(at + PART - HALF, HALF), :] = own[i].astype(F32)
+            sums[pl.ds(at, HALF), :] = other[i].astype(F32)
+
+        return carry
+
+    lax.fori_loop(0, DEVICES, one, 0)
+    runs = EARLY + LATE
+
+    def place(out, columns, first, rows, share, offset):
+        done = 0
+        while done < rows:
+            w, r = divmod(first + done, share)
+            take = min(rows - done, share - r)
+            at = w * runs + offset + r
+            out[done : done + take, columns] = sums[at : at + take, :]
+            done += take
+
     for c in range(4):
         columns = slice(c * 128, (c + 1) * 128)
-        at = lambda first: slice(first + c * WIDTH, first + (c + 1) * WIDTH)
-        up_grad[0, :, columns] = early[at(0), :]
-        ms_grad[1, :, columns] = early[at(SLAB), :]
-        up_grad[1, :, columns] = early[at(2 * SLAB), :]
-        ms_grad[0, :, columns] = late[at(0), :]
-        d_embed[:, columns] = late[SLAB + c * TAIL : SLAB + c * TAIL + CHAN, :]
+        place(up_grad.at[0], columns, c * WIDTH, WIDTH, EARLY, 0)
+        place(ms_grad.at[1], columns, SLAB + c * WIDTH, WIDTH, EARLY, 0)
+        place(up_grad.at[1], columns, 2 * SLAB + c * WIDTH, WIDTH, EARLY, 0)
+        place(ms_grad.at[0], columns, c * WIDTH, WIDTH, LATE, EARLY)
+        place(d_embed, columns, SLAB + c * TAIL, CHAN, LATE, EARLY)
 
 
 def shift(value, axis, steps):
@@ -347,8 +397,8 @@
     return (shift(h0, "wide", -1), shift(h1, "wide", 1), shift(h2, "narrow", -1), shift(h3, "narrow", 1))
 
 
-def exchange(parts):
-    return lax.all_to_all(parts, AXES, split_axis=0, concat_axis=0, tiled=True)
+def exchange(parts, axes):
+    return lax.all_to_all(parts, axes, split_axis=0, concat_axis=0, tiled=True)
 
 
 def on_device(
@@ -367,86 +417,93 @@
 
     packed = pl.pallas_call(
         pack_body,
-        grid=(GRID_BLOCKS // 16,),
+        grid=(4,),
         out_shape=jax.ShapeDtypeStruct((GRID_BLOCKS, PACKED, 2 * BLOCK), BF16),
-        in_specs=[SM, pl.BlockSpec((CHAN, GRID_ROWS), lambda i: (0, 0))],
-        out_specs=pl.BlockSpec((16, PACKED, 2 * BLOCK), lambda i: (i, 0, 0)),
-        compiler_params=pltpu.CompilerParams(vmem_limit_bytes=56 * MIB),
+        in_specs=[SM, pl.BlockSpec((CHAN, GRID_ROWS // 4), lambda i: (0, i))],
+        out_specs=pl.BlockSpec((GRID_BLOCKS, PACKED, 2 * BLOCK), lambda i: (0, 0, 0)),
+        scratch_shapes=[pltpu.SMEM((GRID_BLOCKS,), jnp.int32)],
+        compiler_params=pltpu.CompilerParams(vmem_limit_bytes=24 * MIB),
         cost_estimate=pl.CostEstimate(flops=0, bytes_accessed=8 * MIB, transcendentals=0),
     )(grid_send, grid_feat.T)
-    received = exchange(packed)
+    packed, cotangent = lax.optimization_barrier((packed, cotangent))
+    received = exchange(packed, AXES)
 
     g_mix = g2m_coef.transpose(0, 2, 1, 3).reshape(MESH_BLOCKS, BLOCK, G_SLOTS * BLOCK)
     m_mix = mesh_coef.transpose(0, 2, 1, 3).reshape(MESH_BLOCKS, BLOCK, M_SLOTS * BLOCK)
 
     own_1, *halos = kernel_call(
         early_back_body, [rows_f32] + [halo] * 4, [SM] + [VM] * 3, [table_scratch, mesh_scratch],
-        flops=2 * 10**9, moved=8 * MIB,
+        flops=2 * 10**9, moved=8 * MIB, limit=20,
     )(mesh_src, cotangent, w_u[1], m_mix)
     returned_1 = give_back(*halos)
 
-    received, g_mix, m_mix = lax.optimization_barrier((received, g_mix, m_mix))
+    received, g_mix, m_mix, own_1, *returned_1 = lax.optimization_barrier(
+        (received, g_mix, m_mix, own_1, *returned_1)
+    )
     whole = lambda *shape: pl.BlockSpec(shape, lambda i: (0,) * len(shape))
-    points, slope, mesh_0, sent_0, slope_0, mine_0 = pl.pallas_call(
+    points, slope, embedded, mine_0 = pl.pallas_call(
         encode_body,
-        grid=(GRID_ROWS // 512,),
+        grid=(4,),
         out_shape=[
             jax.ShapeDtypeStruct((CHAN, GRID_ROWS), BF16),
             jax.ShapeDtypeStruct((GRID_ROWS, WIDTH), BF16),
-            jax.ShapeDtypeStruct((MESH_ROWS, WIDTH), BF16),
-            jax.ShapeDtypeStruct((MESH_ROWS, WIDTH), BF16),
-            jax.ShapeDtypeStruct((MESH_ROWS, WIDTH), BF16),
+            jax.ShapeDtypeStruct((GRID_ROWS, WIDTH), BF16),
             jax.ShapeDtypeStruct((SHOWN, BLOCK, WIDTH), BF16),
         ],
         in_specs=[
             SM, SM,
-            pl.BlockSpec((8, PACKED, 2 * BLOCK), lambda i: (i, 0, 0)),
+            pl.BlockSpec((32, PACKED, 2 * BLOCK), lambda i: (i, 0, 0)),
             whole(CHAN, WIDTH), whole(MESH_BLOCKS, BLOCK, G_SLOTS * BLOCK), whole(WIDTH, WIDTH),
         ],
         out_specs=[
-            pl.BlockSpec((CHAN, 512), lambda i: (0, i)),
-            pl.BlockSpec((512, WIDTH), lambda i: (i, 0)),
-            whole(MESH_ROWS, WIDTH), whole(MESH_ROWS, WIDTH), whole(MESH_ROWS, WIDTH),
+            pl.BlockSpec((CHAN, 2048), lambda i: (0, i)),
+            pl.BlockSpec((2048, WIDTH), lambda i: (i, 0)),
+            pl.BlockSpec((2048, WIDTH), lambda i: (i, 0)),
             whole(SHOWN, BLOCK, WIDTH),
         ],
-        scratch_shapes=[pltpu.VMEM((GRID_ROWS, WIDTH), BF16)],
+        scratch_shapes=[
+            pltpu.VMEM((GRID_ROWS, WIDTH), BF16), pltpu.VMEM((SHOWN * BLOCK, WIDTH), BF16)
+        ],
         compiler_params=pltpu.CompilerParams(vmem_limit_bytes=56 * MIB),
-        cost_estimate=pl.CostEstimate(flops=4 * 10**9, bytes_accessed=20 * MIB, transcendentals=0),
+        cost_estimate=pl.CostEstimate(flops=4 * 10**9, bytes_accessed=26 * MIB, transcendentals=0),
     )(g2m_src, halo_send, received, w_embed, g_mix, w_m[0])
     shown_0 = show(mine_0)
+    mesh_0, sent_0, slope_0 = kernel_call(
+        mesh_body, [rows_bf16] * 3, [SM] + [VM] * 3, flops=2 * 10**9, moved=12 * MIB, limit=24,
+    )(g2m_src, embedded, g_mix, w_m[0])
 
     aggregate_0, mesh_1, sent_1, slope_1, mine_1 = kernel_call(
         forward_body, [rows_bf16] * 4 + [halo], [SM, SM] + [VM] * 9, [extended_scratch],
-        flops=2 * 10**9, moved=10 * MIB,
+        flops=2 * 10**9, moved=10 * MIB, limit=20,
     )(mesh_src, halo_send, sent_0, *shown_0, m_mix, mesh_0, w_u[0], w_m[1])
     shown_1 = show(mine_1)
 
     grad_pre_1, grad_1, own_0, *halos = kernel_call(
         backward_body, [rows_bf16, rows_f32, rows_f32] + [halo] * 4, [SM, SM] + [VM] * 10,
-        [table_scratch, mesh_scratch, mesh_scratch32], flops=2 * 10**9, moved=16 * MIB,
+        [table_scratch, mesh_scratch, mesh_scratch32], flops=2 * 10**9, moved=16 * MIB, limit=28,
     )(mesh_src, halo_send, own_1, *returned_1, slope_1, cotangent, w_m[1], w_u[0], m_mix)
     returned_0 = give_back(*halos)
 
     mesh_out, early = kernel_call(
         grads_body, [rows_bf16, ((3 * SLAB, 128), BF16)], [SM] + [VM] * 12,
-        [extended_scratch, mesh_scratch], flops=4 * 10**9, moved=14 * MIB,
+        [extended_scratch, mesh_scratch], flops=4 * 10**9, moved=14 * MIB, limit=24,
     )(
         mesh_src, sent_1, *shown_1, m_mix, mesh_1, w_u[1], cotangent, aggregate_0, grad_1,
         grad_pre_1,
     )
     own_0, early = lax.optimization_barrier((own_0, early))
-    early = exchange(early.reshape(DEVICES, EARLY, 128))
+    early = exchange(early.reshape(16, EARLY, 128), "wide")
 
     late = pl.pallas_call(
         final_body,
-        grid=(GRID_ROWS // 512,),
+        grid=(4,),
         out_shape=jax.ShapeDtypeStruct((SLAB + 4 * TAIL, 128), BF16),
         in_specs=[
             SM, SM, whole(MESH_ROWS, WIDTH), *[whole(SHOWN, BLOCK, WIDTH)] * 4,
             whole(MESH_ROWS, WIDTH), whole(MESH_ROWS, WIDTH), whole(WIDTH, WIDTH),
             whole(MESH_ROWS, WIDTH), whole(MESH_BLOCKS, BLOCK, G_SLOTS * BLOCK),
-            pl.BlockSpec((512, WIDTH), lambda i: (i, 0)),
-            pl.BlockSpec((CHAN, 512), lambda i: (0, i)),
+            pl.BlockSpec((2048, WIDTH), lambda i: (i, 0)),
+            pl.BlockSpec((CHAN, 2048), lambda i: (0, i)),
         ],
         out_specs=whole(SLAB + 4 * TAIL, 128),
         scratch_shapes=[
@@ -454,25 +511,30 @@
             mesh_scratch, mesh_scratch, mesh_scratch32,
             pltpu.VMEM((TAIL, WIDTH), F32),
         ],
-        compiler_params=pltpu.CompilerParams(vmem_limit_bytes=56 * MIB),
+        compiler_params=pltpu.CompilerParams(vmem_limit_bytes=50 * MIB),
         cost_estimate=pl.CostEstimate(flops=4 * 10**9, bytes_accessed=24 * MIB, transcendentals=0),
     )(
         g2m_src, halo_send, own_0, *returned_0, slope_0, grad_1, w_m[0], mesh_0, g_mix, slope,
         points,
     )
-    late = exchange(late.reshape(DEVICES, LATE, 128))
-
+    late = exchange(late.reshape(16, LATE, 128), "wide")
+
+    parts = kernel_call(
+        sum_wide_body, [((EARLY + LATE, 128), BF16)], [VM, VM], moved=3 * MIB, limit=16
+    )(early, late)[0]
     totals = kernel_call(
-        sum_body, [((DEVICES, EARLY + LATE, 128), BF16)], [VM, VM],
-        [pltpu.VMEM((EARLY + LATE, 128), F32)], moved=5 * MIB,
-    )(early, late)[0]
+        sum_narrow_body, [((DEVICES, HALF, 128), BF16)], [VM], moved=2 * MIB, limit=16
+    )(exchange(parts.reshape(8, PART, 128), "narrow"))[0]
+    own = exchange(totals, AXES)
+    other = lax.ppermute(own, "narrow", [(i, i ^ 1) for i in range(8)])
     d_embed, ms_grad, up_grad = kernel_call(
         unpack_body,
         [((CHAN, WIDTH), F32), ((2, WIDTH, WIDTH), F32), ((2, WIDTH, WIDTH), F32)],
-        [VM],
-        [pltpu.VMEM((3 * SLAB, 128), F32), pltpu.VMEM((SLAB + 4 * TAIL, 128), F32)],
+        [SM, VM, VM],
+        [pltpu.VMEM((DEVICES * PART, 128), F32)],
         moved=7 * MIB,
-    )(exchange(totals))
+        limit=24,
+    )((lax.axis_index("narrow") % 2).reshape(1).astype(jnp.int32), own, other)
     return mesh_out, d_embed, ms_grad, up_grad
 
 

time: 293 us -> 248 us (0.85)
  Pallas kernels: 111 us -> 77.1 us
  waiting for transfers between devices: 38.1 us -> 22.2 us
  blocking collectives: 91.3 us -> 79.6 us
  local copies, waits for them, and re-layouts: 16.7 us -> 27.7 us
  starting transfers between devices: 34.1 us -> 39.8 us
    all_to_all x1, waiting for transfers between devices: 38 us -> 0.01 us  [exchange(): return lax.all_to_all(parts, axes, split_axis=0, concat_axis=0, tiled=True)]
    pallas_call x4 -> x6, Pallas kernels: 65.3 us -> 43.2 us  [the longest x1 18.6 us: on_device(): pl.pallas_call(final_body, grid=(4,), out_shape=jax.ShapeDtypeStruct((SLA...]
    ppermute x16, waiting for transfers between devices: 0.04 us -> 19.6 us  [shift(): lax.ppermute(value, axis, [(i, (i + steps) % count) for i in range(count)])]
    all_to_all x3 -> x4, blocking collectives: 91.3 us -> 79.6 us  [exchange(): return lax.all_to_all(parts, axes, split_axis=0, concat_axis=0, tiled=True)]
    unnamed x44 -> x38, local copies, waits for them, and re-layouts: 4.43 us -> 11.4 us
    ppermute x16, starting transfers between devices: 22.2 us -> 27 us  [shift(): lax.ppermute(value, axis, [(i, (i + steps) % count) for i in range(count)])]
    pallas_call x1, Pallas kernels: 12.8 us -> 8.82 us  [on_device(): kernel_call(backward_body, [rows_bf16, rows_f32, rows_f32] + [halo] * 4,...]
    pallas_call x1, Pallas kernels: 10.3 us -> 6.35 us  [on_device(): kernel_call(grads_body, [rows_bf16, ((3 * SLAB, 128), BF16)], [SM] + [VM]...]
  transfers between devices with their start and end apart: 17 -> 18, of which waited for: 1 -> 3; matrix products, arithmetic and copies ran while one was open for 5% -> 7% of each run, Pallas kernels for 14% -> 11%
where the time goes in v3:
time: 248 us; the launch traced here: 247 us
  blocking collectives  79.6 us (32%)
  Pallas kernels  77.1 us (31%)
  starting transfers between devices  39.8 us (16%)
  local copies, waits for them, and re-layouts  27.7 us (11%)
  waiting for transfers between devices  22.2 us (9%)
    all_to_all x4, blocking collectives, exchange(): return lax.all_to_all(parts, axes, split_axis=0, concat_axis=0, tiled=True)  79.6 us
    ppermute x16, starting transfers between devices, shift(): lax.ppermute(value, axis, [(i, (i + steps) % count) for i in range(count)])  27 us
    ppermute x16, waiting for transfers between devices, shift(): lax.ppermute(value, axis, [(i, (i + steps) % count) for i in range(count)])  19.6 us
    pallas_call x1, Pallas kernels, on_device(): pl.pallas_call(final_body, grid=(4,), out_shape=jax.ShapeDtypeStruct((SLA...  18.6 us
    pallas_call x1, Pallas kernels, on_device(): pl.pallas_call(encode_body, grid=(4,), out_shape=[jax.ShapeDtypeStruct((C...  16.1 us
    all_to_all x1, starting transfers between devices, exchange(): return lax.all_to_all(parts, axes, split_axis=0, concat_axis=0, tiled=True)  11.9 us
    unnamed x38, local copies, waits for them, and re-layouts  11.4 us
    pallas_call x1, Pallas kernels, on_device(): kernel_call(backward_body, [rows_bf16, rows_f32, rows_f32] + [halo] * 4,...  8.82 us
  transfers between devices with their start and end apart: 18, of which 3 were waited for; matrix products, arithmetic and copies ran while one was open for 7% of the time, Pallas kernels for 11%

profile of v3, /device:TPU:1, one launch (start us, length us, event | category | flops | bytes accessed | tf_op | source)
XLA Modules:
  0.0 247.4 jit_solution(9811989356353774190)
XLA Ops:
  0.6 2.1 copy-done.4
  2.7 0.7 copy-done.9
  3.4 3.3 %shard_map.138 = bf16[128,115,128]{2,1,0:T(8,128)(2,1)S(1)} custom-call(s32[1,128]{1,0:T(1,128)S(1)} %copy-done.9, bf16[227,8192]{1,0:T(8,128)(2,1)S(1)} %bitcast.17), custom_call_target="tpu_custom_call" | custom-call | bytes 8388608 | tf_op jit(solution)/shard_map/pallas_call | solution.py:418
  6.6 1.9 copy-done
  8.5 11.9 %all-to-all-start = ((bf16[128,115,128]{2,1,0:T(8,128)(2,1)}), bf16[128,115,128]{2,1,0:T(8,128)(2,1)}, u32[]{:S(2)}, u32[]{:S(2)}) async-start(bf16[128,115,128]{2,1,0:T(8,128)(2,1)} %copy-done), calls=%async_computation | async-start | bytes 7864320 | tf_op jit(solution)/shard_map/all_to_all | solution.py:401
  20.4 0.1 copy.31.source
  20.5 2.6 %copy.25 = bf16[16,64,6,64]{3,2,1,0:T(8,128)(2,1)} copy(bf16[16,64,6,64]{3,1,2,0:T(8,128)(2,1)S(1)} %bitcast.22) | data formatting | bytes 1572864 | tf_op jit(solution)/shard_map/transpose | solution.py:432
  23.1 3.1 %reshape.27.coeffs = bf16[16,64,384]{2,1,0:T(8,128)(2,1)S(1)} reshape(bf16[16,64,6,64]{3,2,1,0:T(8,128)(2,1)} %copy.25) | data formatting | bytes 1572864 | tf_op jit(solution)/shard_map/reshape | solution.py:432
  26.3 1.3 slice_bitcast_fusion.1
  27.6 0.0 copy-start.14
  27.6 7.9 %shard_map.139 = (f32[1024,512]{1,0:T(8,128)S(1)}, bf16[4,64,512]{2,1,0:T(8,128)(2,1)}, bf16[4,64,512]{2,1,0:T(8,128)(2,1)}, bf16[4,64,512]{2,1,0:T(8,128)(2,1)}, bf16[4,64,512]{2,1,0:T(8,128)(2,1)}) custom-call(s32[16,6]{1,0:T(8,128)S(1)} %copy.31.source, bf16[1024,512]{1,0:T(8,128)(2,1)S(1)} %copy-done.11, bf16[512,512]{1,0:T(8,128)(2,1)S(1)} %get-tuple-element.89.up, ...), custom_call_target="tpu_custom_call" | custom-call | flops 2000000000 | bytes 8388608 | tf_op jit(solution)/shard_map/pallas_call | solution.py:434
  35.5 1.3 copy-done.12
  36.8 5.6 %collective-permute-start = (bf16[4,64,512]{2,1,0:T(8,128)(2,1)}, bf16[4,64,512]{2,1,0:T(8,128)(2,1)}, u32[]{:S(2)}, u32[]{:S(2)}) collective-permute-start(bf16[4,64,512]{2,1,0:T(8,128)(2,1)} %get-tuple-element.48), channel_id=1, source_target_pairs={{0,120},{8,0},{16,8},{24,16},{32,24},{40,32},{48,40},{56,48},{64,5... | collective-permute-start | bytes 786440 | tf_op jit(solution)/shard_map/ppermute | solution.py:389
  42.3 0.0 collective-permute-start.1
  42.3 0.6 collective-permute-start.2
  43.0 1.1 collective-permute-start.3
  44.1 3.1 %copy.24 = bf16[16,64,8,64]{3,2,1,0:T(8,128)(2,1)} copy(bf16[16,64,8,64]{3,1,2,0:T(8,128)(2,1)S(1)} %bitcast.21) | data formatting | bytes 2097152 | tf_op jit(solution)/shard_map/transpose | solution.py:431
  47.2 4.1 %reshape.26.coeffs = bf16[16,64,512]{2,1,0:T(8,128)(2,1)} reshape(bf16[16,64,8,64]{3,2,1,0:T(8,128)(2,1)} %copy.24) | data formatting | bytes 2097152 | tf_op jit(solution)/shard_map/reshape | solution.py:431
  51.3 0.7 copy.28.source
  52.0 2.1 slice_bitcast_fusion
  54.0 15.3 %collective-permute-done.r0 = bf16[4,64,512]{2,1,0:T(8,128)(2,1)} collective-permute-done((bf16[4,64,512]{2,1,0:T(8,128)(2,1)}, bf16[4,64,512]{2,1,0:T(8,128)(2,1)}, u32[]{:S(2)}, u32[]{:S(2)}) %collective-permute-start) | collective-permute-done | bytes 262176 | tf_op jit(solution)/shard_map/ppermute | solution.py:389
  69.4 4.2 %collective-permute-done.1.r1 = bf16[4,64,512]{2,1,0:T(8,128)(2,1)} collective-permute-done((bf16[4,64,512]{2,1,0:T(8,128)(2,1)}, bf16[4,64,512]{2,1,0:T(8,128)(2,1)}, u32[]{:S(2)}, u32[]{:S(2)}) %collective-permute-start.1) | collective-permute-done | bytes 262176 | tf_op jit(solution)/shard_map/ppermute | solution.py:389
  73.6 0.0 collective-permute-done.2.r2
  73.6 0.0 collective-permute-done.3.r3
  73.6 0.0 all-to-all-done.packed
  73.6 0.0 copy-start.3
  73.6 0.0 copy-start.8
  73.6 16.1 %shard_map.140 = (bf16[227,8192]{1,0:T(8,128)(2,1)}, bf16[8192,512]{1,0:T(8,128)(2,1)}, bf16[8192,512]{1,0:T(8,128)(2,1)}, bf16[4,64,512]{2,1,0:T(8,128)(2,1)}) custom-call(s32[16,8]{1,0:T(8,128)} %copy.28.source, s32[1,4]{1,0:T(1,128)} %shown.7, bf16[128,115,128]{2,1,0:T(8,128)(2,1)} %all-to-all-done.packed, bf16[227,512]{1,0:T(8,128)(2,1)} %weight.1, ...), custom_call_target="tpu_custom_call" | custom-call | flops 4000000000 | bytes 27262976 | tf_op jit(solution)/shard_map/pallas_call | solution.py:444
  89.8 0.1 collective-permute-start.4
  89.8 4.8 %collective-permute-start.5 = (bf16[4,64,512]{2,1,0:T(8,128)(2,1)}, bf16[4,64,512]{2,1,0:T(8,128)(2,1)S(1)}, u32[]{:S(2)}, u32[]{:S(2)}) collective-permute-start(bf16[4,64,512]{2,1,0:T(8,128)(2,1)} %get-tuple-element.56), channel_id=1, source_target_pairs={{0,120},{8,0},{16,8},{24,16},{32,24},{40,32},{48,40},{56,48},{64,5... | collective-permute-start | bytes 786440 | tf_op jit(solution)/shard_map/ppermute | solution.py:389
  94.6 2.8 %collective-permute-start.6 = (bf16[4,64,512]{2,1,0:T(8,128)(2,1)}, bf16[4,64,512]{2,1,0:T(8,128)(2,1)S(1)}, u32[]{:S(2)}, u32[]{:S(2)}) collective-permute-start(bf16[4,64,512]{2,1,0:T(8,128)(2,1)} %get-tuple-element.56), channel_id=1, source_target_pairs={{0,1},{1,2},{2,3},{3,4},{4,5},{5,6},{6,7},{7,0},{8,9},{9,10},{10,1... | collective-permute-start | bytes 786440 | tf_op jit(solution)/shard_map/ppermute | solution.py:389
  97.4 0.0 collective-permute-start.7
  97.5 3.4 %copy-done.2 = bf16[8192,512]{1,0:T(8,128)(2,1)S(1)} copy-done((bf16[8192,512]{1,0:T(8,128)(2,1)S(1)}, bf16[8192,512]{1,0:T(8,128)(2,1)}, u32[]{:S(2)}) %copy-start.2) | copy-done | bytes 8388632
  100.9 4.7 %shard_map.141 = (bf16[1024,512]{1,0:T(8,128)(2,1)S(1)}, bf16[1024,512]{1,0:T(8,128)(2,1)S(1)}, bf16[1024,512]{1,0:T(8,128)(2,1)S(1)}) custom-call(s32[16,8]{1,0:T(8,128)S(1)} %copy-done.8, bf16[8192,512]{1,0:T(8,128)(2,1)S(1)} %copy-done.2, bf16[16,64,512]{2,1,0:T(8,128)(2,1)S(1)} %copy-done.1, bf16[512,512]{1,0:T(8,128)(2,1)S(1)} %copy-done.3), custom_call_target="tpu_custom_call" | custom-call | flops 2000000000 | bytes 12582912 | tf_op jit(solution)/shard_map/pallas_call | solution.py:471
  105.6 0.0 collective-permute-done.5.n1
  105.6 0.0 copy-start.13
  105.6 5.4 %shard_map.142 = (bf16[1024,512]{1,0:T(8,128)(2,1)S(1)}, bf16[1024,512]{1,0:T(8,128)(2,1)S(1)}, bf16[1024,512]{1,0:T(8,128)(2,1)S(1)}, bf16[1024,512]{1,0:T(8,128)(2,1)S(1)}, bf16[4,64,512]{2,1,0:T(8,128)(2,1)S(1)}) custom-call(s32[16,6]{1,0:T(8,128)S(1)} %copy.31.source, s32[1,4]{1,0:T(1,128)S(1)} %copy-done.10, ...), custom_call_target="tpu_custom_call" | custom-call | flops 2000000000 | bytes 10485760 | tf_op jit(solution)/shard_map/pallas_call | solution.py:475
  111.1 1.7 collective-permute-start.10
  112.8 0.0 collective-permute-start.11
  112.8 4.8 %collective-permute-start.9 = (bf16[4,64,512]{2,1,0:T(8,128)(2,1)S(1)}, bf16[4,64,512]{2,1,0:T(8,128)(2,1)S(1)}, u32[]{:S(2)}, u32[]{:S(2)}) collective-permute-start(bf16[4,64,512]{2,1,0:T(8,128)(2,1)S(1)} %get-tuple-element.60), channel_id=1, source_target_pairs={{0,120},{8,0},{16,8},{24,16},{32,24},{40,32},{48,40},{56,48},{64,5... | collective-permute-start | bytes 786440 | tf_op jit(solution)/shard_map/ppermute | solution.py:389
  117.6 8.8 %shard_map.143 = (bf16[1024,512]{1,0:T(8,128)(2,1)S(1)}, f32[1024,512]{1,0:T(8,128)S(1)}, f32[1024,512]{1,0:T(8,128)S(1)}, bf16[4,64,512]{2,1,0:T(8,128)(2,1)S(1...) custom-call(s32[16,6]{1,0:T(8,128)S(1)} %copy.31.source, ...), custom_call_target="tpu_custom_call" | custom-call | flops 2000000000 | bytes 16777216 | tf_op jit(solution)/shard_map/pallas_call | solution.py:481
  126.4 0.0 copy-start.6
  126.5 1.3 copy-done.6
  127.8 0.0 collective-permute-start.12
  127.8 0.0 collective-permute-done.10.n2
  127.8 1.5 collective-permute-start.13
  129.2 0.0 collective-permute-done.11.n3
  129.2 4.0 %collective-permute-start.14 = (bf16[4,64,512]{2,1,0:T(8,128)(2,1)S(1)}, bf16[4,64,512]{2,1,0:T(8,128)(2,1)S(1)}, u32[]{:S(2)}, u32[]{:S(2)}) collective-permute-start(bf16[4,64,512]{2,1,0:T(8,128)(2,1)S(1)} %get-tuple-element.78), channel_id=1, source_target_pairs={{0,7},{1,0},{2,1},{3,2},{4,3},{5,4},{6,5},{7,6},{8,15},{9,8},{10,9... | collective-permute-start | bytes 786440 | tf_op jit(solution)/shard_map/ppermute | solution.py:389
  133.3 0.0 collective-permute-start.15
  133.3 0.0 collective-permute-done.9.n1
  133.3 6.3 %shard_map.144 = (bf16[1024,512]{1,0:T(8,128)(2,1)}, bf16[6144,128]{1,0:T(8,128)(2,1)S(1)}) custom-call(s32[16,6]{1,0:T(8,128)S(1)} %copy.31.source, bf16[1024,512]{1,0:T(8,128)(2,1)S(1)} %get-tuple-element.59.sent, bf16[4,64,512]{2,1,0:T(8,128)(2,1)S(1)} %collective-permute-done.8.n0, bf16[4,64,512]{2,1,0:T(8,128)(2,1)S(1)} %collective-permute-done.9.n1, ...), custom_call_target="tpu_custom_call" | custom-call | flops 4000000000 | bytes 14680064 | tf_op jit(solution)/shard_map/pallas_call | solution.py:487
  139.6 0.0 collective-permute-done.12.r0
  139.6 0.0 collective-permute-done.13.r1
  139.7 0.0 collective-permute-done.15.r3
  139.7 18.6 %shard_map.145 = bf16[3072,128]{1,0:T(8,128)(2,1)S(1)} custom-call(s32[16,8]{1,0:T(8,128)S(1)} %copy-done.8, s32[1,4]{1,0:T(1,128)S(1)} %copy-done.10, f32[1024,512]{1,0:T(8,128)} %copy-done.6, bf16[4,64,512]{2,1,0:T(8,128)(2,1)S(1)} %collective-permute-done.12.r0, bf16[4,64,512]{2,1,0:T(8,128)(2,1)S(1)} %collective-permute-done.13.r1, ...), custom_call_target="tpu_custom_call" | custom-call | flops 4000000000 | bytes 25165824 | tf_op jit(solution)/shard_map/pallas_call | solution.py:497
  158.3 17.9 %all_to_all.25.late = bf16[16,192,128]{2,1,0:T(8,128)(2,1)S(1)} all-to-all(bf16[16,192,128]{2,1,0:T(8,128)(2,1)S(1)} %bitcast.18), channel_id=1, replica_groups=mesh['wide'=16,'narrow'=8] {'wide'}, dimensions={0} | all-to-all | bytes 1572864 | tf_op jit(solution)/shard_map/all_to_all | solution.py:401
  176.2 24.6 %all_to_all.26.early = bf16[16,384,128]{2,1,0:T(8,128)(2,1)S(1)} all-to-all(bf16[16,384,128]{2,1,0:T(8,128)(2,1)S(1)} %bitcast.19), channel_id=1, replica_groups=mesh['wide'=16,'narrow'=8] {'wide'}, dimensions={0} | all-to-all | bytes 3145728 | tf_op jit(solution)/shard_map/all_to_all | solution.py:401
  200.7 0.3 shard_map.146
  201.1 11.2 %all_to_all.27.parts = bf16[8,72,128]{2,1,0:T(8,128)(2,1)S(1)} all-to-all(bf16[8,72,128]{2,1,0:T(8,128)(2,1)S(1)} %bitcast.20), channel_id=1, replica_groups=mesh['wide'=16,'narrow'=8] {'narrow'}, dimensions={0} | all-to-all | bytes 294912 | tf_op jit(solution)/shard_map/all_to_all | solution.py:401
  212.2 0.1 shard_map.147
  212.4 26.0 %all_to_all.28.own = bf16[128,40,128]{2,1,0:T(8,128)(2,1)S(1)} all-to-all(bf16[128,40,128]{2,1,0:T(8,128)(2,1)S(1)} %shard_map.147), channel_id=1, replica_groups=mesh['wide'=16,'narrow'=8] {'wide','narrow'}, dimensions={0} | all-to-all | bytes 2621440 | tf_op jit(solution)/shard_map/all_to_all | solution.py:401
  238.3 0.9 collective-permute-start.16
  239.2 2.7 %collective-permute-done.16.other = bf16[128,40,128]{2,1,0:T(8,128)(2,1)S(1)} collective-permute-done((bf16[128,40,128]{2,1,0:T(8,128)(2,1)S(1)}, bf16[128,40,128]{2,1,0:T(8,128)(2,1)S(1)}, u32[]{:S(2)}, u32[]{:S(2)}) %collective-permute-start.16) | collective-permute-done | bytes 1310752 | tf_op jit(solution)/shard_map/ppermute | solution.py:529
  241.9 5.5 %shard_map.148 = (f32[227,512]{1,0:T(8,128)}, f32[2,512,512]{2,1,0:T(8,128)}, f32[2,512,512]{2,1,0:T(8,128)}) custom-call(s32[1]{0:T(128)} %bitcast.7.odd, bf16[128,40,128]{2,1,0:T(8,128)(2,1)S(1)} %all_to_all.28.own, bf16[128,40,128]{2,1,0:T(8,128)(2,1)S(1)} %collective-permute-done.16.other), custom_call_target="tpu_custom_call" | custom-call | bytes 7340032 | tf_op jit(solution)/shard_map/pallas_call | solution.py:530
  (31 shorter events, 0.1 us)
Async XLA Ops:
  0.6 2.1 copy-start.4
  2.7 0.7 copy-start.9
  6.6 1.9 copy-start
  8.5 11.9 %copy-start.16 = (s32[16,6]{0,1:T(8,128)S(1)}, s32[16,6]{0,1:T(8,128)}, u32[]{:S(2)}) copy-start(s32[16,6]{0,1:T(8,128)} %param.16) | copy-start | bytes 1156
  8.5 12.0 %copy-start.15 = (bf16[16,6,64,64]{3,2,1,0:T(8,128)(2,1)S(1)}, bf16[16,6,64,64]{3,2,1,0:T(8,128)(2,1)}, u32[]{:S(2)}) copy-start(bf16[16,6,64,64]{3,2,1,0:T(8,128)(2,1)} %param.17) | copy-start | bytes 2359300
  8.5 65.1 %all-to-all-start = ((bf16[128,115,128]{2,1,0:T(8,128)(2,1)}), bf16[128,115,128]{2,1,0:T(8,128)(2,1)}, u32[]{:S(2)}, u32[]{:S(2)}) async-start(bf16[128,115,128]{2,1,0:T(8,128)(2,1)} %copy-done), calls=%async_computation | async-start | bytes 7864320 | tf_op jit(solution)/shard_map/all_to_all | solution.py:401
  23.1 4.4 %copy-start.11 = (bf16[1024,512]{1,0:T(8,128)(2,1)S(1)}, bf16[1024,512]{1,0:T(8,128)(2,1)}, u32[]{:S(2)}) copy-start(bf16[1024,512]{1,0:T(8,128)(2,1)} %cot.2) | copy-start | bytes 3145732
  27.6 16.5 %copy-start.14 = (bf16[16,8,64,64]{3,2,1,0:T(8,128)(2,1)S(1)}, bf16[16,8,64,64]{3,2,1,0:T(8,128)(2,1)}, u32[]{:S(2)}) copy-start(bf16[16,8,64,64]{3,2,1,0:T(8,128)(2,1)} %param.15) | copy-start | bytes 3145732
  35.5 1.3 copy-start.12
  36.8 32.6 %collective-permute-start = (bf16[4,64,512]{2,1,0:T(8,128)(2,1)}, bf16[4,64,512]{2,1,0:T(8,128)(2,1)}, u32[]{:S(2)}, u32[]{:S(2)}) collective-permute-start(bf16[4,64,512]{2,1,0:T(8,128)(2,1)} %get-tuple-element.48), channel_id=1, source_target_pairs={{0,120},{8,0},{16,8},{24,16},{32,24},{40,32},{48,40},{56,48},{64,5... | collective-permute-start | bytes 786440 | tf_op jit(solution)/shard_map/ppermute | solution.py:389
  42.3 31.2 %collective-permute-start.1 = (bf16[4,64,512]{2,1,0:T(8,128)(2,1)}, bf16[4,64,512]{2,1,0:T(8,128)(2,1)}, u32[]{:S(2)}, u32[]{:S(2)}) collective-permute-start(bf16[4,64,512]{2,1,0:T(8,128)(2,1)} %get-tuple-element.49), channel_id=1, source_target_pairs={{0,8},{8,16},{16,24},{24,32},{32,40},{40,48},{48,56},{56,64},{64,7... | collective-permute-start | bytes 786440 | tf_op jit(solution)/shard_map/ppermute | solution.py:389
  42.3 31.2 %collective-permute-start.2 = (bf16[4,64,512]{2,1,0:T(8,128)(2,1)}, bf16[4,64,512]{2,1,0:T(8,128)(2,1)}, u32[]{:S(2)}, u32[]{:S(2)}) collective-permute-start(bf16[4,64,512]{2,1,0:T(8,128)(2,1)} %get-tuple-element.50), channel_id=1, source_target_pairs={{0,7},{1,0},{2,1},{3,2},{4,3},{5,4},{6,5},{7,6},{8,15},{9,8},{10,9... | collective-permute-start | bytes 786440 | tf_op jit(solution)/shard_map/ppermute | solution.py:389
  43.0 30.6 %collective-permute-start.3 = (bf16[4,64,512]{2,1,0:T(8,128)(2,1)}, bf16[4,64,512]{2,1,0:T(8,128)(2,1)}, u32[]{:S(2)}, u32[]{:S(2)}) collective-permute-start(bf16[4,64,512]{2,1,0:T(8,128)(2,1)} %get-tuple-element.51), channel_id=1, source_target_pairs={{0,1},{1,2},{2,3},{3,4},{4,5},{5,6},{6,7},{7,0},{8,9},{9,10},{10,1... | collective-permute-start | bytes 786440 | tf_op jit(solution)/shard_map/ppermute | solution.py:389
  47.2 4.1 %copy-start.17 = (s32[16,8]{0,1:T(8,128)S(1)}, s32[16,8]{0,1:T(8,128)}, u32[]{:S(2)}) copy-start(s32[16,8]{0,1:T(8,128)} %param.14) | copy-start | bytes 1540
  73.6 23.9 %copy-start.1 = (bf16[16,64,512]{2,1,0:T(8,128)(2,1)S(1)}, bf16[16,64,512]{2,1,0:T(8,128)(2,1)}, u32[]{:S(2)}) copy-start(bf16[16,64,512]{2,1,0:T(8,128)(2,1)} %reshape.26.coeffs) | copy-start | bytes 3145732
  73.6 23.9 %copy-start.3 = (bf16[512,512]{1,0:T(8,128)(2,1)S(1)}, bf16[512,512]{1,0:T(8,128)(2,1)}, u32[]{:S(2)}) copy-start(bf16[512,512]{1,0:T(8,128)(2,1)} %get-tuple-element.87.message) | copy-start | bytes 1572868
  73.6 23.9 %copy-start.8 = (s32[16,8]{1,0:T(8,128)S(1)}, s32[16,8]{1,0:T(8,128)}, u32[]{:S(2)}) copy-start(s32[16,8]{1,0:T(8,128)} %copy.28.source) | copy-start | bytes 1540
  89.8 15.8 %collective-permute-start.4 = (bf16[4,64,512]{2,1,0:T(8,128)(2,1)}, bf16[4,64,512]{2,1,0:T(8,128)(2,1)S(1)}, u32[]{:S(2)}, u32[]{:S(2)}) collective-permute-start(bf16[4,64,512]{2,1,0:T(8,128)(2,1)} %get-tuple-element.56), channel_id=1, source_target_pairs={{0,8},{8,16},{16,24},{24,32},{32,40},{40,48},{48,56},{56,64},{64,7... | collective-permute-start | bytes 786440 | tf_op jit(solution)/shard_map/ppermute | solution.py:389
  89.8 15.7 %collective-permute-start.5 = (bf16[4,64,512]{2,1,0:T(8,128)(2,1)}, bf16[4,64,512]{2,1,0:T(8,128)(2,1)S(1)}, u32[]{:S(2)}, u32[]{:S(2)}) collective-permute-start(bf16[4,64,512]{2,1,0:T(8,128)(2,1)} %get-tuple-element.56), channel_id=1, source_target_pairs={{0,120},{8,0},{16,8},{24,16},{32,24},{40,32},{48,40},{56,48},{64,5... | collective-permute-start | bytes 786440 | tf_op jit(solution)/shard_map/ppermute | solution.py:389
  94.6 11.0 %collective-permute-start.6 = (bf16[4,64,512]{2,1,0:T(8,128)(2,1)}, bf16[4,64,512]{2,1,0:T(8,128)(2,1)S(1)}, u32[]{:S(2)}, u32[]{:S(2)}) collective-permute-start(bf16[4,64,512]{2,1,0:T(8,128)(2,1)} %get-tuple-element.56), channel_id=1, source_target_pairs={{0,1},{1,2},{2,3},{3,4},{4,5},{5,6},{6,7},{7,0},{8,9},{9,10},{10,1... | collective-permute-start | bytes 786440 | tf_op jit(solution)/shard_map/ppermute | solution.py:389
  97.4 8.2 %collective-permute-start.7 = (bf16[4,64,512]{2,1,0:T(8,128)(2,1)}, bf16[4,64,512]{2,1,0:T(8,128)(2,1)S(1)}, u32[]{:S(2)}, u32[]{:S(2)}) collective-permute-start(bf16[4,64,512]{2,1,0:T(8,128)(2,1)} %get-tuple-element.56), channel_id=1, source_target_pairs={{0,7},{1,0},{2,1},{3,2},{4,3},{5,4},{6,5},{7,6},{8,15},{9,8},{10,9... | collective-permute-start | bytes 786440 | tf_op jit(solution)/shard_map/ppermute | solution.py:389
  97.5 3.4 %copy-start.2 = (bf16[8192,512]{1,0:T(8,128)(2,1)S(1)}, bf16[8192,512]{1,0:T(8,128)(2,1)}, u32[]{:S(2)}) copy-start(bf16[8192,512]{1,0:T(8,128)(2,1)} %get-tuple-element.54.embedded) | copy-start | bytes 25165828
  100.9 4.8 %copy-start.10 = (s32[1,4]{1,0:T(1,128)S(1)}, s32[1,4]{1,0:T(1,128)}, u32[]{:S(2)}) copy-start(s32[1,4]{1,0:T(1,128)} %shown.7) | copy-start | bytes 52
  105.6 5.5 %copy-start.7 = (bf16[1024,512]{1,0:T(8,128)(2,1)}, bf16[1024,512]{1,0:T(8,128)(2,1)S(1)}, u32[]{:S(2)}) copy-start(bf16[1024,512]{1,0:T(8,128)(2,1)S(1)} %get-tuple-element.58.mesh) | copy-start | bytes 3145732
  105.6 12.0 %copy-start.13 = (f32[1024,512]{1,0:T(8,128)S(1)}, f32[1024,512]{1,0:T(8,128)}, u32[]{:S(2)}) copy-start(f32[1024,512]{1,0:T(8,128)} %copy-done.12) | copy-start | bytes 6291460
  111.1 16.7 %collective-permute-start.10 = (bf16[4,64,512]{2,1,0:T(8,128)(2,1)S(1)}, bf16[4,64,512]{2,1,0:T(8,128)(2,1)S(1)}, u32[]{:S(2)}, u32[]{:S(2)}) collective-permute-start(bf16[4,64,512]{2,1,0:T(8,128)(2,1)S(1)} %get-tuple-element.60), channel_id=1, source_target_pairs={{0,1},{1,2},{2,3},{3,4},{4,5},{5,6},{6,7},{7,0},{8,9},{9,10},{10,1... | collective-permute-start | bytes 786440 | tf_op jit(solution)/shard_map/ppermute | solution.py:389
  112.8 16.4 %collective-permute-start.11 = (bf16[4,64,512]{2,1,0:T(8,128)(2,1)S(1)}, bf16[4,64,512]{2,1,0:T(8,128)(2,1)S(1)}, u32[]{:S(2)}, u32[]{:S(2)}) collective-permute-start(bf16[4,64,512]{2,1,0:T(8,128)(2,1)S(1)} %get-tuple-element.60), channel_id=1, source_target_pairs={{0,7},{1,0},{2,1},{3,2},{4,3},{5,4},{6,5},{7,6},{8,15},{9,8},{10,9... | collective-permute-start | bytes 786440 | tf_op jit(solution)/shard_map/ppermute | solution.py:389
  112.8 20.5 %collective-permute-start.8 = (bf16[4,64,512]{2,1,0:T(8,128)(2,1)S(1)}, bf16[4,64,512]{2,1,0:T(8,128)(2,1)S(1)}, u32[]{:S(2)}, u32[]{:S(2)}) collective-permute-start(bf16[4,64,512]{2,1,0:T(8,128)(2,1)S(1)} %get-tuple-element.60), channel_id=1, source_target_pairs={{0,8},{8,16},{16,24},{24,32},{32,40},{40,48},{48,56},{56,64},{64,7... | collective-permute-start | bytes 786440 | tf_op jit(solution)/shard_map/ppermute | solution.py:389
  112.8 20.5 %collective-permute-start.9 = (bf16[4,64,512]{2,1,0:T(8,128)(2,1)S(1)}, bf16[4,64,512]{2,1,0:T(8,128)(2,1)S(1)}, u32[]{:S(2)}, u32[]{:S(2)}) collective-permute-start(bf16[4,64,512]{2,1,0:T(8,128)(2,1)S(1)} %get-tuple-element.60), channel_id=1, source_target_pairs={{0,120},{8,0},{16,8},{24,16},{32,24},{40,32},{48,40},{56,48},{64,5... | collective-permute-start | bytes 786440 | tf_op jit(solution)/shard_map/ppermute | solution.py:389
  126.4 1.3 copy-start.6
  127.8 11.9 %copy-start.5 = (f32[1024,512]{1,0:T(8,128)}, f32[1024,512]{1,0:T(8,128)S(1)}, u32[]{:S(2)}) copy-start(f32[1024,512]{1,0:T(8,128)S(1)} %get-tuple-element.69.grad_1) | copy-start | bytes 6291460
  127.8 11.9 %collective-permute-start.12 = (bf16[4,64,512]{2,1,0:T(8,128)(2,1)S(1)}, bf16[4,64,512]{2,1,0:T(8,128)(2,1)S(1)}, u32[]{:S(2)}, u32[]{:S(2)}) collective-permute-start(bf16[4,64,512]{2,1,0:T(8,128)(2,1)S(1)} %get-tuple-element.76), channel_id=1, source_target_pairs={{0,120},{8,0},{16,8},{24,16},{32,24},{40,32},{48,40},{56,48},{64,5... | collective-permute-start | bytes 786440 | tf_op jit(solution)/shard_map/ppermute | solution.py:389
  127.8 11.9 %collective-permute-start.13 = (bf16[4,64,512]{2,1,0:T(8,128)(2,1)S(1)}, bf16[4,64,512]{2,1,0:T(8,128)(2,1)S(1)}, u32[]{:S(2)}, u32[]{:S(2)}) collective-permute-start(bf16[4,64,512]{2,1,0:T(8,128)(2,1)S(1)} %get-tuple-element.77), channel_id=1, source_target_pairs={{0,8},{8,16},{16,24},{24,32},{32,40},{40,48},{48,56},{56,64},{64,7... | collective-permute-start | bytes 786440 | tf_op jit(solution)/shard_map/ppermute | solution.py:389
  129.2 10.4 %collective-permute-start.14 = (bf16[4,64,512]{2,1,0:T(8,128)(2,1)S(1)}, bf16[4,64,512]{2,1,0:T(8,128)(2,1)S(1)}, u32[]{:S(2)}, u32[]{:S(2)}) collective-permute-start(bf16[4,64,512]{2,1,0:T(8,128)(2,1)S(1)} %get-tuple-element.78), channel_id=1, source_target_pairs={{0,7},{1,0},{2,1},{3,2},{4,3},{5,4},{6,5},{7,6},{8,15},{9,8},{10,9... | collective-permute-start | bytes 786440 | tf_op jit(solution)/shard_map/ppermute | solution.py:389
  133.3 6.4 %collective-permute-start.15 = (bf16[4,64,512]{2,1,0:T(8,128)(2,1)S(1)}, bf16[4,64,512]{2,1,0:T(8,128)(2,1)S(1)}, u32[]{:S(2)}, u32[]{:S(2)}) collective-permute-start(bf16[4,64,512]{2,1,0:T(8,128)(2,1)S(1)} %get-tuple-element.79), channel_id=1, source_target_pairs={{0,1},{1,2},{2,3},{3,4},{4,5},{5,6},{6,7},{7,0},{8,9},{9,10},{10,1... | collective-permute-start | bytes 786440 | tf_op jit(solution)/shard_map/ppermute | solution.py:389
  238.3 3.5 %collective-permute-start.16 = (bf16[128,40,128]{2,1,0:T(8,128)(2,1)S(1)}, bf16[128,40,128]{2,1,0:T(8,128)(2,1)S(1)}, u32[]{:S(2)}, u32[]{:S(2)}) collective-permute-start(bf16[128,40,128]{2,1,0:T(8,128)(2,1)S(1)} %all_to_all.28.own), channel_id=1, source_target_pairs={{0,1},{1,0},{2,3},{3,2},{4,5},{5,4},{6,7},{7,6},{8,9},{9,8},{10,11... | collective-permute-start | bytes 3932168 | tf_op jit(solution)/shard_map/ppermute | solution.py:529

commit v4 on v3

--- a/solution.py
+++ b/solution.py
@@ -21,9 +21,9 @@
 TAIL = 256
 DEVICES = 128
 SLAB = 4 * WIDTH
-EARLY = 3 * SLAB // 16
-LATE = (SLAB + 4 * TAIL) // 16
-PART = (EARLY + LATE) // 8
+EARLY = 3 * SLAB // DEVICES
+LATE = (SLAB + 4 * TAIL) // DEVICES
+PART = EARLY + LATE
 HALF = 40
 AXES = ("wide", "narrow")
 BF16 = jnp.bfloat16
@@ -330,14 +330,10 @@
         write_slabs(grads, SLAB, total[...])
 
 
-def sum_wide_body(early, late, out):
-    out[0:EARLY, :] = jnp.sum(early[...].astype(F32), axis=0).astype(BF16)
-    out[EARLY : EARLY + LATE, :] = jnp.sum(late[...].astype(F32), axis=0).astype(BF16)
-
-
-def sum_narrow_body(parts, out):
-    total = jnp.sum(parts[...].astype(F32), axis=0)
-    halves = (total[0:HALF].astype(BF16), total[PART - HALF : PART].astype(BF16))
+def sum_body(early, late, out, total):
+    total[0:EARLY, :] = jnp.sum(early[...].astype(F32), axis=0)
+    total[EARLY:PART, :] = jnp.sum(late[...].astype(F32), axis=0)
+    halves = (total[0:HALF, :].astype(BF16), total[PART - HALF : PART, :].astype(BF16))
 
     def one(i, carry):
         out[2 * i] = halves[0]
@@ -347,41 +343,37 @@
     lax.fori_loop(0, DEVICES // 2, one, 0, unroll=8)
 
 
-def unpack_body(odd, own, other, d_embed, ms_grad, up_grad, sums):
-    def one(i, carry):
-        at = pl.multiple_of(i * PART, 8)
-
-        @pl.when(odd[0] == 0)
-        def _():
-            sums[pl.ds(at + PART - HALF, HALF), :] = other[i].astype(F32)
-            sums[pl.ds(at, HALF), :] = own[i].astype(F32)
-
-        @pl.when(odd[0] == 1)
-        def _():
-            sums[pl.ds(at + PART - HALF, HALF), :] = own[i].astype(F32)
-            sums[pl.ds(at, HALF), :] = other[i].astype(F32)
-
-        return carry
-
-    lax.fori_loop(0, DEVICES, one, 0)
-    runs = EARLY + LATE
-
-    def place(out, columns, first, rows, share, offset):
-        done = 0
-        while done < rows:
-            w, r = divmod(first + done, share)
-            take = min(rows - done, share - r)
-            at = w * runs + offset + r
-            out[done : done + take, columns] = sums[at : at + take, :]
-            done += take
-
-    for c in range(4):
-        columns = slice(c * 128, (c + 1) * 128)
-        place(up_grad.at[0], columns, c * WIDTH, WIDTH, EARLY, 0)
-        place(ms_grad.at[1], columns, SLAB + c * WIDTH, WIDTH, EARLY, 0)
-        place(up_grad.at[1], columns, 2 * SLAB + c * WIDTH, WIDTH, EARLY, 0)
-        place(ms_grad.at[0], columns, c * WIDTH, WIDTH, LATE, EARLY)
-        place(d_embed, columns, SLAB + c * TAIL, CHAN, LATE, EARLY)
+def unpack_body(odd, own, other, d_embed, ms_grad, up_grad):
+    slabs = []
+    for out, rows in ((up_grad.at[0], WIDTH), (ms_grad.at[1], WIDTH), (up_grad.at[1], WIDTH)):
+        slabs += [(out, slice(c * 128, c * 128 + 128), rows) for c in range(4)]
+    late_slabs = [(ms_grad.at[0], slice(c * 128, c * 128 + 128), WIDTH) for c in range(4)]
+    late_slabs += [(d_embed, slice(c * 128, c * 128 + 128), TAIL) for c in range(4)]
+
+    def place(values, slabs, first):
+        begin = 0
+        for out, columns, rows in slabs:
+            low, high = max(first, begin), min(first + values.shape[0], begin + rows)
+            limit = min(high, begin + out.shape[0])
+            if low < limit:
+                out[low - begin : limit - begin, columns] = values[low - first : limit - first]
+            begin += rows
+
+    def unpack(lower, upper):
+        for q in range(DEVICES):
+            low = lower[q].astype(F32)
+            high = upper[q].astype(F32)
+            place(low, slabs, q * EARLY)
+            place(high[2 * HALF - PART : HALF - LATE], slabs, q * EARLY + HALF)
+            place(high[HALF - LATE :], late_slabs, q * LATE)
+
+    @pl.when(odd[0] == 0)
+    def _():
+        unpack(own, other)
+
+    @pl.when(odd[0] == 1)
+    def _():
+        unpack(other, own)
 
 
 def shift(value, axis, steps):
@@ -397,8 +389,8 @@
     return (shift(h0, "wide", -1), shift(h1, "wide", 1), shift(h2, "narrow", -1), shift(h3, "narrow", 1))
 
 
-def exchange(parts, axes):
-    return lax.all_to_all(parts, axes, split_axis=0, concat_axis=0, tiled=True)
+def exchange(parts):
+    return lax.all_to_all(parts, AXES, split_axis=0, concat_axis=0, tiled=True)
 
 
 def on_device(
@@ -422,11 +414,11 @@
         in_specs=[SM, pl.BlockSpec((CHAN, GRID_ROWS // 4), lambda i: (0, i))],
         out_specs=pl.BlockSpec((GRID_BLOCKS, PACKED, 2 * BLOCK), lambda i: (0, 0, 0)),
         scratch_shapes=[pltpu.SMEM((GRID_BLOCKS,), jnp.int32)],
-        compiler_params=pltpu.CompilerParams(vmem_limit_bytes=24 * MIB),
+        compiler_params=pltpu.CompilerParams(vmem_limit_bytes=56 * MIB),
         cost_estimate=pl.CostEstimate(flops=0, bytes_accessed=8 * MIB, transcendentals=0),
     )(grid_send, grid_feat.T)
     packed, cotangent = lax.optimization_barrier((packed, cotangent))
-    received = exchange(packed, AXES)
+    received = exchange(packed)
 
     g_mix = g2m_coef.transpose(0, 2, 1, 3).reshape(MESH_BLOCKS, BLOCK, G_SLOTS * BLOCK)
     m_mix = mesh_coef.transpose(0, 2, 1, 3).reshape(MESH_BLOCKS, BLOCK, M_SLOTS * BLOCK)
@@ -445,15 +437,15 @@
         encode_body,
         grid=(4,),
         out_shape=[
-            jax.ShapeDtypeStruct((CHAN, GRID_ROWS), BF16),
-            jax.ShapeDtypeStruct((GRID_ROWS, WIDTH), BF16),
+            pltpu.HBM((CHAN, GRID_ROWS), BF16),
+            pltpu.HBM((GRID_ROWS, WIDTH), BF16),
             jax.ShapeDtypeStruct((GRID_ROWS, WIDTH), BF16),
             jax.ShapeDtypeStruct((SHOWN, BLOCK, WIDTH), BF16),
         ],
         in_specs=[
             SM, SM,
             pl.BlockSpec((32, PACKED, 2 * BLOCK), lambda i: (i, 0, 0)),
-            whole(CHAN, WIDTH), whole(MESH_BLOCKS, BLOCK, G_SLOTS * BLOCK), whole(WIDTH, WIDTH),
+            VM, VM, VM,
         ],
         out_specs=[
             pl.BlockSpec((CHAN, 2048), lambda i: (0, i)),
@@ -464,7 +456,7 @@
         scratch_shapes=[
             pltpu.VMEM((GRID_ROWS, WIDTH), BF16), pltpu.VMEM((SHOWN * BLOCK, WIDTH), BF16)
         ],
-        compiler_params=pltpu.CompilerParams(vmem_limit_bytes=56 * MIB),
+        compiler_params=pltpu.CompilerParams(vmem_limit_bytes=28 * MIB),
         cost_estimate=pl.CostEstimate(flops=4 * 10**9, bytes_accessed=26 * MIB, transcendentals=0),
     )(g2m_src, halo_send, received, w_embed, g_mix, w_m[0])
     shown_0 = show(mine_0)
@@ -492,16 +484,14 @@
         grad_pre_1,
     )
     own_0, early = lax.optimization_barrier((own_0, early))
-    early = exchange(early.reshape(16, EARLY, 128), "wide")
+    early = exchange(early.reshape(DEVICES, EARLY, 128))
 
     late = pl.pallas_call(
         final_body,
         grid=(4,),
         out_shape=jax.ShapeDtypeStruct((SLAB + 4 * TAIL, 128), BF16),
         in_specs=[
-            SM, SM, whole(MESH_ROWS, WIDTH), *[whole(SHOWN, BLOCK, WIDTH)] * 4,
-            whole(MESH_ROWS, WIDTH), whole(MESH_ROWS, WIDTH), whole(WIDTH, WIDTH),
-            whole(MESH_ROWS, WIDTH), whole(MESH_BLOCKS, BLOCK, G_SLOTS * BLOCK),
+            SM, SM, *[VM] * 10,
             pl.BlockSpec((2048, WIDTH), lambda i: (i, 0)),
             pl.BlockSpec((CHAN, 2048), lambda i: (0, i)),
         ],
@@ -511,27 +501,25 @@
             mesh_scratch, mesh_scratch, mesh_scratch32,
             pltpu.VMEM((TAIL, WIDTH), F32),
         ],
-        compiler_params=pltpu.CompilerParams(vmem_limit_bytes=50 * MIB),
+        compiler_params=pltpu.CompilerParams(vmem_limit_bytes=34 * MIB),
         cost_estimate=pl.CostEstimate(flops=4 * 10**9, bytes_accessed=24 * MIB, transcendentals=0),
     )(
         g2m_src, halo_send, own_0, *returned_0, slope_0, grad_1, w_m[0], mesh_0, g_mix, slope,
         points,
     )
-    late = exchange(late.reshape(16, LATE, 128), "wide")
-
-    parts = kernel_call(
-        sum_wide_body, [((EARLY + LATE, 128), BF16)], [VM, VM], moved=3 * MIB, limit=16
+    late, early = lax.optimization_barrier((late, early))
+    late = exchange(late.reshape(DEVICES, LATE, 128))
+
+    totals = kernel_call(
+        sum_body, [((DEVICES, HALF, 128), BF16)], [VM, VM], [pltpu.VMEM((PART, 128), F32)],
+        moved=4 * MIB, limit=16,
     )(early, late)[0]
-    totals = kernel_call(
-        sum_narrow_body, [((DEVICES, HALF, 128), BF16)], [VM], moved=2 * MIB, limit=16
-    )(exchange(parts.reshape(8, PART, 128), "narrow"))[0]
-    own = exchange(totals, AXES)
+    own = exchange(totals)
     other = lax.ppermute(own, "narrow", [(i, i ^ 1) for i in range(8)])
     d_embed, ms_grad, up_grad = kernel_call(
         unpack_body,
         [((CHAN, WIDTH), F32), ((2, WIDTH, WIDTH), F32), ((2, WIDTH, WIDTH), F32)],
         [SM, VM, VM],
-        [pltpu.VMEM((DEVICES * PART, 128), F32)],
         moved=7 * MIB,
         limit=24,
     )((lax.axis_index("narrow") % 2).reshape(1).astype(jnp.int32), own, other)

time: 248 us -> 246 us (level)
  blocking collectives: 79.6 us -> 48.4 us
  waiting for transfers between devices: 22.2 us -> 44.7 us
  starting transfers between devices: 39.8 us -> 48.8 us
  Pallas kernels: 77.1 us -> 73.7 us
    all_to_all x4 -> x2, blocking collectives: 79.6 us -> 48.4 us  [exchange(): return lax.all_to_all(parts, AXES, split_axis=0, concat_axis=0, tiled=True)]
    ppermute x16, waiting for transfers between devices: 19.6 us -> 42 us  [shift(): lax.ppermute(value, axis, [(i, (i + steps) % count) for i in range(count)])]
    all_to_all x1 -> x2, starting transfers between devices: 11.9 us -> 18.9 us  [exchange(): return lax.all_to_all(parts, AXES, split_axis=0, concat_axis=0, tiled=True)]
    pallas_call x1, Pallas kernels: 3.26 us -> 6.29 us  [on_device(): pl.pallas_call(pack_body, grid=(4,), out_shape=jax.ShapeDtypeStruct((GRID...]
    pallas_call x1, Pallas kernels: 5.5 us -> 2.69 us  [on_device(): kernel_call(unpack_body, [((CHAN, WIDTH), F32), ((2, WIDTH, WIDTH), F32),...]
    unnamed x38 -> x56, local copies, waits for them, and re-layouts: 11.4 us -> 13.2 us
    pallas_call x3 -> x2, Pallas kernels: 16.6 us -> 15.3 us  [the longest x1 14.8 us: on_device(): pl.pallas_call(encode_body, grid=(4,), out_shape=[pltpu.HBM((CHAN, GRID_R...]
  transfers between devices with their start and end apart: 18 -> 19, of which waited for: 3 -> 6; matrix products, arithmetic and copies ran while one was open for 7% -> 6% of each run, Pallas kernels for 11% -> 15%
where the time goes in v4:
time: 246 us; the launch traced here: 245 us
  Pallas kernels  73.7 us (30%)
  starting transfers between devices  48.8 us (20%)
  blocking collectives  48.4 us (20%)
  waiting for transfers between devices  44.7 us (18%)
  local copies, waits for them, and re-layouts  28.6 us (12%)
    all_to_all x2, blocking collectives, exchange(): return lax.all_to_all(parts, AXES, split_axis=0, concat_axis=0, tiled=True)  48.4 us
    ppermute x16, waiting for transfers between devices, shift(): lax.ppermute(value, axis, [(i, (i + steps) % count) for i in range(count)])  42 us
    ppermute x16, starting transfers between devices, shift(): lax.ppermute(value, axis, [(i, (i + steps) % count) for i in range(count)])  29 us
    all_to_all x2, starting transfers between devices, exchange(): return lax.all_to_all(parts, AXES, split_axis=0, concat_axis=0, tiled=True)  18.9 us
    pallas_call x1, Pallas kernels, on_device(): pl.pallas_call(final_body, grid=(4,), out_shape=jax.ShapeDtypeStruct((SLA...  16.3 us
    pallas_call x1, Pallas kernels, on_device(): pl.pallas_call(encode_body, grid=(4,), out_shape=[pltpu.HBM((CHAN, GRID_R...  14.8 us
    unnamed x56, local copies, waits for them, and re-layouts  13.2 us
    pallas_call x1, Pallas kernels, on_device(): kernel_call(backward_body, [rows_bf16, rows_f32, rows_f32] + [halo] * 4,...  8.82 us
  transfers between devices with their start and end apart: 19, of which 6 were waited for; matrix products, arithmetic and copies ran while one was open for 6% of the time, Pallas kernels for 15%

profile of v4, /device:TPU:1, one launch (start us, length us, event | category | flops | bytes accessed | tf_op | source)
XLA Modules:
  0.0 245.2 jit_solution(14084829814080801408)
XLA Ops:
  0.6 6.3 %shard_map.138 = bf16[128,115,128]{2,1,0:T(8,128)(2,1)} custom-call(s32[1,128]{1,0:T(1,128)} %send.1, bf16[227,8192]{1,0:T(8,128)(2,1)} %bitcast.18), custom_call_target="tpu_custom_call" | custom-call | bytes 8388608 | tf_op jit(solution)/shard_map/pallas_call | solution.py:410
  6.9 11.9 %all-to-all-start = ((bf16[128,115,128]{2,1,0:T(8,128)(2,1)}), bf16[128,115,128]{2,1,0:T(8,128)(2,1)}, u32[]{:S(2)}, u32[]{:S(2)}) async-start(bf16[128,115,128]{2,1,0:T(8,128)(2,1)} %shard_map.138), calls=%async_computation | async-start | bytes 7864320 | tf_op jit(solution)/shard_map/all_to_all | solution.py:393
  18.8 0.1 copy.31.source
  18.9 2.6 %copy.25 = bf16[16,64,6,64]{3,2,1,0:T(8,128)(2,1)} copy(bf16[16,64,6,64]{3,1,2,0:T(8,128)(2,1)S(1)} %bitcast.20) | data formatting | bytes 1572864 | tf_op jit(solution)/shard_map/transpose | solution.py:424
  21.6 3.1 %reshape.24.coeffs = bf16[16,64,384]{2,1,0:T(8,128)(2,1)S(1)} reshape(bf16[16,64,6,64]{3,2,1,0:T(8,128)(2,1)} %copy.25) | data formatting | bytes 1572864 | tf_op jit(solution)/shard_map/reshape | solution.py:424
  24.7 1.3 slice_bitcast_fusion.1
  26.0 0.0 copy-start.23
  26.0 7.8 %shard_map.139 = (f32[1024,512]{1,0:T(8,128)S(1)}, bf16[4,64,512]{2,1,0:T(8,128)(2,1)}, bf16[4,64,512]{2,1,0:T(8,128)(2,1)}, bf16[4,64,512]{2,1,0:T(8,128)(2,1)}, bf16[4,64,512]{2,1,0:T(8,128)(2,1)}) custom-call(s32[16,6]{1,0:T(8,128)S(1)} %copy.31.source, bf16[1024,512]{1,0:T(8,128)(2,1)S(1)} %copy-done.13, bf16[512,512]{1,0:T(8,128)(2,1)S(1)} %get-tuple-element.93.up, ...), custom_call_target="tpu_custom_call" | custom-call | flops 2000000000 | bytes 8388608 | tf_op jit(solution)/shard_map/pallas_call | solution.py:426
  33.9 1.3 copy-done.21
  35.2 5.6 %collective-permute-start = (bf16[4,64,512]{2,1,0:T(8,128)(2,1)}, bf16[4,64,512]{2,1,0:T(8,128)(2,1)}, u32[]{:S(2)}, u32[]{:S(2)}) collective-permute-start(bf16[4,64,512]{2,1,0:T(8,128)(2,1)} %get-tuple-element.50), channel_id=1, source_target_pairs={{0,120},{8,0},{16,8},{24,16},{32,24},{40,32},{48,40},{56,48},{64,5... | collective-permute-start | bytes 786440 | tf_op jit(solution)/shard_map/ppermute | solution.py:381
  40.7 0.0 collective-permute-start.1
  40.7 0.7 collective-permute-start.2
  41.4 1.1 collective-permute-start.3
  42.5 3.1 %copy.24 = bf16[16,64,8,64]{3,2,1,0:T(8,128)(2,1)} copy(bf16[16,64,8,64]{3,1,2,0:T(8,128)(2,1)S(1)} %bitcast.19) | data formatting | bytes 2097152 | tf_op jit(solution)/shard_map/transpose | solution.py:423
  45.6 3.2 %reshape.23.coeffs = bf16[16,64,512]{2,1,0:T(8,128)(2,1)S(1)} reshape(bf16[16,64,8,64]{3,2,1,0:T(8,128)(2,1)} %copy.24) | data formatting | bytes 2097152 | tf_op jit(solution)/shard_map/reshape | solution.py:423
  48.9 0.1 copy.28.source
  48.9 2.1 slice_bitcast_fusion
  51.0 16.8 %collective-permute-done.r0 = bf16[4,64,512]{2,1,0:T(8,128)(2,1)} collective-permute-done((bf16[4,64,512]{2,1,0:T(8,128)(2,1)}, bf16[4,64,512]{2,1,0:T(8,128)(2,1)}, u32[]{:S(2)}, u32[]{:S(2)}) %collective-permute-start) | collective-permute-done | bytes 262176 | tf_op jit(solution)/shard_map/ppermute | solution.py:381
  67.8 4.2 %collective-permute-done.1.r1 = bf16[4,64,512]{2,1,0:T(8,128)(2,1)} collective-permute-done((bf16[4,64,512]{2,1,0:T(8,128)(2,1)}, bf16[4,64,512]{2,1,0:T(8,128)(2,1)}, u32[]{:S(2)}, u32[]{:S(2)}) %collective-permute-start.1) | collective-permute-done | bytes 262176 | tf_op jit(solution)/shard_map/ppermute | solution.py:381
  72.0 0.0 copy-start.20
  72.0 0.9 copy-done.20
  72.9 14.8 %shard_map.140 = (bf16[227,8192]{1,0:T(8,128)(2,1)}, bf16[8192,512]{1,0:T(8,128)(2,1)}, bf16[8192,512]{1,0:T(8,128)(2,1)S(1)}, bf16[4,64,512]{2,1,0:T(8,128)(2,1)S(1)}) custom-call(s32[16,8]{1,0:T(8,128)S(1)} %copy.28.source, s32[1,4]{1,0:T(1,128)S(1)} %copy-done.12, bf16[128,115,128]{2,1,0:T(8,128)(2,1)} %all-to-all-done.packed, ...), custom_call_target="tpu_custom_call" | custom-call | flops 4000000000 | bytes 27262976 | tf_op jit(solution)/shard_map/pallas_call | solution.py:436
  87.7 0.0 collective-permute-start.4
  87.7 4.8 %collective-permute-start.5 = (bf16[4,64,512]{2,1,0:T(8,128)(2,1)S(1)}, bf16[4,64,512]{2,1,0:T(8,128)(2,1)S(1)}, u32[]{:S(2)}, u32[]{:S(2)}) collective-permute-start(bf16[4,64,512]{2,1,0:T(8,128)(2,1)S(1)} %get-tuple-element.58), channel_id=1, source_target_pairs={{0,120},{8,0},{16,8},{24,16},{32,24},{40,32},{48,40},{56,48},{64,5... | collective-permute-start | bytes 786440 | tf_op jit(solution)/shard_map/ppermute | solution.py:381
  92.5 2.8 %collective-permute-start.6 = (bf16[4,64,512]{2,1,0:T(8,128)(2,1)S(1)}, bf16[4,64,512]{2,1,0:T(8,128)(2,1)S(1)}, u32[]{:S(2)}, u32[]{:S(2)}) collective-permute-start(bf16[4,64,512]{2,1,0:T(8,128)(2,1)S(1)} %get-tuple-element.58), channel_id=1, source_target_pairs={{0,1},{1,2},{2,3},{3,4},{4,5},{5,6},{6,7},{7,0},{8,9},{9,10},{10,1... | collective-permute-start | bytes 786440 | tf_op jit(solution)/shard_map/ppermute | solution.py:381
  95.3 0.0 collective-permute-start.7
  95.3 4.7 %shard_map.141 = (bf16[1024,512]{1,0:T(8,128)(2,1)S(1)}, bf16[1024,512]{1,0:T(8,128)(2,1)S(1)}, bf16[1024,512]{1,0:T(8,128)(2,1)S(1)}) custom-call(s32[16,8]{1,0:T(8,128)S(1)} %copy.28.source, bf16[8192,512]{1,0:T(8,128)(2,1)S(1)} %get-tuple-element.56.embedded, bf16[16,64,512]{2,1,0:T(8,128)(2,1)S(1)} %reshape.23.coeffs, ...), custom_call_target="tpu_custom_call" | custom-call | flops 2000000000 | bytes 12582912 | tf_op jit(solution)/shard_map/pallas_call | solution.py:463
  100.1 1.0 copy-done.9
  101.1 0.0 collective-permute-done.6.n2
  101.1 0.1 collective-permute-done.7.n3
  101.1 5.4 %shard_map.142 = (bf16[1024,512]{1,0:T(8,128)(2,1)S(1)}, bf16[1024,512]{1,0:T(8,128)(2,1)S(1)}, bf16[1024,512]{1,0:T(8,128)(2,1)S(1)}, bf16[1024,512]{1,0:T(8,128)(2,1)S(1)}, bf16[4,64,512]{2,1,0:T(8,128)(2,1)S(1)}) custom-call(s32[16,6]{1,0:T(8,128)S(1)} %copy.31.source, s32[1,4]{1,0:T(1,128)S(1)} %copy-done.12, ...), custom_call_target="tpu_custom_call" | custom-call | flops 2000000000 | bytes 10485760 | tf_op jit(solution)/shard_map/pallas_call | solution.py:467
  106.6 1.7 collective-permute-start.10
  108.3 4.8 %collective-permute-start.9 = (bf16[4,64,512]{2,1,0:T(8,128)(2,1)S(1)}, bf16[4,64,512]{2,1,0:T(8,128)(2,1)S(1)}, u32[]{:S(2)}, u32[]{:S(2)}) collective-permute-start(bf16[4,64,512]{2,1,0:T(8,128)(2,1)S(1)} %get-tuple-element.62), channel_id=1, source_target_pairs={{0,120},{8,0},{16,8},{24,16},{32,24},{40,32},{48,40},{56,48},{64,5... | collective-permute-start | bytes 786440 | tf_op jit(solution)/shard_map/ppermute | solution.py:381
  113.1 8.8 %shard_map.143 = (bf16[1024,512]{1,0:T(8,128)(2,1)S(1)}, f32[1024,512]{1,0:T(8,128)S(1)}, f32[1024,512]{1,0:T(8,128)S(1)}, bf16[4,64,512]{2,1,0:T(8,128)(2,1)S(1...) custom-call(s32[16,6]{1,0:T(8,128)S(1)} %copy.31.source, ...), custom_call_target="tpu_custom_call" | custom-call | flops 2000000000 | bytes 16777216 | tf_op jit(solution)/shard_map/pallas_call | solution.py:473
  121.9 0.0 copy-start.2
  122.0 0.0 copy-start.4
  122.0 0.0 copy-start.19
  122.0 0.0 collective-permute-done.10.n2
  122.0 0.0 collective-permute-done.8.n0
  122.0 0.0 collective-permute-done.9.n1
  122.1 6.3 %shard_map.144 = (bf16[1024,512]{1,0:T(8,128)(2,1)}, bf16[6144,128]{1,0:T(8,128)(2,1)S(1)}) custom-call(s32[16,6]{1,0:T(8,128)S(1)} %copy.31.source, bf16[1024,512]{1,0:T(8,128)(2,1)S(1)} %get-tuple-element.61.sent, bf16[4,64,512]{2,1,0:T(8,128)(2,1)S(1)} %collective-permute-done.8.n0, bf16[4,64,512]{2,1,0:T(8,128)(2,1)S(1)} %collective-permute-done.9.n1, ...), custom_call_target="tpu_custom_call" | custom-call | flops 4000000000 | bytes 14680064 | tf_op jit(solution)/shard_map/pallas_call | solution.py:479
  128.4 1.1 copy-done.6
  129.6 7.0 %all-to-all-start.1 = ((bf16[128,48,128]{2,1,0:T(8,128)(2,1)}), bf16[128,48,128]{2,1,0:T(8,128)(2,1)S(1)}, u32[]{:S(2)}, u32[]{:S(2)}) async-start(bf16[128,48,128]{2,1,0:T(8,128)(2,1)} %bitcast.17), calls=%async_computation.1 | async-start | bytes 3145728 | tf_op jit(solution)/shard_map/all_to_all | solution.py:393
  136.6 5.8 %collective-permute-start.12 = (bf16[4,64,512]{2,1,0:T(8,128)(2,1)}, bf16[4,64,512]{2,1,0:T(8,128)(2,1)S(1)}, u32[]{:S(2)}, u32[]{:S(2)}) collective-permute-start(bf16[4,64,512]{2,1,0:T(8,128)(2,1)} %copy-done.19), channel_id=1, source_target_pairs={{0,120},{8,0},{16,8},{24,16},{32,24},{40,32},{48,40},{56,48},{64,5... | collective-permute-start | bytes 786440 | tf_op jit(solution)/shard_map/ppermute | solution.py:381
  142.4 0.0 collective-permute-start.13
  142.4 0.6 collective-permute-start.14
  143.0 1.1 collective-permute-start.15
  144.1 16.5 %collective-permute-done.12.r0 = bf16[4,64,512]{2,1,0:T(8,128)(2,1)S(1)} collective-permute-done((bf16[4,64,512]{2,1,0:T(8,128)(2,1)}, bf16[4,64,512]{2,1,0:T(8,128)(2,1)S(1)}, u32[]{:S(2)}, u32[]{:S(2)}) %collective-permute-start.12) | collective-permute-done | bytes 262176 | tf_op jit(solution)/shard_map/ppermute | solution.py:381
  160.6 4.4 %collective-permute-done.13.r1 = bf16[4,64,512]{2,1,0:T(8,128)(2,1)S(1)} collective-permute-done((bf16[4,64,512]{2,1,0:T(8,128)(2,1)}, bf16[4,64,512]{2,1,0:T(8,128)(2,1)S(1)}, u32[]{:S(2)}, u32[]{:S(2)}) %collective-permute-start.13) | collective-permute-done | bytes 262176 | tf_op jit(solution)/shard_map/ppermute | solution.py:381
  165.0 0.0 collective-permute-done.15.r3
  165.1 2.1 copy-done
  167.1 1.6 copy-done.3
  168.7 1.6 copy-done.5
  170.3 1.2 copy-done.8
  171.5 1.2 copy-done.10
  172.8 16.3 %shard_map.145 = bf16[3072,128]{1,0:T(8,128)(2,1)S(1)} custom-call(s32[16,8]{1,0:T(8,128)S(1)} %copy.28.source, s32[1,4]{1,0:T(1,128)S(1)} %copy-done.12, f32[1024,512]{1,0:T(8,128)S(1)} %copy-done.5, bf16[4,64,512]{2,1,0:T(8,128)(2,1)S(1)} %collective-permute-done.12.r0, bf16[4,64,512]{2,1,0:T(8,128)(2,1)S(1)} %collective-permute-done.13.r1, ...), custom_call_target="tpu_custom_call" | custom-call | flops 4000000000 | bytes 25165824 | tf_op jit(solution)/shard_map/pallas_call | solution.py:489
  189.1 0.0 copy-start.1
  189.1 0.9 copy-done.1
  190.0 22.0 %all_to_all.20.late = bf16[128,24,128]{2,1,0:T(8,128)(2,1)S(1)} all-to-all(bf16[128,24,128]{2,1,0:T(8,128)(2,1)} %bitcast.16), channel_id=1, replica_groups=mesh['wide'=16,'narrow'=8] {'wide','narrow'}, dimensions={0} | all-to-all | bytes 1572864 | tf_op jit(solution)/shard_map/all_to_all | solution.py:393
  212.0 0.6 shard_map.146
  212.6 26.4 %all_to_all.21.own = bf16[128,40,128]{2,1,0:T(8,128)(2,1)S(1)} all-to-all(bf16[128,40,128]{2,1,0:T(8,128)(2,1)S(1)} %shard_map.146), channel_id=1, replica_groups=mesh['wide'=16,'narrow'=8] {'wide','narrow'}, dimensions={0} | all-to-all | bytes 2621440 | tf_op jit(solution)/shard_map/all_to_all | solution.py:393
  238.9 0.9 collective-permute-start.16
  239.8 2.7 %collective-permute-done.16.other = bf16[128,40,128]{2,1,0:T(8,128)(2,1)S(1)} collective-permute-done((bf16[128,40,128]{2,1,0:T(8,128)(2,1)S(1)}, bf16[128,40,128]{2,1,0:T(8,128)(2,1)S(1)}, u32[]{:S(2)}, u32[]{:S(2)}) %collective-permute-start.16) | collective-permute-done | bytes 1310752 | tf_op jit(solution)/shard_map/ppermute | solution.py:518
  242.5 2.7 %shard_map.147 = (f32[227,512]{1,0:T(8,128)}, f32[2,512,512]{2,1,0:T(8,128)}, f32[2,512,512]{2,1,0:T(8,128)}) custom-call(s32[1]{0:T(128)} %bitcast.7.odd, bf16[128,40,128]{2,1,0:T(8,128)(2,1)S(1)} %all_to_all.21.own, bf16[128,40,128]{2,1,0:T(8,128)(2,1)S(1)} %collective-permute-done.16.other), custom_call_target="tpu_custom_call" | custom-call | bytes 7340032 | tf_op jit(solution)/shard_map/pallas_call | solution.py:519
  (48 shorter events, 0.1 us)
Async XLA Ops:
  6.9 11.9 %copy-start.25 = (s32[16,6]{0,1:T(8,128)S(1)}, s32[16,6]{0,1:T(8,128)}, u32[]{:S(2)}) copy-start(s32[16,6]{0,1:T(8,128)} %param.16) | copy-start | bytes 1156
  6.9 12.0 %copy-start.24 = (bf16[16,6,64,64]{3,2,1,0:T(8,128)(2,1)S(1)}, bf16[16,6,64,64]{3,2,1,0:T(8,128)(2,1)}, u32[]{:S(2)}) copy-start(bf16[16,6,64,64]{3,2,1,0:T(8,128)(2,1)} %param.17) | copy-start | bytes 2359300
  6.9 65.1 %all-to-all-start = ((bf16[128,115,128]{2,1,0:T(8,128)(2,1)}), bf16[128,115,128]{2,1,0:T(8,128)(2,1)}, u32[]{:S(2)}, u32[]{:S(2)}) async-start(bf16[128,115,128]{2,1,0:T(8,128)(2,1)} %shard_map.138), calls=%async_computation | async-start | bytes 7864320 | tf_op jit(solution)/shard_map/all_to_all | solution.py:393
  21.6 4.4 %copy-start.13 = (bf16[1024,512]{1,0:T(8,128)(2,1)S(1)}, bf16[1024,512]{1,0:T(8,128)(2,1)}, u32[]{:S(2)}) copy-start(bf16[1024,512]{1,0:T(8,128)(2,1)} %cot.2) | copy-start | bytes 3145732
  26.0 16.5 %copy-start.23 = (bf16[16,8,64,64]{3,2,1,0:T(8,128)(2,1)S(1)}, bf16[16,8,64,64]{3,2,1,0:T(8,128)(2,1)}, u32[]{:S(2)}) copy-start(bf16[16,8,64,64]{3,2,1,0:T(8,128)(2,1)} %param.15) | copy-start | bytes 3145732
  33.9 1.3 copy-start.21
  35.2 32.6 %collective-permute-start = (bf16[4,64,512]{2,1,0:T(8,128)(2,1)}, bf16[4,64,512]{2,1,0:T(8,128)(2,1)}, u32[]{:S(2)}, u32[]{:S(2)}) collective-permute-start(bf16[4,64,512]{2,1,0:T(8,128)(2,1)} %get-tuple-element.50), channel_id=1, source_target_pairs={{0,120},{8,0},{16,8},{24,16},{32,24},{40,32},{48,40},{56,48},{64,5... | collective-permute-start | bytes 786440 | tf_op jit(solution)/shard_map/ppermute | solution.py:381
  40.7 31.2 %collective-permute-start.1 = (bf16[4,64,512]{2,1,0:T(8,128)(2,1)}, bf16[4,64,512]{2,1,0:T(8,128)(2,1)}, u32[]{:S(2)}, u32[]{:S(2)}) collective-permute-start(bf16[4,64,512]{2,1,0:T(8,128)(2,1)} %get-tuple-element.51), channel_id=1, source_target_pairs={{0,8},{8,16},{16,24},{24,32},{32,40},{40,48},{48,56},{56,64},{64,7... | collective-permute-start | bytes 786440 | tf_op jit(solution)/shard_map/ppermute | solution.py:381
  40.7 31.2 %collective-permute-start.2 = (bf16[4,64,512]{2,1,0:T(8,128)(2,1)}, bf16[4,64,512]{2,1,0:T(8,128)(2,1)}, u32[]{:S(2)}, u32[]{:S(2)}) collective-permute-start(bf16[4,64,512]{2,1,0:T(8,128)(2,1)} %get-tuple-element.52), channel_id=1, source_target_pairs={{0,7},{1,0},{2,1},{3,2},{4,3},{5,4},{6,5},{7,6},{8,15},{9,8},{10,9... | collective-permute-start | bytes 786440 | tf_op jit(solution)/shard_map/ppermute | solution.py:381
  41.4 30.6 %collective-permute-start.3 = (bf16[4,64,512]{2,1,0:T(8,128)(2,1)}, bf16[4,64,512]{2,1,0:T(8,128)(2,1)}, u32[]{:S(2)}, u32[]{:S(2)}) collective-permute-start(bf16[4,64,512]{2,1,0:T(8,128)(2,1)} %get-tuple-element.53), channel_id=1, source_target_pairs={{0,1},{1,2},{2,3},{3,4},{4,5},{5,6},{6,7},{7,0},{8,9},{9,10},{10,1... | collective-permute-start | bytes 786440 | tf_op jit(solution)/shard_map/ppermute | solution.py:381
  45.6 3.2 %copy-start.26 = (s32[16,8]{0,1:T(8,128)S(1)}, s32[16,8]{0,1:T(8,128)}, u32[]{:S(2)}) copy-start(s32[16,8]{0,1:T(8,128)} %param.14) | copy-start | bytes 1540
  45.6 26.4 %copy-start.12 = (s32[1,4]{1,0:T(1,128)S(1)}, s32[1,4]{1,0:T(1,128)}, u32[]{:S(2)}) copy-start(s32[1,4]{1,0:T(1,128)} %shown.7) | copy-start | bytes 52
  72.0 0.9 copy-start.20
  87.7 13.3 %collective-permute-start.4 = (bf16[4,64,512]{2,1,0:T(8,128)(2,1)S(1)}, bf16[4,64,512]{2,1,0:T(8,128)(2,1)S(1)}, u32[]{:S(2)}, u32[]{:S(2)}) collective-permute-start(bf16[4,64,512]{2,1,0:T(8,128)(2,1)S(1)} %get-tuple-element.58), channel_id=1, source_target_pairs={{0,8},{8,16},{16,24},{24,32},{32,40},{40,48},{48,56},{56,64},{64,7... | collective-permute-start | bytes 786440 | tf_op jit(solution)/shard_map/ppermute | solution.py:381
  87.7 13.3 %collective-permute-start.5 = (bf16[4,64,512]{2,1,0:T(8,128)(2,1)S(1)}, bf16[4,64,512]{2,1,0:T(8,128)(2,1)S(1)}, u32[]{:S(2)}, u32[]{:S(2)}) collective-permute-start(bf16[4,64,512]{2,1,0:T(8,128)(2,1)S(1)} %get-tuple-element.58), channel_id=1, source_target_pairs={{0,120},{8,0},{16,8},{24,16},{32,24},{40,32},{48,40},{56,48},{64,5... | collective-permute-start | bytes 786440 | tf_op jit(solution)/shard_map/ppermute | solution.py:381
  92.5 8.6 %collective-permute-start.6 = (bf16[4,64,512]{2,1,0:T(8,128)(2,1)S(1)}, bf16[4,64,512]{2,1,0:T(8,128)(2,1)S(1)}, u32[]{:S(2)}, u32[]{:S(2)}) collective-permute-start(bf16[4,64,512]{2,1,0:T(8,128)(2,1)S(1)} %get-tuple-element.58), channel_id=1, source_target_pairs={{0,1},{1,2},{2,3},{3,4},{4,5},{5,6},{6,7},{7,0},{8,9},{9,10},{10,1... | collective-permute-start | bytes 786440 | tf_op jit(solution)/shard_map/ppermute | solution.py:381
  95.3 5.8 %collective-permute-start.7 = (bf16[4,64,512]{2,1,0:T(8,128)(2,1)S(1)}, bf16[4,64,512]{2,1,0:T(8,128)(2,1)S(1)}, u32[]{:S(2)}, u32[]{:S(2)}) collective-permute-start(bf16[4,64,512]{2,1,0:T(8,128)(2,1)S(1)} %get-tuple-element.58), channel_id=1, source_target_pairs={{0,7},{1,0},{2,1},{3,2},{4,3},{5,4},{6,5},{7,6},{8,15},{9,8},{10,9... | collective-permute-start | bytes 786440 | tf_op jit(solution)/shard_map/ppermute | solution.py:381
  95.3 5.8 %copy-start.11 = (bf16[512,512]{1,0:T(8,128)(2,1)S(1)}, bf16[512,512]{1,0:T(8,128)(2,1)}, u32[]{:S(2)}) copy-start(bf16[512,512]{1,0:T(8,128)(2,1)} %get-tuple-element.90.message) | copy-start | bytes 1572868
  100.1 1.0 copy-start.9
  101.1 5.5 %copy-start.7 = (bf16[1024,512]{1,0:T(8,128)(2,1)}, bf16[1024,512]{1,0:T(8,128)(2,1)S(1)}, u32[]{:S(2)}) copy-start(bf16[1024,512]{1,0:T(8,128)(2,1)S(1)} %get-tuple-element.60.mesh) | copy-start | bytes 3145732
  101.1 12.0 %copy-start.14 = (bf16[1024,512]{1,0:T(8,128)(2,1)S(1)}, bf16[1024,512]{1,0:T(8,128)(2,1)}, u32[]{:S(2)}) copy-start(bf16[1024,512]{1,0:T(8,128)(2,1)} %cot.2) | copy-start | bytes 3145732
  101.1 12.0 %copy-start.22 = (f32[1024,512]{1,0:T(8,128)S(1)}, f32[1024,512]{1,0:T(8,128)}, u32[]{:S(2)}) copy-start(f32[1024,512]{1,0:T(8,128)} %copy-done.21) | copy-start | bytes 6291460
  106.6 15.4 %collective-permute-start.10 = (bf16[4,64,512]{2,1,0:T(8,128)(2,1)S(1)}, bf16[4,64,512]{2,1,0:T(8,128)(2,1)S(1)}, u32[]{:S(2)}, u32[]{:S(2)}) collective-permute-start(bf16[4,64,512]{2,1,0:T(8,128)(2,1)S(1)} %get-tuple-element.62), channel_id=1, source_target_pairs={{0,1},{1,2},{2,3},{3,4},{4,5},{5,6},{6,7},{7,0},{8,9},{9,10},{10,1... | collective-permute-start | bytes 786440 | tf_op jit(solution)/shard_map/ppermute | solution.py:381
  108.3 13.7 %collective-permute-start.11 = (bf16[4,64,512]{2,1,0:T(8,128)(2,1)S(1)}, bf16[4,64,512]{2,1,0:T(8,128)(2,1)S(1)}, u32[]{:S(2)}, u32[]{:S(2)}) collective-permute-start(bf16[4,64,512]{2,1,0:T(8,128)(2,1)S(1)} %get-tuple-element.62), channel_id=1, source_target_pairs={{0,7},{1,0},{2,1},{3,2},{4,3},{5,4},{6,5},{7,6},{8,15},{9,8},{10,9... | collective-permute-start | bytes 786440 | tf_op jit(solution)/shard_map/ppermute | solution.py:381
  108.3 13.7 %collective-permute-start.8 = (bf16[4,64,512]{2,1,0:T(8,128)(2,1)S(1)}, bf16[4,64,512]{2,1,0:T(8,128)(2,1)S(1)}, u32[]{:S(2)}, u32[]{:S(2)}) collective-permute-start(bf16[4,64,512]{2,1,0:T(8,128)(2,1)S(1)} %get-tuple-element.62), channel_id=1, source_target_pairs={{0,8},{8,16},{16,24},{24,32},{32,40},{40,48},{48,56},{56,64},{64,7... | collective-permute-start | bytes 786440 | tf_op jit(solution)/shard_map/ppermute | solution.py:381
  108.3 13.7 %collective-permute-start.9 = (bf16[4,64,512]{2,1,0:T(8,128)(2,1)S(1)}, bf16[4,64,512]{2,1,0:T(8,128)(2,1)S(1)}, u32[]{:S(2)}, u32[]{:S(2)}) collective-permute-start(bf16[4,64,512]{2,1,0:T(8,128)(2,1)S(1)} %get-tuple-element.62), channel_id=1, source_target_pairs={{0,120},{8,0},{16,8},{24,16},{32,24},{40,32},{48,40},{56,48},{64,5... | collective-permute-start | bytes 786440 | tf_op jit(solution)/shard_map/ppermute | solution.py:381
  121.9 6.4 %copy-start.2 = (f32[1024,512]{1,0:T(8,128)}, f32[1024,512]{1,0:T(8,128)S(1)}, u32[]{:S(2)}) copy-start(f32[1024,512]{1,0:T(8,128)S(1)} %get-tuple-element.71.grad_1) | copy-start | bytes 6291460
  122.0 6.4 %copy-start.4 = (f32[1024,512]{1,0:T(8,128)}, f32[1024,512]{1,0:T(8,128)S(1)}, u32[]{:S(2)}) copy-start(f32[1024,512]{1,0:T(8,128)S(1)} %get-tuple-element.76.own) | copy-start | bytes 6291460
  122.0 6.4 %copy-start.15 = (bf16[4,64,512]{2,1,0:T(8,128)(2,1)}, bf16[4,64,512]{2,1,0:T(8,128)(2,1)S(1)}, u32[]{:S(2)}) copy-start(bf16[4,64,512]{2,1,0:T(8,128)(2,1)S(1)} %get-tuple-element.80) | copy-start | bytes 786436
  122.0 6.4 %copy-start.17 = (bf16[4,64,512]{2,1,0:T(8,128)(2,1)}, bf16[4,64,512]{2,1,0:T(8,128)(2,1)S(1)}, u32[]{:S(2)}) copy-start(bf16[4,64,512]{2,1,0:T(8,128)(2,1)S(1)} %get-tuple-element.79) | copy-start | bytes 786436
  122.0 6.4 %copy-start.18 = (bf16[4,64,512]{2,1,0:T(8,128)(2,1)}, bf16[4,64,512]{2,1,0:T(8,128)(2,1)S(1)}, u32[]{:S(2)}) copy-start(bf16[4,64,512]{2,1,0:T(8,128)(2,1)S(1)} %get-tuple-element.78) | copy-start | bytes 786436
  122.0 6.4 %copy-start.19 = (bf16[4,64,512]{2,1,0:T(8,128)(2,1)}, bf16[4,64,512]{2,1,0:T(8,128)(2,1)S(1)}, u32[]{:S(2)}) copy-start(bf16[4,64,512]{2,1,0:T(8,128)(2,1)S(1)} %get-tuple-element.77) | copy-start | bytes 786436
  128.4 1.2 copy-start.6
  129.6 13.5 %copy-start.16 = (bf16[4,64,512]{2,1,0:T(8,128)(2,1)S(1)}, bf16[4,64,512]{2,1,0:T(8,128)(2,1)}, u32[]{:S(2)}) copy-start(bf16[4,64,512]{2,1,0:T(8,128)(2,1)} %copy-done.15) | copy-start | bytes 786436
  129.6 60.4 %all-to-all-start.1 = ((bf16[128,48,128]{2,1,0:T(8,128)(2,1)}), bf16[128,48,128]{2,1,0:T(8,128)(2,1)S(1)}, u32[]{:S(2)}, u32[]{:S(2)}) async-start(bf16[128,48,128]{2,1,0:T(8,128)(2,1)} %bitcast.17), calls=%async_computation.1 | async-start | bytes 3145728 | tf_op jit(solution)/shard_map/all_to_all | solution.py:393
  136.6 24.0 %collective-permute-start.12 = (bf16[4,64,512]{2,1,0:T(8,128)(2,1)}, bf16[4,64,512]{2,1,0:T(8,128)(2,1)S(1)}, u32[]{:S(2)}, u32[]{:S(2)}) collective-permute-start(bf16[4,64,512]{2,1,0:T(8,128)(2,1)} %copy-done.19), channel_id=1, source_target_pairs={{0,120},{8,0},{16,8},{24,16},{32,24},{40,32},{48,40},{56,48},{64,5... | collective-permute-start | bytes 786440 | tf_op jit(solution)/shard_map/ppermute | solution.py:381
  142.4 22.7 %collective-permute-start.13 = (bf16[4,64,512]{2,1,0:T(8,128)(2,1)}, bf16[4,64,512]{2,1,0:T(8,128)(2,1)S(1)}, u32[]{:S(2)}, u32[]{:S(2)}) collective-permute-start(bf16[4,64,512]{2,1,0:T(8,128)(2,1)} %copy-done.18), channel_id=1, source_target_pairs={{0,8},{8,16},{16,24},{24,32},{32,40},{40,48},{48,56},{56,64},{64,7... | collective-permute-start | bytes 786440 | tf_op jit(solution)/shard_map/ppermute | solution.py:381
  142.4 22.7 %collective-permute-start.14 = (bf16[4,64,512]{2,1,0:T(8,128)(2,1)}, bf16[4,64,512]{2,1,0:T(8,128)(2,1)S(1)}, u32[]{:S(2)}, u32[]{:S(2)}) collective-permute-start(bf16[4,64,512]{2,1,0:T(8,128)(2,1)} %copy-done.17), channel_id=1, source_target_pairs={{0,7},{1,0},{2,1},{3,2},{4,3},{5,4},{6,5},{7,6},{8,15},{9,8},{10,9... | collective-permute-start | bytes 786440 | tf_op jit(solution)/shard_map/ppermute | solution.py:381
  143.0 22.0 %collective-permute-start.15 = (bf16[4,64,512]{2,1,0:T(8,128)(2,1)S(1)}, bf16[4,64,512]{2,1,0:T(8,128)(2,1)S(1)}, u32[]{:S(2)}, u32[]{:S(2)}) collective-permute-start(bf16[4,64,512]{2,1,0:T(8,128)(2,1)S(1)} %copy-done.16), channel_id=1, source_target_pairs={{0,1},{1,2},{2,3},{3,4},{4,5},{5,6},{6,7},{7,0},{8,9},{9,10},{10,1... | collective-permute-start | bytes 786440 | tf_op jit(solution)/shard_map/ppermute | solution.py:381
  165.0 2.1 copy-start
  167.1 1.6 copy-start.3
  168.7 1.6 copy-start.5
  170.3 1.2 copy-start.8
  171.5 1.2 copy-start.10
  189.1 0.9 copy-start.1
  238.9 3.5 %collective-permute-start.16 = (bf16[128,40,128]{2,1,0:T(8,128)(2,1)S(1)}, bf16[128,40,128]{2,1,0:T(8,128)(2,1)S(1)}, u32[]{:S(2)}, u32[]{:S(2)}) collective-permute-start(bf16[128,40,128]{2,1,0:T(8,128)(2,1)S(1)} %all_to_all.21.own), channel_id=1, source_target_pairs={{0,1},{1,0},{2,3},{3,2},{4,5},{5,4},{6,7},{7,6},{8,9},{9,8},{10,11... | collective-permute-start | bytes 3932168 | tf_op jit(solution)/shard_map/ppermute | solution.py:518

commit v5 on v4

--- a/solution.py
+++ b/solution.py
@@ -18,13 +18,12 @@
 GRID_ROWS = GRID_BLOCKS * BLOCK
 SPLIT = 112
 PACKED = CHAN - SPLIT
-TAIL = 256
 DEVICES = 128
-SLAB = 4 * WIDTH
-EARLY = 3 * SLAB // DEVICES
-LATE = (SLAB + 4 * TAIL) // DEVICES
-PART = EARLY + LATE
-HALF = 40
+COLUMNS = WIDTH // 2
+SLABS = 2 * WIDTH
+EARLY = 3 * SLABS // DEVICES
+LATE = 2 * SLABS // DEVICES
+PART = LATE + EARLY
 AXES = ("wide", "narrow")
 BF16 = jnp.bfloat16
 F32 = jnp.float32
@@ -175,7 +174,7 @@
         slope[rows, :] = (s + e * (1.0 - s)).astype(BF16)
         return carry
 
-    lax.fori_loop(0, 4, embed, 0)
+    lax.fori_loop(0, 4, embed, 0, unroll=2)
 
     @pl.when(step == 3)
     def _():
@@ -268,18 +267,30 @@
     write_halo(table, own_0, (h0, h1, h2, h3))
 
 
-def write_slabs(out, first, values):
-    rows = values.shape[0]
-    for c in range(4):
-        out[first + c * rows : first + (c + 1) * rows, :] = values[:, c * 128 : (c + 1) * 128].astype(BF16)
+def write_slabs(odd, keep, give, first, values):
+    def write(out, column):
+        for c in range(2):
+            at = first + c * WIDTH
+            slab = values[:, column + c * 128 : column + (c + 1) * 128]
+            out[at : at + values.shape[0], :] = slab.astype(BF16)
+
+    @pl.when(odd[0] == 0)
+    def _():
+        write(keep, 0)
+        write(give, COLUMNS)
+
+    @pl.when(odd[0] == 1)
+    def _():
+        write(keep, COLUMNS)
+        write(give, 0)
 
 
 def grads_body(
-    source, sent, n0, n1, n2, n3, coeffs, mesh, up, cot, aggregate_0, grad_1, grad_pre,
-    mesh_out, grads, extended, aggregate,
+    odd, source, sent, n0, n1, n2, n3, coeffs, mesh, up, cot, aggregate_0, grad_1, grad_pre,
+    mesh_out, keep, give, extended, aggregate,
 ):
-    write_slabs(grads, 0, times(aggregate_0[...], grad_1[...].astype(BF16), 0, 0))
-    write_slabs(grads, SLAB, times(mesh[...], grad_pre[...], 0, 0))
+    write_slabs(odd, keep, give, 0, times(aggregate_0[...], grad_1[...].astype(BF16), 0, 0))
+    write_slabs(odd, keep, give, SLABS, times(mesh[...], grad_pre[...], 0, 0))
     extend(extended, sent, (n0, n1, n2, n3))
     mix_mesh(coeffs, extended, source, aggregate)
 
@@ -290,12 +301,12 @@
         return carry
 
     lax.fori_loop(0, MESH_ROWS // 256, step, 0)
-    write_slabs(grads, 2 * SLAB, times(aggregate[...], cot[...], 0, 0))
+    write_slabs(odd, keep, give, 2 * SLABS, times(aggregate[...], cot[...], 0, 0))
 
 
 def final_body(
-    source, shown, own, r0, r1, r2, r3, slope_m, grad_1, message, mesh, coeffs, slope, points,
-    grads, table, grad_pre, lowered, grad_msg, total,
+    odd, source, shown, own, r0, r1, r2, r3, slope_m, grad_1, message, mesh, coeffs, slope, points,
+    keep, give, table, grad_pre, lowered, grad_msg, total,
 ):
     c = pl.program_id(0)
 
@@ -313,7 +324,7 @@
 
         lax.fori_loop(0, MESH_ROWS // 256, step, 0)
         scatter_back(coeffs, lowered, source, table, G_SLOTS, GRID_BLOCKS)
-        write_slabs(grads, 0, times(mesh[...], grad_pre[...], 0, 0))
+        write_slabs(odd, keep, give, 0, times(mesh[...], grad_pre[...], 0, 0))
         total[...] = jnp.zeros_like(total)
 
     def grid_step(i, carry):
@@ -327,53 +338,62 @@
 
     @pl.when(c == 3)
     def _():
-        write_slabs(grads, SLAB, total[...])
-
-
-def sum_body(early, late, out, total):
-    total[0:EARLY, :] = jnp.sum(early[...].astype(F32), axis=0)
-    total[EARLY:PART, :] = jnp.sum(late[...].astype(F32), axis=0)
-    halves = (total[0:HALF, :].astype(BF16), total[PART - HALF : PART, :].astype(BF16))
-
+        write_slabs(odd, keep, give, SLABS, total[...])
+
+
+def pair_body(late, late_other, early, early_other, out):
     def one(i, carry):
-        out[2 * i] = halves[0]
-        out[2 * i + 1] = halves[1]
+        out[i, 0:LATE, :] = (late[i].astype(F32) + late_other[i].astype(F32)).astype(BF16)
+        out[i, LATE:PART, :] = (early[i].astype(F32) + early_other[i].astype(F32)).astype(BF16)
+        return carry
+
+    lax.fori_loop(0, DEVICES, one, 0, unroll=8)
+
+
+def sum_body(parts, out):
+    zero = jnp.zeros((PART, 128), F32)
+
+    def add(i, carry):
+        return carry[0] + parts[2 * i].astype(F32), carry[1] + parts[2 * i + 1].astype(F32)
+
+    even, odd = lax.fori_loop(0, DEVICES // 2, add, (zero, zero), unroll=8)
+    even, odd = even.astype(BF16), odd.astype(BF16)
+
+    def one(i, carry):
+        out[2 * i] = even
+        out[2 * i + 1] = odd
         return carry
 
     lax.fori_loop(0, DEVICES // 2, one, 0, unroll=8)
 
 
 def unpack_body(odd, own, other, d_embed, ms_grad, up_grad):
-    slabs = []
-    for out, rows in ((up_grad.at[0], WIDTH), (ms_grad.at[1], WIDTH), (up_grad.at[1], WIDTH)):
-        slabs += [(out, slice(c * 128, c * 128 + 128), rows) for c in range(4)]
-    late_slabs = [(ms_grad.at[0], slice(c * 128, c * 128 + 128), WIDTH) for c in range(4)]
-    late_slabs += [(d_embed, slice(c * 128, c * 128 + 128), TAIL) for c in range(4)]
-
-    def place(values, slabs, first):
+    def place(values, outs, column, first):
         begin = 0
-        for out, columns, rows in slabs:
-            low, high = max(first, begin), min(first + values.shape[0], begin + rows)
-            limit = min(high, begin + out.shape[0])
-            if low < limit:
-                out[low - begin : limit - begin, columns] = values[low - first : limit - first]
-            begin += rows
-
-    def unpack(lower, upper):
+        for out in outs:
+            for c in range(2):
+                low = max(first, begin)
+                high = min(first + values.shape[0], begin + out.shape[0])
+                if low < high:
+                    at = column + c * 128
+                    out[low - begin : high - begin, at : at + 128] = values[low - first : high - first]
+                begin += WIDTH
+
+    def unpack(parts, column):
         for q in range(DEVICES):
-            low = lower[q].astype(F32)
-            high = upper[q].astype(F32)
-            place(low, slabs, q * EARLY)
-            place(high[2 * HALF - PART : HALF - LATE], slabs, q * EARLY + HALF)
-            place(high[HALF - LATE :], late_slabs, q * LATE)
+            values = parts[q].astype(F32)
+            place(values[0:LATE], (ms_grad.at[0], d_embed), column, q * LATE)
+            place(values[LATE:PART], (up_grad.at[0], ms_grad.at[1], up_grad.at[1]), column, q * EARLY)
 
     @pl.when(odd[0] == 0)
     def _():
-        unpack(own, other)
+        unpack(own, 0)
+        unpack(other, COLUMNS)
 
     @pl.when(odd[0] == 1)
     def _():
-        unpack(other, own)
+        unpack(other, 0)
+        unpack(own, COLUMNS)
 
 
 def shift(value, axis, steps):
@@ -387,6 +407,10 @@
 
 def give_back(h0, h1, h2, h3):
     return (shift(h0, "wide", -1), shift(h1, "wide", 1), shift(h2, "narrow", -1), shift(h3, "narrow", 1))
+
+
+def swap_cores(value):
+    return lax.ppermute(value, "narrow", [(i, i ^ 1) for i in range(lax.axis_size("narrow"))])
 
 
 def exchange(parts):
@@ -404,6 +428,7 @@
     mesh_scratch32 = pltpu.VMEM((MESH_ROWS, WIDTH), F32)
     extended_scratch = pltpu.VMEM((EXTENDED * BLOCK, WIDTH), BF16)
     table_scratch = pltpu.VMEM((EXTENDED, BLOCK, WIDTH), F32)
+    odd = (lax.axis_index("narrow") % 2).reshape(1).astype(jnp.int32)
     w_m = (message_weight[0], message_weight[1])
     w_u = (update_weight[0], update_weight[1])
 
@@ -476,53 +501,52 @@
     )(mesh_src, halo_send, own_1, *returned_1, slope_1, cotangent, w_m[1], w_u[0], m_mix)
     returned_0 = give_back(*halos)
 
-    mesh_out, early = kernel_call(
-        grads_body, [rows_bf16, ((3 * SLAB, 128), BF16)], [SM] + [VM] * 12,
-        [extended_scratch, mesh_scratch], flops=4 * 10**9, moved=14 * MIB, limit=24,
+    mesh_out, early, early_give = kernel_call(
+        grads_body, [rows_bf16, ((3 * SLABS, 128), BF16), ((3 * SLABS, 128), BF16)],
+        [SM, SM] + [VM] * 12, [extended_scratch, mesh_scratch], flops=4 * 10**9, moved=14 * MIB,
+        limit=24,
     )(
-        mesh_src, sent_1, *shown_1, m_mix, mesh_1, w_u[1], cotangent, aggregate_0, grad_1,
+        odd, mesh_src, sent_1, *shown_1, m_mix, mesh_1, w_u[1], cotangent, aggregate_0, grad_1,
         grad_pre_1,
     )
-    own_0, early = lax.optimization_barrier((own_0, early))
-    early = exchange(early.reshape(DEVICES, EARLY, 128))
-
-    late = pl.pallas_call(
+    early_other = swap_cores(early_give)
+
+    late, late_give = pl.pallas_call(
         final_body,
         grid=(4,),
-        out_shape=jax.ShapeDtypeStruct((SLAB + 4 * TAIL, 128), BF16),
+        out_shape=[jax.ShapeDtypeStruct((2 * SLABS, 128), BF16)] * 2,
         in_specs=[
-            SM, SM, *[VM] * 10,
+            SM, SM, SM, *[VM] * 10,
             pl.BlockSpec((2048, WIDTH), lambda i: (i, 0)),
             pl.BlockSpec((CHAN, 2048), lambda i: (0, i)),
         ],
-        out_specs=whole(SLAB + 4 * TAIL, 128),
+        out_specs=[VM, VM],
         scratch_shapes=[
             pltpu.VMEM((GRID_BLOCKS, BLOCK, WIDTH), F32),
             mesh_scratch, mesh_scratch, mesh_scratch32,
-            pltpu.VMEM((TAIL, WIDTH), F32),
+            pltpu.VMEM((WIDTH, WIDTH), F32),
         ],
         compiler_params=pltpu.CompilerParams(vmem_limit_bytes=34 * MIB),
         cost_estimate=pl.CostEstimate(flops=4 * 10**9, bytes_accessed=24 * MIB, transcendentals=0),
     )(
-        g2m_src, halo_send, own_0, *returned_0, slope_0, grad_1, w_m[0], mesh_0, g_mix, slope,
+        odd, g2m_src, halo_send, own_0, *returned_0, slope_0, grad_1, w_m[0], mesh_0, g_mix, slope,
         points,
     )
-    late, early = lax.optimization_barrier((late, early))
-    late = exchange(late.reshape(DEVICES, LATE, 128))
-
+    late_other = swap_cores(late_give)
+
+    by_device = lambda part: part.reshape(DEVICES, -1, 128)
+    pairs = kernel_call(
+        pair_body, [((DEVICES, PART, 128), BF16)], [VM] * 4, moved=6 * MIB, limit=16
+    )(by_device(late), by_device(late_other), by_device(early), by_device(early_other))[0]
     totals = kernel_call(
-        sum_body, [((DEVICES, HALF, 128), BF16)], [VM, VM], [pltpu.VMEM((PART, 128), F32)],
-        moved=4 * MIB, limit=16,
-    )(early, late)[0]
+        sum_body, [((DEVICES, PART, 128), BF16)], [VM], moved=3 * MIB, limit=16
+    )(exchange(pairs))[0]
     own = exchange(totals)
-    other = lax.ppermute(own, "narrow", [(i, i ^ 1) for i in range(8)])
     d_embed, ms_grad, up_grad = kernel_call(
         unpack_body,
         [((CHAN, WIDTH), F32), ((2, WIDTH, WIDTH), F32), ((2, WIDTH, WIDTH), F32)],
-        [SM, VM, VM],
-        moved=7 * MIB,
-        limit=24,
-    )((lax.axis_index("narrow") % 2).reshape(1).astype(jnp.int32), own, other)
+        [SM, VM, VM], moved=7 * MIB, limit=24,
+    )(odd, own, swap_cores(own))
     return mesh_out, d_embed, ms_grad, up_grad
 
 

time: 246 us -> 229 us (0.931)
  waiting for transfers between devices: 44.7 us -> 26.8 us
  starting transfers between devices: 48.8 us -> 39.5 us
  blocking collectives: 48.4 us -> 54.7 us
  local copies, waits for them, and re-layouts: 28.6 us -> 31.7 us
    ppermute x16, waiting for transfers between devices: 42 us -> 22.2 us  [shift(): lax.ppermute(value, axis, [(i, (i + steps) % count) for i in range(count)])]
    all_to_all x2 -> x1, starting transfers between devices: 18.9 us -> 11.9 us  [exchange(): return lax.all_to_all(parts, AXES, split_axis=0, concat_axis=0, tiled=True)]
    all_to_all x2, blocking collectives: 48.4 us -> 54.7 us  [exchange(): return lax.all_to_all(parts, AXES, split_axis=0, concat_axis=0, tiled=True)]
    unnamed x56 -> x74, local copies, waits for them, and re-layouts: 13.2 us -> 16.5 us
    ppermute x16, starting transfers between devices: 29 us -> 26.1 us  [shift(): lax.ppermute(value, axis, [(i, (i + steps) % count) for i in range(count)])]
    pallas_call x3 -> x4, Pallas kernels: 23.2 us -> 25.4 us  [the longest x1 16.5 us: on_device(): pl.pallas_call(final_body, grid=(4,), out_shape=[jax.ShapeDtypeStruct((2...]
  transfers between devices with their start and end apart: 19 -> 20, of which waited for: 6 -> 5; matrix products, arithmetic and copies ran while one was open for 6% -> 7% of each run, Pallas kernels for 15% -> 20%
where the time goes in v5:
time: 229 us; the launch traced here: 228 us
  Pallas kernels  74.1 us (32%)
  blocking collectives  54.7 us (24%)
  starting transfers between devices  39.5 us (17%)
  local copies, waits for them, and re-layouts  31.7 us (14%)
  waiting for transfers between devices  26.8 us (12%)
    all_to_all x2, blocking collectives, exchange(): return lax.all_to_all(parts, AXES, split_axis=0, concat_axis=0, tiled=True)  54.7 us
    ppermute x16, starting transfers between devices, shift(): lax.ppermute(value, axis, [(i, (i + steps) % count) for i in range(count)])  26.1 us
    ppermute x16, waiting for transfers between devices, shift(): lax.ppermute(value, axis, [(i, (i + steps) % count) for i in range(count)])  22.2 us
    unnamed x74, local copies, waits for them, and re-layouts  16.5 us
    pallas_call x1, Pallas kernels, on_device(): pl.pallas_call(final_body, grid=(4,), out_shape=[jax.ShapeDtypeStruct((2...  16.5 us
    pallas_call x1, Pallas kernels, on_device(): pl.pallas_call(encode_body, grid=(4,), out_shape=[pltpu.HBM((CHAN, GRID_R...  12.7 us
    all_to_all x1, starting transfers between devices, exchange(): return lax.all_to_all(parts, AXES, split_axis=0, concat_axis=0, tiled=True)  11.9 us
    pallas_call x1, Pallas kernels, on_device(): kernel_call(backward_body, [rows_bf16, rows_f32, rows_f32] + [halo] * 4,...  8.3 us
  transfers between devices with their start and end apart: 20, of which 5 were waited for; matrix products, arithmetic and copies ran while one was open for 7% of the time, Pallas kernels for 20%

profile of v5, /device:TPU:1, one launch (start us, length us, event | category | flops | bytes accessed | tf_op | source)
XLA Modules:
  0.0 227.7 jit_solution(11056200542309838204)
XLA Ops:
  0.6 6.3 %shard_map.138 = bf16[128,115,128]{2,1,0:T(8,128)(2,1)} custom-call(s32[1,128]{1,0:T(1,128)} %send.1, bf16[227,8192]{1,0:T(8,128)(2,1)} %bitcast.22), custom_call_target="tpu_custom_call" | custom-call | bytes 8388608 | tf_op jit(solution)/shard_map/pallas_call | solution.py:435
  6.9 11.9 %all-to-all-start = ((bf16[128,115,128]{2,1,0:T(8,128)(2,1)}), bf16[128,115,128]{2,1,0:T(8,128)(2,1)}, u32[]{:S(2)}, u32[]{:S(2)}) async-start(bf16[128,115,128]{2,1,0:T(8,128)(2,1)} %shard_map.138), calls=%async_computation | async-start | bytes 7864320 | tf_op jit(solution)/shard_map/all_to_all | solution.py:417
  18.8 0.1 copy.31.source
  18.9 2.6 %copy.25 = bf16[16,64,6,64]{3,2,1,0:T(8,128)(2,1)} copy(bf16[16,64,6,64]{3,1,2,0:T(8,128)(2,1)S(1)} %bitcast.24) | data formatting | bytes 1572864 | tf_op jit(solution)/shard_map/transpose | solution.py:449
  21.5 3.2 %reshape.31.coeffs = bf16[16,64,384]{2,1,0:T(8,128)(2,1)S(1)} reshape(bf16[16,64,6,64]{3,2,1,0:T(8,128)(2,1)} %copy.25) | data formatting | bytes 1572864 | tf_op jit(solution)/shard_map/reshape | solution.py:449
  24.8 0.9 slice_bitcast_fusion.1
  25.7 7.9 %shard_map.139 = (f32[1024,512]{1,0:T(8,128)S(1)}, bf16[4,64,512]{2,1,0:T(8,128)(2,1)}, bf16[4,64,512]{2,1,0:T(8,128)(2,1)}, bf16[4,64,512]{2,1,0:T(8,128)(2,1)}, bf16[4,64,512]{2,1,0:T(8,128)(2,1)}) custom-call(s32[16,6]{1,0:T(8,128)S(1)} %copy.31.source, bf16[1024,512]{1,0:T(8,128)(2,1)S(1)} %copy-done.10, bf16[512,512]{1,0:T(8,128)(2,1)S(1)} %get-tuple-element.91.up, ...), custom_call_target="tpu_custom_call" | custom-call | flops 2000000000 | bytes 8388608 | tf_op jit(solution)/shard_map/pallas_call | solution.py:451
  33.5 1.3 copy-done.21
  34.8 5.6 %collective-permute-start = (bf16[4,64,512]{2,1,0:T(8,128)(2,1)}, bf16[4,64,512]{2,1,0:T(8,128)(2,1)S(1)}, u32[]{:S(2)}, u32[]{:S(2)}) collective-permute-start(bf16[4,64,512]{2,1,0:T(8,128)(2,1)} %get-tuple-element.49), channel_id=1, source_target_pairs={{0,120},{8,0},{16,8},{24,16},{32,24},{40,32},{48,40},{56,48},{64,5... | collective-permute-start | bytes 786440 | tf_op jit(solution)/shard_map/ppermute | solution.py:401
  40.4 0.6 collective-permute-start.2
  41.0 1.1 collective-permute-start.3
  42.1 3.1 %copy.24 = bf16[16,64,8,64]{3,2,1,0:T(8,128)(2,1)} copy(bf16[16,64,8,64]{3,1,2,0:T(8,128)(2,1)S(1)} %bitcast.23) | data formatting | bytes 2097152 | tf_op jit(solution)/shard_map/transpose | solution.py:448
  45.3 3.2 %reshape.30.coeffs = bf16[16,64,512]{2,1,0:T(8,128)(2,1)S(1)} reshape(bf16[16,64,8,64]{3,2,1,0:T(8,128)(2,1)} %copy.24) | data formatting | bytes 2097152 | tf_op jit(solution)/shard_map/reshape | solution.py:448
  48.5 0.1 copy.28.source
  48.6 2.1 slice_bitcast_fusion
  50.7 17.1 %collective-permute-done.r0 = bf16[4,64,512]{2,1,0:T(8,128)(2,1)S(1)} collective-permute-done((bf16[4,64,512]{2,1,0:T(8,128)(2,1)}, bf16[4,64,512]{2,1,0:T(8,128)(2,1)S(1)}, u32[]{:S(2)}, u32[]{:S(2)}) %collective-permute-start) | collective-permute-done | bytes 262176 | tf_op jit(solution)/shard_map/ppermute | solution.py:401
  67.8 4.1 %collective-permute-done.1.r1 = bf16[4,64,512]{2,1,0:T(8,128)(2,1)S(1)} collective-permute-done((bf16[4,64,512]{2,1,0:T(8,128)(2,1)}, bf16[4,64,512]{2,1,0:T(8,128)(2,1)S(1)}, u32[]{:S(2)}, u32[]{:S(2)}) %collective-permute-start.1) | collective-permute-done | bytes 262176 | tf_op jit(solution)/shard_map/ppermute | solution.py:401
  71.9 0.0 collective-permute-done.3.r3
  71.9 0.0 copy-start.20
  71.9 1.2 copy-done.20
  73.1 12.7 %shard_map.140 = (bf16[227,8192]{1,0:T(8,128)(2,1)}, bf16[8192,512]{1,0:T(8,128)(2,1)}, bf16[8192,512]{1,0:T(8,128)(2,1)S(1)}, bf16[4,64,512]{2,1,0:T(8,128)(2,1)S(1)}) custom-call(s32[16,8]{1,0:T(8,128)S(1)} %copy.28.source, s32[1,4]{1,0:T(1,128)S(1)} %copy-done.9, bf16[128,115,128]{2,1,0:T(8,128)(2,1)} %all-to-all-done.packed, ...), custom_call_target="tpu_custom_call" | custom-call | flops 4000000000 | bytes 27262976 | tf_op jit(solution)/shard_map/pallas_call | solution.py:461
  85.9 0.1 collective-permute-start.4
  86.0 4.8 %collective-permute-start.5 = (bf16[4,64,512]{2,1,0:T(8,128)(2,1)S(1)}, bf16[4,64,512]{2,1,0:T(8,128)(2,1)S(1)}, u32[]{:S(2)}, u32[]{:S(2)}) collective-permute-start(bf16[4,64,512]{2,1,0:T(8,128)(2,1)S(1)} %get-tuple-element.57), channel_id=1, source_target_pairs={{0,120},{8,0},{16,8},{24,16},{32,24},{40,32},{48,40},{56,48},{64,5... | collective-permute-start | bytes 786440 | tf_op jit(solution)/shard_map/ppermute | solution.py:401
  90.7 2.8 %collective-permute-start.6 = (bf16[4,64,512]{2,1,0:T(8,128)(2,1)S(1)}, bf16[4,64,512]{2,1,0:T(8,128)(2,1)S(1)}, u32[]{:S(2)}, u32[]{:S(2)}) collective-permute-start(bf16[4,64,512]{2,1,0:T(8,128)(2,1)S(1)} %get-tuple-element.57), channel_id=1, source_target_pairs={{0,1},{1,2},{2,3},{3,4},{4,5},{5,6},{6,7},{7,0},{8,9},{9,10},{10,1... | collective-permute-start | bytes 786440 | tf_op jit(solution)/shard_map/ppermute | solution.py:401
  93.6 4.7 %shard_map.141 = (bf16[1024,512]{1,0:T(8,128)(2,1)S(1)}, bf16[1024,512]{1,0:T(8,128)(2,1)S(1)}, bf16[1024,512]{1,0:T(8,128)(2,1)S(1)}) custom-call(s32[16,8]{1,0:T(8,128)S(1)} %copy.28.source, bf16[8192,512]{1,0:T(8,128)(2,1)S(1)} %get-tuple-element.55.embedded, bf16[16,64,512]{2,1,0:T(8,128)(2,1)S(1)} %reshape.30.coeffs, ...), custom_call_target="tpu_custom_call" | custom-call | flops 2000000000 | bytes 12582912 | tf_op jit(solution)/shard_map/pallas_call | solution.py:488
  98.3 0.0 collective-permute-done.4.n0
  98.3 0.0 collective-permute-done.6.n2
  98.3 1.0 collective-permute-done.7.n3
  99.3 6.2 %shard_map.142 = (bf16[1024,512]{1,0:T(8,128)(2,1)S(1)}, bf16[1024,512]{1,0:T(8,128)(2,1)S(1)}, bf16[1024,512]{1,0:T(8,128)(2,1)S(1)}, bf16[1024,512]{1,0:T(8,128)(2,1)S(1)}, bf16[4,64,512]{2,1,0:T(8,128)(2,1)}) custom-call(s32[16,6]{1,0:T(8,128)S(1)} %copy.31.source, s32[1,4]{1,0:T(1,128)S(1)} %copy-done.9, bf16[1024,512]{1,0:T(8,128)(2,1)S(1)} %get-tuple-element.56.sent, ...), custom_call_target="tpu_custom_call" | custom-call | flops 2000000000 | bytes 10485760 | tf_op jit(solution)/shard_map/pallas_call | solution.py:492
  105.5 1.0 copy-done.23
  106.5 1.0 copy-done.25
  107.5 1.0 copy-done.27
  108.4 1.0 copy-done.29
  109.4 0.8 collective-permute-start.10
  110.2 0.0 collective-permute-start.11
  110.2 0.0 collective-permute-start.8
  110.2 4.8 %collective-permute-start.9 = (bf16[4,64,512]{2,1,0:T(8,128)(2,1)}, bf16[4,64,512]{2,1,0:T(8,128)(2,1)}, u32[]{:S(2)}, u32[]{:S(2)}) collective-permute-start(bf16[4,64,512]{2,1,0:T(8,128)(2,1)} %get-tuple-element.61), channel_id=1, source_target_pairs={{0,120},{8,0},{16,8},{24,16},{32,24},{40,32},{48,40},{56,48},{64,5... | collective-permute-start | bytes 786440 | tf_op jit(solution)/shard_map/ppermute | solution.py:401
  114.9 1.0 copy-done.6
  116.0 1.0 copy-done.8
  117.0 1.2 copy-done.11
  118.3 0.9 copy-done.13
  119.2 0.9 copy-done.15
  120.2 0.9 copy-done.17
  121.1 0.9 copy-done.19
  122.1 1.6 copy-done.22
  123.6 1.2 copy-done.24
  124.9 8.3 %shard_map.143 = (bf16[1024,512]{1,0:T(8,128)(2,1)S(1)}, f32[1024,512]{1,0:T(8,128)S(1)}, f32[1024,512]{1,0:T(8,128)S(1)}, bf16[4,64,512]{2,1,0:T(8,128)(2,1)S(1...) custom-call(s32[16,6]{1,0:T(8,128)S(1)} %copy.31.source, ...), custom_call_target="tpu_custom_call" | custom-call | flops 2000000000 | bytes 16777216 | tf_op jit(solution)/shard_map/pallas_call | solution.py:498
  133.2 1.1 collective-permute-start.12
  134.3 0.0 collective-permute-done.10.n2
  134.3 0.5 collective-permute-start.13
  134.7 0.0 collective-permute-done.11.n3
  134.7 4.0 %collective-permute-start.14 = (bf16[4,64,512]{2,1,0:T(8,128)(2,1)S(1)}, bf16[4,64,512]{2,1,0:T(8,128)(2,1)S(1)}, u32[]{:S(2)}, u32[]{:S(2)}) collective-permute-start(bf16[4,64,512]{2,1,0:T(8,128)(2,1)S(1)} %get-tuple-element.76), channel_id=1, source_target_pairs={{0,7},{1,0},{2,1},{3,2},{4,3},{5,4},{6,5},{7,6},{8,15},{9,8},{10,9... | collective-permute-start | bytes 786440 | tf_op jit(solution)/shard_map/ppermute | solution.py:401
  138.8 8.2 %shard_map.144 = (bf16[1024,512]{1,0:T(8,128)(2,1)}, bf16[3072,128]{1,0:T(8,128)(2,1)S(1)}, bf16[3072,128]{1,0:T(8,128)(2,1)S(1)}) custom-call(s32[1]{0:T(128)} %bitcast.odd, s32[16,6]{1,0:T(8,128)S(1)} %copy.31.source, bf16[1024,512]{1,0:T(8,128)(2,1)S(1)} %copy-done.30, bf16[4,64,512]{2,1,0:T(8,128)(2,1)} %collective-permute-done.8.n0, ...), custom_call_target="tpu_custom_call" | custom-call | flops 4000000000 | bytes 14680064 | tf_op jit(solution)/shard_map/pallas_call | solution.py:504
  147.0 0.5 collective-permute-start.17
  147.5 16.5 %shard_map.145 = (bf16[2048,128]{1,0:T(8,128)(2,1)S(1)}, bf16[2048,128]{1,0:T(8,128)(2,1)S(1)}) custom-call(s32[1]{0:T(128)} %bitcast.odd, s32[16,8]{1,0:T(8,128)S(1)} %copy.28.source, s32[1,4]{1,0:T(1,128)S(1)} %copy-done.9, f32[1024,512]{1,0:T(8,128)S(1)} %get-tuple-element.73.own, bf16[4,64,512]{2,1,0:T(8,128)(2,1)S(1)} %collective-permute-done.12.r0, ...), custom_call_target="tpu_custom_call" | custom-call | flops 4000000000 | bytes 25165824 | tf_op jit(solution)/shard_map/pallas_call | solution.py:514
  164.1 0.1 collective-permute-start.16
  164.2 1.9 collective-permute-done.16
  166.1 0.4 shard_map.146
  166.5 28.5 %all_to_all.15.parts = bf16[128,40,128]{2,1,0:T(8,128)(2,1)S(1)} all-to-all(bf16[128,40,128]{2,1,0:T(8,128)(2,1)S(1)} %shard_map.146), channel_id=1, replica_groups=mesh['wide'=16,'narrow'=8] {'wide','narrow'}, dimensions={0} | all-to-all | bytes 2621440 | tf_op jit(solution)/shard_map/all_to_all | solution.py:417
  195.0 0.3 shard_map.147
  195.3 26.2 %all_to_all.16.own = bf16[128,40,128]{2,1,0:T(8,128)(2,1)S(1)} all-to-all(bf16[128,40,128]{2,1,0:T(8,128)(2,1)S(1)} %shard_map.147), channel_id=1, replica_groups=mesh['wide'=16,'narrow'=8] {'wide','narrow'}, dimensions={0} | all-to-all | bytes 2621440 | tf_op jit(solution)/shard_map/all_to_all | solution.py:417
  221.5 0.9 collective-permute-start.18
  222.4 2.7 %collective-permute-done.18.other = bf16[128,40,128]{2,1,0:T(8,128)(2,1)S(1)} collective-permute-done((bf16[128,40,128]{2,1,0:T(8,128)(2,1)S(1)}, bf16[128,40,128]{2,1,0:T(8,128)(2,1)S(1)}, u32[]{:S(2)}, u32[]{:S(2)}) %collective-permute-start.18) | collective-permute-done | bytes 1310752 | tf_op jit(solution)/shard_map/ppermute | solution.py:413
  225.1 2.7 %shard_map.148 = (f32[227,512]{1,0:T(8,128)}, f32[2,512,512]{2,1,0:T(8,128)}, f32[2,512,512]{2,1,0:T(8,128)}) custom-call(s32[1]{0:T(128)} %bitcast.odd, bf16[128,40,128]{2,1,0:T(8,128)(2,1)S(1)} %all_to_all.16.own, bf16[128,40,128]{2,1,0:T(8,128)(2,1)S(1)} %collective-permute-done.18.other), custom_call_target="tpu_custom_call" | custom-call | bytes 7340032 | tf_op jit(solution)/shard_map/pallas_call | solution.py:545
  (69 shorter events, 0.1 us)
Async XLA Ops:
  6.9 11.9 %copy-start.34 = (s32[16,6]{0,1:T(8,128)S(1)}, s32[16,6]{0,1:T(8,128)}, u32[]{:S(2)}) copy-start(s32[16,6]{0,1:T(8,128)} %param.16) | copy-start | bytes 1156
  6.9 12.0 %copy-start.32 = (bf16[16,6,64,64]{3,2,1,0:T(8,128)(2,1)S(1)}, bf16[16,6,64,64]{3,2,1,0:T(8,128)(2,1)}, u32[]{:S(2)}) copy-start(bf16[16,6,64,64]{3,2,1,0:T(8,128)(2,1)} %param.17) | copy-start | bytes 2359300
  6.9 65.0 %all-to-all-start = ((bf16[128,115,128]{2,1,0:T(8,128)(2,1)}), bf16[128,115,128]{2,1,0:T(8,128)(2,1)}, u32[]{:S(2)}, u32[]{:S(2)}) async-start(bf16[128,115,128]{2,1,0:T(8,128)(2,1)} %shard_map.138), calls=%async_computation | async-start | bytes 7864320 | tf_op jit(solution)/shard_map/all_to_all | solution.py:417
  21.5 3.2 %copy-start.33 = (bf16[2,512,512]{2,1,0:T(8,128)(2,1)S(1)}, bf16[2,512,512]{2,1,0:T(8,128)(2,1)}, u32[]{:S(2)}) copy-start(bf16[2,512,512]{2,1,0:T(8,128)(2,1)} %param.20) | copy-start | bytes 3145732
  21.5 4.1 %copy-start.10 = (bf16[1024,512]{1,0:T(8,128)(2,1)S(1)}, bf16[1024,512]{1,0:T(8,128)(2,1)}, u32[]{:S(2)}) copy-start(bf16[1024,512]{1,0:T(8,128)(2,1)} %cot.2) | copy-start | bytes 3145732
  25.6 7.9 %copy-start.3 = (bf16[512,512]{1,0:T(8,128)(2,1)}, bf16[512,512]{1,0:T(8,128)(2,1)S(1)}, u32[]{:S(2)}) copy-start(bf16[512,512]{1,0:T(8,128)(2,1)S(1)} %get-tuple-element.91.up) | copy-start | bytes 1572868
  25.6 16.5 %copy-start.31 = (bf16[16,8,64,64]{3,2,1,0:T(8,128)(2,1)S(1)}, bf16[16,8,64,64]{3,2,1,0:T(8,128)(2,1)}, u32[]{:S(2)}) copy-start(bf16[16,8,64,64]{3,2,1,0:T(8,128)(2,1)} %param.15) | copy-start | bytes 3145732
  33.5 1.3 copy-start.21
  34.8 32.9 %collective-permute-start = (bf16[4,64,512]{2,1,0:T(8,128)(2,1)}, bf16[4,64,512]{2,1,0:T(8,128)(2,1)S(1)}, u32[]{:S(2)}, u32[]{:S(2)}) collective-permute-start(bf16[4,64,512]{2,1,0:T(8,128)(2,1)} %get-tuple-element.49), channel_id=1, source_target_pairs={{0,120},{8,0},{16,8},{24,16},{32,24},{40,32},{48,40},{56,48},{64,5... | collective-permute-start | bytes 786440 | tf_op jit(solution)/shard_map/ppermute | solution.py:401
  40.4 31.5 %collective-permute-start.1 = (bf16[4,64,512]{2,1,0:T(8,128)(2,1)}, bf16[4,64,512]{2,1,0:T(8,128)(2,1)S(1)}, u32[]{:S(2)}, u32[]{:S(2)}) collective-permute-start(bf16[4,64,512]{2,1,0:T(8,128)(2,1)} %get-tuple-element.50), channel_id=1, source_target_pairs={{0,8},{8,16},{16,24},{24,32},{32,40},{40,48},{48,56},{56,64},{64,7... | collective-permute-start | bytes 786440 | tf_op jit(solution)/shard_map/ppermute | solution.py:401
  40.4 31.5 %collective-permute-start.2 = (bf16[4,64,512]{2,1,0:T(8,128)(2,1)}, bf16[4,64,512]{2,1,0:T(8,128)(2,1)S(1)}, u32[]{:S(2)}, u32[]{:S(2)}) collective-permute-start(bf16[4,64,512]{2,1,0:T(8,128)(2,1)} %get-tuple-element.51), channel_id=1, source_target_pairs={{0,7},{1,0},{2,1},{3,2},{4,3},{5,4},{6,5},{7,6},{8,15},{9,8},{10,9... | collective-permute-start | bytes 786440 | tf_op jit(solution)/shard_map/ppermute | solution.py:401
  41.0 30.8 %collective-permute-start.3 = (bf16[4,64,512]{2,1,0:T(8,128)(2,1)}, bf16[4,64,512]{2,1,0:T(8,128)(2,1)S(1)}, u32[]{:S(2)}, u32[]{:S(2)}) collective-permute-start(bf16[4,64,512]{2,1,0:T(8,128)(2,1)} %get-tuple-element.52), channel_id=1, source_target_pairs={{0,1},{1,2},{2,3},{3,4},{4,5},{5,6},{6,7},{7,0},{8,9},{9,10},{10,1... | collective-permute-start | bytes 786440 | tf_op jit(solution)/shard_map/ppermute | solution.py:401
  45.3 3.2 %copy-start.35 = (s32[16,8]{0,1:T(8,128)S(1)}, s32[16,8]{0,1:T(8,128)}, u32[]{:S(2)}) copy-start(s32[16,8]{0,1:T(8,128)} %param.14) | copy-start | bytes 1540
  45.3 26.6 %copy-start.9 = (s32[1,4]{1,0:T(1,128)S(1)}, s32[1,4]{1,0:T(1,128)}, u32[]{:S(2)}) copy-start(s32[1,4]{1,0:T(1,128)} %shown.7) | copy-start | bytes 52
  67.8 18.1 %copy-start.12 = (bf16[4,64,512]{2,1,0:T(8,128)(2,1)}, bf16[4,64,512]{2,1,0:T(8,128)(2,1)S(1)}, u32[]{:S(2)}) copy-start(bf16[4,64,512]{2,1,0:T(8,128)(2,1)S(1)} %collective-permute-done.r0) | copy-start | bytes 786436
  71.9 14.0 %copy-start.14 = (bf16[4,64,512]{2,1,0:T(8,128)(2,1)}, bf16[4,64,512]{2,1,0:T(8,128)(2,1)S(1)}, u32[]{:S(2)}) copy-start(bf16[4,64,512]{2,1,0:T(8,128)(2,1)S(1)} %collective-permute-done.1.r1) | copy-start | bytes 786436
  71.9 14.0 %copy-start.16 = (bf16[4,64,512]{2,1,0:T(8,128)(2,1)}, bf16[4,64,512]{2,1,0:T(8,128)(2,1)S(1)}, u32[]{:S(2)}) copy-start(bf16[4,64,512]{2,1,0:T(8,128)(2,1)S(1)} %collective-permute-done.2.r2) | copy-start | bytes 786436
  71.9 14.0 %copy-start.18 = (bf16[4,64,512]{2,1,0:T(8,128)(2,1)}, bf16[4,64,512]{2,1,0:T(8,128)(2,1)S(1)}, u32[]{:S(2)}) copy-start(bf16[4,64,512]{2,1,0:T(8,128)(2,1)S(1)} %collective-permute-done.3.r3) | copy-start | bytes 786436
  71.9 1.2 copy-start.20
  85.9 12.4 %collective-permute-start.4 = (bf16[4,64,512]{2,1,0:T(8,128)(2,1)S(1)}, bf16[4,64,512]{2,1,0:T(8,128)(2,1)S(1)}, u32[]{:S(2)}, u32[]{:S(2)}) collective-permute-start(bf16[4,64,512]{2,1,0:T(8,128)(2,1)S(1)} %get-tuple-element.57), channel_id=1, source_target_pairs={{0,8},{8,16},{16,24},{24,32},{32,40},{40,48},{48,56},{56,64},{64,7... | collective-permute-start | bytes 786440 | tf_op jit(solution)/shard_map/ppermute | solution.py:401
  86.0 12.4 %collective-permute-start.5 = (bf16[4,64,512]{2,1,0:T(8,128)(2,1)S(1)}, bf16[4,64,512]{2,1,0:T(8,128)(2,1)S(1)}, u32[]{:S(2)}, u32[]{:S(2)}) collective-permute-start(bf16[4,64,512]{2,1,0:T(8,128)(2,1)S(1)} %get-tuple-element.57), channel_id=1, source_target_pairs={{0,120},{8,0},{16,8},{24,16},{32,24},{40,32},{48,40},{56,48},{64,5... | collective-permute-start | bytes 786440 | tf_op jit(solution)/shard_map/ppermute | solution.py:401
  90.7 7.6 %collective-permute-start.6 = (bf16[4,64,512]{2,1,0:T(8,128)(2,1)S(1)}, bf16[4,64,512]{2,1,0:T(8,128)(2,1)S(1)}, u32[]{:S(2)}, u32[]{:S(2)}) collective-permute-start(bf16[4,64,512]{2,1,0:T(8,128)(2,1)S(1)} %get-tuple-element.57), channel_id=1, source_target_pairs={{0,1},{1,2},{2,3},{3,4},{4,5},{5,6},{6,7},{7,0},{8,9},{9,10},{10,1... | collective-permute-start | bytes 786440 | tf_op jit(solution)/shard_map/ppermute | solution.py:401
  93.5 5.8 %collective-permute-start.7 = (bf16[4,64,512]{2,1,0:T(8,128)(2,1)S(1)}, bf16[4,64,512]{2,1,0:T(8,128)(2,1)S(1)}, u32[]{:S(2)}, u32[]{:S(2)}) collective-permute-start(bf16[4,64,512]{2,1,0:T(8,128)(2,1)S(1)} %get-tuple-element.57), channel_id=1, source_target_pairs={{0,7},{1,0},{2,1},{3,2},{4,3},{5,4},{6,5},{7,6},{8,15},{9,8},{10,9... | collective-permute-start | bytes 786440 | tf_op jit(solution)/shard_map/ppermute | solution.py:401
  93.5 5.8 %copy-start.5 = (bf16[512,512]{1,0:T(8,128)(2,1)S(1)}, bf16[512,512]{1,0:T(8,128)(2,1)}, u32[]{:S(2)}) copy-start(bf16[512,512]{1,0:T(8,128)(2,1)} %get-tuple-element.90.up) | copy-start | bytes 1572868
  93.5 5.8 %copy-start.7 = (bf16[512,512]{1,0:T(8,128)(2,1)S(1)}, bf16[512,512]{1,0:T(8,128)(2,1)}, u32[]{:S(2)}) copy-start(bf16[512,512]{1,0:T(8,128)(2,1)} %get-tuple-element.88.message) | copy-start | bytes 1572868
  98.3 7.2 %copy-start.1 = (bf16[1024,512]{1,0:T(8,128)(2,1)}, bf16[1024,512]{1,0:T(8,128)(2,1)S(1)}, u32[]{:S(2)}) copy-start(bf16[1024,512]{1,0:T(8,128)(2,1)S(1)} %get-tuple-element.78.slope_m) | copy-start | bytes 3145732
  105.5 1.0 copy-start.23
  106.5 1.0 copy-start.25
  107.5 1.0 copy-start.27
  108.4 1.0 copy-start.29
  109.4 24.9 %collective-permute-start.10 = (bf16[4,64,512]{2,1,0:T(8,128)(2,1)}, bf16[4,64,512]{2,1,0:T(8,128)(2,1)}, u32[]{:S(2)}, u32[]{:S(2)}) collective-permute-start(bf16[4,64,512]{2,1,0:T(8,128)(2,1)} %get-tuple-element.61), channel_id=1, source_target_pairs={{0,1},{1,2},{2,3},{3,4},{4,5},{5,6},{6,7},{7,0},{8,9},{9,10},{10,1... | collective-permute-start | bytes 786440 | tf_op jit(solution)/shard_map/ppermute | solution.py:401
  110.2 24.6 %collective-permute-start.11 = (bf16[4,64,512]{2,1,0:T(8,128)(2,1)}, bf16[4,64,512]{2,1,0:T(8,128)(2,1)}, u32[]{:S(2)}, u32[]{:S(2)}) collective-permute-start(bf16[4,64,512]{2,1,0:T(8,128)(2,1)} %get-tuple-element.61), channel_id=1, source_target_pairs={{0,7},{1,0},{2,1},{3,2},{4,3},{5,4},{6,5},{7,6},{8,15},{9,8},{10,9... | collective-permute-start | bytes 786440 | tf_op jit(solution)/shard_map/ppermute | solution.py:401
  110.2 28.6 %collective-permute-start.8 = (bf16[4,64,512]{2,1,0:T(8,128)(2,1)}, bf16[4,64,512]{2,1,0:T(8,128)(2,1)}, u32[]{:S(2)}, u32[]{:S(2)}) collective-permute-start(bf16[4,64,512]{2,1,0:T(8,128)(2,1)} %get-tuple-element.61), channel_id=1, source_target_pairs={{0,8},{8,16},{16,24},{24,32},{32,40},{40,48},{48,56},{56,64},{64,7... | collective-permute-start | bytes 786440 | tf_op jit(solution)/shard_map/ppermute | solution.py:401
  110.2 28.6 %collective-permute-start.9 = (bf16[4,64,512]{2,1,0:T(8,128)(2,1)}, bf16[4,64,512]{2,1,0:T(8,128)(2,1)}, u32[]{:S(2)}, u32[]{:S(2)}) collective-permute-start(bf16[4,64,512]{2,1,0:T(8,128)(2,1)} %get-tuple-element.61), channel_id=1, source_target_pairs={{0,120},{8,0},{16,8},{24,16},{32,24},{40,32},{48,40},{56,48},{64,5... | collective-permute-start | bytes 786440 | tf_op jit(solution)/shard_map/ppermute | solution.py:401
  114.9 1.0 copy-start.6
  116.0 1.0 copy-start.8
  117.0 1.2 copy-start.11
  118.3 0.9 copy-start.13
  119.2 0.9 copy-start.15
  120.2 0.9 copy-start.17
  121.1 0.9 copy-start.19
  122.1 1.6 copy-start.22
  123.6 1.2 copy-start.24
  124.9 13.9 %copy-start.4 = (bf16[512,512]{1,0:T(8,128)(2,1)S(1)}, bf16[512,512]{1,0:T(8,128)(2,1)}, u32[]{:S(2)}) copy-start(bf16[512,512]{1,0:T(8,128)(2,1)} %copy-done.3) | copy-start | bytes 1572868
  124.9 13.9 %copy-start.26 = (bf16[1024,512]{1,0:T(8,128)(2,1)S(1)}, bf16[1024,512]{1,0:T(8,128)(2,1)}, u32[]{:S(2)}) copy-start(bf16[1024,512]{1,0:T(8,128)(2,1)} %copy-done.25) | copy-start | bytes 3145732
  124.9 13.9 %copy-start.28 = (bf16[1024,512]{1,0:T(8,128)(2,1)S(1)}, bf16[1024,512]{1,0:T(8,128)(2,1)}, u32[]{:S(2)}) copy-start(bf16[1024,512]{1,0:T(8,128)(2,1)} %copy-done.27) | copy-start | bytes 3145732
  124.9 13.9 %copy-start.30 = (bf16[1024,512]{1,0:T(8,128)(2,1)S(1)}, bf16[1024,512]{1,0:T(8,128)(2,1)}, u32[]{:S(2)}) copy-start(bf16[1024,512]{1,0:T(8,128)(2,1)} %copy-done.29) | copy-start | bytes 3145732
  133.2 14.3 %collective-permute-start.12 = (bf16[4,64,512]{2,1,0:T(8,128)(2,1)S(1)}, bf16[4,64,512]{2,1,0:T(8,128)(2,1)S(1)}, u32[]{:S(2)}, u32[]{:S(2)}) collective-permute-start(bf16[4,64,512]{2,1,0:T(8,128)(2,1)S(1)} %get-tuple-element.74), channel_id=1, source_target_pairs={{0,120},{8,0},{16,8},{24,16},{32,24},{40,32},{48,40},{56,48},{64,5... | collective-permute-start | bytes 786440 | tf_op jit(solution)/shard_map/ppermute | solution.py:401
  134.3 13.2 %collective-permute-start.13 = (bf16[4,64,512]{2,1,0:T(8,128)(2,1)S(1)}, bf16[4,64,512]{2,1,0:T(8,128)(2,1)S(1)}, u32[]{:S(2)}, u32[]{:S(2)}) collective-permute-start(bf16[4,64,512]{2,1,0:T(8,128)(2,1)S(1)} %get-tuple-element.75), channel_id=1, source_target_pairs={{0,8},{8,16},{16,24},{24,32},{32,40},{40,48},{48,56},{56,64},{64,7... | collective-permute-start | bytes 786440 | tf_op jit(solution)/shard_map/ppermute | solution.py:401
  134.7 12.8 %collective-permute-start.14 = (bf16[4,64,512]{2,1,0:T(8,128)(2,1)S(1)}, bf16[4,64,512]{2,1,0:T(8,128)(2,1)S(1)}, u32[]{:S(2)}, u32[]{:S(2)}) collective-permute-start(bf16[4,64,512]{2,1,0:T(8,128)(2,1)S(1)} %get-tuple-element.76), channel_id=1, source_target_pairs={{0,7},{1,0},{2,1},{3,2},{4,3},{5,4},{6,5},{7,6},{8,15},{9,8},{10,9... | collective-permute-start | bytes 786440 | tf_op jit(solution)/shard_map/ppermute | solution.py:401
  138.8 8.8 %collective-permute-start.15 = (bf16[4,64,512]{2,1,0:T(8,128)(2,1)S(1)}, bf16[4,64,512]{2,1,0:T(8,128)(2,1)S(1)}, u32[]{:S(2)}, u32[]{:S(2)}) collective-permute-start(bf16[4,64,512]{2,1,0:T(8,128)(2,1)S(1)} %get-tuple-element.77), channel_id=1, source_target_pairs={{0,1},{1,2},{2,3},{3,4},{4,5},{5,6},{6,7},{7,0},{8,9},{9,10},{10,1... | collective-permute-start | bytes 786440 | tf_op jit(solution)/shard_map/ppermute | solution.py:401
  138.8 8.7 %copy-start = (bf16[227,8192]{1,0:T(8,128)(2,1)S(1)}, bf16[227,8192]{1,0:T(8,128)(2,1)}, u32[]{:S(2)}) copy-start(bf16[227,8192]{1,0:T(8,128)(2,1)} %get-tuple-element.80.points) | copy-start | bytes 11157508
  138.8 8.7 %copy-start.2 = (bf16[1024,512]{1,0:T(8,128)(2,1)S(1)}, bf16[1024,512]{1,0:T(8,128)(2,1)}, u32[]{:S(2)}) copy-start(bf16[1024,512]{1,0:T(8,128)(2,1)} %copy-done.1) | copy-start | bytes 3145732
  147.0 19.1 %collective-permute-start.17 = (bf16[3072,128]{1,0:T(8,128)(2,1)S(1)}, bf16[3072,128]{1,0:T(8,128)(2,1)S(1)}, u32[]{:S(2)}, u32[]{:S(2)}) collective-permute-start(bf16[3072,128]{1,0:T(8,128)(2,1)S(1)} %get-tuple-element.84), channel_id=1, source_target_pairs={{0,1},{1,0},{2,3},{3,2},{4,5},{5,4},{6,7},{7,6},{8,9},{9,8},{10,11... | collective-permute-start | bytes 2359304 | tf_op jit(solution)/shard_map/ppermute | solution.py:413
  164.1 2.0 collective-permute-start.16
  221.5 3.5 %collective-permute-start.18 = (bf16[128,40,128]{2,1,0:T(8,128)(2,1)S(1)}, bf16[128,40,128]{2,1,0:T(8,128)(2,1)S(1)}, u32[]{:S(2)}, u32[]{:S(2)}) collective-permute-start(bf16[128,40,128]{2,1,0:T(8,128)(2,1)S(1)} %all_to_all.16.own), channel_id=1, source_target_pairs={{0,1},{1,0},{2,3},{3,2},{4,5},{5,4},{6,7},{7,6},{8,9},{9,8},{10,11... | collective-permute-start | bytes 3932168 | tf_op jit(solution)/shard_map/ppermute | solution.py:413

commit v6 on v5

--- a/solution.py
+++ b/solution.py
@@ -3,7 +3,7 @@
 from jax import lax
 from jax.experimental import pallas as pl
 from jax.experimental.pallas import tpu as pltpu
-from jax.sharding import PartitionSpec as P
+from jax.sharding import Mesh, PartitionSpec as P
 
 CHAN = 227
 WIDTH = 512
@@ -19,12 +19,16 @@
 SPLIT = 112
 PACKED = CHAN - SPLIT
 DEVICES = 128
+CHIPS = DEVICES // 2
 COLUMNS = WIDTH // 2
 SLABS = 2 * WIDTH
-EARLY = 3 * SLABS // DEVICES
-LATE = 2 * SLABS // DEVICES
-PART = LATE + EARLY
-AXES = ("wide", "narrow")
+TAIL = 256
+EARLY = 3 * SLABS // CHIPS
+LATE = (SLABS + 2 * TAIL) // CHIPS
+PART = EARLY + LATE
+NARROW = ("x", "core")
+AXES = ("wide", "x", "core")
+CHIP_AXES = ("wide", "x")
 BF16 = jnp.bfloat16
 F32 = jnp.float32
 MIB = 1 << 20
@@ -115,7 +119,7 @@
             table[at] = table[at] + parts[k * BLOCK : (k + 1) * BLOCK]
         return carry
 
-    lax.fori_loop(0, MESH_BLOCKS, one, 0)
+    lax.fori_loop(0, MESH_BLOCKS, one, 0, unroll=2)
 
 
 def gather_mix(coeffs, pick, slots, b):
@@ -146,7 +150,7 @@
         lowered[rows, :] = times(cot[rows, :], up[...], 1, 1).astype(BF16)
         return carry
 
-    lax.fori_loop(0, MESH_ROWS // 256, step, 0)
+    lax.fori_loop(0, MESH_ROWS // 256, step, 0, unroll=2)
     scatter_back(coeffs, lowered, source, table, M_SLOTS, EXTENDED)
     write_halo(table, own, (h0, h1, h2, h3))
 
@@ -174,7 +178,7 @@
         slope[rows, :] = (s + e * (1.0 - s)).astype(BF16)
         return carry
 
-    lax.fori_loop(0, 4, embed, 0, unroll=2)
+    lax.fori_loop(0, 4, embed, 0, unroll=4)
 
     @pl.when(step == 3)
     def _():
@@ -192,7 +196,7 @@
         mesh[rows_of(b), :] = gather_mix(coeffs, pick, G_SLOTS, b).astype(BF16)
         return carry
 
-    lax.fori_loop(0, MESH_BLOCKS, mix, 0, unroll=2)
+    lax.fori_loop(0, MESH_BLOCKS, mix, 0, unroll=4)
 
     def talk(c, carry):
         rows = chunk(c, 256)
@@ -220,7 +224,7 @@
         aggregate[rows_of(b), :] = gather_mix(coeffs, pick, M_SLOTS, b).astype(BF16)
         return carry
 
-    lax.fori_loop(0, MESH_BLOCKS, mix, 0, unroll=2)
+    lax.fori_loop(0, MESH_BLOCKS, mix, 0, unroll=4)
 
 
 def forward_body(
@@ -241,7 +245,7 @@
         slope_m[rows, :] = (s + e * (1.0 - s)).astype(BF16)
         return carry
 
-    lax.fori_loop(0, MESH_ROWS // 256, step, 0)
+    lax.fori_loop(0, MESH_ROWS // 256, step, 0, unroll=2)
     for h in range(SHOWN):
         mine[h] = sent_1[rows_of(shown[0, h]), :]
 
@@ -262,7 +266,7 @@
         lowered[rows, :] = times(g.astype(BF16), up[...], 1, 1).astype(BF16)
         return carry
 
-    lax.fori_loop(0, MESH_ROWS // 256, step, 0)
+    lax.fori_loop(0, MESH_ROWS // 256, step, 0, unroll=2)
     scatter_back(coeffs, lowered, source, table, M_SLOTS, EXTENDED)
     write_halo(table, own_0, (h0, h1, h2, h3))
 
@@ -270,7 +274,7 @@
 def write_slabs(odd, keep, give, first, values):
     def write(out, column):
         for c in range(2):
-            at = first + c * WIDTH
+            at = first + c * values.shape[0]
             slab = values[:, column + c * 128 : column + (c + 1) * 128]
             out[at : at + values.shape[0], :] = slab.astype(BF16)
 
@@ -300,7 +304,7 @@
         mesh_out[rows, :] = (mesh[rows, :].astype(F32) + update).astype(BF16)
         return carry
 
-    lax.fori_loop(0, MESH_ROWS // 256, step, 0)
+    lax.fori_loop(0, MESH_ROWS // 256, step, 0, unroll=2)
     write_slabs(odd, keep, give, 2 * SLABS, times(aggregate[...], cot[...], 0, 0))
 
 
@@ -322,7 +326,7 @@
             lowered[rows, :] = (grad_1[rows, :] + times(gp, message[...], 1, 1)).astype(BF16)
             return carry
 
-        lax.fori_loop(0, MESH_ROWS // 256, step, 0)
+        lax.fori_loop(0, MESH_ROWS // 256, step, 0, unroll=2)
         scatter_back(coeffs, lowered, source, table, G_SLOTS, GRID_BLOCKS)
         write_slabs(odd, keep, give, 0, times(mesh[...], grad_pre[...], 0, 0))
         total[...] = jnp.zeros_like(total)
@@ -334,56 +338,54 @@
         total[0:CHAN, :] = total[0:CHAN, :] + times(points[:, rows], grad)
         return carry
 
-    lax.fori_loop(0, 4, grid_step, 0)
+    lax.fori_loop(0, 4, grid_step, 0, unroll=4)
 
     @pl.when(c == 3)
     def _():
         write_slabs(odd, keep, give, SLABS, total[...])
 
 
-def pair_body(late, late_other, early, early_other, out):
+def pair_body(early, early_other, late, late_other, out):
     def one(i, carry):
-        out[i, 0:LATE, :] = (late[i].astype(F32) + late_other[i].astype(F32)).astype(BF16)
-        out[i, LATE:PART, :] = (early[i].astype(F32) + early_other[i].astype(F32)).astype(BF16)
-        return carry
-
-    lax.fori_loop(0, DEVICES, one, 0, unroll=8)
+        out[i, 0:EARLY, :] = (early[i].astype(F32) + early_other[i].astype(F32)).astype(BF16)
+        out[i, EARLY:PART, :] = (late[i].astype(F32) + late_other[i].astype(F32)).astype(BF16)
+        return carry
+
+    lax.fori_loop(0, CHIPS, one, 0, unroll=8)
 
 
 def sum_body(parts, out):
-    zero = jnp.zeros((PART, 128), F32)
-
     def add(i, carry):
-        return carry[0] + parts[2 * i].astype(F32), carry[1] + parts[2 * i + 1].astype(F32)
-
-    even, odd = lax.fori_loop(0, DEVICES // 2, add, (zero, zero), unroll=8)
-    even, odd = even.astype(BF16), odd.astype(BF16)
+        return carry + parts[i].astype(F32)
+
+    total = lax.fori_loop(0, CHIPS, add, jnp.zeros((PART, 128), F32), unroll=8).astype(BF16)
 
     def one(i, carry):
-        out[2 * i] = even
-        out[2 * i + 1] = odd
-        return carry
-
-    lax.fori_loop(0, DEVICES // 2, one, 0, unroll=8)
+        out[i] = total
+        return carry
+
+    lax.fori_loop(0, CHIPS, one, 0, unroll=8)
 
 
 def unpack_body(odd, own, other, d_embed, ms_grad, up_grad):
     def place(values, outs, column, first):
         begin = 0
-        for out in outs:
+        for out, rows in outs:
             for c in range(2):
                 low = max(first, begin)
                 high = min(first + values.shape[0], begin + out.shape[0])
                 if low < high:
                     at = column + c * 128
                     out[low - begin : high - begin, at : at + 128] = values[low - first : high - first]
-                begin += WIDTH
+                begin += rows
 
     def unpack(parts, column):
-        for q in range(DEVICES):
+        early = ((up_grad.at[0], WIDTH), (ms_grad.at[1], WIDTH), (up_grad.at[1], WIDTH))
+        late = ((ms_grad.at[0], WIDTH), (d_embed, TAIL))
+        for q in range(CHIPS):
             values = parts[q].astype(F32)
-            place(values[0:LATE], (ms_grad.at[0], d_embed), column, q * LATE)
-            place(values[LATE:PART], (up_grad.at[0], ms_grad.at[1], up_grad.at[1]), column, q * EARLY)
+            place(values[0:EARLY], early, column, q * EARLY)
+            place(values[EARLY:PART], late, column, q * LATE)
 
     @pl.when(odd[0] == 0)
     def _():
@@ -397,6 +399,7 @@
 
 
 def shift(value, axis, steps):
+    axis = NARROW if axis == "narrow" else axis
     count = lax.axis_size(axis)
     return lax.ppermute(value, axis, [(i, (i + steps) % count) for i in range(count)])
 
@@ -410,11 +413,11 @@
 
 
 def swap_cores(value):
-    return lax.ppermute(value, "narrow", [(i, i ^ 1) for i in range(lax.axis_size("narrow"))])
-
-
-def exchange(parts):
-    return lax.all_to_all(parts, AXES, split_axis=0, concat_axis=0, tiled=True)
+    return lax.ppermute(value, "core", [(0, 1), (1, 0)])
+
+
+def exchange(parts, axes):
+    return lax.all_to_all(parts, axes, split_axis=0, concat_axis=0, tiled=True)
 
 
 def on_device(
@@ -428,7 +431,7 @@
     mesh_scratch32 = pltpu.VMEM((MESH_ROWS, WIDTH), F32)
     extended_scratch = pltpu.VMEM((EXTENDED * BLOCK, WIDTH), BF16)
     table_scratch = pltpu.VMEM((EXTENDED, BLOCK, WIDTH), F32)
-    odd = (lax.axis_index("narrow") % 2).reshape(1).astype(jnp.int32)
+    odd = lax.axis_index("core").reshape(1).astype(jnp.int32)
     w_m = (message_weight[0], message_weight[1])
     w_u = (update_weight[0], update_weight[1])
 
@@ -442,8 +445,8 @@
         compiler_params=pltpu.CompilerParams(vmem_limit_bytes=56 * MIB),
         cost_estimate=pl.CostEstimate(flops=0, bytes_accessed=8 * MIB, transcendentals=0),
     )(grid_send, grid_feat.T)
-    packed, cotangent = lax.optimization_barrier((packed, cotangent))
-    received = exchange(packed)
+    packed, cotangent, odd = lax.optimization_barrier((packed, cotangent, odd))
+    received = exchange(packed, AXES)
 
     g_mix = g2m_coef.transpose(0, 2, 1, 3).reshape(MESH_BLOCKS, BLOCK, G_SLOTS * BLOCK)
     m_mix = mesh_coef.transpose(0, 2, 1, 3).reshape(MESH_BLOCKS, BLOCK, M_SLOTS * BLOCK)
@@ -514,7 +517,7 @@
     late, late_give = pl.pallas_call(
         final_body,
         grid=(4,),
-        out_shape=[jax.ShapeDtypeStruct((2 * SLABS, 128), BF16)] * 2,
+        out_shape=[jax.ShapeDtypeStruct((SLABS + 2 * TAIL, 128), BF16)] * 2,
         in_specs=[
             SM, SM, SM, *[VM] * 10,
             pl.BlockSpec((2048, WIDTH), lambda i: (i, 0)),
@@ -524,7 +527,7 @@
         scratch_shapes=[
             pltpu.VMEM((GRID_BLOCKS, BLOCK, WIDTH), F32),
             mesh_scratch, mesh_scratch, mesh_scratch32,
-            pltpu.VMEM((WIDTH, WIDTH), F32),
+            pltpu.VMEM((TAIL, WIDTH), F32),
         ],
         compiler_params=pltpu.CompilerParams(vmem_limit_bytes=34 * MIB),
         cost_estimate=pl.CostEstimate(flops=4 * 10**9, bytes_accessed=24 * MIB, transcendentals=0),
@@ -534,14 +537,14 @@
     )
     late_other = swap_cores(late_give)
 
-    by_device = lambda part: part.reshape(DEVICES, -1, 128)
+    by_chip = lambda part: part.reshape(CHIPS, -1, 128)
     pairs = kernel_call(
-        pair_body, [((DEVICES, PART, 128), BF16)], [VM] * 4, moved=6 * MIB, limit=16
-    )(by_device(late), by_device(late_other), by_device(early), by_device(early_other))[0]
+        pair_body, [((CHIPS, PART, 128), BF16)], [VM] * 4, moved=6 * MIB, limit=16
+    )(by_chip(early), by_chip(early_other), by_chip(late), by_chip(late_other))[0]
     totals = kernel_call(
-        sum_body, [((DEVICES, PART, 128), BF16)], [VM], moved=3 * MIB, limit=16
-    )(exchange(pairs))[0]
-    own = exchange(totals)
+        sum_body, [((CHIPS, PART, 128), BF16)], [VM], moved=3 * MIB, limit=16
+    )(exchange(pairs, CHIP_AXES))[0]
+    own = exchange(totals, CHIP_AXES)
     d_embed, ms_grad, up_grad = kernel_call(
         unpack_body,
         [((CHAN, WIDTH), F32), ((2, WIDTH, WIDTH), F32), ((2, WIDTH, WIDTH), F32)],
@@ -551,10 +554,11 @@
 
 
 def solution(mesh):
+    by_core = Mesh(mesh.devices.reshape(16, 4, 2), AXES)
     split = P(AXES, None)
     return jax.shard_map(
         on_device,
-        mesh=mesh,
+        mesh=by_core,
         in_specs=(
             split, split, P(), split, P(AXES, None, None, None), split, P(AXES, None, None, None),
             split, P(), P(), split,

time: 229 us -> 201 us (0.88)
  local copies, waits for them, and re-layouts: 31.7 us -> 17.9 us
  Pallas kernels: 74.1 us -> 62.8 us
  blocking collectives: 54.7 us -> 48.6 us
  starting transfers between devices: 39.5 us -> 42.2 us
    unnamed x74 -> x26, local copies, waits for them, and re-layouts: 16.5 us -> 2.45 us
    all_to_all x2, blocking collectives: 54.7 us -> 48.6 us  [exchange(): return lax.all_to_all(parts, axes, split_axis=0, concat_axis=0, tiled=True)]
    pallas_call x3, Pallas kernels: 17.2 us -> 13.5 us  [the longest x1 12.9 us: on_device(): pl.pallas_call(final_body, grid=(4,), out_shape=[jax.ShapeDtypeStruct((SL...]
    ppermute x3, starting transfers between devices: 1.49 us -> 4.68 us  [swap_cores(): return lax.ppermute(value, 'core', [(0, 1), (1, 0)])]
  transfers between devices with their start and end apart: 20 -> 20, of which waited for: 5 -> 5; matrix products, arithmetic and copies ran while one was open for 7% -> 8% of each run, Pallas kernels for 20% -> 18%
where the time goes in v6:
time: 201 us
  Pallas kernels  62.8 us (31%)
  blocking collectives  48.6 us (24%)
  starting transfers between devices  42.2 us (21%)
  waiting for transfers between devices  28.2 us (14%)
  local copies, waits for them, and re-layouts  17.9 us (9%)
    all_to_all x2, blocking collectives, exchange(): return lax.all_to_all(parts, axes, split_axis=0, concat_axis=0, tiled=True)  48.6 us
    ppermute x16, starting transfers between devices, shift(): lax.ppermute(value, axis, [(i, (i + steps) % count) for i in range(count)])  25.6 us
    ppermute x16, waiting for transfers between devices, shift(): lax.ppermute(value, axis, [(i, (i + steps) % count) for i in range(count)])  24.4 us
    pallas_call x1, Pallas kernels, on_device(): pl.pallas_call(final_body, grid=(4,), out_shape=[jax.ShapeDtypeStruct((SL...  12.9 us
    pallas_call x1, Pallas kernels, on_device(): pl.pallas_call(encode_body, grid=(4,), out_shape=[pltpu.HBM((CHAN, GRID_R...  12.1 us
    all_to_all x1, starting transfers between devices, exchange(): return lax.all_to_all(parts, axes, split_axis=0, concat_axis=0, tiled=True)  11.9 us
    pallas_call x1, Pallas kernels, on_device(): kernel_call(backward_body, [rows_bf16, rows_f32, rows_f32] + [halo] * 4,...  6.98 us
    pallas_call x1, Pallas kernels, on_device(): kernel_call(grads_body, [rows_bf16, ((3 * SLABS, 128), BF16), ((3 * SLABS...  6.66 us
  transfers between devices with their start and end apart: 20, of which 5 were waited for; matrix products, arithmetic and copies ran while one was open for 8% of the time, Pallas kernels for 18%

profile of v6, /device:TPU:1, one launch (start us, length us, event | category | flops | bytes accessed | tf_op | source)
XLA Modules:
  0.0 200.6 jit_solution(6780582705079549541)
XLA Ops:
  0.6 6.3 %shard_map.138 = bf16[128,115,128]{2,1,0:T(8,128)(2,1)} custom-call(s32[1,128]{1,0:T(1,128)} %send.1, bf16[227,8192]{1,0:T(8,128)(2,1)} %bitcast.22), custom_call_target="tpu_custom_call" | custom-call | bytes 8388608 | tf_op jit(solution)/shard_map/pallas_call | solution.py:438
  6.9 11.9 %all-to-all-start = ((bf16[128,115,128]{2,1,0:T(8,128)(2,1)}), bf16[128,115,128]{2,1,0:T(8,128)(2,1)}, u32[]{:S(2)}, u32[]{:S(2)}) async-start(bf16[128,115,128]{2,1,0:T(8,128)(2,1)} %shard_map.138), calls=%async_computation | async-start | bytes 7864320 | tf_op jit(solution)/shard_map/all_to_all | solution.py:420
  18.8 0.1 copy.31.source
  18.9 2.6 %copy.25 = bf16[16,64,6,64]{3,2,1,0:T(8,128)(2,1)} copy(bf16[16,64,6,64]{3,1,2,0:T(8,128)(2,1)S(1)} %bitcast.24) | data formatting | bytes 1572864 | tf_op jit(solution)/shard_map/transpose | solution.py:452
  21.5 3.1 %reshape.31.coeffs = bf16[16,64,384]{2,1,0:T(8,128)(2,1)S(1)} reshape(bf16[16,64,6,64]{3,2,1,0:T(8,128)(2,1)} %copy.25) | data formatting | bytes 1572864 | tf_op jit(solution)/shard_map/reshape | solution.py:452
  24.7 1.3 slice_bitcast_fusion.1
  26.0 0.0 copy-start.8
  26.0 6.0 %shard_map.139 = (f32[1024,512]{1,0:T(8,128)S(1)}, bf16[4,64,512]{2,1,0:T(8,128)(2,1)}, bf16[4,64,512]{2,1,0:T(8,128)(2,1)}, bf16[4,64,512]{2,1,0:T(8,128)(2,1)}, bf16[4,64,512]{2,1,0:T(8,128)(2,1)}) custom-call(s32[16,6]{1,0:T(8,128)S(1)} %copy.31.source, bf16[1024,512]{1,0:T(8,128)(2,1)S(1)} %copy-done.3, bf16[512,512]{1,0:T(8,128)(2,1)S(1)} %get-tuple-element.93.up, ...), custom_call_target="tpu_custom_call" | custom-call | flops 2000000000 | bytes 8388608 | tf_op jit(solution)/shard_map/pallas_call | solution.py:454
  32.0 1.3 copy-done.6
  33.3 5.6 %collective-permute-start = (bf16[4,64,512]{2,1,0:T(8,128)(2,1)}, bf16[4,64,512]{2,1,0:T(8,128)(2,1)}, u32[]{:S(2)}, u32[]{:S(2)}) collective-permute-start(bf16[4,64,512]{2,1,0:T(8,128)(2,1)} %get-tuple-element.51), channel_id=1, source_target_pairs={{0,120},{8,0},{16,8},{24,16},{32,24},{40,32},{48,40},{56,48},{64,5... | collective-permute-start | bytes 786440 | tf_op jit(solution)/shard_map/ppermute | solution.py:404
  38.9 0.0 collective-permute-start.1
  38.9 0.6 collective-permute-start.2
  39.5 1.1 collective-permute-start.3
  40.6 3.1 %copy.24 = bf16[16,64,8,64]{3,2,1,0:T(8,128)(2,1)} copy(bf16[16,64,8,64]{3,1,2,0:T(8,128)(2,1)S(1)} %bitcast.23) | data formatting | bytes 2097152 | tf_op jit(solution)/shard_map/transpose | solution.py:451
  43.7 3.2 %reshape.30.coeffs = bf16[16,64,512]{2,1,0:T(8,128)(2,1)S(1)} reshape(bf16[16,64,8,64]{3,2,1,0:T(8,128)(2,1)} %copy.24) | data formatting | bytes 2097152 | tf_op jit(solution)/shard_map/reshape | solution.py:451
  47.0 0.1 copy.28.source
  47.0 2.1 %slice_bitcast_fusion = (bf16[512,512]{1,0:T(8,128)(2,1)}, bf16[512,512]{1,0:T(8,128)(2,1)S(1)}) fusion(bf16[2,512,512]{2,1,0:T(8,128)(2,1)} %param.19), kind=kLoop, calls=%fused_computation | loop fusion | bytes 2097152 | tf_op jit(solution)/shard_map/squeeze | solution.py:435
  49.1 18.7 %collective-permute-done.r0 = bf16[4,64,512]{2,1,0:T(8,128)(2,1)} collective-permute-done((bf16[4,64,512]{2,1,0:T(8,128)(2,1)}, bf16[4,64,512]{2,1,0:T(8,128)(2,1)}, u32[]{:S(2)}, u32[]{:S(2)}) %collective-permute-start) | collective-permute-done | bytes 262176 | tf_op jit(solution)/shard_map/ppermute | solution.py:404
  67.8 4.2 %collective-permute-done.1.r1 = bf16[4,64,512]{2,1,0:T(8,128)(2,1)} collective-permute-done((bf16[4,64,512]{2,1,0:T(8,128)(2,1)}, bf16[4,64,512]{2,1,0:T(8,128)(2,1)}, u32[]{:S(2)}, u32[]{:S(2)}) %collective-permute-start.1) | collective-permute-done | bytes 262176 | tf_op jit(solution)/shard_map/ppermute | solution.py:404
  72.0 0.0 collective-permute-done.2.r2
  72.0 0.0 collective-permute-done.3.r3
  72.0 0.0 all-to-all-done.packed
  72.0 0.0 copy-start.5
  72.0 0.9 copy-done.5
  72.9 12.1 %shard_map.140 = (bf16[227,8192]{1,0:T(8,128)(2,1)}, bf16[8192,512]{1,0:T(8,128)(2,1)}, bf16[8192,512]{1,0:T(8,128)(2,1)S(1)}, bf16[4,64,512]{2,1,0:T(8,128)(2,1)S(1)}) custom-call(s32[16,8]{1,0:T(8,128)S(1)} %copy.28.source, s32[1,4]{1,0:T(1,128)S(1)} %copy-done.2, bf16[128,115,128]{2,1,0:T(8,128)(2,1)} %all-to-all-done.packed, ...), custom_call_target="tpu_custom_call" | custom-call | flops 4000000000 | bytes 27262976 | tf_op jit(solution)/shard_map/pallas_call | solution.py:464
  85.0 0.0 collective-permute-start.4
  85.0 4.8 %collective-permute-start.5 = (bf16[4,64,512]{2,1,0:T(8,128)(2,1)S(1)}, bf16[4,64,512]{2,1,0:T(8,128)(2,1)S(1)}, u32[]{:S(2)}, u32[]{:S(2)}) collective-permute-start(bf16[4,64,512]{2,1,0:T(8,128)(2,1)S(1)} %get-tuple-element.59), channel_id=1, source_target_pairs={{0,120},{8,0},{16,8},{24,16},{32,24},{40,32},{48,40},{56,48},{64,5... | collective-permute-start | bytes 786440 | tf_op jit(solution)/shard_map/ppermute | solution.py:404
  89.8 2.8 %collective-permute-start.6 = (bf16[4,64,512]{2,1,0:T(8,128)(2,1)S(1)}, bf16[4,64,512]{2,1,0:T(8,128)(2,1)S(1)}, u32[]{:S(2)}, u32[]{:S(2)}) collective-permute-start(bf16[4,64,512]{2,1,0:T(8,128)(2,1)S(1)} %get-tuple-element.59), channel_id=1, source_target_pairs={{0,1},{1,2},{2,3},{3,4},{4,5},{5,6},{6,7},{7,0},{8,9},{9,10},{10,1... | collective-permute-start | bytes 786440 | tf_op jit(solution)/shard_map/ppermute | solution.py:404
  92.6 0.0 collective-permute-start.7
  92.6 4.3 %shard_map.141 = (bf16[1024,512]{1,0:T(8,128)(2,1)S(1)}, bf16[1024,512]{1,0:T(8,128)(2,1)S(1)}, bf16[1024,512]{1,0:T(8,128)(2,1)S(1)}) custom-call(s32[16,8]{1,0:T(8,128)S(1)} %copy.28.source, bf16[8192,512]{1,0:T(8,128)(2,1)S(1)} %get-tuple-element.57.embedded, bf16[16,64,512]{2,1,0:T(8,128)(2,1)S(1)} %reshape.30.coeffs, ...), custom_call_target="tpu_custom_call" | custom-call | flops 2000000000 | bytes 12582912 | tf_op jit(solution)/shard_map/pallas_call | solution.py:491
  96.9 0.0 collective-permute-done.4.n0
  96.9 0.0 collective-permute-done.5.n1
  96.9 0.0 collective-permute-done.6.n2
  96.9 1.5 collective-permute-done.7.n3
  98.4 4.4 %shard_map.142 = (bf16[1024,512]{1,0:T(8,128)(2,1)S(1)}, bf16[1024,512]{1,0:T(8,128)(2,1)S(1)}, bf16[1024,512]{1,0:T(8,128)(2,1)S(1)}, bf16[1024,512]{1,0:T(8,128)(2,1)S(1)}, bf16[4,64,512]{2,1,0:T(8,128)(2,1)S(1)}) custom-call(s32[16,6]{1,0:T(8,128)S(1)} %copy.31.source, s32[1,4]{1,0:T(1,128)S(1)} %copy-done.2, ...), custom_call_target="tpu_custom_call" | custom-call | flops 2000000000 | bytes 10485760 | tf_op jit(solution)/shard_map/pallas_call | solution.py:495
  102.9 0.3 collective-permute-start.10
  103.2 0.2 collective-permute-start.11
  103.4 0.0 collective-permute-start.8
  103.4 4.8 %collective-permute-start.9 = (bf16[4,64,512]{2,1,0:T(8,128)(2,1)S(1)}, bf16[4,64,512]{2,1,0:T(8,128)(2,1)S(1)}, u32[]{:S(2)}, u32[]{:S(2)}) collective-permute-start(bf16[4,64,512]{2,1,0:T(8,128)(2,1)S(1)} %get-tuple-element.63), channel_id=1, source_target_pairs={{0,120},{8,0},{16,8},{24,16},{32,24},{40,32},{48,40},{56,48},{64,5... | collective-permute-start | bytes 786440 | tf_op jit(solution)/shard_map/ppermute | solution.py:404
  108.2 7.0 %shard_map.143 = (bf16[1024,512]{1,0:T(8,128)(2,1)S(1)}, f32[1024,512]{1,0:T(8,128)S(1)}, f32[1024,512]{1,0:T(8,128)S(1)}, bf16[4,64,512]{2,1,0:T(8,128)(2,1)S(1...) custom-call(s32[16,6]{1,0:T(8,128)S(1)} %copy.31.source, ...), custom_call_target="tpu_custom_call" | custom-call | flops 2000000000 | bytes 16777216 | tf_op jit(solution)/shard_map/pallas_call | solution.py:501
  115.2 1.4 collective-permute-start.13
  116.5 0.0 collective-permute-done.10.n2
  116.5 0.2 collective-permute-start.14
  116.7 0.0 collective-permute-done.11.n3
  116.7 3.8 %collective-permute-start.15 = (bf16[4,64,512]{2,1,0:T(8,128)(2,1)S(1)}, bf16[4,64,512]{2,1,0:T(8,128)(2,1)S(1)}, u32[]{:S(2)}, u32[]{:S(2)}) collective-permute-start(bf16[4,64,512]{2,1,0:T(8,128)(2,1)S(1)} %get-tuple-element.80), channel_id=1, source_target_pairs={{0,7},{1,0},{2,1},{3,2},{4,3},{5,4},{6,5},{7,6},{8,15},{9,8},{10,9... | collective-permute-start | bytes 786440 | tf_op jit(solution)/shard_map/ppermute | solution.py:404
  120.5 0.0 collective-permute-done.8.n0
  120.5 0.0 collective-permute-start.16
  120.5 0.0 collective-permute-done.9.n1
  120.5 6.7 %shard_map.144 = (bf16[1024,512]{1,0:T(8,128)(2,1)}, bf16[3072,128]{1,0:T(8,128)(2,1)S(1)}, bf16[3072,128]{1,0:T(8,128)(2,1)S(1)}) custom-call(s32[1]{0:T(128)} %bitcast.1.odd, s32[16,6]{1,0:T(8,128)S(1)} %copy.31.source, bf16[1024,512]{1,0:T(8,128)(2,1)S(1)} %get-tuple-element.62.sent, bf16[4,64,512]{2,1,0:T(8,128)(2,1)S(1)} %collective-permute-done.8.n0, ...), custom_call_target="tpu_custom_call" | custom-call | flops 4000000000 | bytes 14680064 | tf_op jit(solution)/shard_map/pallas_call | solution.py:507
  127.2 0.5 collective-permute-start.12
  127.7 0.0 collective-permute-done.13.r0
  127.7 0.0 collective-permute-done.14.r1
  127.7 0.0 collective-permute-done.15.r2
  127.7 12.9 %shard_map.145 = (bf16[1536,128]{1,0:T(8,128)(2,1)S(1)}, bf16[1536,128]{1,0:T(8,128)(2,1)S(1)}) custom-call(s32[1]{0:T(128)} %bitcast.1.odd, s32[16,8]{1,0:T(8,128)S(1)} %copy.28.source, s32[1,4]{1,0:T(1,128)S(1)} %copy-done.2, f32[1024,512]{1,0:T(8,128)S(1)} %get-tuple-element.77.own, bf16[4,64,512]{2,1,0:T(8,128)(2,1)S(1)} %collective-permute-done.13.r0, ...), custom_call_target="tpu_custom_call" | custom-call | flops 4000000000 | bytes 25165824 | tf_op jit(solution)/shard_map/pallas_call | solution.py:517
  140.6 0.9 collective-permute-start.17
  141.5 1.3 collective-permute-done.17
  142.9 0.0 collective-permute-done.12
  142.9 0.3 shard_map.146
  143.2 26.1 %all_to_all.15.parts = bf16[64,72,128]{2,1,0:T(8,128)(2,1)S(1)} all-to-all(bf16[64,72,128]{2,1,0:T(8,128)(2,1)S(1)} %shard_map.146), channel_id=1, replica_groups=mesh['wide'=16,'x'=4,'core'=2] {'wide','x'}, dimensions={0} | all-to-all | bytes 2359296 | tf_op jit(solution)/shard_map/all_to_all | solution.py:420
  169.4 0.3 shard_map.147
  169.6 22.5 %all_to_all.16.own = bf16[64,72,128]{2,1,0:T(8,128)(2,1)S(1)} all-to-all(bf16[64,72,128]{2,1,0:T(8,128)(2,1)S(1)} %shard_map.147), channel_id=1, replica_groups=mesh['wide'=16,'x'=4,'core'=2] {'wide','x'}, dimensions={0} | all-to-all | bytes 2359296 | tf_op jit(solution)/shard_map/all_to_all | solution.py:420
  192.1 3.2 %collective-permute-start.18 = (bf16[64,72,128]{2,1,0:T(8,128)(2,1)S(1)}, bf16[64,72,128]{2,1,0:T(8,128)(2,1)S(1)}, u32[]{:S(2)}, u32[]{:S(2)}) collective-permute-start(bf16[64,72,128]{2,1,0:T(8,128)(2,1)S(1)} %all_to_all.16.own), channel_id=1, source_target_pairs={{0,1},{1,0},{2,3},{3,2},{4,5},{5,4},{6,7},{7,6},{8,9},{9,8},{10,11... | collective-permute-start | bytes 3538952 | tf_op jit(solution)/shard_map/ppermute | solution.py:416
  195.4 2.5 %collective-permute-done.18.other = bf16[64,72,128]{2,1,0:T(8,128)(2,1)S(1)} collective-permute-done((bf16[64,72,128]{2,1,0:T(8,128)(2,1)S(1)}, bf16[64,72,128]{2,1,0:T(8,128)(2,1)S(1)}, u32[]{:S(2)}, u32[]{:S(2)}) %collective-permute-start.18) | collective-permute-done | bytes 1179680 | tf_op jit(solution)/shard_map/ppermute | solution.py:416
  197.9 2.7 %shard_map.148 = (f32[227,512]{1,0:T(8,128)}, f32[2,512,512]{2,1,0:T(8,128)}, f32[2,512,512]{2,1,0:T(8,128)}) custom-call(s32[1]{0:T(128)} %bitcast.1.odd, bf16[64,72,128]{2,1,0:T(8,128)(2,1)S(1)} %all_to_all.16.own, bf16[64,72,128]{2,1,0:T(8,128)(2,1)S(1)} %collective-permute-done.18.other), custom_call_target="tpu_custom_call" | custom-call | bytes 7340032 | tf_op jit(solution)/shard_map/pallas_call | solution.py:548
  (21 shorter events, 0.0 us)
Async XLA Ops:
  6.9 11.9 %copy-start.10 = (s32[16,6]{0,1:T(8,128)S(1)}, s32[16,6]{0,1:T(8,128)}, u32[]{:S(2)}) copy-start(s32[16,6]{0,1:T(8,128)} %param.16) | copy-start | bytes 1156
  6.9 12.0 %copy-start.9 = (bf16[16,6,64,64]{3,2,1,0:T(8,128)(2,1)S(1)}, bf16[16,6,64,64]{3,2,1,0:T(8,128)(2,1)}, u32[]{:S(2)}) copy-start(bf16[16,6,64,64]{3,2,1,0:T(8,128)(2,1)} %param.17) | copy-start | bytes 2359300
  6.9 65.1 %all-to-all-start = ((bf16[128,115,128]{2,1,0:T(8,128)(2,1)}), bf16[128,115,128]{2,1,0:T(8,128)(2,1)}, u32[]{:S(2)}, u32[]{:S(2)}) async-start(bf16[128,115,128]{2,1,0:T(8,128)(2,1)} %shard_map.138), calls=%async_computation | async-start | bytes 7864320 | tf_op jit(solution)/shard_map/all_to_all | solution.py:420
  21.5 4.4 %copy-start.3 = (bf16[1024,512]{1,0:T(8,128)(2,1)S(1)}, bf16[1024,512]{1,0:T(8,128)(2,1)}, u32[]{:S(2)}) copy-start(bf16[1024,512]{1,0:T(8,128)(2,1)} %cot.2) | copy-start | bytes 3145732
  26.0 14.6 %copy-start.8 = (bf16[16,8,64,64]{3,2,1,0:T(8,128)(2,1)S(1)}, bf16[16,8,64,64]{3,2,1,0:T(8,128)(2,1)}, u32[]{:S(2)}) copy-start(bf16[16,8,64,64]{3,2,1,0:T(8,128)(2,1)} %param.15) | copy-start | bytes 3145732
  32.0 1.3 copy-start.6
  33.3 34.5 %collective-permute-start = (bf16[4,64,512]{2,1,0:T(8,128)(2,1)}, bf16[4,64,512]{2,1,0:T(8,128)(2,1)}, u32[]{:S(2)}, u32[]{:S(2)}) collective-permute-start(bf16[4,64,512]{2,1,0:T(8,128)(2,1)} %get-tuple-element.51), channel_id=1, source_target_pairs={{0,120},{8,0},{16,8},{24,16},{32,24},{40,32},{48,40},{56,48},{64,5... | collective-permute-start | bytes 786440 | tf_op jit(solution)/shard_map/ppermute | solution.py:404
  38.9 33.1 %collective-permute-start.1 = (bf16[4,64,512]{2,1,0:T(8,128)(2,1)}, bf16[4,64,512]{2,1,0:T(8,128)(2,1)}, u32[]{:S(2)}, u32[]{:S(2)}) collective-permute-start(bf16[4,64,512]{2,1,0:T(8,128)(2,1)} %get-tuple-element.52), channel_id=1, source_target_pairs={{0,8},{8,16},{16,24},{24,32},{32,40},{40,48},{48,56},{56,64},{64,7... | collective-permute-start | bytes 786440 | tf_op jit(solution)/shard_map/ppermute | solution.py:404
  38.9 33.1 %collective-permute-start.2 = (bf16[4,64,512]{2,1,0:T(8,128)(2,1)}, bf16[4,64,512]{2,1,0:T(8,128)(2,1)}, u32[]{:S(2)}, u32[]{:S(2)}) collective-permute-start(bf16[4,64,512]{2,1,0:T(8,128)(2,1)} %get-tuple-element.53), channel_id=1, source_target_pairs={{0,7},{1,0},{2,1},{3,2},{4,3},{5,4},{6,5},{7,6},{8,15},{9,8},{10,9... | collective-permute-start | bytes 786440 | tf_op jit(solution)/shard_map/ppermute | solution.py:404
  39.5 32.5 %collective-permute-start.3 = (bf16[4,64,512]{2,1,0:T(8,128)(2,1)}, bf16[4,64,512]{2,1,0:T(8,128)(2,1)}, u32[]{:S(2)}, u32[]{:S(2)}) collective-permute-start(bf16[4,64,512]{2,1,0:T(8,128)(2,1)} %get-tuple-element.54), channel_id=1, source_target_pairs={{0,1},{1,2},{2,3},{3,4},{4,5},{5,6},{6,7},{7,0},{8,9},{9,10},{10,1... | collective-permute-start | bytes 786440 | tf_op jit(solution)/shard_map/ppermute | solution.py:404
  43.7 3.2 %copy-start.11 = (s32[16,8]{0,1:T(8,128)S(1)}, s32[16,8]{0,1:T(8,128)}, u32[]{:S(2)}) copy-start(s32[16,8]{0,1:T(8,128)} %param.14) | copy-start | bytes 1540
  43.7 28.2 %copy-start.2 = (s32[1,4]{1,0:T(1,128)S(1)}, s32[1,4]{1,0:T(1,128)}, u32[]{:S(2)}) copy-start(s32[1,4]{1,0:T(1,128)} %shown.7) | copy-start | bytes 52
  72.0 0.9 copy-start.5
  85.0 11.9 %collective-permute-start.4 = (bf16[4,64,512]{2,1,0:T(8,128)(2,1)S(1)}, bf16[4,64,512]{2,1,0:T(8,128)(2,1)S(1)}, u32[]{:S(2)}, u32[]{:S(2)}) collective-permute-start(bf16[4,64,512]{2,1,0:T(8,128)(2,1)S(1)} %get-tuple-element.59), channel_id=1, source_target_pairs={{0,8},{8,16},{16,24},{24,32},{32,40},{40,48},{48,56},{56,64},{64,7... | collective-permute-start | bytes 786440 | tf_op jit(solution)/shard_map/ppermute | solution.py:404
  85.0 11.9 %collective-permute-start.5 = (bf16[4,64,512]{2,1,0:T(8,128)(2,1)S(1)}, bf16[4,64,512]{2,1,0:T(8,128)(2,1)S(1)}, u32[]{:S(2)}, u32[]{:S(2)}) collective-permute-start(bf16[4,64,512]{2,1,0:T(8,128)(2,1)S(1)} %get-tuple-element.59), channel_id=1, source_target_pairs={{0,120},{8,0},{16,8},{24,16},{32,24},{40,32},{48,40},{56,48},{64,5... | collective-permute-start | bytes 786440 | tf_op jit(solution)/shard_map/ppermute | solution.py:404
  89.8 7.1 %collective-permute-start.6 = (bf16[4,64,512]{2,1,0:T(8,128)(2,1)S(1)}, bf16[4,64,512]{2,1,0:T(8,128)(2,1)S(1)}, u32[]{:S(2)}, u32[]{:S(2)}) collective-permute-start(bf16[4,64,512]{2,1,0:T(8,128)(2,1)S(1)} %get-tuple-element.59), channel_id=1, source_target_pairs={{0,1},{1,2},{2,3},{3,4},{4,5},{5,6},{6,7},{7,0},{8,9},{9,10},{10,1... | collective-permute-start | bytes 786440 | tf_op jit(solution)/shard_map/ppermute | solution.py:404
  92.6 5.8 %collective-permute-start.7 = (bf16[4,64,512]{2,1,0:T(8,128)(2,1)S(1)}, bf16[4,64,512]{2,1,0:T(8,128)(2,1)S(1)}, u32[]{:S(2)}, u32[]{:S(2)}) collective-permute-start(bf16[4,64,512]{2,1,0:T(8,128)(2,1)S(1)} %get-tuple-element.59), channel_id=1, source_target_pairs={{0,7},{1,0},{2,1},{3,2},{4,3},{5,4},{6,5},{7,6},{8,15},{9,8},{10,9... | collective-permute-start | bytes 786440 | tf_op jit(solution)/shard_map/ppermute | solution.py:404
  92.6 5.8 %copy-start.1 = (bf16[512,512]{1,0:T(8,128)(2,1)S(1)}, bf16[512,512]{1,0:T(8,128)(2,1)}, u32[]{:S(2)}) copy-start(bf16[512,512]{1,0:T(8,128)(2,1)} %get-tuple-element.90.message) | copy-start | bytes 1572868
  98.4 9.8 %copy-start.4 = (bf16[1024,512]{1,0:T(8,128)(2,1)S(1)}, bf16[1024,512]{1,0:T(8,128)(2,1)}, u32[]{:S(2)}) copy-start(bf16[1024,512]{1,0:T(8,128)(2,1)} %cot.2) | copy-start | bytes 3145732
  98.4 9.8 %copy-start.7 = (f32[1024,512]{1,0:T(8,128)S(1)}, f32[1024,512]{1,0:T(8,128)}, u32[]{:S(2)}) copy-start(f32[1024,512]{1,0:T(8,128)} %copy-done.6) | copy-start | bytes 6291460
  102.9 13.7 %collective-permute-start.10 = (bf16[4,64,512]{2,1,0:T(8,128)(2,1)S(1)}, bf16[4,64,512]{2,1,0:T(8,128)(2,1)S(1)}, u32[]{:S(2)}, u32[]{:S(2)}) collective-permute-start(bf16[4,64,512]{2,1,0:T(8,128)(2,1)S(1)} %get-tuple-element.63), channel_id=1, source_target_pairs={{0,1},{1,2},{2,3},{3,4},{4,5},{5,6},{6,7},{7,0},{8,9},{9,10},{10,1... | collective-permute-start | bytes 786440 | tf_op jit(solution)/shard_map/ppermute | solution.py:404
  103.2 13.5 %collective-permute-start.11 = (bf16[4,64,512]{2,1,0:T(8,128)(2,1)S(1)}, bf16[4,64,512]{2,1,0:T(8,128)(2,1)S(1)}, u32[]{:S(2)}, u32[]{:S(2)}) collective-permute-start(bf16[4,64,512]{2,1,0:T(8,128)(2,1)S(1)} %get-tuple-element.63), channel_id=1, source_target_pairs={{0,7},{1,0},{2,1},{3,2},{4,3},{5,4},{6,5},{7,6},{8,15},{9,8},{10,9... | collective-permute-start | bytes 786440 | tf_op jit(solution)/shard_map/ppermute | solution.py:404
  103.4 17.1 %collective-permute-start.8 = (bf16[4,64,512]{2,1,0:T(8,128)(2,1)S(1)}, bf16[4,64,512]{2,1,0:T(8,128)(2,1)S(1)}, u32[]{:S(2)}, u32[]{:S(2)}) collective-permute-start(bf16[4,64,512]{2,1,0:T(8,128)(2,1)S(1)} %get-tuple-element.63), channel_id=1, source_target_pairs={{0,8},{8,16},{16,24},{24,32},{32,40},{40,48},{48,56},{56,64},{64,7... | collective-permute-start | bytes 786440 | tf_op jit(solution)/shard_map/ppermute | solution.py:404
  103.4 17.1 %collective-permute-start.9 = (bf16[4,64,512]{2,1,0:T(8,128)(2,1)S(1)}, bf16[4,64,512]{2,1,0:T(8,128)(2,1)S(1)}, u32[]{:S(2)}, u32[]{:S(2)}) collective-permute-start(bf16[4,64,512]{2,1,0:T(8,128)(2,1)S(1)} %get-tuple-element.63), channel_id=1, source_target_pairs={{0,120},{8,0},{16,8},{24,16},{32,24},{40,32},{48,40},{56,48},{64,5... | collective-permute-start | bytes 786440 | tf_op jit(solution)/shard_map/ppermute | solution.py:404
  115.2 12.5 %collective-permute-start.13 = (bf16[4,64,512]{2,1,0:T(8,128)(2,1)S(1)}, bf16[4,64,512]{2,1,0:T(8,128)(2,1)S(1)}, u32[]{:S(2)}, u32[]{:S(2)}) collective-permute-start(bf16[4,64,512]{2,1,0:T(8,128)(2,1)S(1)} %get-tuple-element.78), channel_id=1, source_target_pairs={{0,120},{8,0},{16,8},{24,16},{32,24},{40,32},{48,40},{56,48},{64,5... | collective-permute-start | bytes 786440 | tf_op jit(solution)/shard_map/ppermute | solution.py:404
  116.5 11.2 %collective-permute-start.14 = (bf16[4,64,512]{2,1,0:T(8,128)(2,1)S(1)}, bf16[4,64,512]{2,1,0:T(8,128)(2,1)S(1)}, u32[]{:S(2)}, u32[]{:S(2)}) collective-permute-start(bf16[4,64,512]{2,1,0:T(8,128)(2,1)S(1)} %get-tuple-element.79), channel_id=1, source_target_pairs={{0,8},{8,16},{16,24},{24,32},{32,40},{40,48},{48,56},{56,64},{64,7... | collective-permute-start | bytes 786440 | tf_op jit(solution)/shard_map/ppermute | solution.py:404
  116.7 11.0 %collective-permute-start.15 = (bf16[4,64,512]{2,1,0:T(8,128)(2,1)S(1)}, bf16[4,64,512]{2,1,0:T(8,128)(2,1)S(1)}, u32[]{:S(2)}, u32[]{:S(2)}) collective-permute-start(bf16[4,64,512]{2,1,0:T(8,128)(2,1)S(1)} %get-tuple-element.80), channel_id=1, source_target_pairs={{0,7},{1,0},{2,1},{3,2},{4,3},{5,4},{6,5},{7,6},{8,15},{9,8},{10,9... | collective-permute-start | bytes 786440 | tf_op jit(solution)/shard_map/ppermute | solution.py:404
  120.5 7.2 %collective-permute-start.16 = (bf16[4,64,512]{2,1,0:T(8,128)(2,1)S(1)}, bf16[4,64,512]{2,1,0:T(8,128)(2,1)S(1)}, u32[]{:S(2)}, u32[]{:S(2)}) collective-permute-start(bf16[4,64,512]{2,1,0:T(8,128)(2,1)S(1)} %get-tuple-element.81), channel_id=1, source_target_pairs={{0,1},{1,2},{2,3},{3,4},{4,5},{5,6},{6,7},{7,0},{8,9},{9,10},{10,1... | collective-permute-start | bytes 786440 | tf_op jit(solution)/shard_map/ppermute | solution.py:404
  120.5 7.2 %copy-start = (bf16[227,8192]{1,0:T(8,128)(2,1)S(1)}, bf16[227,8192]{1,0:T(8,128)(2,1)}, u32[]{:S(2)}) copy-start(bf16[227,8192]{1,0:T(8,128)(2,1)} %get-tuple-element.84.points) | copy-start | bytes 11157508
  127.2 15.7 %collective-permute-start.12 = (bf16[3072,128]{1,0:T(8,128)(2,1)S(1)}, bf16[3072,128]{1,0:T(8,128)(2,1)S(1)}, u32[]{:S(2)}, u32[]{:S(2)}) collective-permute-start(bf16[3072,128]{1,0:T(8,128)(2,1)S(1)} %get-tuple-element.76), channel_id=1, source_target_pairs={{0,1},{1,0},{2,3},{3,2},{4,5},{5,4},{6,7},{7,6},{8,9},{9,8},{10,11... | collective-permute-start | bytes 2359304 | tf_op jit(solution)/shard_map/ppermute | solution.py:416
  140.6 2.3 %collective-permute-start.17 = (bf16[1536,128]{1,0:T(8,128)(2,1)S(1)}, bf16[1536,128]{1,0:T(8,128)(2,1)S(1)}, u32[]{:S(2)}, u32[]{:S(2)}) collective-permute-start(bf16[1536,128]{1,0:T(8,128)(2,1)S(1)} %get-tuple-element.86), channel_id=1, source_target_pairs={{0,1},{1,0},{2,3},{3,2},{4,5},{5,4},{6,7},{7,6},{8,9},{9,8},{10,11... | collective-permute-start | bytes 1179656 | tf_op jit(solution)/shard_map/ppermute | solution.py:416
  192.1 5.7 %collective-permute-start.18 = (bf16[64,72,128]{2,1,0:T(8,128)(2,1)S(1)}, bf16[64,72,128]{2,1,0:T(8,128)(2,1)S(1)}, u32[]{:S(2)}, u32[]{:S(2)}) collective-permute-start(bf16[64,72,128]{2,1,0:T(8,128)(2,1)S(1)} %all_to_all.16.own), channel_id=1, source_target_pairs={{0,1},{1,0},{2,3},{3,2},{4,5},{5,4},{6,7},{7,6},{8,9},{9,8},{10,11... | collective-permute-start | bytes 3538952 | tf_op jit(solution)/shard_map/ppermute | solution.py:416

commit v7 on v6

--- a/solution.py
+++ b/solution.py
@@ -102,7 +102,7 @@
         out[target[at + 1]] = jnp.where(low, swap_halves(first), second)
         return carry
 
-    lax.fori_loop(0, 16, pair, 0, unroll=4)
+    lax.fori_loop(0, 16, pair, 0, unroll=8)
 
 
 def scatter_back(coeffs, gradient, source, table, slots, blocks):
@@ -110,7 +110,7 @@
         table[i] = jnp.zeros((BLOCK, WIDTH), F32)
         return carry
 
-    lax.fori_loop(0, blocks, clear, 0, unroll=4)
+    lax.fori_loop(0, blocks, clear, 0, unroll=16)
 
     def one(b, carry):
         parts = times(coeffs[b], gradient[rows_of(b), :], 0, 0)
@@ -119,7 +119,7 @@
             table[at] = table[at] + parts[k * BLOCK : (k + 1) * BLOCK]
         return carry
 
-    lax.fori_loop(0, MESH_BLOCKS, one, 0, unroll=2)
+    lax.fori_loop(0, MESH_BLOCKS, one, 0, unroll=4)
 
 
 def gather_mix(coeffs, pick, slots, b):
@@ -150,7 +150,7 @@
         lowered[rows, :] = times(cot[rows, :], up[...], 1, 1).astype(BF16)
         return carry
 
-    lax.fori_loop(0, MESH_ROWS // 256, step, 0, unroll=2)
+    lax.fori_loop(0, MESH_ROWS // 256, step, 0, unroll=4)
     scatter_back(coeffs, lowered, source, table, M_SLOTS, EXTENDED)
     write_halo(table, own, (h0, h1, h2, h3))
 
@@ -196,7 +196,7 @@
         mesh[rows_of(b), :] = gather_mix(coeffs, pick, G_SLOTS, b).astype(BF16)
         return carry
 
-    lax.fori_loop(0, MESH_BLOCKS, mix, 0, unroll=4)
+    lax.fori_loop(0, MESH_BLOCKS, mix, 0, unroll=8)
 
     def talk(c, carry):
         rows = chunk(c, 256)
@@ -207,7 +207,7 @@
         slope_m[rows, :] = (s + e * (1.0 - s)).astype(BF16)
         return carry
 
-    lax.fori_loop(0, MESH_ROWS // 256, talk, 0)
+    lax.fori_loop(0, MESH_ROWS // 256, talk, 0, unroll=4)
 
 
 def extend(extended, sent, halos):
@@ -224,7 +224,7 @@
         aggregate[rows_of(b), :] = gather_mix(coeffs, pick, M_SLOTS, b).astype(BF16)
         return carry
 
-    lax.fori_loop(0, MESH_BLOCKS, mix, 0, unroll=4)
+    lax.fori_loop(0, MESH_BLOCKS, mix, 0, unroll=8)
 
 
 def forward_body(
@@ -245,7 +245,7 @@
         slope_m[rows, :] = (s + e * (1.0 - s)).astype(BF16)
         return carry
 
-    lax.fori_loop(0, MESH_ROWS // 256, step, 0, unroll=2)
+    lax.fori_loop(0, MESH_ROWS // 256, step, 0, unroll=4)
     for h in range(SHOWN):
         mine[h] = sent_1[rows_of(shown[0, h]), :]
 
@@ -266,7 +266,7 @@
         lowered[rows, :] = times(g.astype(BF16), up[...], 1, 1).astype(BF16)
         return carry
 
-    lax.fori_loop(0, MESH_ROWS // 256, step, 0, unroll=2)
+    lax.fori_loop(0, MESH_ROWS // 256, step, 0, unroll=4)
     scatter_back(coeffs, lowered, source, table, M_SLOTS, EXTENDED)
     write_halo(table, own_0, (h0, h1, h2, h3))
 
@@ -304,7 +304,7 @@
         mesh_out[rows, :] = (mesh[rows, :].astype(F32) + update).astype(BF16)
         return carry
 
-    lax.fori_loop(0, MESH_ROWS // 256, step, 0, unroll=2)
+    lax.fori_loop(0, MESH_ROWS // 256, step, 0, unroll=4)
     write_slabs(odd, keep, give, 2 * SLABS, times(aggregate[...], cot[...], 0, 0))
 
 
@@ -326,7 +326,7 @@
             lowered[rows, :] = (grad_1[rows, :] + times(gp, message[...], 1, 1)).astype(BF16)
             return carry
 
-        lax.fori_loop(0, MESH_ROWS // 256, step, 0, unroll=2)
+        lax.fori_loop(0, MESH_ROWS // 256, step, 0, unroll=4)
         scatter_back(coeffs, lowered, source, table, G_SLOTS, GRID_BLOCKS)
         write_slabs(odd, keep, give, 0, times(mesh[...], grad_pre[...], 0, 0))
         total[...] = jnp.zeros_like(total)
@@ -457,9 +457,7 @@
     )(mesh_src, cotangent, w_u[1], m_mix)
     returned_1 = give_back(*halos)
 
-    received, g_mix, m_mix, own_1, *returned_1 = lax.optimization_barrier(
-        (received, g_mix, m_mix, own_1, *returned_1)
-    )
+    received, g_mix, m_mix, own_1 = lax.optimization_barrier((received, g_mix, m_mix, own_1))
     whole = lambda *shape: pl.BlockSpec(shape, lambda i: (0,) * len(shape))
     points, slope, embedded, mine_0 = pl.pallas_call(
         encode_body,

time: 201 us -> 203 us (level)
  Pallas kernels: 62.8 us -> 56.4 us
  local copies, waits for them, and re-layouts: 17.9 us -> 22.2 us
  starting transfers between devices: 42.2 us -> 45.3 us
    all_to_all x1, waiting for transfers between devices: 0.01 us -> 24.3 us  [exchange(): return lax.all_to_all(parts, axes, split_axis=0, concat_axis=0, tiled=True)]
    ppermute x16, waiting for transfers between devices: 24.4 us -> 1.1 us  [shift(): lax.ppermute(value, axis, [(i, (i + steps) % count) for i in range(count)])]
    unnamed x26 -> x42, local copies, waits for them, and re-layouts: 2.45 us -> 6.5 us
    ppermute x3, starting transfers between devices: 4.68 us -> 6.8 us  [swap_cores(): return lax.ppermute(value, 'core', [(0, 1), (1, 0)])]
  transfers between devices with their start and end apart: 20 -> 20, of which waited for: 5 -> 4; matrix products, arithmetic and copies ran while one was open for 8% -> 8% of each run, Pallas kernels for 18% -> 17%
where the time goes in v7:
time: 203 us; the launch traced here: 202 us
  Pallas kernels  56.4 us (28%)
  blocking collectives  48.3 us (24%)
  starting transfers between devices  45.3 us (22%)
  waiting for transfers between devices  29.3 us (14%)
  local copies, waits for them, and re-layouts  22.2 us (11%)
    all_to_all x2, blocking collectives, exchange(): return lax.all_to_all(parts, axes, split_axis=0, concat_axis=0, tiled=True)  48.3 us
    ppermute x16, starting transfers between devices, shift(): lax.ppermute(value, axis, [(i, (i + steps) % count) for i in range(count)])  26.6 us
    all_to_all x1, waiting for transfers between devices, exchange(): return lax.all_to_all(parts, axes, split_axis=0, concat_axis=0, tiled=True)  24.3 us
    pallas_call x1, Pallas kernels, on_device(): pl.pallas_call(encode_body, grid=(4,), out_shape=[pltpu.HBM((CHAN, GRID_R...  12.2 us
    all_to_all x1, starting transfers between devices, exchange(): return lax.all_to_all(parts, axes, split_axis=0, concat_axis=0, tiled=True)  11.9 us
    pallas_call x1, Pallas kernels, on_device(): pl.pallas_call(final_body, grid=(4,), out_shape=[jax.ShapeDtypeStruct((SL...  11.9 us
    ppermute x3, starting transfers between devices, swap_cores(): return lax.ppermute(value, 'core', [(0, 1), (1, 0)])  6.8 us
    unnamed x42, local copies, waits for them, and re-layouts  6.5 us
  transfers between devices with their start and end apart: 20, of which 4 were waited for; matrix products, arithmetic and copies ran while one was open for 8% of the time, Pallas kernels for 17%

profile of v7, /device:TPU:1, one launch (start us, length us, event | category | flops | bytes accessed | tf_op | source)
XLA Modules:
  0.0 202.3 jit_solution(13301642316291764691)
XLA Ops:
  0.6 5.9 %shard_map.138 = bf16[128,115,128]{2,1,0:T(8,128)(2,1)} custom-call(s32[1,128]{1,0:T(1,128)} %send.1, bf16[227,8192]{1,0:T(8,128)(2,1)} %bitcast.22), custom_call_target="tpu_custom_call" | custom-call | bytes 8388608 | tf_op jit(solution)/shard_map/pallas_call | solution.py:438
  6.6 11.9 %all-to-all-start = ((bf16[128,115,128]{2,1,0:T(8,128)(2,1)}), bf16[128,115,128]{2,1,0:T(8,128)(2,1)}, u32[]{:S(2)}, u32[]{:S(2)}) async-start(bf16[128,115,128]{2,1,0:T(8,128)(2,1)} %shard_map.138), calls=%async_computation | async-start | bytes 7864320 | tf_op jit(solution)/shard_map/all_to_all | solution.py:420
  18.5 0.1 copy.31.source
  18.6 2.6 %copy.25 = bf16[16,64,6,64]{3,2,1,0:T(8,128)(2,1)} copy(bf16[16,64,6,64]{3,1,2,0:T(8,128)(2,1)S(1)} %bitcast.24) | data formatting | bytes 1572864 | tf_op jit(solution)/shard_map/transpose | solution.py:452
  21.2 3.1 %reshape.31.coeffs = bf16[16,64,384]{2,1,0:T(8,128)(2,1)S(1)} reshape(bf16[16,64,6,64]{3,2,1,0:T(8,128)(2,1)} %copy.25) | data formatting | bytes 1572864 | tf_op jit(solution)/shard_map/reshape | solution.py:452
  24.3 4.7 %copy.24 = bf16[16,64,8,64]{3,2,1,0:T(8,128)(2,1)} copy(bf16[16,64,8,64]{3,1,2,0:T(8,128)(2,1)} %bitcast.23) | data formatting | bytes 2097152 | tf_op jit(solution)/shard_map/transpose | solution.py:451
  29.0 3.2 %reshape.30.coeffs = bf16[16,64,512]{2,1,0:T(8,128)(2,1)S(1)} reshape(bf16[16,64,8,64]{3,2,1,0:T(8,128)(2,1)} %copy.24) | data formatting | bytes 2097152 | tf_op jit(solution)/shard_map/reshape | solution.py:451
  32.2 0.1 copy.28.source
  32.2 1.3 slice_bitcast_fusion.1
  33.5 0.0 copy-start.3
  33.5 1.2 copy-done.3
  34.8 4.3 %shard_map.139 = (f32[1024,512]{1,0:T(8,128)S(1)}, bf16[4,64,512]{2,1,0:T(8,128)(2,1)S(1)}, bf16[4,64,512]{2,1,0:T(8,128)(2,1)S(1)}, bf16[4,64,512]{2,1,0:T(8,128)(2,1)S(1)}, bf16[4,64,512]{2,1,0:T(8,128)(2,1)S(1)}) custom-call(s32[16,6]{1,0:T(8,128)S(1)} %copy.31.source, bf16[1024,512]{1,0:T(8,128)(2,1)S(1)} %copy-done.3, ...), custom_call_target="tpu_custom_call" | custom-call | flops 2000000000 | bytes 8388608 | tf_op jit(solution)/shard_map/pallas_call | solution.py:454
  39.1 0.0 copy-start.5
  39.1 0.7 copy-done.5
  39.8 0.7 copy-done.7
  40.5 0.7 copy-done.9
  41.2 0.7 copy-done.11
  41.9 1.3 copy-done.14
  43.2 0.9 slice_bitcast_fusion
  44.1 24.3 %all-to-all-done.packed = bf16[128,115,128]{2,1,0:T(8,128)(2,1)} async-done(((bf16[128,115,128]{2,1,0:T(8,128)(2,1)}), bf16[128,115,128]{2,1,0:T(8,128)(2,1)}, u32[]{:S(2)}, u32[]{:S(2)}) %all-to-all-start) | async-done | bytes 3768352 | tf_op jit(solution)/shard_map/all_to_all | solution.py:420
  68.4 0.9 copy-done.13
  69.4 12.2 %shard_map.140 = (bf16[227,8192]{1,0:T(8,128)(2,1)}, bf16[8192,512]{1,0:T(8,128)(2,1)}, bf16[8192,512]{1,0:T(8,128)(2,1)S(1)}, bf16[4,64,512]{2,1,0:T(8,128)(2,1)S(1)}) custom-call(s32[16,8]{1,0:T(8,128)S(1)} %copy.28.source, s32[1,4]{1,0:T(1,128)S(1)} %copy-done.2, bf16[128,115,128]{2,1,0:T(8,128)(2,1)} %all-to-all-done.packed, ...), custom_call_target="tpu_custom_call" | custom-call | flops 4000000000 | bytes 27262976 | tf_op jit(solution)/shard_map/pallas_call | solution.py:462
  81.5 4.8 %collective-permute-start.1 = (bf16[4,64,512]{2,1,0:T(8,128)(2,1)S(1)}, bf16[4,64,512]{2,1,0:T(8,128)(2,1)S(1)}, u32[]{:S(2)}, u32[]{:S(2)}) collective-permute-start(bf16[4,64,512]{2,1,0:T(8,128)(2,1)S(1)} %get-tuple-element.51), channel_id=1, source_target_pairs={{0,120},{8,0},{16,8},{24,16},{32,24},{40,32},{48,40},{56,48},{64,5... | collective-permute-start | bytes 786440 | tf_op jit(solution)/shard_map/ppermute | solution.py:404
  86.3 1.6 collective-permute-start.2
  87.9 2.8 %collective-permute-start.10 = (bf16[4,64,512]{2,1,0:T(8,128)(2,1)S(1)}, bf16[4,64,512]{2,1,0:T(8,128)(2,1)S(1)}, u32[]{:S(2)}, u32[]{:S(2)}) collective-permute-start(bf16[4,64,512]{2,1,0:T(8,128)(2,1)S(1)} %copy-done.12), channel_id=1, source_target_pairs={{0,7},{1,0},{2,1},{3,2},{4,3},{5,4},{6,5},{7,6},{8,15},{9,8},{10,9... | collective-permute-start | bytes 786440 | tf_op jit(solution)/shard_map/ppermute | solution.py:404
  90.7 1.1 collective-permute-done.n0
  91.8 1.7 collective-permute-start.11
  93.5 0.0 collective-permute-done.1.n1
  93.5 2.8 %collective-permute-start.8 = (bf16[4,64,512]{2,1,0:T(8,128)(2,1)S(1)}, bf16[4,64,512]{2,1,0:T(8,128)(2,1)S(1)}, u32[]{:S(2)}, u32[]{:S(2)}) collective-permute-start(bf16[4,64,512]{2,1,0:T(8,128)(2,1)S(1)} %copy-done.8), channel_id=1, source_target_pairs={{0,120},{8,0},{16,8},{24,16},{32,24},{40,32},{48,40},{56,48},{64,5... | collective-permute-start | bytes 786440 | tf_op jit(solution)/shard_map/ppermute | solution.py:404
  96.3 3.3 %shard_map.141 = (bf16[1024,512]{1,0:T(8,128)(2,1)S(1)}, bf16[1024,512]{1,0:T(8,128)(2,1)S(1)}, bf16[1024,512]{1,0:T(8,128)(2,1)S(1)}) custom-call(s32[16,8]{1,0:T(8,128)S(1)} %copy.28.source, bf16[8192,512]{1,0:T(8,128)(2,1)S(1)} %get-tuple-element.49.embedded, bf16[16,64,512]{2,1,0:T(8,128)(2,1)S(1)} %reshape.30.coeffs, ...), custom_call_target="tpu_custom_call" | custom-call | flops 2000000000 | bytes 12582912 | tf_op jit(solution)/shard_map/pallas_call | solution.py:489
  99.6 0.0 collective-permute-done.2.n2
  99.6 0.1 collective-permute-start.9
  99.7 0.0 collective-permute-done.3.n3
  99.7 0.0 copy-start.4
  99.7 0.0 copy-start.15
  99.7 4.0 %shard_map.142 = (bf16[1024,512]{1,0:T(8,128)(2,1)S(1)}, bf16[1024,512]{1,0:T(8,128)(2,1)S(1)}, bf16[1024,512]{1,0:T(8,128)(2,1)S(1)}, bf16[1024,512]{1,0:T(8,128)(2,1)S(1)}, bf16[4,64,512]{2,1,0:T(8,128)(2,1)S(1)}) custom-call(s32[16,6]{1,0:T(8,128)S(1)} %copy.31.source, s32[1,4]{1,0:T(1,128)S(1)} %copy-done.2, ...), custom_call_target="tpu_custom_call" | custom-call | flops 2000000000 | bytes 10485760 | tf_op jit(solution)/shard_map/pallas_call | solution.py:493
  103.7 0.1 collective-permute-start.4
  103.8 0.0 collective-permute-done.10.r2
  103.8 4.8 %collective-permute-start.5 = (bf16[4,64,512]{2,1,0:T(8,128)(2,1)S(1)}, bf16[4,64,512]{2,1,0:T(8,128)(2,1)S(1)}, u32[]{:S(2)}, u32[]{:S(2)}) collective-permute-start(bf16[4,64,512]{2,1,0:T(8,128)(2,1)S(1)} %get-tuple-element.55), channel_id=1, source_target_pairs={{0,120},{8,0},{16,8},{24,16},{32,24},{40,32},{48,40},{56,48},{64,5... | collective-permute-start | bytes 786440 | tf_op jit(solution)/shard_map/ppermute | solution.py:404
  108.6 0.0 collective-permute-done.11.r3
  108.6 2.8 %collective-permute-start.6 = (bf16[4,64,512]{2,1,0:T(8,128)(2,1)S(1)}, bf16[4,64,512]{2,1,0:T(8,128)(2,1)S(1)}, u32[]{:S(2)}, u32[]{:S(2)}) collective-permute-start(bf16[4,64,512]{2,1,0:T(8,128)(2,1)S(1)} %get-tuple-element.55), channel_id=1, source_target_pairs={{0,1},{1,2},{2,3},{3,4},{4,5},{5,6},{6,7},{7,0},{8,9},{9,10},{10,1... | collective-permute-start | bytes 786440 | tf_op jit(solution)/shard_map/ppermute | solution.py:404
  111.4 0.1 collective-permute-start.7
  111.5 5.5 %shard_map.143 = (bf16[1024,512]{1,0:T(8,128)(2,1)S(1)}, f32[1024,512]{1,0:T(8,128)S(1)}, f32[1024,512]{1,0:T(8,128)S(1)}, bf16[4,64,512]{2,1,0:T(8,128)(2,1)S(1...) custom-call(s32[16,6]{1,0:T(8,128)S(1)} %copy.31.source, ...), custom_call_target="tpu_custom_call" | custom-call | flops 2000000000 | bytes 16777216 | tf_op jit(solution)/shard_map/pallas_call | solution.py:499
  117.0 1.7 collective-permute-start.13
  118.8 0.0 collective-permute-done.4.n0
  118.8 0.0 collective-permute-start.14
  118.8 0.0 collective-permute-done.5.n1
  118.8 3.3 %collective-permute-start.15 = (bf16[4,64,512]{2,1,0:T(8,128)(2,1)S(1)}, bf16[4,64,512]{2,1,0:T(8,128)(2,1)S(1)}, u32[]{:S(2)}, u32[]{:S(2)}) collective-permute-start(bf16[4,64,512]{2,1,0:T(8,128)(2,1)S(1)} %get-tuple-element.72), channel_id=1, source_target_pairs={{0,7},{1,0},{2,1},{3,2},{4,3},{5,4},{6,5},{7,6},{8,15},{9,8},{10,9... | collective-permute-start | bytes 786440 | tf_op jit(solution)/shard_map/ppermute | solution.py:404
  122.1 0.0 collective-permute-done.6.n2
  122.1 0.0 collective-permute-start.16
  122.1 0.0 collective-permute-done.7.n3
  122.1 6.1 %shard_map.144 = (bf16[1024,512]{1,0:T(8,128)(2,1)}, bf16[3072,128]{1,0:T(8,128)(2,1)S(1)}, bf16[3072,128]{1,0:T(8,128)(2,1)S(1)}) custom-call(s32[1]{0:T(128)} %bitcast.1.odd, s32[16,6]{1,0:T(8,128)S(1)} %copy.31.source, bf16[1024,512]{1,0:T(8,128)(2,1)S(1)} %get-tuple-element.54.sent, bf16[4,64,512]{2,1,0:T(8,128)(2,1)S(1)} %collective-permute-done.4.n0, ...), custom_call_target="tpu_custom_call" | custom-call | flops 4000000000 | bytes 14680064 | tf_op jit(solution)/shard_map/pallas_call | solution.py:505
  128.2 0.5 collective-permute-start.12
  128.7 0.0 collective-permute-done.13.r0
  128.7 11.9 %shard_map.145 = (bf16[1536,128]{1,0:T(8,128)(2,1)S(1)}, bf16[1536,128]{1,0:T(8,128)(2,1)S(1)}) custom-call(s32[1]{0:T(128)} %bitcast.1.odd, s32[16,8]{1,0:T(8,128)S(1)} %copy.28.source, s32[1,4]{1,0:T(1,128)S(1)} %copy-done.2, f32[1024,512]{1,0:T(8,128)S(1)} %get-tuple-element.69.own, bf16[4,64,512]{2,1,0:T(8,128)(2,1)S(1)} %collective-permute-done.13.r0, ...), custom_call_target="tpu_custom_call" | custom-call | flops 4000000000 | bytes 25165824 | tf_op jit(solution)/shard_map/pallas_call | solution.py:515
  140.6 3.1 %collective-permute-start.17 = (bf16[1536,128]{1,0:T(8,128)(2,1)S(1)}, bf16[1536,128]{1,0:T(8,128)(2,1)S(1)}, u32[]{:S(2)}, u32[]{:S(2)}) collective-permute-start(bf16[1536,128]{1,0:T(8,128)(2,1)S(1)} %get-tuple-element.78), channel_id=1, source_target_pairs={{0,1},{1,0},{2,3},{3,2},{4,5},{5,4},{6,7},{7,6},{8,9},{9,8},{10,11... | collective-permute-start | bytes 1179656 | tf_op jit(solution)/shard_map/ppermute | solution.py:416
  143.7 1.3 collective-permute-done.17
  145.0 0.3 shard_map.146
  145.3 25.8 %all_to_all.15.parts = bf16[64,72,128]{2,1,0:T(8,128)(2,1)S(1)} all-to-all(bf16[64,72,128]{2,1,0:T(8,128)(2,1)S(1)} %shard_map.146), channel_id=1, replica_groups=mesh['wide'=16,'x'=4,'core'=2] {'wide','x'}, dimensions={0} | all-to-all | bytes 2359296 | tf_op jit(solution)/shard_map/all_to_all | solution.py:420
  171.1 0.3 shard_map.147
  171.4 22.5 %all_to_all.16.own = bf16[64,72,128]{2,1,0:T(8,128)(2,1)S(1)} all-to-all(bf16[64,72,128]{2,1,0:T(8,128)(2,1)S(1)} %shard_map.147), channel_id=1, replica_groups=mesh['wide'=16,'x'=4,'core'=2] {'wide','x'}, dimensions={0} | all-to-all | bytes 2359296 | tf_op jit(solution)/shard_map/all_to_all | solution.py:420
  193.9 3.2 %collective-permute-start.18 = (bf16[64,72,128]{2,1,0:T(8,128)(2,1)S(1)}, bf16[64,72,128]{2,1,0:T(8,128)(2,1)S(1)}, u32[]{:S(2)}, u32[]{:S(2)}) collective-permute-start(bf16[64,72,128]{2,1,0:T(8,128)(2,1)S(1)} %all_to_all.16.own), channel_id=1, source_target_pairs={{0,1},{1,0},{2,3},{3,2},{4,5},{5,4},{6,7},{7,6},{8,9},{9,8},{10,11... | collective-permute-start | bytes 3538952 | tf_op jit(solution)/shard_map/ppermute | solution.py:416
  197.1 2.5 %collective-permute-done.18.other = bf16[64,72,128]{2,1,0:T(8,128)(2,1)S(1)} collective-permute-done((bf16[64,72,128]{2,1,0:T(8,128)(2,1)S(1)}, bf16[64,72,128]{2,1,0:T(8,128)(2,1)S(1)}, u32[]{:S(2)}, u32[]{:S(2)}) %collective-permute-start.18) | collective-permute-done | bytes 1179680 | tf_op jit(solution)/shard_map/ppermute | solution.py:416
  199.6 2.7 %shard_map.148 = (f32[227,512]{1,0:T(8,128)}, f32[2,512,512]{2,1,0:T(8,128)}, f32[2,512,512]{2,1,0:T(8,128)}) custom-call(s32[1]{0:T(128)} %bitcast.1.odd, bf16[64,72,128]{2,1,0:T(8,128)(2,1)S(1)} %all_to_all.16.own, bf16[64,72,128]{2,1,0:T(8,128)(2,1)S(1)} %collective-permute-done.18.other), custom_call_target="tpu_custom_call" | custom-call | bytes 7340032 | tf_op jit(solution)/shard_map/pallas_call | solution.py:546
  (37 shorter events, 0.1 us)
Async XLA Ops:
  6.6 11.9 %copy-start.18 = (s32[16,6]{0,1:T(8,128)S(1)}, s32[16,6]{0,1:T(8,128)}, u32[]{:S(2)}) copy-start(s32[16,6]{0,1:T(8,128)} %param.16) | copy-start | bytes 1156
  6.6 12.0 %copy-start.16 = (bf16[16,6,64,64]{3,2,1,0:T(8,128)(2,1)S(1)}, bf16[16,6,64,64]{3,2,1,0:T(8,128)(2,1)}, u32[]{:S(2)}) copy-start(bf16[16,6,64,64]{3,2,1,0:T(8,128)(2,1)} %param.17) | copy-start | bytes 2359300
  6.6 61.8 %all-to-all-start = ((bf16[128,115,128]{2,1,0:T(8,128)(2,1)}), bf16[128,115,128]{2,1,0:T(8,128)(2,1)}, u32[]{:S(2)}, u32[]{:S(2)}) async-start(bf16[128,115,128]{2,1,0:T(8,128)(2,1)} %shard_map.138), calls=%async_computation | async-start | bytes 7864320 | tf_op jit(solution)/shard_map/all_to_all | solution.py:420
  29.0 3.2 %copy-start.19 = (s32[16,8]{0,1:T(8,128)S(1)}, s32[16,8]{0,1:T(8,128)}, u32[]{:S(2)}) copy-start(s32[16,8]{0,1:T(8,128)} %param.14) | copy-start | bytes 1540
  33.5 1.2 copy-start.3
  34.7 8.5 %copy-start.17 = (bf16[2,512,512]{2,1,0:T(8,128)(2,1)S(1)}, bf16[2,512,512]{2,1,0:T(8,128)(2,1)}, u32[]{:S(2)}) copy-start(bf16[2,512,512]{2,1,0:T(8,128)(2,1)} %param.19) | copy-start | bytes 3145732
  39.1 0.7 copy-start.5
  39.8 0.7 copy-start.7
  40.5 0.7 copy-start.9
  41.2 0.7 copy-start.11
  41.9 1.3 copy-start.14
  43.2 25.2 %copy-start.2 = (s32[1,4]{1,0:T(1,128)S(1)}, s32[1,4]{1,0:T(1,128)}, u32[]{:S(2)}) copy-start(s32[1,4]{1,0:T(1,128)} %shown.7) | copy-start | bytes 52
  68.4 0.9 copy-start.13
  69.4 18.6 %copy-start.12 = (bf16[4,64,512]{2,1,0:T(8,128)(2,1)S(1)}, bf16[4,64,512]{2,1,0:T(8,128)(2,1)}, u32[]{:S(2)}) copy-start(bf16[4,64,512]{2,1,0:T(8,128)(2,1)} %copy-done.11) | copy-start | bytes 786436
  69.4 22.4 %copy-start.10 = (bf16[4,64,512]{2,1,0:T(8,128)(2,1)S(1)}, bf16[4,64,512]{2,1,0:T(8,128)(2,1)}, u32[]{:S(2)}) copy-start(bf16[4,64,512]{2,1,0:T(8,128)(2,1)} %copy-done.9) | copy-start | bytes 786436
  69.4 24.1 %copy-start.8 = (bf16[4,64,512]{2,1,0:T(8,128)(2,1)S(1)}, bf16[4,64,512]{2,1,0:T(8,128)(2,1)}, u32[]{:S(2)}) copy-start(bf16[4,64,512]{2,1,0:T(8,128)(2,1)} %copy-done.7) | copy-start | bytes 786436
  81.5 10.3 %collective-permute-start = (bf16[4,64,512]{2,1,0:T(8,128)(2,1)S(1)}, bf16[4,64,512]{2,1,0:T(8,128)(2,1)S(1)}, u32[]{:S(2)}, u32[]{:S(2)}) collective-permute-start(bf16[4,64,512]{2,1,0:T(8,128)(2,1)S(1)} %get-tuple-element.51), channel_id=1, source_target_pairs={{0,8},{8,16},{16,24},{24,32},{32,40},{40,48},{48,56},{56,64},{64,7... | collective-permute-start | bytes 786440 | tf_op jit(solution)/shard_map/ppermute | solution.py:404
  81.5 12.0 %collective-permute-start.1 = (bf16[4,64,512]{2,1,0:T(8,128)(2,1)S(1)}, bf16[4,64,512]{2,1,0:T(8,128)(2,1)S(1)}, u32[]{:S(2)}, u32[]{:S(2)}) collective-permute-start(bf16[4,64,512]{2,1,0:T(8,128)(2,1)S(1)} %get-tuple-element.51), channel_id=1, source_target_pairs={{0,120},{8,0},{16,8},{24,16},{32,24},{40,32},{48,40},{56,48},{64,5... | collective-permute-start | bytes 786440 | tf_op jit(solution)/shard_map/ppermute | solution.py:404
  86.3 13.3 %collective-permute-start.2 = (bf16[4,64,512]{2,1,0:T(8,128)(2,1)S(1)}, bf16[4,64,512]{2,1,0:T(8,128)(2,1)S(1)}, u32[]{:S(2)}, u32[]{:S(2)}) collective-permute-start(bf16[4,64,512]{2,1,0:T(8,128)(2,1)S(1)} %get-tuple-element.51), channel_id=1, source_target_pairs={{0,1},{1,2},{2,3},{3,4},{4,5},{5,6},{6,7},{7,0},{8,9},{9,10},{10,1... | collective-permute-start | bytes 786440 | tf_op jit(solution)/shard_map/ppermute | solution.py:404
  87.9 11.7 %collective-permute-start.3 = (bf16[4,64,512]{2,1,0:T(8,128)(2,1)S(1)}, bf16[4,64,512]{2,1,0:T(8,128)(2,1)S(1)}, u32[]{:S(2)}, u32[]{:S(2)}) collective-permute-start(bf16[4,64,512]{2,1,0:T(8,128)(2,1)S(1)} %get-tuple-element.51), channel_id=1, source_target_pairs={{0,7},{1,0},{2,1},{3,2},{4,3},{5,4},{6,5},{7,6},{8,15},{9,8},{10,9... | collective-permute-start | bytes 786440 | tf_op jit(solution)/shard_map/ppermute | solution.py:404
  87.9 15.8 %collective-permute-start.10 = (bf16[4,64,512]{2,1,0:T(8,128)(2,1)S(1)}, bf16[4,64,512]{2,1,0:T(8,128)(2,1)S(1)}, u32[]{:S(2)}, u32[]{:S(2)}) collective-permute-start(bf16[4,64,512]{2,1,0:T(8,128)(2,1)S(1)} %copy-done.12), channel_id=1, source_target_pairs={{0,7},{1,0},{2,1},{3,2},{4,3},{5,4},{6,5},{7,6},{8,15},{9,8},{10,9... | collective-permute-start | bytes 786440 | tf_op jit(solution)/shard_map/ppermute | solution.py:404
  91.8 16.8 %collective-permute-start.11 = (bf16[4,64,512]{2,1,0:T(8,128)(2,1)S(1)}, bf16[4,64,512]{2,1,0:T(8,128)(2,1)S(1)}, u32[]{:S(2)}, u32[]{:S(2)}) collective-permute-start(bf16[4,64,512]{2,1,0:T(8,128)(2,1)S(1)} %copy-done.10), channel_id=1, source_target_pairs={{0,1},{1,2},{2,3},{3,4},{4,5},{5,6},{6,7},{7,0},{8,9},{9,10},{10,1... | collective-permute-start | bytes 786440 | tf_op jit(solution)/shard_map/ppermute | solution.py:404
  93.5 17.9 %collective-permute-start.8 = (bf16[4,64,512]{2,1,0:T(8,128)(2,1)S(1)}, bf16[4,64,512]{2,1,0:T(8,128)(2,1)S(1)}, u32[]{:S(2)}, u32[]{:S(2)}) collective-permute-start(bf16[4,64,512]{2,1,0:T(8,128)(2,1)S(1)} %copy-done.8), channel_id=1, source_target_pairs={{0,120},{8,0},{16,8},{24,16},{32,24},{40,32},{48,40},{56,48},{64,5... | collective-permute-start | bytes 786440 | tf_op jit(solution)/shard_map/ppermute | solution.py:404
  96.3 3.3 %copy-start.6 = (bf16[4,64,512]{2,1,0:T(8,128)(2,1)S(1)}, bf16[4,64,512]{2,1,0:T(8,128)(2,1)}, u32[]{:S(2)}) copy-start(bf16[4,64,512]{2,1,0:T(8,128)(2,1)} %copy-done.5) | copy-start | bytes 786436
  96.3 3.4 %copy-start.1 = (bf16[512,512]{1,0:T(8,128)(2,1)S(1)}, bf16[512,512]{1,0:T(8,128)(2,1)}, u32[]{:S(2)}) copy-start(bf16[512,512]{1,0:T(8,128)(2,1)} %get-tuple-element.82.message) | copy-start | bytes 1572868
  99.6 11.9 %collective-permute-start.9 = (bf16[4,64,512]{2,1,0:T(8,128)(2,1)S(1)}, bf16[4,64,512]{2,1,0:T(8,128)(2,1)S(1)}, u32[]{:S(2)}, u32[]{:S(2)}) collective-permute-start(bf16[4,64,512]{2,1,0:T(8,128)(2,1)S(1)} %copy-done.6), channel_id=1, source_target_pairs={{0,8},{8,16},{16,24},{24,32},{32,40},{40,48},{48,56},{56,64},{64,7... | collective-permute-start | bytes 786440 | tf_op jit(solution)/shard_map/ppermute | solution.py:404
  99.7 11.8 %copy-start.4 = (bf16[1024,512]{1,0:T(8,128)(2,1)S(1)}, bf16[1024,512]{1,0:T(8,128)(2,1)}, u32[]{:S(2)}) copy-start(bf16[1024,512]{1,0:T(8,128)(2,1)} %cot.2) | copy-start | bytes 3145732
  99.7 11.8 %copy-start.15 = (f32[1024,512]{1,0:T(8,128)S(1)}, f32[1024,512]{1,0:T(8,128)}, u32[]{:S(2)}) copy-start(f32[1024,512]{1,0:T(8,128)} %copy-done.14) | copy-start | bytes 6291460
  103.7 15.1 %collective-permute-start.4 = (bf16[4,64,512]{2,1,0:T(8,128)(2,1)S(1)}, bf16[4,64,512]{2,1,0:T(8,128)(2,1)S(1)}, u32[]{:S(2)}, u32[]{:S(2)}) collective-permute-start(bf16[4,64,512]{2,1,0:T(8,128)(2,1)S(1)} %get-tuple-element.55), channel_id=1, source_target_pairs={{0,8},{8,16},{16,24},{24,32},{32,40},{40,48},{48,56},{56,64},{64,7... | collective-permute-start | bytes 786440 | tf_op jit(solution)/shard_map/ppermute | solution.py:404
  103.8 15.0 %collective-permute-start.5 = (bf16[4,64,512]{2,1,0:T(8,128)(2,1)S(1)}, bf16[4,64,512]{2,1,0:T(8,128)(2,1)S(1)}, u32[]{:S(2)}, u32[]{:S(2)}) collective-permute-start(bf16[4,64,512]{2,1,0:T(8,128)(2,1)S(1)} %get-tuple-element.55), channel_id=1, source_target_pairs={{0,120},{8,0},{16,8},{24,16},{32,24},{40,32},{48,40},{56,48},{64,5... | collective-permute-start | bytes 786440 | tf_op jit(solution)/shard_map/ppermute | solution.py:404
  108.6 13.5 %collective-permute-start.6 = (bf16[4,64,512]{2,1,0:T(8,128)(2,1)S(1)}, bf16[4,64,512]{2,1,0:T(8,128)(2,1)S(1)}, u32[]{:S(2)}, u32[]{:S(2)}) collective-permute-start(bf16[4,64,512]{2,1,0:T(8,128)(2,1)S(1)} %get-tuple-element.55), channel_id=1, source_target_pairs={{0,1},{1,2},{2,3},{3,4},{4,5},{5,6},{6,7},{7,0},{8,9},{9,10},{10,1... | collective-permute-start | bytes 786440 | tf_op jit(solution)/shard_map/ppermute | solution.py:404
  111.4 10.7 %collective-permute-start.7 = (bf16[4,64,512]{2,1,0:T(8,128)(2,1)S(1)}, bf16[4,64,512]{2,1,0:T(8,128)(2,1)S(1)}, u32[]{:S(2)}, u32[]{:S(2)}) collective-permute-start(bf16[4,64,512]{2,1,0:T(8,128)(2,1)S(1)} %get-tuple-element.55), channel_id=1, source_target_pairs={{0,7},{1,0},{2,1},{3,2},{4,3},{5,4},{6,5},{7,6},{8,15},{9,8},{10,9... | collective-permute-start | bytes 786440 | tf_op jit(solution)/shard_map/ppermute | solution.py:404
  117.0 11.7 %collective-permute-start.13 = (bf16[4,64,512]{2,1,0:T(8,128)(2,1)S(1)}, bf16[4,64,512]{2,1,0:T(8,128)(2,1)S(1)}, u32[]{:S(2)}, u32[]{:S(2)}) collective-permute-start(bf16[4,64,512]{2,1,0:T(8,128)(2,1)S(1)} %get-tuple-element.70), channel_id=1, source_target_pairs={{0,120},{8,0},{16,8},{24,16},{32,24},{40,32},{48,40},{56,48},{64,5... | collective-permute-start | bytes 786440 | tf_op jit(solution)/shard_map/ppermute | solution.py:404
  118.8 9.9 %collective-permute-start.14 = (bf16[4,64,512]{2,1,0:T(8,128)(2,1)S(1)}, bf16[4,64,512]{2,1,0:T(8,128)(2,1)S(1)}, u32[]{:S(2)}, u32[]{:S(2)}) collective-permute-start(bf16[4,64,512]{2,1,0:T(8,128)(2,1)S(1)} %get-tuple-element.71), channel_id=1, source_target_pairs={{0,8},{8,16},{16,24},{24,32},{32,40},{40,48},{48,56},{56,64},{64,7... | collective-permute-start | bytes 786440 | tf_op jit(solution)/shard_map/ppermute | solution.py:404
  118.8 9.9 %collective-permute-start.15 = (bf16[4,64,512]{2,1,0:T(8,128)(2,1)S(1)}, bf16[4,64,512]{2,1,0:T(8,128)(2,1)S(1)}, u32[]{:S(2)}, u32[]{:S(2)}) collective-permute-start(bf16[4,64,512]{2,1,0:T(8,128)(2,1)S(1)} %get-tuple-element.72), channel_id=1, source_target_pairs={{0,7},{1,0},{2,1},{3,2},{4,3},{5,4},{6,5},{7,6},{8,15},{9,8},{10,9... | collective-permute-start | bytes 786440 | tf_op jit(solution)/shard_map/ppermute | solution.py:404
  122.1 6.6 %collective-permute-start.16 = (bf16[4,64,512]{2,1,0:T(8,128)(2,1)S(1)}, bf16[4,64,512]{2,1,0:T(8,128)(2,1)S(1)}, u32[]{:S(2)}, u32[]{:S(2)}) collective-permute-start(bf16[4,64,512]{2,1,0:T(8,128)(2,1)S(1)} %get-tuple-element.73), channel_id=1, source_target_pairs={{0,1},{1,2},{2,3},{3,4},{4,5},{5,6},{6,7},{7,0},{8,9},{9,10},{10,1... | collective-permute-start | bytes 786440 | tf_op jit(solution)/shard_map/ppermute | solution.py:404
  122.1 6.6 %copy-start = (bf16[227,8192]{1,0:T(8,128)(2,1)S(1)}, bf16[227,8192]{1,0:T(8,128)(2,1)}, u32[]{:S(2)}) copy-start(bf16[227,8192]{1,0:T(8,128)(2,1)} %get-tuple-element.76.points) | copy-start | bytes 11157508
  128.2 16.8 %collective-permute-start.12 = (bf16[3072,128]{1,0:T(8,128)(2,1)S(1)}, bf16[3072,128]{1,0:T(8,128)(2,1)S(1)}, u32[]{:S(2)}, u32[]{:S(2)}) collective-permute-start(bf16[3072,128]{1,0:T(8,128)(2,1)S(1)} %get-tuple-element.68), channel_id=1, source_target_pairs={{0,1},{1,0},{2,3},{3,2},{4,5},{5,4},{6,7},{7,6},{8,9},{9,8},{10,11... | collective-permute-start | bytes 2359304 | tf_op jit(solution)/shard_map/ppermute | solution.py:416
  140.6 4.4 %collective-permute-start.17 = (bf16[1536,128]{1,0:T(8,128)(2,1)S(1)}, bf16[1536,128]{1,0:T(8,128)(2,1)S(1)}, u32[]{:S(2)}, u32[]{:S(2)}) collective-permute-start(bf16[1536,128]{1,0:T(8,128)(2,1)S(1)} %get-tuple-element.78), channel_id=1, source_target_pairs={{0,1},{1,0},{2,3},{3,2},{4,5},{5,4},{6,7},{7,6},{8,9},{9,8},{10,11... | collective-permute-start | bytes 1179656 | tf_op jit(solution)/shard_map/ppermute | solution.py:416
  193.9 5.7 %collective-permute-start.18 = (bf16[64,72,128]{2,1,0:T(8,128)(2,1)S(1)}, bf16[64,72,128]{2,1,0:T(8,128)(2,1)S(1)}, u32[]{:S(2)}, u32[]{:S(2)}) collective-permute-start(bf16[64,72,128]{2,1,0:T(8,128)(2,1)S(1)} %all_to_all.16.own), channel_id=1, source_target_pairs={{0,1},{1,0},{2,3},{3,2},{4,5},{5,4},{6,7},{7,6},{8,9},{9,8},{10,11... | collective-permute-start | bytes 3538952 | tf_op jit(solution)/shard_map/ppermute | solution.py:416

commit v8 on v7

--- a/solution.py
+++ b/solution.py
@@ -457,7 +457,9 @@
     )(mesh_src, cotangent, w_u[1], m_mix)
     returned_1 = give_back(*halos)
 
-    received, g_mix, m_mix, own_1 = lax.optimization_barrier((received, g_mix, m_mix, own_1))
+    received, g_mix, m_mix, *returned_1 = lax.optimization_barrier(
+        (received, g_mix, m_mix, *returned_1)
+    )
     whole = lambda *shape: pl.BlockSpec(shape, lambda i: (0,) * len(shape))
     points, slope, embedded, mine_0 = pl.pallas_call(
         encode_body,

time: 203 us -> 198 us (0.975)
  local copies, waits for them, and re-layouts: 22.2 us -> 17.9 us
  starting transfers between devices: 45.3 us -> 42.8 us
    ppermute x16, waiting for transfers between devices: 1.1 us -> 26.3 us  [shift(): lax.ppermute(value, axis, [(i, (i + steps) % count) for i in range(count)])]
    all_to_all x1, waiting for transfers between devices: 24.3 us -> 0.01 us  [exchange(): return lax.all_to_all(parts, axes, split_axis=0, concat_axis=0, tiled=True)]
    unnamed x42 -> x26, local copies, waits for them, and re-layouts: 6.5 us -> 2.45 us
  transfers between devices with their start and end apart: 20 -> 20, of which waited for: 4 -> 5; matrix products, arithmetic and copies ran while one was open for 8% -> 8% of each run, Pallas kernels for 17% -> 16%
where the time goes in v8:
time: 198 us; the launch traced here: 197 us
  Pallas kernels  57.5 us (29%)
  blocking collectives  48.1 us (24%)
  starting transfers between devices  42.8 us (22%)
  waiting for transfers between devices  30.1 us (15%)
  local copies, waits for them, and re-layouts  17.9 us (9%)
    all_to_all x2, blocking collectives, exchange(): return lax.all_to_all(parts, axes, split_axis=0, concat_axis=0, tiled=True)  48.1 us
    ppermute x16, waiting for transfers between devices, shift(): lax.ppermute(value, axis, [(i, (i + steps) % count) for i in range(count)])  26.3 us
    ppermute x16, starting transfers between devices, shift(): lax.ppermute(value, axis, [(i, (i + steps) % count) for i in range(count)])  25.3 us
    pallas_call x1, Pallas kernels, on_device(): pl.pallas_call(encode_body, grid=(4,), out_shape=[pltpu.HBM((CHAN, GRID_R...  12.1 us
    all_to_all x1, starting transfers between devices, exchange(): return lax.all_to_all(parts, axes, split_axis=0, concat_axis=0, tiled=True)  11.9 us
    pallas_call x1, Pallas kernels, on_device(): pl.pallas_call(final_body, grid=(4,), out_shape=[jax.ShapeDtypeStruct((SL...  11.9 us
    pallas_call x1, Pallas kernels, on_device(): kernel_call(grads_body, [rows_bf16, ((3 * SLABS, 128), BF16), ((3 * SLABS...  6.05 us
    pallas_call x1, Pallas kernels, on_device(): kernel_call(backward_body, [rows_bf16, rows_f32, rows_f32] + [halo] * 4,...  6.02 us
  transfers between devices with their start and end apart: 20, of which 5 were waited for; matrix products, arithmetic and copies ran while one was open for 8% of the time, Pallas kernels for 16%

profile of v8, /device:TPU:1, one launch (start us, length us, event | category | flops | bytes accessed | tf_op | source)
XLA Modules:
  0.0 197.2 jit_solution(12463624739044807593)
XLA Ops:
  0.6 5.9 %shard_map.138 = bf16[128,115,128]{2,1,0:T(8,128)(2,1)} custom-call(s32[1,128]{1,0:T(1,128)} %send.1, bf16[227,8192]{1,0:T(8,128)(2,1)} %bitcast.22), custom_call_target="tpu_custom_call" | custom-call | bytes 8388608 | tf_op jit(solution)/shard_map/pallas_call | solution.py:438
  6.6 11.9 %all-to-all-start = ((bf16[128,115,128]{2,1,0:T(8,128)(2,1)}), bf16[128,115,128]{2,1,0:T(8,128)(2,1)}, u32[]{:S(2)}, u32[]{:S(2)}) async-start(bf16[128,115,128]{2,1,0:T(8,128)(2,1)} %shard_map.138), calls=%async_computation | async-start | bytes 7864320 | tf_op jit(solution)/shard_map/all_to_all | solution.py:420
  18.5 0.1 copy.31.source
  18.6 2.6 %copy.25 = bf16[16,64,6,64]{3,2,1,0:T(8,128)(2,1)} copy(bf16[16,64,6,64]{3,1,2,0:T(8,128)(2,1)S(1)} %bitcast.24) | data formatting | bytes 1572864 | tf_op jit(solution)/shard_map/transpose | solution.py:452
  21.2 3.1 %reshape.31.coeffs = bf16[16,64,384]{2,1,0:T(8,128)(2,1)S(1)} reshape(bf16[16,64,6,64]{3,2,1,0:T(8,128)(2,1)} %copy.25) | data formatting | bytes 1572864 | tf_op jit(solution)/shard_map/reshape | solution.py:452
  24.3 1.3 slice_bitcast_fusion.1
  25.6 0.0 copy-start.8
  25.6 5.1 %shard_map.139 = (f32[1024,512]{1,0:T(8,128)S(1)}, bf16[4,64,512]{2,1,0:T(8,128)(2,1)}, bf16[4,64,512]{2,1,0:T(8,128)(2,1)}, bf16[4,64,512]{2,1,0:T(8,128)(2,1)}, bf16[4,64,512]{2,1,0:T(8,128)(2,1)}) custom-call(s32[16,6]{1,0:T(8,128)S(1)} %copy.31.source, bf16[1024,512]{1,0:T(8,128)(2,1)S(1)} %copy-done.3, bf16[512,512]{1,0:T(8,128)(2,1)S(1)} %get-tuple-element.91.up, ...), custom_call_target="tpu_custom_call" | custom-call | flops 2000000000 | bytes 8388608 | tf_op jit(solution)/shard_map/pallas_call | solution.py:454
  30.7 1.3 copy-done.6
  32.0 5.6 %collective-permute-start = (bf16[4,64,512]{2,1,0:T(8,128)(2,1)}, bf16[4,64,512]{2,1,0:T(8,128)(2,1)}, u32[]{:S(2)}, u32[]{:S(2)}) collective-permute-start(bf16[4,64,512]{2,1,0:T(8,128)(2,1)} %get-tuple-element.49), channel_id=1, source_target_pairs={{0,120},{8,0},{16,8},{24,16},{32,24},{40,32},{48,40},{56,48},{64,5... | collective-permute-start | bytes 786440 | tf_op jit(solution)/shard_map/ppermute | solution.py:404
  37.6 0.0 collective-permute-start.1
  37.6 0.6 collective-permute-start.2
  38.2 1.1 collective-permute-start.3
  39.3 3.1 %copy.24 = bf16[16,64,8,64]{3,2,1,0:T(8,128)(2,1)} copy(bf16[16,64,8,64]{3,1,2,0:T(8,128)(2,1)S(1)} %bitcast.23) | data formatting | bytes 2097152 | tf_op jit(solution)/shard_map/transpose | solution.py:451
  42.5 3.2 %reshape.30.coeffs = bf16[16,64,512]{2,1,0:T(8,128)(2,1)S(1)} reshape(bf16[16,64,8,64]{3,2,1,0:T(8,128)(2,1)} %copy.24) | data formatting | bytes 2097152 | tf_op jit(solution)/shard_map/reshape | solution.py:451
  45.7 0.1 copy.28.source
  45.8 2.1 %slice_bitcast_fusion = (bf16[512,512]{1,0:T(8,128)(2,1)}, bf16[512,512]{1,0:T(8,128)(2,1)S(1)}) fusion(bf16[2,512,512]{2,1,0:T(8,128)(2,1)} %param.19), kind=kLoop, calls=%fused_computation | loop fusion | bytes 2097152 | tf_op jit(solution)/shard_map/squeeze | solution.py:435
  47.8 19.6 %collective-permute-done.r0 = bf16[4,64,512]{2,1,0:T(8,128)(2,1)} collective-permute-done((bf16[4,64,512]{2,1,0:T(8,128)(2,1)}, bf16[4,64,512]{2,1,0:T(8,128)(2,1)}, u32[]{:S(2)}, u32[]{:S(2)}) %collective-permute-start) | collective-permute-done | bytes 262176 | tf_op jit(solution)/shard_map/ppermute | solution.py:404
  67.4 4.2 %collective-permute-done.1.r1 = bf16[4,64,512]{2,1,0:T(8,128)(2,1)} collective-permute-done((bf16[4,64,512]{2,1,0:T(8,128)(2,1)}, bf16[4,64,512]{2,1,0:T(8,128)(2,1)}, u32[]{:S(2)}, u32[]{:S(2)}) %collective-permute-start.1) | collective-permute-done | bytes 262176 | tf_op jit(solution)/shard_map/ppermute | solution.py:404
  71.6 0.0 collective-permute-done.2.r2
  71.6 0.0 collective-permute-done.3.r3
  71.6 0.0 all-to-all-done.packed
  71.6 0.0 copy-start.5
  71.6 0.9 copy-done.5
  72.6 12.1 %shard_map.140 = (bf16[227,8192]{1,0:T(8,128)(2,1)}, bf16[8192,512]{1,0:T(8,128)(2,1)}, bf16[8192,512]{1,0:T(8,128)(2,1)S(1)}, bf16[4,64,512]{2,1,0:T(8,128)(2,1)S(1)}) custom-call(s32[16,8]{1,0:T(8,128)S(1)} %copy.28.source, s32[1,4]{1,0:T(1,128)S(1)} %copy-done.2, bf16[128,115,128]{2,1,0:T(8,128)(2,1)} %all-to-all-done.packed, ...), custom_call_target="tpu_custom_call" | custom-call | flops 4000000000 | bytes 27262976 | tf_op jit(solution)/shard_map/pallas_call | solution.py:464
  84.7 0.0 collective-permute-start.4
  84.7 4.8 %collective-permute-start.5 = (bf16[4,64,512]{2,1,0:T(8,128)(2,1)S(1)}, bf16[4,64,512]{2,1,0:T(8,128)(2,1)S(1)}, u32[]{:S(2)}, u32[]{:S(2)}) collective-permute-start(bf16[4,64,512]{2,1,0:T(8,128)(2,1)S(1)} %get-tuple-element.57), channel_id=1, source_target_pairs={{0,120},{8,0},{16,8},{24,16},{32,24},{40,32},{48,40},{56,48},{64,5... | collective-permute-start | bytes 786440 | tf_op jit(solution)/shard_map/ppermute | solution.py:404
  89.4 2.8 %collective-permute-start.6 = (bf16[4,64,512]{2,1,0:T(8,128)(2,1)S(1)}, bf16[4,64,512]{2,1,0:T(8,128)(2,1)S(1)}, u32[]{:S(2)}, u32[]{:S(2)}) collective-permute-start(bf16[4,64,512]{2,1,0:T(8,128)(2,1)S(1)} %get-tuple-element.57), channel_id=1, source_target_pairs={{0,1},{1,2},{2,3},{3,4},{4,5},{5,6},{6,7},{7,0},{8,9},{9,10},{10,1... | collective-permute-start | bytes 786440 | tf_op jit(solution)/shard_map/ppermute | solution.py:404
  92.3 0.0 collective-permute-start.7
  92.3 3.3 %shard_map.141 = (bf16[1024,512]{1,0:T(8,128)(2,1)S(1)}, bf16[1024,512]{1,0:T(8,128)(2,1)S(1)}, bf16[1024,512]{1,0:T(8,128)(2,1)S(1)}) custom-call(s32[16,8]{1,0:T(8,128)S(1)} %copy.28.source, bf16[8192,512]{1,0:T(8,128)(2,1)S(1)} %get-tuple-element.55.embedded, bf16[16,64,512]{2,1,0:T(8,128)(2,1)S(1)} %reshape.30.coeffs, ...), custom_call_target="tpu_custom_call" | custom-call | flops 2000000000 | bytes 12582912 | tf_op jit(solution)/shard_map/pallas_call | solution.py:491
  95.6 0.0 collective-permute-done.4.n0
  95.6 0.0 collective-permute-done.5.n1
  95.6 0.0 collective-permute-done.6.n2
  95.6 2.5 %collective-permute-done.7.n3 = bf16[4,64,512]{2,1,0:T(8,128)(2,1)S(1)} collective-permute-done((bf16[4,64,512]{2,1,0:T(8,128)(2,1)S(1)}, bf16[4,64,512]{2,1,0:T(8,128)(2,1)S(1)}, u32[]{:S(2)}, u32[]{:S(2)}) %collective-permute-start.7) | collective-permute-done | bytes 262176 | tf_op jit(solution)/shard_map/ppermute | solution.py:404
  98.1 3.9 %shard_map.142 = (bf16[1024,512]{1,0:T(8,128)(2,1)S(1)}, bf16[1024,512]{1,0:T(8,128)(2,1)S(1)}, bf16[1024,512]{1,0:T(8,128)(2,1)S(1)}, bf16[1024,512]{1,0:T(8,128)(2,1)S(1)}, bf16[4,64,512]{2,1,0:T(8,128)(2,1)S(1)}) custom-call(s32[16,6]{1,0:T(8,128)S(1)} %copy.31.source, s32[1,4]{1,0:T(1,128)S(1)} %copy-done.2, ...), custom_call_target="tpu_custom_call" | custom-call | flops 2000000000 | bytes 10485760 | tf_op jit(solution)/shard_map/pallas_call | solution.py:495
  102.0 0.3 collective-permute-start.10
  102.4 0.2 collective-permute-start.11
  102.6 0.0 collective-permute-start.8
  102.6 4.8 %collective-permute-start.9 = (bf16[4,64,512]{2,1,0:T(8,128)(2,1)S(1)}, bf16[4,64,512]{2,1,0:T(8,128)(2,1)S(1)}, u32[]{:S(2)}, u32[]{:S(2)}) collective-permute-start(bf16[4,64,512]{2,1,0:T(8,128)(2,1)S(1)} %get-tuple-element.61), channel_id=1, source_target_pairs={{0,120},{8,0},{16,8},{24,16},{32,24},{40,32},{48,40},{56,48},{64,5... | collective-permute-start | bytes 786440 | tf_op jit(solution)/shard_map/ppermute | solution.py:404
  107.3 6.0 %shard_map.143 = (bf16[1024,512]{1,0:T(8,128)(2,1)S(1)}, f32[1024,512]{1,0:T(8,128)S(1)}, f32[1024,512]{1,0:T(8,128)S(1)}, bf16[4,64,512]{2,1,0:T(8,128)(2,1)S(1...) custom-call(s32[16,6]{1,0:T(8,128)S(1)} %copy.31.source, ...), custom_call_target="tpu_custom_call" | custom-call | flops 2000000000 | bytes 16777216 | tf_op jit(solution)/shard_map/pallas_call | solution.py:501
  113.4 1.4 collective-permute-start.13
  114.7 0.0 collective-permute-done.10.n2
  114.7 0.2 collective-permute-start.14
  114.9 0.0 collective-permute-done.11.n3
  114.9 3.6 %collective-permute-start.15 = (bf16[4,64,512]{2,1,0:T(8,128)(2,1)S(1)}, bf16[4,64,512]{2,1,0:T(8,128)(2,1)S(1)}, u32[]{:S(2)}, u32[]{:S(2)}) collective-permute-start(bf16[4,64,512]{2,1,0:T(8,128)(2,1)S(1)} %get-tuple-element.78), channel_id=1, source_target_pairs={{0,7},{1,0},{2,1},{3,2},{4,3},{5,4},{6,5},{7,6},{8,15},{9,8},{10,9... | collective-permute-start | bytes 786440 | tf_op jit(solution)/shard_map/ppermute | solution.py:404
  118.5 0.0 collective-permute-done.8.n0
  118.5 0.0 collective-permute-start.16
  118.5 0.0 collective-permute-done.9.n1
  118.5 6.0 %shard_map.144 = (bf16[1024,512]{1,0:T(8,128)(2,1)}, bf16[3072,128]{1,0:T(8,128)(2,1)S(1)}, bf16[3072,128]{1,0:T(8,128)(2,1)S(1)}) custom-call(s32[1]{0:T(128)} %bitcast.1.odd, s32[16,6]{1,0:T(8,128)S(1)} %copy.31.source, bf16[1024,512]{1,0:T(8,128)(2,1)S(1)} %get-tuple-element.60.sent, bf16[4,64,512]{2,1,0:T(8,128)(2,1)S(1)} %collective-permute-done.8.n0, ...), custom_call_target="tpu_custom_call" | custom-call | flops 4000000000 | bytes 14680064 | tf_op jit(solution)/shard_map/pallas_call | solution.py:507
  124.5 0.5 collective-permute-start.12
  125.1 0.0 collective-permute-done.13.r0
  125.1 0.0 collective-permute-done.14.r1
  125.1 0.0 collective-permute-done.16.r3
  125.1 11.9 %shard_map.145 = (bf16[1536,128]{1,0:T(8,128)(2,1)S(1)}, bf16[1536,128]{1,0:T(8,128)(2,1)S(1)}) custom-call(s32[1]{0:T(128)} %bitcast.1.odd, s32[16,8]{1,0:T(8,128)S(1)} %copy.28.source, s32[1,4]{1,0:T(1,128)S(1)} %copy-done.2, f32[1024,512]{1,0:T(8,128)S(1)} %get-tuple-element.75.own, bf16[4,64,512]{2,1,0:T(8,128)(2,1)S(1)} %collective-permute-done.13.r0, ...), custom_call_target="tpu_custom_call" | custom-call | flops 4000000000 | bytes 25165824 | tf_op jit(solution)/shard_map/pallas_call | solution.py:517
  137.0 1.8 collective-permute-start.17
  138.7 1.3 collective-permute-done.17
  140.1 0.0 collective-permute-done.12
  140.1 0.3 shard_map.146
  140.4 25.6 %all_to_all.15.parts = bf16[64,72,128]{2,1,0:T(8,128)(2,1)S(1)} all-to-all(bf16[64,72,128]{2,1,0:T(8,128)(2,1)S(1)} %shard_map.146), channel_id=1, replica_groups=mesh['wide'=16,'x'=4,'core'=2] {'wide','x'}, dimensions={0} | all-to-all | bytes 2359296 | tf_op jit(solution)/shard_map/all_to_all | solution.py:420
  166.0 0.3 shard_map.147
  166.3 22.5 %all_to_all.16.own = bf16[64,72,128]{2,1,0:T(8,128)(2,1)S(1)} all-to-all(bf16[64,72,128]{2,1,0:T(8,128)(2,1)S(1)} %shard_map.147), channel_id=1, replica_groups=mesh['wide'=16,'x'=4,'core'=2] {'wide','x'}, dimensions={0} | all-to-all | bytes 2359296 | tf_op jit(solution)/shard_map/all_to_all | solution.py:420
  188.8 3.2 %collective-permute-start.18 = (bf16[64,72,128]{2,1,0:T(8,128)(2,1)S(1)}, bf16[64,72,128]{2,1,0:T(8,128)(2,1)S(1)}, u32[]{:S(2)}, u32[]{:S(2)}) collective-permute-start(bf16[64,72,128]{2,1,0:T(8,128)(2,1)S(1)} %all_to_all.16.own), channel_id=1, source_target_pairs={{0,1},{1,0},{2,3},{3,2},{4,5},{5,4},{6,7},{7,6},{8,9},{9,8},{10,11... | collective-permute-start | bytes 3538952 | tf_op jit(solution)/shard_map/ppermute | solution.py:416
  192.0 2.5 %collective-permute-done.18.other = bf16[64,72,128]{2,1,0:T(8,128)(2,1)S(1)} collective-permute-done((bf16[64,72,128]{2,1,0:T(8,128)(2,1)S(1)}, bf16[64,72,128]{2,1,0:T(8,128)(2,1)S(1)}, u32[]{:S(2)}, u32[]{:S(2)}) %collective-permute-start.18) | collective-permute-done | bytes 1179680 | tf_op jit(solution)/shard_map/ppermute | solution.py:416
  194.5 2.7 %shard_map.148 = (f32[227,512]{1,0:T(8,128)}, f32[2,512,512]{2,1,0:T(8,128)}, f32[2,512,512]{2,1,0:T(8,128)}) custom-call(s32[1]{0:T(128)} %bitcast.1.odd, bf16[64,72,128]{2,1,0:T(8,128)(2,1)S(1)} %all_to_all.16.own, bf16[64,72,128]{2,1,0:T(8,128)(2,1)S(1)} %collective-permute-done.18.other), custom_call_target="tpu_custom_call" | custom-call | bytes 7340032 | tf_op jit(solution)/shard_map/pallas_call | solution.py:548
  (21 shorter events, 0.0 us)
Async XLA Ops:
  6.6 11.9 %copy-start.10 = (s32[16,6]{0,1:T(8,128)S(1)}, s32[16,6]{0,1:T(8,128)}, u32[]{:S(2)}) copy-start(s32[16,6]{0,1:T(8,128)} %param.16) | copy-start | bytes 1156
  6.6 12.0 %copy-start.9 = (bf16[16,6,64,64]{3,2,1,0:T(8,128)(2,1)S(1)}, bf16[16,6,64,64]{3,2,1,0:T(8,128)(2,1)}, u32[]{:S(2)}) copy-start(bf16[16,6,64,64]{3,2,1,0:T(8,128)(2,1)} %param.17) | copy-start | bytes 2359300
  6.6 65.1 %all-to-all-start = ((bf16[128,115,128]{2,1,0:T(8,128)(2,1)}), bf16[128,115,128]{2,1,0:T(8,128)(2,1)}, u32[]{:S(2)}, u32[]{:S(2)}) async-start(bf16[128,115,128]{2,1,0:T(8,128)(2,1)} %shard_map.138), calls=%async_computation | async-start | bytes 7864320 | tf_op jit(solution)/shard_map/all_to_all | solution.py:420
  21.2 4.4 %copy-start.3 = (bf16[1024,512]{1,0:T(8,128)(2,1)S(1)}, bf16[1024,512]{1,0:T(8,128)(2,1)}, u32[]{:S(2)}) copy-start(bf16[1024,512]{1,0:T(8,128)(2,1)} %cot.2) | copy-start | bytes 3145732
  25.6 13.7 %copy-start.8 = (bf16[16,8,64,64]{3,2,1,0:T(8,128)(2,1)S(1)}, bf16[16,8,64,64]{3,2,1,0:T(8,128)(2,1)}, u32[]{:S(2)}) copy-start(bf16[16,8,64,64]{3,2,1,0:T(8,128)(2,1)} %param.15) | copy-start | bytes 3145732
  30.7 1.3 copy-start.6
  32.0 35.4 %collective-permute-start = (bf16[4,64,512]{2,1,0:T(8,128)(2,1)}, bf16[4,64,512]{2,1,0:T(8,128)(2,1)}, u32[]{:S(2)}, u32[]{:S(2)}) collective-permute-start(bf16[4,64,512]{2,1,0:T(8,128)(2,1)} %get-tuple-element.49), channel_id=1, source_target_pairs={{0,120},{8,0},{16,8},{24,16},{32,24},{40,32},{48,40},{56,48},{64,5... | collective-permute-start | bytes 786440 | tf_op jit(solution)/shard_map/ppermute | solution.py:404
  37.6 34.0 %collective-permute-start.1 = (bf16[4,64,512]{2,1,0:T(8,128)(2,1)}, bf16[4,64,512]{2,1,0:T(8,128)(2,1)}, u32[]{:S(2)}, u32[]{:S(2)}) collective-permute-start(bf16[4,64,512]{2,1,0:T(8,128)(2,1)} %get-tuple-element.50), channel_id=1, source_target_pairs={{0,8},{8,16},{16,24},{24,32},{32,40},{40,48},{48,56},{56,64},{64,7... | collective-permute-start | bytes 786440 | tf_op jit(solution)/shard_map/ppermute | solution.py:404
  37.6 34.0 %collective-permute-start.2 = (bf16[4,64,512]{2,1,0:T(8,128)(2,1)}, bf16[4,64,512]{2,1,0:T(8,128)(2,1)}, u32[]{:S(2)}, u32[]{:S(2)}) collective-permute-start(bf16[4,64,512]{2,1,0:T(8,128)(2,1)} %get-tuple-element.51), channel_id=1, source_target_pairs={{0,7},{1,0},{2,1},{3,2},{4,3},{5,4},{6,5},{7,6},{8,15},{9,8},{10,9... | collective-permute-start | bytes 786440 | tf_op jit(solution)/shard_map/ppermute | solution.py:404
  38.2 33.4 %collective-permute-start.3 = (bf16[4,64,512]{2,1,0:T(8,128)(2,1)}, bf16[4,64,512]{2,1,0:T(8,128)(2,1)}, u32[]{:S(2)}, u32[]{:S(2)}) collective-permute-start(bf16[4,64,512]{2,1,0:T(8,128)(2,1)} %get-tuple-element.52), channel_id=1, source_target_pairs={{0,1},{1,2},{2,3},{3,4},{4,5},{5,6},{6,7},{7,0},{8,9},{9,10},{10,1... | collective-permute-start | bytes 786440 | tf_op jit(solution)/shard_map/ppermute | solution.py:404
  42.5 3.2 %copy-start.11 = (s32[16,8]{0,1:T(8,128)S(1)}, s32[16,8]{0,1:T(8,128)}, u32[]{:S(2)}) copy-start(s32[16,8]{0,1:T(8,128)} %param.14) | copy-start | bytes 1540
  42.5 29.2 %copy-start.2 = (s32[1,4]{1,0:T(1,128)S(1)}, s32[1,4]{1,0:T(1,128)}, u32[]{:S(2)}) copy-start(s32[1,4]{1,0:T(1,128)} %shown.7) | copy-start | bytes 52
  71.6 0.9 copy-start.5
  84.7 10.9 %collective-permute-start.4 = (bf16[4,64,512]{2,1,0:T(8,128)(2,1)S(1)}, bf16[4,64,512]{2,1,0:T(8,128)(2,1)S(1)}, u32[]{:S(2)}, u32[]{:S(2)}) collective-permute-start(bf16[4,64,512]{2,1,0:T(8,128)(2,1)S(1)} %get-tuple-element.57), channel_id=1, source_target_pairs={{0,8},{8,16},{16,24},{24,32},{32,40},{40,48},{48,56},{56,64},{64,7... | collective-permute-start | bytes 786440 | tf_op jit(solution)/shard_map/ppermute | solution.py:404
  84.7 10.9 %collective-permute-start.5 = (bf16[4,64,512]{2,1,0:T(8,128)(2,1)S(1)}, bf16[4,64,512]{2,1,0:T(8,128)(2,1)S(1)}, u32[]{:S(2)}, u32[]{:S(2)}) collective-permute-start(bf16[4,64,512]{2,1,0:T(8,128)(2,1)S(1)} %get-tuple-element.57), channel_id=1, source_target_pairs={{0,120},{8,0},{16,8},{24,16},{32,24},{40,32},{48,40},{56,48},{64,5... | collective-permute-start | bytes 786440 | tf_op jit(solution)/shard_map/ppermute | solution.py:404
  89.4 6.2 %collective-permute-start.6 = (bf16[4,64,512]{2,1,0:T(8,128)(2,1)S(1)}, bf16[4,64,512]{2,1,0:T(8,128)(2,1)S(1)}, u32[]{:S(2)}, u32[]{:S(2)}) collective-permute-start(bf16[4,64,512]{2,1,0:T(8,128)(2,1)S(1)} %get-tuple-element.57), channel_id=1, source_target_pairs={{0,1},{1,2},{2,3},{3,4},{4,5},{5,6},{6,7},{7,0},{8,9},{9,10},{10,1... | collective-permute-start | bytes 786440 | tf_op jit(solution)/shard_map/ppermute | solution.py:404
  92.3 5.8 %collective-permute-start.7 = (bf16[4,64,512]{2,1,0:T(8,128)(2,1)S(1)}, bf16[4,64,512]{2,1,0:T(8,128)(2,1)S(1)}, u32[]{:S(2)}, u32[]{:S(2)}) collective-permute-start(bf16[4,64,512]{2,1,0:T(8,128)(2,1)S(1)} %get-tuple-element.57), channel_id=1, source_target_pairs={{0,7},{1,0},{2,1},{3,2},{4,3},{5,4},{6,5},{7,6},{8,15},{9,8},{10,9... | collective-permute-start | bytes 786440 | tf_op jit(solution)/shard_map/ppermute | solution.py:404
  92.3 5.8 %copy-start.1 = (bf16[512,512]{1,0:T(8,128)(2,1)S(1)}, bf16[512,512]{1,0:T(8,128)(2,1)}, u32[]{:S(2)}) copy-start(bf16[512,512]{1,0:T(8,128)(2,1)} %get-tuple-element.88.message) | copy-start | bytes 1572868
  98.1 9.3 %copy-start.4 = (bf16[1024,512]{1,0:T(8,128)(2,1)S(1)}, bf16[1024,512]{1,0:T(8,128)(2,1)}, u32[]{:S(2)}) copy-start(bf16[1024,512]{1,0:T(8,128)(2,1)} %cot.2) | copy-start | bytes 3145732
  98.1 9.3 %copy-start.7 = (f32[1024,512]{1,0:T(8,128)S(1)}, f32[1024,512]{1,0:T(8,128)}, u32[]{:S(2)}) copy-start(f32[1024,512]{1,0:T(8,128)} %copy-done.6) | copy-start | bytes 6291460
  102.0 12.7 %collective-permute-start.10 = (bf16[4,64,512]{2,1,0:T(8,128)(2,1)S(1)}, bf16[4,64,512]{2,1,0:T(8,128)(2,1)S(1)}, u32[]{:S(2)}, u32[]{:S(2)}) collective-permute-start(bf16[4,64,512]{2,1,0:T(8,128)(2,1)S(1)} %get-tuple-element.61), channel_id=1, source_target_pairs={{0,1},{1,2},{2,3},{3,4},{4,5},{5,6},{6,7},{7,0},{8,9},{9,10},{10,1... | collective-permute-start | bytes 786440 | tf_op jit(solution)/shard_map/ppermute | solution.py:404
  102.4 12.5 %collective-permute-start.11 = (bf16[4,64,512]{2,1,0:T(8,128)(2,1)S(1)}, bf16[4,64,512]{2,1,0:T(8,128)(2,1)S(1)}, u32[]{:S(2)}, u32[]{:S(2)}) collective-permute-start(bf16[4,64,512]{2,1,0:T(8,128)(2,1)S(1)} %get-tuple-element.61), channel_id=1, source_target_pairs={{0,7},{1,0},{2,1},{3,2},{4,3},{5,4},{6,5},{7,6},{8,15},{9,8},{10,9... | collective-permute-start | bytes 786440 | tf_op jit(solution)/shard_map/ppermute | solution.py:404
  102.6 15.9 %collective-permute-start.8 = (bf16[4,64,512]{2,1,0:T(8,128)(2,1)S(1)}, bf16[4,64,512]{2,1,0:T(8,128)(2,1)S(1)}, u32[]{:S(2)}, u32[]{:S(2)}) collective-permute-start(bf16[4,64,512]{2,1,0:T(8,128)(2,1)S(1)} %get-tuple-element.61), channel_id=1, source_target_pairs={{0,8},{8,16},{16,24},{24,32},{32,40},{40,48},{48,56},{56,64},{64,7... | collective-permute-start | bytes 786440 | tf_op jit(solution)/shard_map/ppermute | solution.py:404
  102.6 15.9 %collective-permute-start.9 = (bf16[4,64,512]{2,1,0:T(8,128)(2,1)S(1)}, bf16[4,64,512]{2,1,0:T(8,128)(2,1)S(1)}, u32[]{:S(2)}, u32[]{:S(2)}) collective-permute-start(bf16[4,64,512]{2,1,0:T(8,128)(2,1)S(1)} %get-tuple-element.61), channel_id=1, source_target_pairs={{0,120},{8,0},{16,8},{24,16},{32,24},{40,32},{48,40},{56,48},{64,5... | collective-permute-start | bytes 786440 | tf_op jit(solution)/shard_map/ppermute | solution.py:404
  113.4 11.7 %collective-permute-start.13 = (bf16[4,64,512]{2,1,0:T(8,128)(2,1)S(1)}, bf16[4,64,512]{2,1,0:T(8,128)(2,1)S(1)}, u32[]{:S(2)}, u32[]{:S(2)}) collective-permute-start(bf16[4,64,512]{2,1,0:T(8,128)(2,1)S(1)} %get-tuple-element.76), channel_id=1, source_target_pairs={{0,120},{8,0},{16,8},{24,16},{32,24},{40,32},{48,40},{56,48},{64,5... | collective-permute-start | bytes 786440 | tf_op jit(solution)/shard_map/ppermute | solution.py:404
  114.7 10.3 %collective-permute-start.14 = (bf16[4,64,512]{2,1,0:T(8,128)(2,1)S(1)}, bf16[4,64,512]{2,1,0:T(8,128)(2,1)S(1)}, u32[]{:S(2)}, u32[]{:S(2)}) collective-permute-start(bf16[4,64,512]{2,1,0:T(8,128)(2,1)S(1)} %get-tuple-element.77), channel_id=1, source_target_pairs={{0,8},{8,16},{16,24},{24,32},{32,40},{40,48},{48,56},{56,64},{64,7... | collective-permute-start | bytes 786440 | tf_op jit(solution)/shard_map/ppermute | solution.py:404
  114.9 10.2 %collective-permute-start.15 = (bf16[4,64,512]{2,1,0:T(8,128)(2,1)S(1)}, bf16[4,64,512]{2,1,0:T(8,128)(2,1)S(1)}, u32[]{:S(2)}, u32[]{:S(2)}) collective-permute-start(bf16[4,64,512]{2,1,0:T(8,128)(2,1)S(1)} %get-tuple-element.78), channel_id=1, source_target_pairs={{0,7},{1,0},{2,1},{3,2},{4,3},{5,4},{6,5},{7,6},{8,15},{9,8},{10,9... | collective-permute-start | bytes 786440 | tf_op jit(solution)/shard_map/ppermute | solution.py:404
  118.5 6.6 %collective-permute-start.16 = (bf16[4,64,512]{2,1,0:T(8,128)(2,1)S(1)}, bf16[4,64,512]{2,1,0:T(8,128)(2,1)S(1)}, u32[]{:S(2)}, u32[]{:S(2)}) collective-permute-start(bf16[4,64,512]{2,1,0:T(8,128)(2,1)S(1)} %get-tuple-element.79), channel_id=1, source_target_pairs={{0,1},{1,2},{2,3},{3,4},{4,5},{5,6},{6,7},{7,0},{8,9},{9,10},{10,1... | collective-permute-start | bytes 786440 | tf_op jit(solution)/shard_map/ppermute | solution.py:404
  118.5 6.6 %copy-start = (bf16[227,8192]{1,0:T(8,128)(2,1)S(1)}, bf16[227,8192]{1,0:T(8,128)(2,1)}, u32[]{:S(2)}) copy-start(bf16[227,8192]{1,0:T(8,128)(2,1)} %get-tuple-element.82.points) | copy-start | bytes 11157508
  124.5 15.5 %collective-permute-start.12 = (bf16[3072,128]{1,0:T(8,128)(2,1)S(1)}, bf16[3072,128]{1,0:T(8,128)(2,1)S(1)}, u32[]{:S(2)}, u32[]{:S(2)}) collective-permute-start(bf16[3072,128]{1,0:T(8,128)(2,1)S(1)} %get-tuple-element.74), channel_id=1, source_target_pairs={{0,1},{1,0},{2,3},{3,2},{4,5},{5,4},{6,7},{7,6},{8,9},{9,8},{10,11... | collective-permute-start | bytes 2359304 | tf_op jit(solution)/shard_map/ppermute | solution.py:416
  137.0 3.1 %collective-permute-start.17 = (bf16[1536,128]{1,0:T(8,128)(2,1)S(1)}, bf16[1536,128]{1,0:T(8,128)(2,1)S(1)}, u32[]{:S(2)}, u32[]{:S(2)}) collective-permute-start(bf16[1536,128]{1,0:T(8,128)(2,1)S(1)} %get-tuple-element.84), channel_id=1, source_target_pairs={{0,1},{1,0},{2,3},{3,2},{4,5},{5,4},{6,7},{7,6},{8,9},{9,8},{10,11... | collective-permute-start | bytes 1179656 | tf_op jit(solution)/shard_map/ppermute | solution.py:416
  188.8 5.7 %collective-permute-start.18 = (bf16[64,72,128]{2,1,0:T(8,128)(2,1)S(1)}, bf16[64,72,128]{2,1,0:T(8,128)(2,1)S(1)}, u32[]{:S(2)}, u32[]{:S(2)}) collective-permute-start(bf16[64,72,128]{2,1,0:T(8,128)(2,1)S(1)} %all_to_all.16.own), channel_id=1, source_target_pairs={{0,1},{1,0},{2,3},{3,2},{4,5},{5,4},{6,7},{7,6},{8,9},{9,8},{10,11... | collective-permute-start | bytes 3538952 | tf_op jit(solution)/shard_map/ppermute | solution.py:416

commit v9 on v7

--- a/solution.py
+++ b/solution.py
@@ -485,6 +485,7 @@
         compiler_params=pltpu.CompilerParams(vmem_limit_bytes=28 * MIB),
         cost_estimate=pl.CostEstimate(flops=4 * 10**9, bytes_accessed=26 * MIB, transcendentals=0),
     )(g2m_src, halo_send, received, w_embed, g_mix, w_m[0])
+    mine_0, *returned_1 = lax.optimization_barrier((mine_0, *returned_1))
     shown_0 = show(mine_0)
     mesh_0, sent_0, slope_0 = kernel_call(
         mesh_body, [rows_bf16] * 3, [SM] + [VM] * 3, flops=2 * 10**9, moved=12 * MIB, limit=24,

time: 203 us -> 195 us (0.961)
  local copies, waits for them, and re-layouts: 22.2 us -> 16.8 us
  starting transfers between devices: 45.3 us -> 42.4 us
    unnamed x42 -> x28, local copies, waits for them, and re-layouts: 6.5 us -> 2.46 us
    all_to_all x1, waiting for transfers between devices: 24.3 us -> 21.7 us  [exchange(): return lax.all_to_all(parts, axes, split_axis=0, concat_axis=0, tiled=True)]
  transfers between devices with their start and end apart: 20 -> 20, of which waited for: 4 -> 4; matrix products, arithmetic and copies ran while one was open for 8% -> 7% of each run, Pallas kernels for 17% -> 23%
where the time goes in v9:
time: 195 us; the launch traced here: 194 us
  Pallas kernels  57.5 us (29%)
  blocking collectives  48.2 us (25%)
  starting transfers between devices  42.4 us (22%)
  waiting for transfers between devices  28.2 us (14%)
  local copies, waits for them, and re-layouts  16.8 us (9%)
    all_to_all x2, blocking collectives, exchange(): return lax.all_to_all(parts, axes, split_axis=0, concat_axis=0, tiled=True)  48.2 us
    ppermute x16, starting transfers between devices, shift(): lax.ppermute(value, axis, [(i, (i + steps) % count) for i in range(count)])  25.5 us
    all_to_all x1, waiting for transfers between devices, exchange(): return lax.all_to_all(parts, axes, split_axis=0, concat_axis=0, tiled=True)  21.7 us
    pallas_call x1, Pallas kernels, on_device(): pl.pallas_call(encode_body, grid=(4,), out_shape=[pltpu.HBM((CHAN, GRID_R...  12.1 us
    all_to_all x1, starting transfers between devices, exchange(): return lax.all_to_all(parts, axes, split_axis=0, concat_axis=0, tiled=True)  11.9 us
    pallas_call x1, Pallas kernels, on_device(): pl.pallas_call(final_body, grid=(4,), out_shape=[jax.ShapeDtypeStruct((SL...  11.9 us
    pallas_call x1, Pallas kernels, on_device(): kernel_call(grads_body, [rows_bf16, ((3 * SLABS, 128), BF16), ((3 * SLABS...  6.06 us
    pallas_call x1, Pallas kernels, on_device(): kernel_call(backward_body, [rows_bf16, rows_f32, rows_f32] + [halo] * 4,...  6 us
  transfers between devices with their start and end apart: 20, of which 4 were waited for; matrix products, arithmetic and copies ran while one was open for 7% of the time, Pallas kernels for 23%

profile of v9, /device:TPU:1, one launch (start us, length us, event | category | flops | bytes accessed | tf_op | source)
XLA Modules:
  0.0 194.0 jit_solution(14333534954513195691)
XLA Ops:
  0.6 5.9 %shard_map.138 = bf16[128,115,128]{2,1,0:T(8,128)(2,1)} custom-call(s32[1,128]{1,0:T(1,128)} %send.1, bf16[227,8192]{1,0:T(8,128)(2,1)} %bitcast.22), custom_call_target="tpu_custom_call" | custom-call | bytes 8388608 | tf_op jit(solution)/shard_map/pallas_call | solution.py:438
  6.6 11.9 %all-to-all-start = ((bf16[128,115,128]{2,1,0:T(8,128)(2,1)}), bf16[128,115,128]{2,1,0:T(8,128)(2,1)}, u32[]{:S(2)}, u32[]{:S(2)}) async-start(bf16[128,115,128]{2,1,0:T(8,128)(2,1)} %shard_map.138), calls=%async_computation | async-start | bytes 7864320 | tf_op jit(solution)/shard_map/all_to_all | solution.py:420
  18.5 0.0 copy-done.11
  18.5 0.1 copy.31.source
  18.6 2.6 %copy.25 = bf16[16,64,6,64]{3,2,1,0:T(8,128)(2,1)} copy(bf16[16,64,6,64]{3,1,2,0:T(8,128)(2,1)S(1)} %bitcast.24) | data formatting | bytes 1572864 | tf_op jit(solution)/shard_map/transpose | solution.py:452
  21.2 3.1 %reshape.31.coeffs = bf16[16,64,384]{2,1,0:T(8,128)(2,1)S(1)} reshape(bf16[16,64,6,64]{3,2,1,0:T(8,128)(2,1)} %copy.25) | data formatting | bytes 1572864 | tf_op jit(solution)/shard_map/reshape | solution.py:452
  24.4 0.0 copy-start.3
  24.4 2.2 %slice_bitcast_fusion = (bf16[512,512]{1,0:T(8,128)(2,1)S(1)}, bf16[512,512]{1,0:T(8,128)(2,1)S(1)}, bf16[512,512]{1,0:T(8,128)(2,1)S(1)}, bf16[512,512]{1,0:T(8,128)(2,1)}) fusion(bf16[2,512,512]{2,1,0:T(8,128)(2,1)S(1)} %copy-done.10, bf16[2,512,512]{2,1,0:T(8,128)(2,1)} %param.20), kind=kLoop, calls=%fused_computation | loop fusion | bytes 4194304 | tf_op jit(solution)/shard_map/squeeze | solution.py:435
  26.6 5.1 %shard_map.139 = (f32[1024,512]{1,0:T(8,128)S(1)}, bf16[4,64,512]{2,1,0:T(8,128)(2,1)}, bf16[4,64,512]{2,1,0:T(8,128)(2,1)}, bf16[4,64,512]{2,1,0:T(8,128)(2,1)}, bf16[4,64,512]{2,1,0:T(8,128)(2,1)}) custom-call(s32[16,6]{1,0:T(8,128)S(1)} %copy.31.source, bf16[1024,512]{1,0:T(8,128)(2,1)S(1)} %copy-done.3, bf16[512,512]{1,0:T(8,128)(2,1)S(1)} %get-tuple-element.96.up, ...), custom_call_target="tpu_custom_call" | custom-call | flops 2000000000 | bytes 8388608 | tf_op jit(solution)/shard_map/pallas_call | solution.py:454
  31.7 1.3 copy-done.6
  33.0 5.6 %collective-permute-start = (bf16[4,64,512]{2,1,0:T(8,128)(2,1)}, bf16[4,64,512]{2,1,0:T(8,128)(2,1)}, u32[]{:S(2)}, u32[]{:S(2)}) collective-permute-start(bf16[4,64,512]{2,1,0:T(8,128)(2,1)} %get-tuple-element.57), channel_id=1, source_target_pairs={{0,120},{8,0},{16,8},{24,16},{32,24},{40,32},{48,40},{56,48},{64,5... | collective-permute-start | bytes 786440 | tf_op jit(solution)/shard_map/ppermute | solution.py:404
  38.5 0.0 collective-permute-start.1
  38.5 0.6 collective-permute-start.2
  39.2 1.1 collective-permute-start.3
  40.3 3.1 %copy.24 = bf16[16,64,8,64]{3,2,1,0:T(8,128)(2,1)} copy(bf16[16,64,8,64]{3,1,2,0:T(8,128)(2,1)S(1)} %bitcast.23) | data formatting | bytes 2097152 | tf_op jit(solution)/shard_map/transpose | solution.py:451
  43.4 3.2 %reshape.30.coeffs = bf16[16,64,512]{2,1,0:T(8,128)(2,1)S(1)} reshape(bf16[16,64,8,64]{3,2,1,0:T(8,128)(2,1)} %copy.24) | data formatting | bytes 2097152 | tf_op jit(solution)/shard_map/reshape | solution.py:451
  46.6 0.1 copy.28.source
  46.7 21.7 %all-to-all-done.packed = bf16[128,115,128]{2,1,0:T(8,128)(2,1)} async-done(((bf16[128,115,128]{2,1,0:T(8,128)(2,1)}), bf16[128,115,128]{2,1,0:T(8,128)(2,1)}, u32[]{:S(2)}, u32[]{:S(2)}) %all-to-all-start) | async-done | bytes 3768352 | tf_op jit(solution)/shard_map/all_to_all | solution.py:420
  68.4 0.9 copy-done.5
  69.4 12.1 %shard_map.140 = (bf16[227,8192]{1,0:T(8,128)(2,1)}, bf16[8192,512]{1,0:T(8,128)(2,1)}, bf16[8192,512]{1,0:T(8,128)(2,1)S(1)}, bf16[4,64,512]{2,1,0:T(8,128)(2,1)S(1)}) custom-call(s32[16,8]{1,0:T(8,128)S(1)} %copy.28.source, s32[1,4]{1,0:T(1,128)S(1)} %copy-done.2, bf16[128,115,128]{2,1,0:T(8,128)(2,1)} %all-to-all-done.packed, ...), custom_call_target="tpu_custom_call" | custom-call | flops 4000000000 | bytes 27262976 | tf_op jit(solution)/shard_map/pallas_call | solution.py:462
  81.4 0.0 collective-permute-done.r0
  81.4 0.0 collective-permute-done.1.r1
  81.4 0.0 collective-permute-done.2.r2
  81.4 0.0 collective-permute-done.3.r3
  81.5 0.1 collective-permute-start.4
  81.5 4.8 %collective-permute-start.5 = (bf16[4,64,512]{2,1,0:T(8,128)(2,1)S(1)}, bf16[4,64,512]{2,1,0:T(8,128)(2,1)S(1)}, u32[]{:S(2)}, u32[]{:S(2)}) collective-permute-start(bf16[4,64,512]{2,1,0:T(8,128)(2,1)S(1)} %get-tuple-element.61), channel_id=1, source_target_pairs={{0,120},{8,0},{16,8},{24,16},{32,24},{40,32},{48,40},{56,48},{64,5... | collective-permute-start | bytes 786440 | tf_op jit(solution)/shard_map/ppermute | solution.py:404
  86.3 1.8 collective-permute-start.6
  88.1 0.1 collective-permute-start.7
  88.2 3.3 %shard_map.141 = (bf16[1024,512]{1,0:T(8,128)(2,1)S(1)}, bf16[1024,512]{1,0:T(8,128)(2,1)S(1)}, bf16[1024,512]{1,0:T(8,128)(2,1)S(1)}) custom-call(s32[16,8]{1,0:T(8,128)S(1)} %copy.28.source, bf16[8192,512]{1,0:T(8,128)(2,1)S(1)} %get-tuple-element.54.embedded, bf16[16,64,512]{2,1,0:T(8,128)(2,1)S(1)} %reshape.30.coeffs, ...), custom_call_target="tpu_custom_call" | custom-call | flops 2000000000 | bytes 12582912 | tf_op jit(solution)/shard_map/pallas_call | solution.py:490
  91.5 0.0 collective-permute-done.4.n0
  91.6 0.0 collective-permute-done.5.n1
  91.6 0.0 collective-permute-done.6.n2
  91.6 2.7 %collective-permute-done.7.n3 = bf16[4,64,512]{2,1,0:T(8,128)(2,1)S(1)} collective-permute-done((bf16[4,64,512]{2,1,0:T(8,128)(2,1)S(1)}, bf16[4,64,512]{2,1,0:T(8,128)(2,1)S(1)}, u32[]{:S(2)}, u32[]{:S(2)}) %collective-permute-start.7) | collective-permute-done | bytes 262176 | tf_op jit(solution)/shard_map/ppermute | solution.py:404
  94.2 4.0 %shard_map.142 = (bf16[1024,512]{1,0:T(8,128)(2,1)S(1)}, bf16[1024,512]{1,0:T(8,128)(2,1)S(1)}, bf16[1024,512]{1,0:T(8,128)(2,1)S(1)}, bf16[1024,512]{1,0:T(8,128)(2,1)S(1)}, bf16[4,64,512]{2,1,0:T(8,128)(2,1)S(1)}) custom-call(s32[16,6]{1,0:T(8,128)S(1)} %copy.31.source, s32[1,4]{1,0:T(1,128)S(1)} %copy-done.2, ...), custom_call_target="tpu_custom_call" | custom-call | flops 2000000000 | bytes 10485760 | tf_op jit(solution)/shard_map/pallas_call | solution.py:494
  98.2 0.0 collective-permute-start.10
  98.3 1.0 collective-permute-start.11
  99.3 0.0 collective-permute-start.8
  99.3 4.8 %collective-permute-start.9 = (bf16[4,64,512]{2,1,0:T(8,128)(2,1)S(1)}, bf16[4,64,512]{2,1,0:T(8,128)(2,1)S(1)}, u32[]{:S(2)}, u32[]{:S(2)}) collective-permute-start(bf16[4,64,512]{2,1,0:T(8,128)(2,1)S(1)} %get-tuple-element.65), channel_id=1, source_target_pairs={{0,120},{8,0},{16,8},{24,16},{32,24},{40,32},{48,40},{56,48},{64,5... | collective-permute-start | bytes 786440 | tf_op jit(solution)/shard_map/ppermute | solution.py:404
  104.1 6.0 %shard_map.143 = (bf16[1024,512]{1,0:T(8,128)(2,1)S(1)}, f32[1024,512]{1,0:T(8,128)S(1)}, f32[1024,512]{1,0:T(8,128)S(1)}, bf16[4,64,512]{2,1,0:T(8,128)(2,1)S(1...) custom-call(s32[16,6]{1,0:T(8,128)S(1)} %copy.31.source, ...), custom_call_target="tpu_custom_call" | custom-call | flops 2000000000 | bytes 16777216 | tf_op jit(solution)/shard_map/pallas_call | solution.py:500
  110.1 0.1 collective-permute-start.13
  110.2 0.0 collective-permute-done.10.n2
  110.2 1.4 collective-permute-start.14
  111.6 0.0 collective-permute-done.11.n3
  111.6 4.1 %collective-permute-start.15 = (bf16[4,64,512]{2,1,0:T(8,128)(2,1)S(1)}, bf16[4,64,512]{2,1,0:T(8,128)(2,1)S(1)}, u32[]{:S(2)}, u32[]{:S(2)}) collective-permute-start(bf16[4,64,512]{2,1,0:T(8,128)(2,1)S(1)} %get-tuple-element.82), channel_id=1, source_target_pairs={{0,7},{1,0},{2,1},{3,2},{4,3},{5,4},{6,5},{7,6},{8,15},{9,8},{10,9... | collective-permute-start | bytes 786440 | tf_op jit(solution)/shard_map/ppermute | solution.py:404
  115.7 0.0 collective-permute-done.8.n0
  115.7 0.0 collective-permute-start.16
  115.7 0.0 collective-permute-done.9.n1
  115.7 6.1 %shard_map.144 = (bf16[1024,512]{1,0:T(8,128)(2,1)}, bf16[3072,128]{1,0:T(8,128)(2,1)S(1)}, bf16[3072,128]{1,0:T(8,128)(2,1)S(1)}) custom-call(s32[1]{0:T(128)} %bitcast.1.odd, s32[16,6]{1,0:T(8,128)S(1)} %copy.31.source, bf16[1024,512]{1,0:T(8,128)(2,1)S(1)} %get-tuple-element.64.sent, bf16[4,64,512]{2,1,0:T(8,128)(2,1)S(1)} %collective-permute-done.8.n0, ...), custom_call_target="tpu_custom_call" | custom-call | flops 4000000000 | bytes 14680064 | tf_op jit(solution)/shard_map/pallas_call | solution.py:506
  121.8 0.5 collective-permute-start.12
  122.3 0.0 collective-permute-done.13.r0
  122.3 0.0 collective-permute-done.14.r1
  122.3 0.0 collective-permute-done.15.r2
  122.3 0.0 collective-permute-done.16.r3
  122.3 11.9 %shard_map.145 = (bf16[1536,128]{1,0:T(8,128)(2,1)S(1)}, bf16[1536,128]{1,0:T(8,128)(2,1)S(1)}) custom-call(s32[1]{0:T(128)} %bitcast.1.odd, s32[16,8]{1,0:T(8,128)S(1)} %copy.28.source, s32[1,4]{1,0:T(1,128)S(1)} %copy-done.2, f32[1024,512]{1,0:T(8,128)S(1)} %get-tuple-element.79.own, bf16[4,64,512]{2,1,0:T(8,128)(2,1)S(1)} %collective-permute-done.13.r0, ...), custom_call_target="tpu_custom_call" | custom-call | flops 4000000000 | bytes 25165824 | tf_op jit(solution)/shard_map/pallas_call | solution.py:516
  134.2 1.2 collective-permute-start.17
  135.4 1.3 collective-permute-done.17
  136.8 0.0 collective-permute-done.12
  136.8 0.3 shard_map.146
  137.1 25.7 %all_to_all.15.parts = bf16[64,72,128]{2,1,0:T(8,128)(2,1)S(1)} all-to-all(bf16[64,72,128]{2,1,0:T(8,128)(2,1)S(1)} %shard_map.146), channel_id=1, replica_groups=mesh['wide'=16,'x'=4,'core'=2] {'wide','x'}, dimensions={0} | all-to-all | bytes 2359296 | tf_op jit(solution)/shard_map/all_to_all | solution.py:420
  162.8 0.3 shard_map.147
  163.1 22.5 %all_to_all.16.own = bf16[64,72,128]{2,1,0:T(8,128)(2,1)S(1)} all-to-all(bf16[64,72,128]{2,1,0:T(8,128)(2,1)S(1)} %shard_map.147), channel_id=1, replica_groups=mesh['wide'=16,'x'=4,'core'=2] {'wide','x'}, dimensions={0} | all-to-all | bytes 2359296 | tf_op jit(solution)/shard_map/all_to_all | solution.py:420
  185.6 3.2 %collective-permute-start.18 = (bf16[64,72,128]{2,1,0:T(8,128)(2,1)S(1)}, bf16[64,72,128]{2,1,0:T(8,128)(2,1)S(1)}, u32[]{:S(2)}, u32[]{:S(2)}) collective-permute-start(bf16[64,72,128]{2,1,0:T(8,128)(2,1)S(1)} %all_to_all.16.own), channel_id=1, source_target_pairs={{0,1},{1,0},{2,3},{3,2},{4,5},{5,4},{6,7},{7,6},{8,9},{9,8},{10,11... | collective-permute-start | bytes 3538952 | tf_op jit(solution)/shard_map/ppermute | solution.py:416
  188.8 2.5 %collective-permute-done.18.other = bf16[64,72,128]{2,1,0:T(8,128)(2,1)S(1)} collective-permute-done((bf16[64,72,128]{2,1,0:T(8,128)(2,1)S(1)}, bf16[64,72,128]{2,1,0:T(8,128)(2,1)S(1)}, u32[]{:S(2)}, u32[]{:S(2)}) %collective-permute-start.18) | collective-permute-done | bytes 1179680 | tf_op jit(solution)/shard_map/ppermute | solution.py:416
  191.3 2.7 %shard_map.148 = (f32[227,512]{1,0:T(8,128)}, f32[2,512,512]{2,1,0:T(8,128)}, f32[2,512,512]{2,1,0:T(8,128)}) custom-call(s32[1]{0:T(128)} %bitcast.1.odd, bf16[64,72,128]{2,1,0:T(8,128)(2,1)S(1)} %all_to_all.16.own, bf16[64,72,128]{2,1,0:T(8,128)(2,1)S(1)} %collective-permute-done.18.other), custom_call_target="tpu_custom_call" | custom-call | bytes 7340032 | tf_op jit(solution)/shard_map/pallas_call | solution.py:547
  (22 shorter events, 0.0 us)
Async XLA Ops:
  6.6 11.9 %copy-start.11 = (s32[16,6]{0,1:T(8,128)S(1)}, s32[16,6]{0,1:T(8,128)}, u32[]{:S(2)}) copy-start(s32[16,6]{0,1:T(8,128)} %param.16) | copy-start | bytes 1156
  6.6 12.0 %copy-start.9 = (bf16[16,6,64,64]{3,2,1,0:T(8,128)(2,1)S(1)}, bf16[16,6,64,64]{3,2,1,0:T(8,128)(2,1)}, u32[]{:S(2)}) copy-start(bf16[16,6,64,64]{3,2,1,0:T(8,128)(2,1)} %param.17) | copy-start | bytes 2359300
  6.6 61.9 %all-to-all-start = ((bf16[128,115,128]{2,1,0:T(8,128)(2,1)}), bf16[128,115,128]{2,1,0:T(8,128)(2,1)}, u32[]{:S(2)}, u32[]{:S(2)}) async-start(bf16[128,115,128]{2,1,0:T(8,128)(2,1)} %shard_map.138), calls=%async_computation | async-start | bytes 7864320 | tf_op jit(solution)/shard_map/all_to_all | solution.py:420
  21.2 3.2 %copy-start.10 = (bf16[2,512,512]{2,1,0:T(8,128)(2,1)S(1)}, bf16[2,512,512]{2,1,0:T(8,128)(2,1)}, u32[]{:S(2)}) copy-start(bf16[2,512,512]{2,1,0:T(8,128)(2,1)} %param.19) | copy-start | bytes 3145732
  24.4 2.2 %copy-start.3 = (bf16[1024,512]{1,0:T(8,128)(2,1)S(1)}, bf16[1024,512]{1,0:T(8,128)(2,1)}, u32[]{:S(2)}) copy-start(bf16[1024,512]{1,0:T(8,128)(2,1)} %cot.2) | copy-start | bytes 3145732
  26.6 13.7 %copy-start.8 = (bf16[16,8,64,64]{3,2,1,0:T(8,128)(2,1)S(1)}, bf16[16,8,64,64]{3,2,1,0:T(8,128)(2,1)}, u32[]{:S(2)}) copy-start(bf16[16,8,64,64]{3,2,1,0:T(8,128)(2,1)} %param.15) | copy-start | bytes 3145732
  31.6 1.3 copy-start.6
  33.0 48.5 %collective-permute-start = (bf16[4,64,512]{2,1,0:T(8,128)(2,1)}, bf16[4,64,512]{2,1,0:T(8,128)(2,1)}, u32[]{:S(2)}, u32[]{:S(2)}) collective-permute-start(bf16[4,64,512]{2,1,0:T(8,128)(2,1)} %get-tuple-element.57), channel_id=1, source_target_pairs={{0,120},{8,0},{16,8},{24,16},{32,24},{40,32},{48,40},{56,48},{64,5... | collective-permute-start | bytes 786440 | tf_op jit(solution)/shard_map/ppermute | solution.py:404
  38.5 42.9 %collective-permute-start.1 = (bf16[4,64,512]{2,1,0:T(8,128)(2,1)}, bf16[4,64,512]{2,1,0:T(8,128)(2,1)}, u32[]{:S(2)}, u32[]{:S(2)}) collective-permute-start(bf16[4,64,512]{2,1,0:T(8,128)(2,1)} %get-tuple-element.58), channel_id=1, source_target_pairs={{0,8},{8,16},{16,24},{24,32},{32,40},{40,48},{48,56},{56,64},{64,7... | collective-permute-start | bytes 786440 | tf_op jit(solution)/shard_map/ppermute | solution.py:404
  38.5 42.9 %collective-permute-start.2 = (bf16[4,64,512]{2,1,0:T(8,128)(2,1)}, bf16[4,64,512]{2,1,0:T(8,128)(2,1)}, u32[]{:S(2)}, u32[]{:S(2)}) collective-permute-start(bf16[4,64,512]{2,1,0:T(8,128)(2,1)} %get-tuple-element.59), channel_id=1, source_target_pairs={{0,7},{1,0},{2,1},{3,2},{4,3},{5,4},{6,5},{7,6},{8,15},{9,8},{10,9... | collective-permute-start | bytes 786440 | tf_op jit(solution)/shard_map/ppermute | solution.py:404
  39.2 42.3 %collective-permute-start.3 = (bf16[4,64,512]{2,1,0:T(8,128)(2,1)}, bf16[4,64,512]{2,1,0:T(8,128)(2,1)}, u32[]{:S(2)}, u32[]{:S(2)}) collective-permute-start(bf16[4,64,512]{2,1,0:T(8,128)(2,1)} %get-tuple-element.60), channel_id=1, source_target_pairs={{0,1},{1,2},{2,3},{3,4},{4,5},{5,6},{6,7},{7,0},{8,9},{9,10},{10,1... | collective-permute-start | bytes 786440 | tf_op jit(solution)/shard_map/ppermute | solution.py:404
  43.4 3.2 %copy-start.12 = (s32[16,8]{0,1:T(8,128)S(1)}, s32[16,8]{0,1:T(8,128)}, u32[]{:S(2)}) copy-start(s32[16,8]{0,1:T(8,128)} %param.14) | copy-start | bytes 1540
  43.4 25.0 %copy-start.2 = (s32[1,4]{1,0:T(1,128)S(1)}, s32[1,4]{1,0:T(1,128)}, u32[]{:S(2)}) copy-start(s32[1,4]{1,0:T(1,128)} %shown.7) | copy-start | bytes 52
  68.4 0.9 copy-start.5
  81.5 10.1 %collective-permute-start.4 = (bf16[4,64,512]{2,1,0:T(8,128)(2,1)S(1)}, bf16[4,64,512]{2,1,0:T(8,128)(2,1)S(1)}, u32[]{:S(2)}, u32[]{:S(2)}) collective-permute-start(bf16[4,64,512]{2,1,0:T(8,128)(2,1)S(1)} %get-tuple-element.61), channel_id=1, source_target_pairs={{0,8},{8,16},{16,24},{24,32},{32,40},{40,48},{48,56},{56,64},{64,7... | collective-permute-start | bytes 786440 | tf_op jit(solution)/shard_map/ppermute | solution.py:404
  81.5 10.0 %collective-permute-start.5 = (bf16[4,64,512]{2,1,0:T(8,128)(2,1)S(1)}, bf16[4,64,512]{2,1,0:T(8,128)(2,1)S(1)}, u32[]{:S(2)}, u32[]{:S(2)}) collective-permute-start(bf16[4,64,512]{2,1,0:T(8,128)(2,1)S(1)} %get-tuple-element.61), channel_id=1, source_target_pairs={{0,120},{8,0},{16,8},{24,16},{32,24},{40,32},{48,40},{56,48},{64,5... | collective-permute-start | bytes 786440 | tf_op jit(solution)/shard_map/ppermute | solution.py:404
  86.3 5.3 %collective-permute-start.6 = (bf16[4,64,512]{2,1,0:T(8,128)(2,1)S(1)}, bf16[4,64,512]{2,1,0:T(8,128)(2,1)S(1)}, u32[]{:S(2)}, u32[]{:S(2)}) collective-permute-start(bf16[4,64,512]{2,1,0:T(8,128)(2,1)S(1)} %get-tuple-element.61), channel_id=1, source_target_pairs={{0,1},{1,2},{2,3},{3,4},{4,5},{5,6},{6,7},{7,0},{8,9},{9,10},{10,1... | collective-permute-start | bytes 786440 | tf_op jit(solution)/shard_map/ppermute | solution.py:404
  88.1 6.1 %collective-permute-start.7 = (bf16[4,64,512]{2,1,0:T(8,128)(2,1)S(1)}, bf16[4,64,512]{2,1,0:T(8,128)(2,1)S(1)}, u32[]{:S(2)}, u32[]{:S(2)}) collective-permute-start(bf16[4,64,512]{2,1,0:T(8,128)(2,1)S(1)} %get-tuple-element.61), channel_id=1, source_target_pairs={{0,7},{1,0},{2,1},{3,2},{4,3},{5,4},{6,5},{7,6},{8,15},{9,8},{10,9... | collective-permute-start | bytes 786440 | tf_op jit(solution)/shard_map/ppermute | solution.py:404
  88.2 6.0 %copy-start.1 = (bf16[512,512]{1,0:T(8,128)(2,1)S(1)}, bf16[512,512]{1,0:T(8,128)(2,1)}, u32[]{:S(2)}) copy-start(bf16[512,512]{1,0:T(8,128)(2,1)} %get-tuple-element.97.up) | copy-start | bytes 1572868
  94.2 9.8 %copy-start.4 = (bf16[1024,512]{1,0:T(8,128)(2,1)S(1)}, bf16[1024,512]{1,0:T(8,128)(2,1)}, u32[]{:S(2)}) copy-start(bf16[1024,512]{1,0:T(8,128)(2,1)} %cot.2) | copy-start | bytes 3145732
  94.2 9.8 %copy-start.7 = (f32[1024,512]{1,0:T(8,128)S(1)}, f32[1024,512]{1,0:T(8,128)}, u32[]{:S(2)}) copy-start(f32[1024,512]{1,0:T(8,128)} %copy-done.6) | copy-start | bytes 6291460
  98.2 12.0 %collective-permute-start.10 = (bf16[4,64,512]{2,1,0:T(8,128)(2,1)S(1)}, bf16[4,64,512]{2,1,0:T(8,128)(2,1)S(1)}, u32[]{:S(2)}, u32[]{:S(2)}) collective-permute-start(bf16[4,64,512]{2,1,0:T(8,128)(2,1)S(1)} %get-tuple-element.65), channel_id=1, source_target_pairs={{0,1},{1,2},{2,3},{3,4},{4,5},{5,6},{6,7},{7,0},{8,9},{9,10},{10,1... | collective-permute-start | bytes 786440 | tf_op jit(solution)/shard_map/ppermute | solution.py:404
  98.3 13.4 %collective-permute-start.11 = (bf16[4,64,512]{2,1,0:T(8,128)(2,1)S(1)}, bf16[4,64,512]{2,1,0:T(8,128)(2,1)S(1)}, u32[]{:S(2)}, u32[]{:S(2)}) collective-permute-start(bf16[4,64,512]{2,1,0:T(8,128)(2,1)S(1)} %get-tuple-element.65), channel_id=1, source_target_pairs={{0,7},{1,0},{2,1},{3,2},{4,3},{5,4},{6,5},{7,6},{8,15},{9,8},{10,9... | collective-permute-start | bytes 786440 | tf_op jit(solution)/shard_map/ppermute | solution.py:404
  99.3 16.4 %collective-permute-start.8 = (bf16[4,64,512]{2,1,0:T(8,128)(2,1)S(1)}, bf16[4,64,512]{2,1,0:T(8,128)(2,1)S(1)}, u32[]{:S(2)}, u32[]{:S(2)}) collective-permute-start(bf16[4,64,512]{2,1,0:T(8,128)(2,1)S(1)} %get-tuple-element.65), channel_id=1, source_target_pairs={{0,8},{8,16},{16,24},{24,32},{32,40},{40,48},{48,56},{56,64},{64,7... | collective-permute-start | bytes 786440 | tf_op jit(solution)/shard_map/ppermute | solution.py:404
  99.3 16.4 %collective-permute-start.9 = (bf16[4,64,512]{2,1,0:T(8,128)(2,1)S(1)}, bf16[4,64,512]{2,1,0:T(8,128)(2,1)S(1)}, u32[]{:S(2)}, u32[]{:S(2)}) collective-permute-start(bf16[4,64,512]{2,1,0:T(8,128)(2,1)S(1)} %get-tuple-element.65), channel_id=1, source_target_pairs={{0,120},{8,0},{16,8},{24,16},{32,24},{40,32},{48,40},{56,48},{64,5... | collective-permute-start | bytes 786440 | tf_op jit(solution)/shard_map/ppermute | solution.py:404
  110.1 12.2 %collective-permute-start.13 = (bf16[4,64,512]{2,1,0:T(8,128)(2,1)S(1)}, bf16[4,64,512]{2,1,0:T(8,128)(2,1)S(1)}, u32[]{:S(2)}, u32[]{:S(2)}) collective-permute-start(bf16[4,64,512]{2,1,0:T(8,128)(2,1)S(1)} %get-tuple-element.80), channel_id=1, source_target_pairs={{0,120},{8,0},{16,8},{24,16},{32,24},{40,32},{48,40},{56,48},{64,5... | collective-permute-start | bytes 786440 | tf_op jit(solution)/shard_map/ppermute | solution.py:404
  110.2 12.1 %collective-permute-start.14 = (bf16[4,64,512]{2,1,0:T(8,128)(2,1)S(1)}, bf16[4,64,512]{2,1,0:T(8,128)(2,1)S(1)}, u32[]{:S(2)}, u32[]{:S(2)}) collective-permute-start(bf16[4,64,512]{2,1,0:T(8,128)(2,1)S(1)} %get-tuple-element.81), channel_id=1, source_target_pairs={{0,8},{8,16},{16,24},{24,32},{32,40},{40,48},{48,56},{56,64},{64,7... | collective-permute-start | bytes 786440 | tf_op jit(solution)/shard_map/ppermute | solution.py:404
  111.6 10.7 %collective-permute-start.15 = (bf16[4,64,512]{2,1,0:T(8,128)(2,1)S(1)}, bf16[4,64,512]{2,1,0:T(8,128)(2,1)S(1)}, u32[]{:S(2)}, u32[]{:S(2)}) collective-permute-start(bf16[4,64,512]{2,1,0:T(8,128)(2,1)S(1)} %get-tuple-element.82), channel_id=1, source_target_pairs={{0,7},{1,0},{2,1},{3,2},{4,3},{5,4},{6,5},{7,6},{8,15},{9,8},{10,9... | collective-permute-start | bytes 786440 | tf_op jit(solution)/shard_map/ppermute | solution.py:404
  115.7 6.6 %collective-permute-start.16 = (bf16[4,64,512]{2,1,0:T(8,128)(2,1)S(1)}, bf16[4,64,512]{2,1,0:T(8,128)(2,1)S(1)}, u32[]{:S(2)}, u32[]{:S(2)}) collective-permute-start(bf16[4,64,512]{2,1,0:T(8,128)(2,1)S(1)} %get-tuple-element.83), channel_id=1, source_target_pairs={{0,1},{1,2},{2,3},{3,4},{4,5},{5,6},{6,7},{7,0},{8,9},{9,10},{10,1... | collective-permute-start | bytes 786440 | tf_op jit(solution)/shard_map/ppermute | solution.py:404
  115.7 6.6 %copy-start = (bf16[227,8192]{1,0:T(8,128)(2,1)S(1)}, bf16[227,8192]{1,0:T(8,128)(2,1)}, u32[]{:S(2)}) copy-start(bf16[227,8192]{1,0:T(8,128)(2,1)} %get-tuple-element.86.points) | copy-start | bytes 11157508
  121.8 15.0 %collective-permute-start.12 = (bf16[3072,128]{1,0:T(8,128)(2,1)S(1)}, bf16[3072,128]{1,0:T(8,128)(2,1)S(1)}, u32[]{:S(2)}, u32[]{:S(2)}) collective-permute-start(bf16[3072,128]{1,0:T(8,128)(2,1)S(1)} %get-tuple-element.78), channel_id=1, source_target_pairs={{0,1},{1,0},{2,3},{3,2},{4,5},{5,4},{6,7},{7,6},{8,9},{9,8},{10,11... | collective-permute-start | bytes 2359304 | tf_op jit(solution)/shard_map/ppermute | solution.py:416
  134.2 2.6 %collective-permute-start.17 = (bf16[1536,128]{1,0:T(8,128)(2,1)S(1)}, bf16[1536,128]{1,0:T(8,128)(2,1)S(1)}, u32[]{:S(2)}, u32[]{:S(2)}) collective-permute-start(bf16[1536,128]{1,0:T(8,128)(2,1)S(1)} %get-tuple-element.88), channel_id=1, source_target_pairs={{0,1},{1,0},{2,3},{3,2},{4,5},{5,4},{6,7},{7,6},{8,9},{9,8},{10,11... | collective-permute-start | bytes 1179656 | tf_op jit(solution)/shard_map/ppermute | solution.py:416
  185.6 5.7 %collective-permute-start.18 = (bf16[64,72,128]{2,1,0:T(8,128)(2,1)S(1)}, bf16[64,72,128]{2,1,0:T(8,128)(2,1)S(1)}, u32[]{:S(2)}, u32[]{:S(2)}) collective-permute-start(bf16[64,72,128]{2,1,0:T(8,128)(2,1)S(1)} %all_to_all.16.own), channel_id=1, source_target_pairs={{0,1},{1,0},{2,3},{3,2},{4,5},{5,4},{6,7},{7,6},{8,9},{9,8},{10,11... | collective-permute-start | bytes 3538952 | tf_op jit(solution)/shard_map/ppermute | solution.py:416
